TPU v7x, 32 devices: a whole 2x2x4 slice. The times are simulated.
32 devices in a mesh: img: 8 (over z, y), row: 4 (over x, core).
Axes of the slice: x: 2, y: 2, z: 4, core: 2. Of those that a mesh axis runs over, the one named last changes fastest.
Arguments:
- tokens: bfloat16 [8, 4064, 1024], P('img', 'row'), may hold values from -6 to 6
- counts: int32 [8, 8], P('img'), may hold values from 1 to 1024, 4032 in all within a row
- owner: int32 [8, 8], P('img'), may hold values from 0 to 7, each once within a row
- w_qkv: bfloat16 [1024, 3072], replicated, may hold values from -0.1875 to 0.1875
- qv_bias: float32 [2, 1024], replicated, may hold values from -3 to 3
- w_out: bfloat16 [1024, 1024], replicated, may hold values from -0.5 to 0.5
- out_bias: float32 [1024], replicated, may hold values from -3 to 3
- w_up: bfloat16 [1024, 4096], replicated, may hold values from -0.1875 to 0.1875
- up_bias: float32 [4096], replicated, may hold values from -3 to 3
- w_down: bfloat16 [4096, 1024], replicated, may hold values from -0.09375 to 0.09375
- down_bias: float32 [1024], replicated, may hold values from -3 to 3
- norm_gain: float32 [3, 1024], replicated, may hold values from 0.25 to 1.75
- norm_bias: float32 [3, 1024], replicated, may hold values from -2 to 2
- learn_in: bfloat16 [1024, 1024], replicated, may hold values from -0.1875 to 0.1875
- learn_in_bias: float32 [1024], replicated, may hold values from -3 to 3
- learn_out: bfloat16 [1024, 8], replicated, may hold values from -0.75 to 0.75
- learn_out_bias: float32 [8], replicated, may hold values from -3 to 3
- cotangent: float32 [8, 8, 8, 1024], P('img', 'row'), may hold values from -6 to 6
Outputs:
- learned: float32 [8, 8, 8, 1024], P('img', 'row')
- grad_tokens: float32 [8, 4064, 1024], P('img', 'row')
- grad_w_qkv: float32 [1024, 3072], P('img')
- grad_qv_bias: float32 [2, 1024], replicated
- grad_w_out: float32 [1024, 1024], P('img')
- grad_out_bias: float32 [1024], replicated
- grad_w_up: float32 [1024, 4096], P('img')
- grad_up_bias: float32 [4096], replicated
- grad_w_down: float32 [4096, 1024], P('img')
- grad_down_bias: float32 [1024], replicated
- grad_norm_gain: float32 [3, 1024], replicated
- grad_norm_bias: float32 [3, 1024], replicated
- grad_learn_in: float32 [1024, 1024], P('img')
- grad_learn_in_bias: float32 [1024], replicated
- grad_learn_out: float32 [1024, 8], P('img')
- grad_learn_out_bias: float32 [8], replicated
Inputs may be any that keep to these rules, and one draw needn't show every extreme that they name: counts[g, i] is the number of patches of image i of group g; each group's counts sum to 4032, and one image of each group has exactly 1024. Each row of owner is a permutation: image i of group g has its learned tokens at slot owner[g, i].
All inputs are finite; a program needn't handle non-finite values.
Results may differ from a plain program's by a relative error of at most 0.018.
Values may be sent and summed in bfloat16 or wider, within the bound.
A program may use at most 512 MiB of HBM per device.

v0:
```python
import jax
import jax.numpy as jnp
from jax import lax
from jax.sharding import PartitionSpec as P

HEADS = 16
HEAD = 64
LT = 8
IMGS = 8


highest = lax.Precision.HIGHEST
epsilon = 1e-06


def normalize(values, gain, shift):
    centre = values - jnp.mean(values, axis=-1, keepdims=True)
    spread = jnp.mean(centre * centre, axis=-1, keepdims=True)
    return centre * lax.rsqrt(spread + epsilon) * gain + shift


def smooth(values):
    return jax.nn.gelu(values, approximate=False)


def row_images(counts, device, local_rows, row_count):
    upper_end = counts * (device + 1) // row_count
    lower_end = counts * device // row_count
    run_ends = jnp.cumsum(upper_end - lower_end)
    positions = jnp.arange(local_rows, dtype=jnp.int32)
    return jnp.sum((positions[:, None] >= run_ends[None, :]).astype(jnp.int32), axis=1)


def split_heads(array, per_turn):
    return array.reshape(array.shape[0], HEADS // per_turn, per_turn, HEAD).transpose(1, 0, 2, 3)


def join_heads(array):
    turns, length, per_turn, head_size = array.shape
    return array.transpose(1, 0, 2, 3).reshape(length, turns * per_turn * head_size)


def attend(queries, key_all, value_all, allowed, per_turn):

    def one_turn(inputs):
        query_part, key_part, value_part = inputs
        scores = jnp.einsum(
            "qhd,khd->hqk", query_part, key_part, preferred_element_type=jnp.float32
        )
        scores = jnp.where(allowed[None], scores, -1e30)
        row_max = jnp.max(scores, axis=2, keepdims=True)
        exponent = jnp.exp(scores - row_max)
        row_total = jnp.sum(exponent, axis=2, keepdims=True)
        probability = (exponent / row_total).astype(jnp.bfloat16)
        output = jnp.einsum(
            "hqk,khd->qhd", probability, value_part, preferred_element_type=jnp.float32
        )
        return (output, (row_max + jnp.log(row_total))[:, :, 0])

    outputs, logsum = lax.map(
        one_turn,
        (
            split_heads(queries, per_turn),
            split_heads(key_all, per_turn),
            split_heads(value_all, per_turn),
        ),
    )
    return (join_heads(outputs), logsum)


def attend_back(queries, key_all, value_all, grad_low, logsum, allowed, per_turn):

    def one_turn(inputs):
        query_part, key_part, value_part, grad_part, logsum_part = inputs
        scores = jnp.einsum(
            "qhd,khd->hqk", query_part, key_part, preferred_element_type=jnp.float32
        )
        scores = jnp.where(allowed[None], scores, -1e30)
        probability = jnp.exp(scores - logsum_part[:, :, None])
        grad_weight = jnp.einsum(
            "qhd,khd->hqk", grad_part, value_part, preferred_element_type=jnp.float32
        )
        row_delta = jnp.sum(probability * grad_weight, axis=2, keepdims=True)
        grad_scores = (probability * (grad_weight - row_delta)).astype(jnp.bfloat16)
        grad_query = jnp.einsum(
            "hqk,khd->qhd", grad_scores, key_part, preferred_element_type=jnp.float32
        )
        grad_key = jnp.einsum(
            "hqk,qhd->khd", grad_scores, query_part, preferred_element_type=jnp.float32
        )
        grad_value = jnp.einsum(
            "hqk,qhd->khd",
            probability.astype(jnp.bfloat16),
            grad_part,
            preferred_element_type=jnp.float32,
        )
        return (grad_query, grad_key, grad_value)

    results = lax.map(
        one_turn,
        (
            split_heads(queries, per_turn),
            split_heads(key_all, per_turn),
            split_heads(value_all, per_turn),
            split_heads(grad_low, per_turn),
            logsum,
        ),
    )
    return (join_heads(results[0]), join_heads(results[1]), join_heads(results[2]))


def matmul(left, right):
    return jnp.dot(left, right, preferred_element_type=jnp.float32)


def on_device(
    tokens,
    counts,
    owner,
    w_qkv,
    qv_bias,
    w_out,
    out_bias,
    w_up,
    up_bias,
    w_down,
    down_bias,
    norm_gain,
    norm_bias,
    learn_in,
    learn_in_bias,
    learn_out,
    learn_out_bias,
    cotangent,
):
    width = tokens.shape[2]
    local_rows = tokens.shape[1]
    row_count = lax.axis_size("row")
    device = lax.axis_index("row")
    per_turn = 4
    group_counts = counts[0]
    image_here = row_images(group_counts, device, local_rows, row_count)

    def images_of(position):
        return row_images(group_counts, position, local_rows, row_count)

    image_all = jax.vmap(images_of)(jnp.arange(row_count, dtype=jnp.int32)).reshape(-1)
    allowed = image_here[:, None] == image_all[None, :]
    inputs_f32 = tokens[0].astype(jnp.float32)
    normed_one, back_one = jax.vjp(normalize, inputs_f32, norm_gain[0], norm_bias[0])
    normed_one_low = normed_one.astype(jnp.bfloat16)
    mixed = matmul(normed_one_low, w_qkv)
    queries = ((mixed[:, :width] + qv_bias[0]) * 0.125).astype(jnp.bfloat16)
    key_rows = mixed[:, width : 2 * width].astype(jnp.bfloat16)
    value_rows = (mixed[:, 2 * width :] + qv_bias[1]).astype(jnp.bfloat16)
    key_all, value_all = (
        lax.all_gather(key_rows, "row", axis=0, tiled=True),
        lax.all_gather(value_rows, "row", axis=0, tiled=True),
    )
    attended, logsum = attend(queries, key_all, value_all, allowed, per_turn)
    attended_low = attended.astype(jnp.bfloat16)
    hidden = inputs_f32 + matmul(attended_low, w_out) + out_bias
    normed_two, back_two = jax.vjp(normalize, hidden, norm_gain[1], norm_bias[1])
    normed_two_low = normed_two.astype(jnp.bfloat16)
    gated, back_gate = jax.vjp(smooth, matmul(normed_two_low, w_up) + up_bias)
    gated_low = gated.astype(jnp.bfloat16)
    result = hidden + matmul(gated_low, w_down) + down_bias
    normed_three, back_three = jax.vjp(normalize, result, norm_gain[2], norm_bias[2])
    normed_three_low = normed_three.astype(jnp.bfloat16)
    inner, back_inner = jax.vjp(smooth, matmul(normed_three_low, learn_in) + learn_in_bias)
    inner_low = inner.astype(jnp.bfloat16)
    maps = jax.nn.sigmoid(matmul(inner_low, learn_out) + learn_out_bias)
    maps_low = maps.astype(jnp.bfloat16)
    result_low = result.astype(jnp.bfloat16)
    member = (image_here[:, None] == jnp.arange(IMGS, dtype=jnp.int32)[None, :]).astype(
        jnp.bfloat16
    )
    spread_maps = (member[:, :, None] * maps_low[:, None, :]).reshape(local_rows, IMGS * LT)
    partial_value = matmul(spread_maps.T, result_low)
    select = (owner[0][:, None] == jnp.arange(IMGS, dtype=jnp.int32)[None, :]).astype(jnp.float32)
    scale = lax.rsqrt(group_counts.astype(jnp.float32))
    by_slot = jnp.dot(select.T, partial_value.reshape(IMGS, LT * width), precision=highest)
    arrived = lax.all_to_all(
        by_slot.astype(jnp.bfloat16), "row", split_axis=0, concat_axis=0, tiled=True
    ).astype(by_slot.dtype)
    slots_here = IMGS // row_count
    summed = jnp.sum(arrived.reshape(row_count, slots_here, LT * width), axis=0)
    slot_scale = jnp.dot(scale, select, precision=highest)
    scale_here = lax.dynamic_slice_in_dim(slot_scale, device * slots_here, slots_here)
    learned = (summed * scale_here[:, None]).reshape(1, slots_here, LT, width)
    incoming = lax.all_gather(
        cotangent[0].reshape(slots_here, LT * width).astype(jnp.bfloat16), "row", axis=0, tiled=True
    ).astype(jnp.float32)
    grad_pooled = jnp.dot(select, incoming, precision=highest) * scale[:, None]
    grad_pooled_low = grad_pooled.reshape(IMGS * LT, width).astype(jnp.bfloat16)
    grad_result = matmul(spread_maps, grad_pooled_low)
    grad_spread = matmul(result_low, grad_pooled_low.T)
    grad_maps = jnp.sum(
        grad_spread.reshape(local_rows, IMGS, LT) * member.astype(jnp.float32)[:, :, None], axis=1
    )
    grad_logit = grad_maps * maps * (1.0 - maps)
    grad_learn_out_bias = jnp.sum(grad_logit, axis=0)
    grad_logit_low = grad_logit.astype(jnp.bfloat16)
    grad_learn_out = matmul(inner_low.T, grad_logit_low)
    (grad_learn_pre,) = back_inner(matmul(grad_logit_low, learn_out.T))
    grad_learn_in_bias = jnp.sum(grad_learn_pre, axis=0)
    grad_learn_low = grad_learn_pre.astype(jnp.bfloat16)
    grad_learn_in = matmul(normed_three_low.T, grad_learn_low)
    grad_from_three, gain_three, shift_three = back_three(matmul(grad_learn_low, learn_in.T))
    grad_result = grad_result + grad_from_three
    grad_down_bias = jnp.sum(grad_result, axis=0)
    grad_result_low = grad_result.astype(jnp.bfloat16)
    grad_w_down = matmul(gated_low.T, grad_result_low)
    (grad_up_pre,) = back_gate(matmul(grad_result_low, w_down.T))
    grad_up_bias = jnp.sum(grad_up_pre, axis=0)
    grad_up_low = grad_up_pre.astype(jnp.bfloat16)
    grad_w_up = matmul(normed_two_low.T, grad_up_low)
    grad_from_two, gain_two, shift_two = back_two(matmul(grad_up_low, w_up.T))
    grad_hidden = grad_result + grad_from_two
    grad_out_bias = jnp.sum(grad_hidden, axis=0)
    grad_hidden_low = grad_hidden.astype(jnp.bfloat16)
    grad_w_out = matmul(attended_low.T, grad_hidden_low)
    grad_attended_low = matmul(grad_hidden_low, w_out.T).astype(jnp.bfloat16)
    key_back, value_back = (key_all, value_all)
    grad_query, grad_key_all, grad_value_all = attend_back(
        queries, key_back, value_back, grad_attended_low, logsum, allowed, per_turn
    )
    grad_key, grad_value = (
        lax.psum_scatter(
            grad_key_all.astype(jnp.bfloat16), "row", scatter_dimension=0, tiled=True
        ).astype(jnp.float32),
        lax.psum_scatter(
            grad_value_all.astype(jnp.bfloat16), "row", scatter_dimension=0, tiled=True
        ).astype(jnp.float32),
    )
    grad_query = grad_query * 0.125
    grad_qv_bias = jnp.stack([jnp.sum(grad_query, axis=0), jnp.sum(grad_value, axis=0)])
    grad_mixed_low = jnp.concatenate([grad_query, grad_key, grad_value], axis=1).astype(
        jnp.bfloat16
    )
    grad_w_qkv = matmul(normed_one_low.T, grad_mixed_low)
    grad_from_one, gain_one, shift_one = back_one(matmul(grad_mixed_low, w_qkv.T))
    grad_tokens = (grad_hidden + grad_from_one)[None]
    matrices = (grad_w_qkv, grad_w_out, grad_w_up, grad_w_down, grad_learn_in, grad_learn_out)
    shares = (
        lax.psum_scatter(
            matrices[0].astype(jnp.bfloat16), "img", scatter_dimension=0, tiled=True
        ).astype(jnp.float32),
        lax.psum_scatter(
            matrices[1].astype(jnp.bfloat16), "img", scatter_dimension=0, tiled=True
        ).astype(jnp.float32),
        lax.psum_scatter(
            matrices[2].astype(jnp.bfloat16), "img", scatter_dimension=0, tiled=True
        ).astype(jnp.float32),
        lax.psum_scatter(
            matrices[3].astype(jnp.bfloat16), "img", scatter_dimension=0, tiled=True
        ).astype(jnp.float32),
        lax.psum_scatter(
            matrices[4].astype(jnp.bfloat16), "img", scatter_dimension=0, tiled=True
        ).astype(jnp.float32),
        lax.psum_scatter(
            matrices[5].astype(jnp.bfloat16), "img", scatter_dimension=0, tiled=True
        ).astype(jnp.float32),
    )
    shares = (
        lax.psum(shares[0].astype(jnp.bfloat16), "row").astype(jnp.float32),
        lax.psum(shares[1].astype(jnp.bfloat16), "row").astype(jnp.float32),
        lax.psum(shares[2].astype(jnp.bfloat16), "row").astype(jnp.float32),
        lax.psum(shares[3].astype(jnp.bfloat16), "row").astype(jnp.float32),
        lax.psum(shares[4].astype(jnp.bfloat16), "row").astype(jnp.float32),
        lax.psum(shares[5].astype(jnp.bfloat16), "row").astype(jnp.float32),
    )
    vectors = lax.psum(
        (
            grad_qv_bias,
            grad_out_bias,
            grad_up_bias,
            grad_down_bias,
            jnp.stack([gain_one, gain_two, gain_three]),
            jnp.stack([shift_one, shift_two, shift_three]),
            grad_learn_in_bias,
            grad_learn_out_bias,
        ),
        ("img", "row"),
    )
    return (
        learned,
        grad_tokens,
        shares[0],
        vectors[0],
        shares[1],
        vectors[1],
        shares[2],
        vectors[2],
        shares[3],
        vectors[3],
        vectors[4],
        vectors[5],
        shares[4],
        vectors[6],
        shares[5],
        vectors[7],
    )


def solution(mesh):
    in_specs = (
        P("img", "row", None),
        P("img", None),
        P("img", None),
        P(),
        P(),
        P(),
        P(),
        P(),
        P(),
        P(),
        P(),
        P(),
        P(),
        P(),
        P(),
        P(),
        P(),
        P("img", "row", None, None),
    )
    out_specs = (
        P("img", "row", None, None),
        P("img", "row", None),
        P("img", None),
        P(),
        P("img", None),
        P(),
        P("img", None),
        P(),
        P("img", None),
        P(),
        P(),
        P(),
        P("img", None),
        P(),
        P("img", None),
        P(),
    )
    return jax.shard_map(
        on_device, mesh=mesh, in_specs=in_specs, out_specs=out_specs, check_vma=False
    )
```

profile of v0, /device:TPU:0, one launch (start us, length us, event | category | flops | bytes accessed | tf_op | source)
XLA Modules:
  0.0 2293.7 jit_solution(3694543301791081184)
XLA Ops:
  12.9 9.7 fusion.151
  51.1 38.5 %all-gather.6.cloned.1.call-done = bf16[4064,1024]{1,0:T(8,128)(2,1)} async-done(((bf16[1016,1024]{1,0:T(8,128)(2,1)}), bf16[4064,1024]{1,0:T(8,128)(2,1)}) %all-gather.6.cloned.1.call-update) | async-done | bytes 8323088 | tf_op jit(solution)/shard_map/all_gather | solution.py:157
  89.6 12.1 copy.53
  101.7 48.6 %all-gather.4.cloned.1.call-done = bf16[4064,1024]{1,0:T(8,128)(2,1)} async-done(((bf16[1016,1024]{1,0:T(8,128)(2,1)}), bf16[4064,1024]{1,0:T(8,128)(2,1)}) %all-gather.4.cloned.1.call-update) | async-done | bytes 8323088 | tf_op jit(solution)/shard_map/all_gather | solution.py:158
  150.3 11.4 copy.51
  161.8 332.0 %while.30 = (s32[]{:T(128)}, bf16[4,1016,4,64]{1,3,2,0:T(8,128)(2,1)}, f32[4,4,1016]{2,1,0:T(4,128)}, bf16[4,4064,4,64]{1,3,2,0:T(8,128)(2,1)}, bf16[4,1016,4,64...) while((s32[]{:T(128)}, ...), condition=%wide.region_9.10_spmd.clone.clone, body=%wide.region_6.9_spmd.clone.sunk.clone | while | flops 4380890112 | bytes 221246832 | solution.py:60
  167.2 27.1 %select_reduce_fusion.3 = (f32[4,1016]{1,0:T(4,128)S(1)}, f32[4,1016,4064]{2,1,0:T(8,128)}) fusion(pred[1016,4064]{1,0:T(8,128)(4,1)} %broadcast_compare_fusion.6, bf16[4,4064,4,64]{1,3,2,0:T(8,128)(2,1)} %get-tuple-element.463, s32[]{:T(128)S(6)} %copy.74, bf16[4,1016,4,64]{1,3,2,0:T(8,128)(2,1)} %get-tuple-element.462), kind=kOutput, calls=%fused_computation.4.clone.1.clone | convolution fusion | flops 2147088384 | bytes 72864640 | tf_op jit(solution)/shard_map/while/body/eval_jaxpr/qhd,khd->hqk/dot_general | solution.py:47
  194.3 22.5 fusion.229
  216.8 27.3 %fusion.230 = bf16[4,1016,4,64]{1,3,2,0:T(8,128)(2,1)} fusion(bf16[4,1016,4,64]{1,3,2,0:T(8,128)(2,1)} %get-tuple-element.451, s32[]{:T(128)S(6)} %copy.74, f32[4,1016,4064]{2,1,0:T(8,128)} %get-tuple-element.405, f32[4,1016]{1,0:T(4,128)S(1)} %fusion.229, f32[4,1016]{1,0:T(4,128)S(1)} %get-tuple-element.406, ...), kind=kOutput, calls=%fused_computation.14.clone.1.clone | convolution fusion | flops 2180124672 | bytes 73925376 | tf_op jit(solution)/shard_map/while/body/eval_jaxpr/hqk,khd->qhd/dot_general | solution.py:55
  250.1 27.1 %select_reduce_fusion.3 = (f32[4,1016]{1,0:T(4,128)S(1)}, f32[4,1016,4064]{2,1,0:T(8,128)}) fusion(pred[1016,4064]{1,0:T(8,128)(4,1)} %broadcast_compare_fusion.6, bf16[4,4064,4,64]{1,3,2,0:T(8,128)(2,1)} %get-tuple-element.463, s32[]{:T(128)S(6)} %copy.74, bf16[4,1016,4,64]{1,3,2,0:T(8,128)(2,1)} %get-tuple-element.462), kind=kOutput, calls=%fused_computation.4.clone.1.clone | convolution fusion | flops 2147088384 | bytes 72864640 | tf_op jit(solution)/shard_map/while/body/eval_jaxpr/qhd,khd->hqk/dot_general | solution.py:47
  277.2 22.5 fusion.229
  299.7 27.2 %fusion.230 = bf16[4,1016,4,64]{1,3,2,0:T(8,128)(2,1)} fusion(bf16[4,1016,4,64]{1,3,2,0:T(8,128)(2,1)} %get-tuple-element.451, s32[]{:T(128)S(6)} %copy.74, f32[4,1016,4064]{2,1,0:T(8,128)} %get-tuple-element.405, f32[4,1016]{1,0:T(4,128)S(1)} %fusion.229, f32[4,1016]{1,0:T(4,128)S(1)} %get-tuple-element.406, ...), kind=kOutput, calls=%fused_computation.14.clone.1.clone | convolution fusion | flops 2180124672 | bytes 73925376 | tf_op jit(solution)/shard_map/while/body/eval_jaxpr/hqk,khd->qhd/dot_general | solution.py:55
  333.0 27.1 %select_reduce_fusion.3 = (f32[4,1016]{1,0:T(4,128)S(1)}, f32[4,1016,4064]{2,1,0:T(8,128)}) fusion(pred[1016,4064]{1,0:T(8,128)(4,1)} %broadcast_compare_fusion.6, bf16[4,4064,4,64]{1,3,2,0:T(8,128)(2,1)} %get-tuple-element.463, s32[]{:T(128)S(6)} %copy.74, bf16[4,1016,4,64]{1,3,2,0:T(8,128)(2,1)} %get-tuple-element.462), kind=kOutput, calls=%fused_computation.4.clone.1.clone | convolution fusion | flops 2147088384 | bytes 72864640 | tf_op jit(solution)/shard_map/while/body/eval_jaxpr/qhd,khd->hqk/dot_general | solution.py:47
  360.1 22.5 fusion.229
  382.6 27.3 %fusion.230 = bf16[4,1016,4,64]{1,3,2,0:T(8,128)(2,1)} fusion(bf16[4,1016,4,64]{1,3,2,0:T(8,128)(2,1)} %get-tuple-element.451, s32[]{:T(128)S(6)} %copy.74, f32[4,1016,4064]{2,1,0:T(8,128)} %get-tuple-element.405, f32[4,1016]{1,0:T(4,128)S(1)} %fusion.229, f32[4,1016]{1,0:T(4,128)S(1)} %get-tuple-element.406, ...), kind=kOutput, calls=%fused_computation.14.clone.1.clone | convolution fusion | flops 2180124672 | bytes 73925376 | tf_op jit(solution)/shard_map/while/body/eval_jaxpr/hqk,khd->qhd/dot_general | solution.py:55
  415.9 27.1 %select_reduce_fusion.3 = (f32[4,1016]{1,0:T(4,128)S(1)}, f32[4,1016,4064]{2,1,0:T(8,128)}) fusion(pred[1016,4064]{1,0:T(8,128)(4,1)} %broadcast_compare_fusion.6, bf16[4,4064,4,64]{1,3,2,0:T(8,128)(2,1)} %get-tuple-element.463, s32[]{:T(128)S(6)} %copy.74, bf16[4,1016,4,64]{1,3,2,0:T(8,128)(2,1)} %get-tuple-element.462), kind=kOutput, calls=%fused_computation.4.clone.1.clone | convolution fusion | flops 2147088384 | bytes 72864640 | tf_op jit(solution)/shard_map/while/body/eval_jaxpr/qhd,khd->hqk/dot_general | solution.py:47
  443.0 22.5 fusion.229
  465.5 27.2 %fusion.230 = bf16[4,1016,4,64]{1,3,2,0:T(8,128)(2,1)} fusion(bf16[4,1016,4,64]{1,3,2,0:T(8,128)(2,1)} %get-tuple-element.451, s32[]{:T(128)S(6)} %copy.74, f32[4,1016,4064]{2,1,0:T(8,128)} %get-tuple-element.405, f32[4,1016]{1,0:T(4,128)S(1)} %fusion.229, f32[4,1016]{1,0:T(4,128)S(1)} %get-tuple-element.406, ...), kind=kOutput, calls=%fused_computation.14.clone.1.clone | convolution fusion | flops 2180124672 | bytes 73925376 | tf_op jit(solution)/shard_map/while/body/eval_jaxpr/hqk,khd->qhd/dot_general | solution.py:55
  500.1 51.5 %multiply_convert_fusion.1 = (bf16[1016,4096]{1,0:T(8,128)(2,1)}, f32[1016,4096]{1,0:T(8,128)}, f32[1016,4096]{1,0:T(8,128)}) fusion(f32[4096]{0:T(1024)S(1)} %copy-done.80, bf16[1024,4096]{1,0:T(8,128)(2,1)} %param.29, f32[1016,1024]{1,0:T(8,128)S(1)} %get-tuple-element.253, f32[1024]{0:T(1024)S(1)} %bitcast.311, f32[1024]{0:T(1024)S(1)} %bitcast.293, ...), kind=kOutput, calls=%fused_computation.61 | convolution fusion | flops 8802689024 | bytes 54198208 | tf_op jit(solution)/shard_map/dot_general | solution.py:113
  551.6 11.8 fusion.166
  565.4 11.0 multiply_convert_fusion.2
  590.4 24.5 %fusion.167 = (f32[4096]{0:T(1024)}, bf16[1016,4096]{1,0:T(8,128)(2,1)}) fusion(f32[1016,4096]{1,0:T(8,128)} %get-tuple-element.229, bf16[4096,1024]{1,0:T(8,128)(2,1)} %param.31, f32[1016,1024]{1,0:T(8,128)} %add_add_fusion.4, f32[1016,4096]{1,0:T(8,128)} %get-tuple-element.254, f32[4096]{0:T(1024)S(1)} %copy-done.80), kind=kOutput, calls=%fused_computation.258 | convolution fusion | flops 8590446592 | bytes 54198272 | tf_op jit(solution)/shard_map/dot_general | solution.py:113
  614.9 16.4 multiply_reduce_fusion.2
  644.8 769.3 %while.31 = (s32[]{:T(128)}, f32[4,1016,4,64]{1,3,2,0:T(8,128)}, bf16[4,4064,4,64]{1,3,2,0:T(8,128)(2,1)}, bf16[4,4064,4,64]{1,3,2,0:T(8,128)(2,1)}, bf16[4,4064...) while((s32[]{:T(128)}, f32[4,1016,4,64]{1,3,2,0:T(8,128)}, ...), condition=%wide.region_22.23_spmd.clone.clone, body=%wide.region_20.22_spmd.clone.sunk.clone | while | flops 10772619264 | bytes 531606016 | solution.py:99
  651.0 24.9 %fusion.239 = f32[4,1016,4064]{2,1,0:T(8,128)} fusion(bf16[4,4064,4,64]{1,3,2,0:T(8,128)(2,1)} %get-tuple-element.492, s32[]{:T(128)S(6)} %copy.84, bf16[4,1016,4,64]{1,3,2,0:T(8,128)(2,1)S(1)} %get-tuple-element.493), kind=kOutput, calls=%fused_computation.36.clone.1.clone | convolution fusion | flops 2114060288 | bytes 68686848 | tf_op jit(solution)/shard_map/while/body/eval_jaxpr/qhd,khd->hqk/dot_general | solution.py:75
  675.9 27.3 %fusion.242 = bf16[4,4064,4,64]{1,3,2,0:T(8,128)(2,1)} fusion(bf16[4,4064,4,64]{1,3,2,0:T(8,128)(2,1)} %get-tuple-element.480, s32[]{:T(128)S(6)} %copy.84, f32[4,1016,4064]{2,1,0:T(8,128)} %fusion.239, f32[4,1016]{1,0:T(4,128)S(1)} %dynamic-slice_bitcast_fusion.3, pred[1016,4064]{1,0:T(8,128)(4,1)} %broadcast_compare_fusion.7, ...), kind=kOutput, calls=%fused_computation.29.clone.1.clone | convolution fusion | flops 2163608576 | bytes 75481984 | tf_op jit(solution)/shard_map/while/body/eval_jaxpr/hqk,qhd->khd/dot_general | solution.py:91
  703.2 49.0 %multiply_reduce_fusion.10 = (f32[4,1016]{1,0:T(4,128)S(1)}, f32[4,1016,4064]{2,1,0:T(8,128)}) fusion(f32[4,1016,4064]{2,1,0:T(8,128)} %fusion.239, f32[4,1016]{1,0:T(4,128)S(1)} %dynamic-slice_bitcast_fusion.3, pred[1016,4064]{1,0:T(8,128)(4,1)} %broadcast_compare_fusion.7, bf16[4,4064,4,64]{1,3,2,0:T(8,128)(2,1)} %get-tuple-element.496, ...), kind=kOutput, calls=%fused_computation.22.clone.3.clone | convolution fusion | flops 2180120576 | bytes 139465472 | tf_op jit(solution)/shard_map/while/body/eval_jaxpr/qhd,khd->hqk/dot_general | solution.py:80
  752.2 53.4 %multiply_convert_fusion.6 = bf16[4,1016,4064]{2,1,0:T(8,128)(2,1)} fusion(f32[4,1016,4064]{2,1,0:T(8,128)} %get-tuple-element.428, f32[4,1016,4064]{2,1,0:T(8,128)} %fusion.239, f32[4,1016]{1,0:T(4,128)S(1)} %get-tuple-element.429, f32[4,1016]{1,0:T(4,128)S(1)} %dynamic-slice_bitcast_fusion.3, pred[1016,4064]{1,0:T(8,128)(4,1)} %broadcast_compare_fusion.7), kind=kLoop, calls=%fused_computation.21.clone.1.clone | loop fusion | flops 82580480 | bytes 169322496 | tf_op jit(solution)/shard_map/while/body/eval_jaxpr/convert_element_type | solution.py:84
  805.6 16.5 fusion.240
  822.1 15.0 fusion.241
  843.2 24.9 %fusion.239 = f32[4,1016,4064]{2,1,0:T(8,128)} fusion(bf16[4,4064,4,64]{1,3,2,0:T(8,128)(2,1)} %get-tuple-element.492, s32[]{:T(128)S(6)} %copy.84, bf16[4,1016,4,64]{1,3,2,0:T(8,128)(2,1)S(1)} %get-tuple-element.493), kind=kOutput, calls=%fused_computation.36.clone.1.clone | convolution fusion | flops 2114060288 | bytes 68686848 | tf_op jit(solution)/shard_map/while/body/eval_jaxpr/qhd,khd->hqk/dot_general | solution.py:75
  868.0 27.3 %fusion.242 = bf16[4,4064,4,64]{1,3,2,0:T(8,128)(2,1)} fusion(bf16[4,4064,4,64]{1,3,2,0:T(8,128)(2,1)} %get-tuple-element.480, s32[]{:T(128)S(6)} %copy.84, f32[4,1016,4064]{2,1,0:T(8,128)} %fusion.239, f32[4,1016]{1,0:T(4,128)S(1)} %dynamic-slice_bitcast_fusion.3, pred[1016,4064]{1,0:T(8,128)(4,1)} %broadcast_compare_fusion.7, ...), kind=kOutput, calls=%fused_computation.29.clone.1.clone | convolution fusion | flops 2163608576 | bytes 75481984 | tf_op jit(solution)/shard_map/while/body/eval_jaxpr/hqk,qhd->khd/dot_general | solution.py:91
  895.4 49.0 %multiply_reduce_fusion.10 = (f32[4,1016]{1,0:T(4,128)S(1)}, f32[4,1016,4064]{2,1,0:T(8,128)}) fusion(f32[4,1016,4064]{2,1,0:T(8,128)} %fusion.239, f32[4,1016]{1,0:T(4,128)S(1)} %dynamic-slice_bitcast_fusion.3, pred[1016,4064]{1,0:T(8,128)(4,1)} %broadcast_compare_fusion.7, bf16[4,4064,4,64]{1,3,2,0:T(8,128)(2,1)} %get-tuple-element.496, ...), kind=kOutput, calls=%fused_computation.22.clone.3.clone | convolution fusion | flops 2180120576 | bytes 139465472 | tf_op jit(solution)/shard_map/while/body/eval_jaxpr/qhd,khd->hqk/dot_general | solution.py:80
  944.4 53.4 %multiply_convert_fusion.6 = bf16[4,1016,4064]{2,1,0:T(8,128)(2,1)} fusion(f32[4,1016,4064]{2,1,0:T(8,128)} %get-tuple-element.428, f32[4,1016,4064]{2,1,0:T(8,128)} %fusion.239, f32[4,1016]{1,0:T(4,128)S(1)} %get-tuple-element.429, f32[4,1016]{1,0:T(4,128)S(1)} %dynamic-slice_bitcast_fusion.3, pred[1016,4064]{1,0:T(8,128)(4,1)} %broadcast_compare_fusion.7), kind=kLoop, calls=%fused_computation.21.clone.1.clone | loop fusion | flops 82580480 | bytes 169322496 | tf_op jit(solution)/shard_map/while/body/eval_jaxpr/convert_element_type | solution.py:84
  997.8 16.5 fusion.240
  1014.3 15.0 fusion.241
  1035.4 24.9 %fusion.239 = f32[4,1016,4064]{2,1,0:T(8,128)} fusion(bf16[4,4064,4,64]{1,3,2,0:T(8,128)(2,1)} %get-tuple-element.492, s32[]{:T(128)S(6)} %copy.84, bf16[4,1016,4,64]{1,3,2,0:T(8,128)(2,1)S(1)} %get-tuple-element.493), kind=kOutput, calls=%fused_computation.36.clone.1.clone | convolution fusion | flops 2114060288 | bytes 68686848 | tf_op jit(solution)/shard_map/while/body/eval_jaxpr/qhd,khd->hqk/dot_general | solution.py:75
  1060.2 27.3 %fusion.242 = bf16[4,4064,4,64]{1,3,2,0:T(8,128)(2,1)} fusion(bf16[4,4064,4,64]{1,3,2,0:T(8,128)(2,1)} %get-tuple-element.480, s32[]{:T(128)S(6)} %copy.84, f32[4,1016,4064]{2,1,0:T(8,128)} %fusion.239, f32[4,1016]{1,0:T(4,128)S(1)} %dynamic-slice_bitcast_fusion.3, pred[1016,4064]{1,0:T(8,128)(4,1)} %broadcast_compare_fusion.7, ...), kind=kOutput, calls=%fused_computation.29.clone.1.clone | convolution fusion | flops 2163608576 | bytes 75481984 | tf_op jit(solution)/shard_map/while/body/eval_jaxpr/hqk,qhd->khd/dot_general | solution.py:91
  1087.6 49.0 %multiply_reduce_fusion.10 = (f32[4,1016]{1,0:T(4,128)S(1)}, f32[4,1016,4064]{2,1,0:T(8,128)}) fusion(f32[4,1016,4064]{2,1,0:T(8,128)} %fusion.239, f32[4,1016]{1,0:T(4,128)S(1)} %dynamic-slice_bitcast_fusion.3, pred[1016,4064]{1,0:T(8,128)(4,1)} %broadcast_compare_fusion.7, bf16[4,4064,4,64]{1,3,2,0:T(8,128)(2,1)} %get-tuple-element.496, ...), kind=kOutput, calls=%fused_computation.22.clone.3.clone | convolution fusion | flops 2180120576 | bytes 139465472 | tf_op jit(solution)/shard_map/while/body/eval_jaxpr/qhd,khd->hqk/dot_general | solution.py:80
  1136.6 53.4 %multiply_convert_fusion.6 = bf16[4,1016,4064]{2,1,0:T(8,128)(2,1)} fusion(f32[4,1016,4064]{2,1,0:T(8,128)} %get-tuple-element.428, f32[4,1016,4064]{2,1,0:T(8,128)} %fusion.239, f32[4,1016]{1,0:T(4,128)S(1)} %get-tuple-element.429, f32[4,1016]{1,0:T(4,128)S(1)} %dynamic-slice_bitcast_fusion.3, pred[1016,4064]{1,0:T(8,128)(4,1)} %broadcast_compare_fusion.7), kind=kLoop, calls=%fused_computation.21.clone.1.clone | loop fusion | flops 82580480 | bytes 169322496 | tf_op jit(solution)/shard_map/while/body/eval_jaxpr/convert_element_type | solution.py:84
  1189.9 16.5 fusion.240
  1206.5 15.1 fusion.241
  1227.6 24.9 %fusion.239 = f32[4,1016,4064]{2,1,0:T(8,128)} fusion(bf16[4,4064,4,64]{1,3,2,0:T(8,128)(2,1)} %get-tuple-element.492, s32[]{:T(128)S(6)} %copy.84, bf16[4,1016,4,64]{1,3,2,0:T(8,128)(2,1)S(1)} %get-tuple-element.493), kind=kOutput, calls=%fused_computation.36.clone.1.clone | convolution fusion | flops 2114060288 | bytes 68686848 | tf_op jit(solution)/shard_map/while/body/eval_jaxpr/qhd,khd->hqk/dot_general | solution.py:75
  1252.5 27.3 %fusion.242 = bf16[4,4064,4,64]{1,3,2,0:T(8,128)(2,1)} fusion(bf16[4,4064,4,64]{1,3,2,0:T(8,128)(2,1)} %get-tuple-element.480, s32[]{:T(128)S(6)} %copy.84, f32[4,1016,4064]{2,1,0:T(8,128)} %fusion.239, f32[4,1016]{1,0:T(4,128)S(1)} %dynamic-slice_bitcast_fusion.3, pred[1016,4064]{1,0:T(8,128)(4,1)} %broadcast_compare_fusion.7, ...), kind=kOutput, calls=%fused_computation.29.clone.1.clone | convolution fusion | flops 2163608576 | bytes 75481984 | tf_op jit(solution)/shard_map/while/body/eval_jaxpr/hqk,qhd->khd/dot_general | solution.py:91
  1279.8 49.0 %multiply_reduce_fusion.10 = (f32[4,1016]{1,0:T(4,128)S(1)}, f32[4,1016,4064]{2,1,0:T(8,128)}) fusion(f32[4,1016,4064]{2,1,0:T(8,128)} %fusion.239, f32[4,1016]{1,0:T(4,128)S(1)} %dynamic-slice_bitcast_fusion.3, pred[1016,4064]{1,0:T(8,128)(4,1)} %broadcast_compare_fusion.7, bf16[4,4064,4,64]{1,3,2,0:T(8,128)(2,1)} %get-tuple-element.496, ...), kind=kOutput, calls=%fused_computation.22.clone.3.clone | convolution fusion | flops 2180120576 | bytes 139465472 | tf_op jit(solution)/shard_map/while/body/eval_jaxpr/qhd,khd->hqk/dot_general | solution.py:80
  1328.8 53.4 %multiply_convert_fusion.6 = bf16[4,1016,4064]{2,1,0:T(8,128)(2,1)} fusion(f32[4,1016,4064]{2,1,0:T(8,128)} %get-tuple-element.428, f32[4,1016,4064]{2,1,0:T(8,128)} %fusion.239, f32[4,1016]{1,0:T(4,128)S(1)} %get-tuple-element.429, f32[4,1016]{1,0:T(4,128)S(1)} %dynamic-slice_bitcast_fusion.3, pred[1016,4064]{1,0:T(8,128)(4,1)} %broadcast_compare_fusion.7), kind=kLoop, calls=%fused_computation.21.clone.1.clone | loop fusion | flops 82580480 | bytes 169322496 | tf_op jit(solution)/shard_map/while/body/eval_jaxpr/convert_element_type | solution.py:84
  1382.2 16.5 fusion.240
  1398.7 15.0 fusion.241
  1414.1 12.0 copy.58
  1426.1 12.3 copy.56
  1441.9 7.2 convolution_convert_fusion.4
  1455.5 15.5 convolution_convert_fusion.1
  1471.8 15.9 convolution_convert_fusion.2
  1501.5 70.0 %reduce-scatter.25.cloned.1.call-done = bf16[1016,1024]{1,0:T(8,128)(2,1)} async-done(((bf16[4064,1024]{1,0:T(8,128)(2,1)}), bf16[1016,1024]{1,0:T(8,128)(2,1)}) %reduce-scatter.25.cloned.1.call-update) | async-done | bytes 2080784
  1575.4 12.9 convolution_convert_fusion.3
  1596.8 39.8 %reduce-scatter.29.cloned.1.call-done = bf16[128,8]{1,0:T(8,128)(2,1)} async-done(((bf16[1024,8]{1,0:T(8,128)(2,1)}), bf16[128,8]{1,0:T(8,128)(2,1)}) %reduce-scatter.29.cloned.1.call-update) | async-done | bytes 2064
  1646.7 12.8 fusion.156
  1659.4 47.4 %reduce-scatter.23.cloned.1.call-done = bf16[128,1024]{1,0:T(8,128)(2,1)} async-done(((bf16[1024,1024]{1,0:T(8,128)(2,1)}), bf16[128,1024]{1,0:T(8,128)(2,1)}) %reduce-scatter.23.cloned.1.call-update) | async-done | bytes 262160 | tf_op jit(solution)/shard_map/reduce_scatter | solution.py:258
  1706.8 70.4 %reduce-scatter.17.cloned.1.call-done = bf16[128,1024]{1,0:T(8,128)(2,1)} async-done(((bf16[1024,1024]{1,0:T(8,128)(2,1)}), bf16[128,1024]{1,0:T(8,128)(2,1)}) %reduce-scatter.17.cloned.1.call-update) | async-done | bytes 262160 | tf_op jit(solution)/shard_map/reduce_scatter | solution.py:249
  1777.3 151.7 %reduce-scatter.21.cloned.1.call-done = bf16[512,1024]{1,0:T(8,128)(2,1)} async-done(((bf16[4096,1024]{1,0:T(8,128)(2,1)}), bf16[512,1024]{1,0:T(8,128)(2,1)}) %reduce-scatter.21.cloned.1.call-update) | async-done | bytes 1048592 | tf_op jit(solution)/shard_map/reduce_scatter | solution.py:255
  1928.9 152.1 %reduce-scatter.19.cloned.1.call-done = bf16[128,4096]{1,0:T(8,128)(2,1)} async-done(((bf16[1024,4096]{1,0:T(8,128)(2,1)}), bf16[128,4096]{1,0:T(8,128)(2,1)}) %reduce-scatter.19.cloned.1.call-update) | async-done | bytes 1048592 | tf_op jit(solution)/shard_map/reduce_scatter | solution.py:252
  2081.0 120.4 %reduce-scatter.15.cloned.1.call-done = bf16[128,3072]{1,0:T(8,128)(2,1)} async-done(((bf16[1024,3072]{1,0:T(8,128)(2,1)}), bf16[128,3072]{1,0:T(8,128)(2,1)}) %reduce-scatter.15.cloned.1.call-update) | async-done | bytes 786448 | tf_op jit(solution)/shard_map/reduce_scatter | solution.py:246
  2205.5 41.9 %all-reduce = (f32[2,1024]{1,0:T(2,128)}, f32[1024]{0:T(1024)}, f32[4096]{0:T(1024)}, f32[1024]{0:T(1024)}, f32[3,1024]{1,0:T(4,128)}, /*index=5*/f32[3,1024]{1,0:T(4,128)}, f32[1024]{0:T(1024)}, f32[8]{0:T(128)}) all-reduce(f32[2,1024]{1,0:T(2,128)S(1)} %pad_maximum_fusion.5, ...), channel_id=1, replica_groups=mesh['img'=8,'row'=4] {'img','row'}, use_global_device_ids=true, to_apply=%region_31.32 | all-reduce | flops 15368 | bytes 122944 | tf_op jit(solution)/shard_map/psum | solution.py:273
  2253.4 24.0 %all-reduce.4.cloned.1.call-done = (bf16[128,3072]{1,0:T(8,128)(2,1)}, bf16[128,1024]{1,0:T(8,128)(2,1)}, bf16[128,4096]{1,0:T(8,128)(2,1)}, bf16[512,1024]{1,0:T(8,128)(2,1)}, bf16[128,1024]{1,0:T(8,128)(2,1)}) async-done(((bf16[128,3072]{1,0:T(8,128)(2,1)}, bf16[128,1024]{1,0:T(8,128)(2,1)}, bf16[128,4096]{1,0:T(8,128)(2,1)}, bf16[512,1024]{1,0:T(8,128)(2,1)}, bf16[128,1024]{1,0:T(8,128)(2,1)}), ...) | async-done | bytes 3407888 | tf_op jit(solution)/shard_map/psum | solution.py:266
  (311 shorter events, 183.9 us)
Async XLA Ops:
  7.2 558.1 %copy-start = (bf16[1024,1024]{1,0:T(8,128)(2,1)S(1)}, bf16[1024,1024]{1,0:T(8,128)(2,1)}, u32[]{:S(2)}) copy-start(bf16[1024,1024]{1,0:T(8,128)(2,1)} %param.35) | copy-start | bytes 6291460
  7.2 4.5 copy-start.58
  7.2 5.1 copy-start.59
  7.2 82.4 %all-gather.6.cloned.1.call-start = ((), (), s32[]{:S(2)}) async-start(), calls=%async_computation.10 | async-start | bytes 10403840 | tf_op jit(solution)/shard_map/all_gather | solution.py:157
  7.3 5.7 copy-start.4
  9.4 13.3 copy-start.32
  11.7 11.0 copy-start.42
  12.3 10.4 copy-start.44
  12.9 9.8 copy-start.66
  22.7 4.5 copy-start.10
  28.9 121.4 %all-gather.4.cloned.1.call-start = ((), (), s32[]{:S(2)}) async-start(), calls=%async_computation.9 | async-start | bytes 10403840 | tf_op jit(solution)/shard_map/all_gather | solution.py:158
  28.9 6.9 copy-start.74
  29.0 8.2 copy-start.31
  29.0 14.9 copy-start.72
  35.7 1461.9 %reduce-scatter.27.cloned.1.call-start = ((), (), s32[]{:S(2)}) async-start(), calls=%async_computation.17 | async-start | bytes 10403840
  44.1 57.6 %copy-start.15 = (bf16[8,8192]{1,0:T(8,128)(2,1)}, bf16[8,8192]{1,0:T(8,128)(2,1)S(1)}, u32[]{:S(2)}) copy-start(bf16[8,8192]{1,0:T(8,128)(2,1)S(1)} %fusion.68) | copy-start | bytes 393220
  161.7 332.0 %copy-start.81 = (f32[1024]{0:T(1024)S(1)}, f32[1024]{0:T(1024)}, u32[]{:S(2)}) copy-start(f32[1024]{0:T(1024)} %param.28) | copy-start | bytes 12292
  161.8 32.5 %copy-start.19 = (s32[1016]{0:T(1024)}, s32[1016]{0:T(1024)S(1)}, u32[]{:S(2)}) copy-start(s32[1016]{0:T(1024)S(1)} %get-tuple-element.465) | copy-start | bytes 12196 | tf_op jit(solution)/shard_map/while
  216.7 28.0 %copy-start.20 = (s32[1016]{0:T(1024)S(1)}, s32[1016]{0:T(1024)}, u32[]{:S(2)}) copy-start(s32[1016]{0:T(1024)} %copy-done.19) | copy-start | bytes 12196 | tf_op jit(solution)/shard_map/while
  244.7 32.5 %copy-start.19 = (s32[1016]{0:T(1024)}, s32[1016]{0:T(1024)S(1)}, u32[]{:S(2)}) copy-start(s32[1016]{0:T(1024)S(1)} %get-tuple-element.465) | copy-start | bytes 12196 | tf_op jit(solution)/shard_map/while
  299.7 27.9 %copy-start.20 = (s32[1016]{0:T(1024)S(1)}, s32[1016]{0:T(1024)}, u32[]{:S(2)}) copy-start(s32[1016]{0:T(1024)} %copy-done.19) | copy-start | bytes 12196 | tf_op jit(solution)/shard_map/while
  327.6 32.5 %copy-start.19 = (s32[1016]{0:T(1024)}, s32[1016]{0:T(1024)S(1)}, u32[]{:S(2)}) copy-start(s32[1016]{0:T(1024)S(1)} %get-tuple-element.465) | copy-start | bytes 12196 | tf_op jit(solution)/shard_map/while
  382.6 28.0 %copy-start.20 = (s32[1016]{0:T(1024)S(1)}, s32[1016]{0:T(1024)}, u32[]{:S(2)}) copy-start(s32[1016]{0:T(1024)} %copy-done.19) | copy-start | bytes 12196 | tf_op jit(solution)/shard_map/while
  410.5 32.5 %copy-start.19 = (s32[1016]{0:T(1024)}, s32[1016]{0:T(1024)S(1)}, u32[]{:S(2)}) copy-start(s32[1016]{0:T(1024)S(1)} %get-tuple-element.465) | copy-start | bytes 12196 | tf_op jit(solution)/shard_map/while
  465.5 27.8 %copy-start.20 = (s32[1016]{0:T(1024)S(1)}, s32[1016]{0:T(1024)}, u32[]{:S(2)}) copy-start(s32[1016]{0:T(1024)} %copy-done.19) | copy-start | bytes 12196 | tf_op jit(solution)/shard_map/while
  493.7 5.5 copy-start.21
  499.2 52.3 %copy-start.7 = (f32[1016,1024]{1,0:T(8,128)}, f32[1016,1024]{1,0:T(8,128)S(1)}, u32[]{:S(2)}) copy-start(f32[1016,1024]{1,0:T(8,128)S(1)} %get-tuple-element.253) | copy-start | bytes 12484612
  499.3 132.1 %copy-start.36 = (f32[1016]{0:T(1024)}, f32[1016]{0:T(1024)S(1)}, u32[]{:S(2)}) copy-start(f32[1016]{0:T(1024)S(1)} %broadcast_multiply_fusion.1) | copy-start | bytes 12196
  499.9 51.7 %copy-start.40 = (f32[1016]{0:T(1024)}, f32[1016]{0:T(1024)S(1)}, u32[]{:S(2)}) copy-start(f32[1016]{0:T(1024)S(1)} %multiply_reduce_fusion.6) | copy-start | bytes 12196
  499.9 131.5 %copy-start.49 = (f32[1016]{0:T(1024)}, f32[1016]{0:T(1024)S(1)}, u32[]{:S(2)}) copy-start(f32[1016]{0:T(1024)S(1)} %fusion.134) | copy-start | bytes 12196
  500.1 51.5 %copy-start.78 = (bf16[4096,1024]{1,0:T(8,128)(2,1)S(1)}, bf16[4096,1024]{1,0:T(8,128)(2,1)}, u32[]{:S(2)}) copy-start(bf16[4096,1024]{1,0:T(8,128)(2,1)} %param.31) | copy-start | bytes 25165828
  500.1 51.5 %copy-start.82 = (f32[1024]{0:T(1024)S(1)}, f32[1024]{0:T(1024)}, u32[]{:S(2)}) copy-start(f32[1024]{0:T(1024)} %param.32) | copy-start | bytes 12292
  563.4 22.4 copy-start.2
  563.4 22.3 copy-start.38
  564.0 21.7 copy-start.51
  565.4 12.4 copy-start.48
  565.4 12.4 copy-start.77
  579.3 8.2 copy-start.25
  614.9 16.4 copy-start.41
  614.9 16.5 copy-start.8
  822.1 15.0 copy-start.23
  1014.3 15.0 copy-start.23
  1206.5 15.1 copy-start.23
  1398.7 15.0 copy-start.23
  1426.1 145.4 %reduce-scatter.25.cloned.1.call-start = ((), (), s32[]{:S(2)}) async-start(), calls=%async_computation.16 | async-start | bytes 10403840
  1438.5 198.1 %reduce-scatter.29.cloned.1.call-start = ((), (), s32[]{:S(2)}) async-start(), calls=%async_computation.18 | async-start | bytes 294912
  1441.8 7.4 copy-start.14
  1441.8 265.0 %reduce-scatter.23.cloned.1.call-start = ((), (), s32[]{:S(2)}) async-start(), calls=%async_computation.15 | async-start | bytes 2359296 | tf_op jit(solution)/shard_map/reduce_scatter | solution.py:258
  1449.1 328.1 %reduce-scatter.17.cloned.1.call-start = ((), (), s32[]{:S(2)}) async-start(), calls=%async_computation.12 | async-start | bytes 2359296 | tf_op jit(solution)/shard_map/reduce_scatter | solution.py:249
  1455.5 473.4 %reduce-scatter.21.cloned.1.call-start = ((), (), s32[]{:S(2)}) async-start(), calls=%async_computation.14 | async-start | bytes 9437184 | tf_op jit(solution)/shard_map/reduce_scatter | solution.py:255
  1471.1 609.9 %reduce-scatter.19.cloned.1.call-start = ((), (), s32[]{:S(2)}) async-start(), calls=%async_computation.13 | async-start | bytes 9437184 | tf_op jit(solution)/shard_map/reduce_scatter | solution.py:252
  1487.7 713.8 %reduce-scatter.15.cloned.1.call-start = ((), (), s32[]{:S(2)}) async-start(), calls=%async_computation.11 | async-start | bytes 7077888 | tf_op jit(solution)/shard_map/reduce_scatter | solution.py:246
  1491.6 83.8 %copy-start.5 = (bf16[1,1016,1024]{2,1,0:T(8,128)(2,1)S(1)}, bf16[1,1016,1024]{2,1,0:T(8,128)(2,1)}, u32[]{:S(2)}) copy-start(bf16[1,1016,1024]{2,1,0:T(8,128)(2,1)} %param.22) | copy-start | bytes 6242308
  1491.6 83.8 %copy-start.33 = (f32[1016]{0:T(1024)S(1)}, f32[1016]{0:T(1024)}, u32[]{:S(2)}) copy-start(f32[1016]{0:T(1024)} %copy-done.32) | copy-start | bytes 12196
  1491.6 83.8 %copy-start.43 = (f32[1016]{0:T(1024)S(1)}, f32[1016]{0:T(1024)}, u32[]{:S(2)}) copy-start(f32[1016]{0:T(1024)} %copy-done.42) | copy-start | bytes 12196
  1491.6 83.8 %copy-start.45 = (f32[1,1024]{1,0:T(1,128)S(1)}, f32[1,1024]{1,0:T(1,128)}, u32[]{:S(2)}) copy-start(f32[1,1024]{1,0:T(1,128)} %copy-done.44) | copy-start | bytes 12292
  1491.6 83.8 %copy-start.67 = (f32[1,1024]{1,0:T(1,128)S(1)}, f32[1,1024]{1,0:T(1,128)}, u32[]{:S(2)}) copy-start(f32[1,1024]{1,0:T(1,128)} %copy-done.66) | copy-start | bytes 12292
  1588.3 8.1 copy-start.75
  1593.0 50.8 %all-to-all-start = ((bf16[4,2,8192]{2,1,0:T(2,128)(2,1)}), bf16[4,2,8192]{2,1,0:T(2,128)(2,1)S(1)}, u32[]{:S(2)}, u32[]{:S(2)}) async-start(bf16[4,2,8192]{2,1,0:T(2,128)(2,1)} %all_to_all.6), calls=%async_computation | async-start | bytes 262144 | tf_op jit(solution)/shard_map/all_to_all | solution.py:183
  1596.4 681.1 %all-reduce.4.cloned.1.call-start = ((), (), s32[]{:S(2)}) async-start(), calls=%async_computation.19 | async-start | bytes 6815744 | tf_op jit(solution)/shard_map/psum | solution.py:266
  1646.6 554.9 %copy-start.35 = (f32[1016]{0:T(1024)S(1)}, f32[1016]{0:T(1024)}, u32[]{:S(2)}) copy-start(f32[1016]{0:T(1024)} %copy-done.34) | copy-start | bytes 12196
  2277.5 6.3 copy-start.18
  2277.5 7.8 copy-start.17
  2281.2 5.7 copy-start.1
  (42 other events, 101.9 us)
Sparse Core Ops, SparseCore 0:
  29.0 60.6 all-gather.5
  91.8 58.4 all-gather.3
  1426.2 71.3 reduce-scatter.26
  1500.1 71.3 reduce-scatter.24
  1575.2 61.2 reduce-scatter.28
  1639.9 66.8 reduce-scatter.22
  1710.3 66.8 reduce-scatter.16
  1780.9 147.9 reduce-scatter.20
  1933.0 147.9 reduce-scatter.18
  2084.4 116.9 reduce-scatter.14
  2204.1 73.2 all-reduce.3
where the time goes:
time: 2300 us; the launch traced here: 2290 us
  matrix products  969 us (42%)
  waiting for transfers between devices  769 us (33%)
  other arithmetic  395 us (17%)
  local copies, waits for them, and re-layouts  86.2 us (4%)
  blocking collectives  54.5 us (2%)
    dot_general x21, matrix products, matmul(): return jnp.dot(left, right, preferred_element_type=jnp.float32)  219 us
    convert_element_type x4, other arithmetic, one_turn(): grad_scores = (probability * (grad_weight - row_delta)).astype(jnp.bfloat16)  213 us
    dot_general x8, matrix products, one_turn(): jnp.einsum('qhd,khd->hqk', query_part, key_part, preferred_element_type=j...  208 us
    dot_general x4, matrix products, one_turn(): jnp.einsum('qhd,khd->hqk', grad_part, value_part, preferred_element_type=...  196 us
    reduce_scatter x1, waiting for transfers between devices, on_device(): lax.psum_scatter(matrices[2].astype(jnp.bfloat16), 'img', scatter_dimensi...  152 us
    reduce_scatter x1, waiting for transfers between devices, on_device(): lax.psum_scatter(matrices[3].astype(jnp.bfloat16), 'img', scatter_dimensi...  152 us
    reduce_scatter x1, waiting for transfers between devices, on_device(): lax.psum_scatter(matrices[0].astype(jnp.bfloat16), 'img', scatter_dimensi...  120 us
    unnamed x14, waiting for transfers between devices  116 us
  transfers between devices with their start and end apart: 12, of which 11 were waited for; matrix products, arithmetic and copies ran while one was open for 6% of the time, Pallas kernels for 0%

commit v1 on v0

v1 whole, which is shorter than its diff:
```python
import functools

import jax
import jax.numpy as jnp
from jax import lax
from jax.experimental import pallas as pl
from jax.experimental.pallas import tpu as pltpu
from jax.sharding import PartitionSpec as P

HEADS = 16
HEAD = 64
LT = 8
IMGS = 8
BLK = 256
NEG = -1e30
VMEM = 58 << 20

highest = lax.Precision.HIGHEST
epsilon = 1e-06
f32 = jnp.float32
bf16 = jnp.bfloat16


def normalize(values, gain, shift):
    centre = values - jnp.mean(values, axis=-1, keepdims=True)
    spread = jnp.mean(centre * centre, axis=-1, keepdims=True)
    return centre * lax.rsqrt(spread + epsilon) * gain + shift


def smooth(values):
    return jax.nn.gelu(values, approximate=False)


def matmul(left, right):
    return jnp.dot(left, right, preferred_element_type=f32)


def nt(left, right):
    return lax.dot_general(left, right, (((1,), (1,)), ((), ())), preferred_element_type=f32)


def tn(left, right):
    return lax.dot_general(left, right, (((0,), (0,)), ((), ())), preferred_element_type=f32)


def row_images(counts, device, local_rows, row_count):
    upper_end = counts * (device + 1) // row_count
    lower_end = counts * device // row_count
    run_ends = jnp.cumsum(upper_end - lower_end)
    positions = jnp.arange(local_rows, dtype=jnp.int32)
    return jnp.sum((positions[:, None] >= run_ends[None, :]).astype(jnp.int32), axis=1)


def swap(value, axis, bit):
    size = lax.axis_size(axis)
    return lax.ppermute(value, axis, [(i, i ^ bit) for i in range(size)])


def bits_of(size):
    return [1 << i for i in range(size.bit_length() - 1)]


def gather_pieces(value, axis):
    pieces = {0: value}
    for d in range(1, lax.axis_size(axis)):
        low = d & -d
        pieces[d] = swap(pieces[d ^ low], axis, low)
    return [pieces[d] for d in range(lax.axis_size(axis))]


def send_pieces(pieces, axis):
    size = lax.axis_size(axis)
    return [pieces[0]] + [
        lax.ppermute(pieces[d], axis, [(i, i ^ d) for i in range(size)]) for d in range(1, size)
    ]


def reduce_pieces(pieces, axis):
    pieces = list(pieces)
    for bit in bits_of(lax.axis_size(axis)):
        half = [d for d in range(len(pieces)) if d % (2 * bit) == 0]
        arrived = {d: swap(pieces[d + bit], axis, bit) for d in reversed(half)}
        for d in half:
            pieces[d] = (pieces[d].astype(f32) + arrived[d].astype(f32)).astype(pieces[d].dtype)
    return pieces[0]


def all_sum(value, axes):
    for axis in axes:
        for bit in bits_of(lax.axis_size(axis)):
            value = value + swap(value, axis, bit)
    return value


def halve(value, axis, bit, dim):
    mine = (lax.axis_index(axis) // bit) % 2
    length = value.shape[dim] // 2
    sent = lax.dynamic_slice_in_dim(value, (1 - mine) * length, length, dim)
    kept = lax.dynamic_slice_in_dim(value, mine * length, length, dim)
    arrived = swap(sent, axis, bit)
    return (kept.astype(f32) + arrived.astype(f32)).astype(bf16)


def double(value, axis, bit, dim):
    mine = (lax.axis_index(axis) // bit) % 2
    arrived = swap(value, axis, bit)
    return jnp.where(
        mine == 0,
        jnp.concatenate([value, arrived], dim),
        jnp.concatenate([arrived, value], dim),
    )


def reduce_weight(grad, row_first):
    rows, columns = grad.shape
    images = lax.axis_size("img")
    row_bits, img_bits = bits_of(lax.axis_size("row")), bits_of(images)
    value = grad.reshape((2,) * len(img_bits) + (rows // images, columns))

    def over_row(value, bits):
        for bit in bits:
            value = halve(value, "row", bit, value.ndim - 1)
        return value

    def over_img(value):
        for bit in img_bits:
            dim = len(img_bits) - bit.bit_length()
            value = halve(value, "img", bit, dim)
        return value

    if row_first:
        value = over_img(over_row(value, row_bits))
    else:
        value = over_row(over_img(over_row(value, row_bits[:1])), row_bits[1:])
    value = value.reshape(rows // images, -1)
    for bit in reversed(row_bits):
        value = double(value, "row", bit, 1)
    return value.astype(f32)


def params(flags=("arbitrary",)):
    return pltpu.CompilerParams(dimension_semantics=flags, vmem_limit_bytes=VMEM)


def valid_rows(block, piece_rows, local_rows):
    position = lax.broadcasted_iota(jnp.int32, (BLK, 1), 0) % piece_rows + block * piece_rows
    return position < local_rows


def load_block(refs, block, piece_rows, local_rows):
    value = jnp.concatenate([ref[...] for ref in refs], axis=0).astype(f32)
    return jnp.where(valid_rows(block, piece_rows, local_rows), value, 0.0)


def norm_parts(value):
    centre = value - jnp.mean(value, axis=-1, keepdims=True)
    rstd = lax.rsqrt(jnp.mean(centre * centre, axis=-1, keepdims=True) + epsilon)
    return centre * rstd, rstd


def qkv_kernel(count, local_rows, features, *refs):
    pieces, (w_ref, bias_ref, gain_ref, shift_ref) = refs[:count], refs[count : count + 4]
    q_ref, k_ref, v_ref, kt_ref, vt_ref = refs[count + 4 :]
    block = pl.program_id(0)
    unit, _ = norm_parts(load_block(pieces, block, BLK // count, local_rows))
    normed = (unit * gain_ref[...] + shift_ref[...]).astype(bf16)
    mixed = matmul(normed, w_ref[...])
    keys = mixed[:, features : 2 * features]
    values = mixed[:, 2 * features :] + bias_ref[1:2, :]
    q_ref[...] = ((mixed[:, :features] + bias_ref[0:1, :]) * 0.125).astype(bf16)
    k_ref[...] = keys.astype(bf16)
    v_ref[...] = values.astype(bf16)
    kt_ref[0] = keys.T.astype(bf16)
    vt_ref[0] = values.T.astype(bf16)


def qkv_call(pieces, weight, bias, gain, shift):
    count, (local_rows, width) = len(pieces), pieces[0].shape
    features = weight.shape[1] // 3
    piece_rows = BLK // count
    blocks = pl.cdiv(local_rows, piece_rows)
    whole = lambda a: pl.BlockSpec(a.shape, lambda b: (0,) * a.ndim)
    flat = pl.BlockSpec((BLK, features), lambda b: (b, 0))
    turned = pl.BlockSpec((1, features, BLK), lambda b: (b, 0, 0))
    return pl.pallas_call(
        functools.partial(qkv_kernel, count, local_rows, features),
        grid=(blocks,),
        in_specs=[pl.BlockSpec((piece_rows, width), lambda b: (b, 0))] * count
        + [whole(weight), whole(bias), whole(gain), whole(shift)],
        out_specs=[flat, flat, flat, turned, turned],
        out_shape=[jax.ShapeDtypeStruct((blocks * BLK, features), bf16)] * 3
        + [jax.ShapeDtypeStruct((blocks, features, BLK), bf16)] * 2,
        compiler_params=params(),
        cost_estimate=pl.CostEstimate(
            flops=2 * blocks * BLK * width * 3 * features,
            bytes_accessed=2 * blocks * BLK * (width + 5 * features),
            transcendentals=0,
        ),
    )(*pieces, weight, bias, gain, shift)


def per_head(stack_ref, value, heads):
    lane = lax.broadcasted_iota(jnp.int32, value.shape, 1) // HEAD
    for h in range(heads):
        stack_ref[h] = jnp.where(lane == h, value, jnp.zeros_like(value))


def attend_kernel(count, heads, lo_ref, hi_ref, *refs):
    q_ref, k_ref, vt_ref, imgq_ref, imgk_ref = refs[:5]
    outs, (ot_ref, lse_ref) = refs[5 : 5 + count], refs[5 + count : 7 + count]
    s_ref, qs_ref, acc_ref = refs[7 + count :]
    block = pl.program_id(0)
    lo, hi = lo_ref[block], hi_ref[block]
    per_head(qs_ref, q_ref[...], heads)
    imgq = imgq_ref[...]

    def first(kb, tops):
        rows = pl.ds(pl.multiple_of(kb * BLK, BLK), BLK)
        keys = k_ref[rows, :]
        allowed = imgk_ref[rows, :] == imgq
        new = []
        for h in range(heads):
            s = jnp.where(allowed, nt(keys, qs_ref[h]), NEG)
            s_ref[kb - lo, h] = s
            new.append(jnp.maximum(tops[h], jnp.max(s.reshape(BLK // 8, 8, BLK), axis=0)))
        return tuple(new)

    tops = lax.fori_loop(lo, hi, first, (jnp.full((8, BLK), NEG, f32),) * heads)
    tops = [jnp.max(t, axis=0, keepdims=True) for t in tops]
    acc_ref[...] = jnp.zeros_like(acc_ref)

    def second(kb, sums):
        new = []
        for h in range(heads):
            p = jnp.exp(s_ref[kb - lo, h] - tops[h])
            new.append(sums[h] + jnp.sum(p.reshape(BLK // 8, 8, BLK), axis=0))
            rows = slice(h * HEAD, (h + 1) * HEAD)
            acc_ref[rows, :] += matmul(vt_ref[kb, rows, :], p.astype(bf16))
        return tuple(new)

    sums = lax.fori_loop(lo, hi, second, (jnp.zeros((8, BLK), f32),) * heads)
    sums = [jnp.sum(t, axis=0, keepdims=True) for t in sums]
    for h in range(heads):
        rows = slice(h * HEAD, (h + 1) * HEAD)
        acc_ref[rows, :] = acc_ref[rows, :] / sums[h]
    lse_ref[...] = jnp.concatenate(
        [t + jnp.log(s) for t, s in zip(tops, sums)] + [jnp.zeros((8 - heads, BLK), f32)], axis=0
    )
    ot_ref[0] = acc_ref[...]
    out = acc_ref[...].T.astype(bf16)
    for d in range(count):
        outs[d][...] = out[d * (BLK // count) : (d + 1) * (BLK // count)]


def attend_call(q, k, vt, imgq, imgk, lo, hi, count, local_rows):
    blocks, features = vt.shape[0], q.shape[1]
    heads = features // HEAD
    piece_rows = BLK // count
    whole = lambda a: pl.BlockSpec(a.shape, lambda b, *_: (0,) * a.ndim)
    return pl.pallas_call(
        functools.partial(attend_kernel, count, heads),
        grid_spec=pltpu.PrefetchScalarGridSpec(
            num_scalar_prefetch=2,
            grid=(blocks,),
            in_specs=[
                pl.BlockSpec((BLK, features), lambda b, *_: (b, 0)),
                whole(k),
                whole(vt),
                pl.BlockSpec((1, BLK), lambda b, *_: (0, b)),
                whole(imgk),
            ],
            out_specs=[pl.BlockSpec((piece_rows, features), lambda b, *_: (b, 0))] * count
            + [
                pl.BlockSpec((1, features, BLK), lambda b, *_: (b, 0, 0)),
                pl.BlockSpec((8, BLK), lambda b, *_: (0, b)),
            ],
            scratch_shapes=[
                pltpu.VMEM((blocks, heads, BLK, BLK), f32),
                pltpu.VMEM((heads, BLK, features), bf16),
                pltpu.VMEM((features, BLK), f32),
            ],
        ),
        out_shape=[jax.ShapeDtypeStruct((local_rows, features), bf16)] * count
        + [
            jax.ShapeDtypeStruct((blocks, features, BLK), f32),
            jax.ShapeDtypeStruct((8, blocks * BLK), f32),
        ],
        compiler_params=params(),
        cost_estimate=pl.CostEstimate(
            flops=2 * (blocks * BLK) ** 2 * features,
            bytes_accessed=2 * blocks * BLK * features * 8,
            transcendentals=(blocks * BLK) ** 2 * heads // 4,
        ),
    )(lo, hi, q, k, vt, imgq, imgk)


def attend_back_kernel(count, heads, local_rows, lo_ref, hi_ref, *refs):
    pieces = refs[:count]
    q_ref, k_ref, v_ref, kt_ref, ot_ref, lse_ref, imgq_ref, imgk_ref = refs[count : count + 8]
    dq_ref, dk_out, dv_out, sums_ref = refs[count + 8 : count + 12]
    qs_ref, dos_ref, p_ref, ds_ref, dqt_ref, dk_ref, dv_ref = refs[count + 12 :]
    block = pl.program_id(0)
    lo, hi = lo_ref[block], hi_ref[block]

    @pl.when(block == 0)
    def _():
        dk_ref[...] = jnp.zeros_like(dk_ref)
        dv_ref[...] = jnp.zeros_like(dv_ref)
        sums_ref[...] = jnp.zeros_like(sums_ref)

    grad = load_block(pieces, block, BLK // count, local_rows)
    per_head(qs_ref, q_ref[...], heads)
    lane = lax.broadcasted_iota(jnp.int32, grad.shape, 1) // HEAD
    for h in range(heads):
        dos_ref[h * BLK : (h + 1) * BLK] = jnp.where(lane == h, grad, 0.0).astype(bf16)
    both = grad.T * ot_ref[0]
    delta = [
        jnp.sum(both[h * HEAD : (h + 1) * HEAD], axis=0, keepdims=True) for h in range(heads)
    ]
    imgq = imgq_ref[...]
    dqt_ref[...] = jnp.zeros_like(dqt_ref)

    def body(kb, _):
        rows = pl.ds(pl.multiple_of(kb * BLK, BLK), BLK)
        keys, values = k_ref[rows, :], v_ref[rows, :]
        allowed = imgk_ref[rows, :] == imgq
        for h in range(heads):
            s = nt(keys, qs_ref[h])
            p = jnp.exp(jnp.where(allowed, s - lse_ref[h : h + 1, :], NEG))
            dp = nt(values, dos_ref[h * BLK : (h + 1) * BLK])
            ds = (p * (dp - delta[h])).astype(bf16)
            p_ref[:, h * BLK : (h + 1) * BLK] = p.astype(bf16)
            ds_ref[:, h * BLK : (h + 1) * BLK] = ds
            feats = slice(h * HEAD, (h + 1) * HEAD)
            dqt_ref[feats, :] += matmul(kt_ref[kb, feats, :], ds)
        dv_ref[rows, :] += matmul(p_ref[...], dos_ref[...])
        dk_ref[rows, :] += matmul(
            ds_ref[...], jnp.concatenate([qs_ref[h] for h in range(heads)], axis=0)
        )
        return 0

    lax.fori_loop(lo, hi, body, 0)
    dq = dqt_ref[...].T * 0.125
    dq_ref[...] = dq.astype(bf16)
    sums_ref[0:1, :] += jnp.sum(dq, axis=0, keepdims=True)

    @pl.when(block == pl.num_programs(0) - 1)
    def _():
        dk_out[...] = dk_ref[...].astype(bf16)
        dv = dv_ref[...]
        dv_out[...] = dv.astype(bf16)
        sums_ref[1:2, :] = jnp.sum(dv, axis=0, keepdims=True)


def attend_back_call(pieces, q, k, v, kt, ot, lse, imgq, imgk, lo, hi):
    count, (local_rows, features) = len(pieces), pieces[0].shape
    blocks = kt.shape[0]
    heads = features // HEAD
    whole = lambda a: pl.BlockSpec(a.shape, lambda b, *_: (0,) * a.ndim)
    once = lambda a: pl.BlockSpec(
        a.shape, lambda b, *_: (0,) * a.ndim, pipeline_mode=pl.Buffered(1)
    )
    flat = jax.ShapeDtypeStruct((blocks * BLK, features), bf16)
    return pl.pallas_call(
        functools.partial(attend_back_kernel, count, heads, local_rows),
        grid_spec=pltpu.PrefetchScalarGridSpec(
            num_scalar_prefetch=2,
            grid=(blocks,),
            in_specs=[pl.BlockSpec((BLK // count, features), lambda b, *_: (b, 0))] * count
            + [
                pl.BlockSpec((BLK, features), lambda b, *_: (b, 0)),
                once(k),
                once(v),
                once(kt),
                pl.BlockSpec((1, features, BLK), lambda b, *_: (b, 0, 0)),
                pl.BlockSpec((8, BLK), lambda b, *_: (0, b)),
                pl.BlockSpec((1, BLK), lambda b, *_: (0, b)),
                once(imgk),
            ],
            out_specs=[
                pl.BlockSpec((BLK, features), lambda b, *_: (b, 0)),
                whole(flat),
                whole(flat),
                pl.BlockSpec((8, features), lambda b, *_: (0, 0)),
            ],
            scratch_shapes=[
                pltpu.VMEM((heads, BLK, features), bf16),
                pltpu.VMEM((heads * BLK, features), bf16),
                pltpu.VMEM((BLK, heads * BLK), bf16),
                pltpu.VMEM((BLK, heads * BLK), bf16),
                pltpu.VMEM((features, BLK), f32),
                pltpu.VMEM((blocks * BLK, features), f32),
                pltpu.VMEM((blocks * BLK, features), f32),
            ],
        ),
        out_shape=[flat, flat, flat, jax.ShapeDtypeStruct((8, features), f32)],
        compiler_params=params(),
        cost_estimate=pl.CostEstimate(
            flops=5 * (blocks * BLK) ** 2 * features,
            bytes_accessed=2 * blocks * BLK * features * 12,
            transcendentals=(blocks * BLK) ** 2 * heads // 4,
        ),
    )(lo, hi, *pieces, q, k, v, kt, ot, lse, imgq, imgk)


def qkv_back_kernel(count, local_rows, features, *refs):
    pieces = refs[:count]
    dq_ref, dk_ref, dv_ref, w_ref, gain_ref, shift_ref = refs[count : count + 6]
    outs = refs[count + 6 : 2 * count + 6]
    gw_ref, sums_ref, acc_ref = refs[2 * count + 6 :]
    block = pl.program_id(0)

    @pl.when(block == 0)
    def _():
        acc_ref[...] = jnp.zeros_like(acc_ref)
        sums_ref[...] = jnp.zeros_like(sums_ref)

    unit, _ = norm_parts(load_block(pieces, block, BLK // count, local_rows))
    normed = (unit * gain_ref[...] + shift_ref[...]).astype(bf16)
    mixed = jnp.concatenate([dq_ref[...], dk_ref[...], dv_ref[...]], axis=1)
    back = nt(mixed, w_ref[...])
    sums_ref[0:1, :] += jnp.sum(back * unit, axis=0, keepdims=True)
    sums_ref[1:2, :] += jnp.sum(back, axis=0, keepdims=True)
    acc_ref[...] += tn(normed, mixed)
    low = back.astype(bf16)
    for d in range(count):
        outs[d][...] = low[d * (BLK // count) : (d + 1) * (BLK // count)]

    @pl.when(block == pl.num_programs(0) - 1)
    def _():
        gw_ref[...] = acc_ref[...].astype(bf16)


def qkv_back_call(pieces, dq, dk, dv, weight, gain, shift):
    count, (local_rows, width) = len(pieces), pieces[0].shape
    features = dq.shape[1]
    piece_rows = BLK // count
    blocks = dq.shape[0] // BLK
    whole = lambda a: pl.BlockSpec(a.shape, lambda b: (0,) * len(a.shape))
    flat = pl.BlockSpec((BLK, features), lambda b: (b, 0))
    piece = pl.BlockSpec((piece_rows, width), lambda b: (b, 0))
    gw = jax.ShapeDtypeStruct(weight.shape, bf16)
    sums = jax.ShapeDtypeStruct((8, width), f32)
    return pl.pallas_call(
        functools.partial(qkv_back_kernel, count, local_rows, features),
        grid=(blocks,),
        in_specs=[piece] * count + [flat] * 3 + [whole(weight), whole(gain), whole(shift)],
        out_specs=[piece] * count + [whole(gw), whole(sums)],
        out_shape=[jax.ShapeDtypeStruct((local_rows, width), bf16)] * count + [gw, sums],
        scratch_shapes=[pltpu.VMEM(weight.shape, f32)],
        compiler_params=params(),
        cost_estimate=pl.CostEstimate(
            flops=4 * blocks * BLK * width * 3 * features,
            bytes_accessed=2 * blocks * BLK * (2 * width + 3 * features),
            transcendentals=0,
        ),
    )(*pieces, dq, dk, dv, weight, gain, shift)


def rows_of(array, index, length):
    return lax.dynamic_slice_in_dim(array, index * length, length, 0)


def on_device(
    tokens,
    counts,
    owner,
    w_qkv,
    qv_bias,
    w_out,
    out_bias,
    w_up,
    up_bias,
    w_down,
    down_bias,
    norm_gain,
    norm_bias,
    learn_in,
    learn_in_bias,
    learn_out,
    learn_out_bias,
    cotangent,
):
    width = tokens.shape[2]
    local_rows = tokens.shape[1]
    row_count = lax.axis_size("row")
    device = lax.axis_index("row")
    image_device = lax.axis_index("img")
    features = width // row_count
    slots_here = IMGS // row_count
    group_counts = counts[0]
    partners = [device ^ d for d in range(row_count)]

    pieces = gather_pieces(tokens[0], "row")
    grads_in = gather_pieces(cotangent[0].reshape(slots_here, LT * width).astype(bf16), "row")

    piece_rows = BLK // row_count
    blocks = pl.cdiv(local_rows, piece_rows)
    images = jnp.stack([row_images(group_counts, p, local_rows, row_count) for p in partners])
    image_here = images[0]
    extra = blocks * piece_rows - local_rows
    images = jnp.pad(images, ((0, 0), (0, extra)), constant_values=IMGS + 1)
    images = images.reshape(row_count, blocks, piece_rows).transpose(1, 0, 2).reshape(blocks, BLK)
    least, most = jnp.min(images, axis=1), jnp.max(images, axis=1)
    lo = jnp.sum((most[None, :] < least[:, None]).astype(jnp.int32), axis=1)
    hi = jnp.sum((least[None, :] <= most[:, None]).astype(jnp.int32), axis=1)
    imgq, imgk = images.reshape(1, -1), images.reshape(-1, 1)

    w_here = lax.dynamic_slice_in_dim(
        w_qkv.reshape(width, 3, width), device * features, features, 2
    ).reshape(width, 3 * features)
    bias_here = lax.dynamic_slice_in_dim(qv_bias, device * features, features, 1)
    q, k, v, kt, vt = qkv_call(pieces, w_here, bias_here, norm_gain[0:1], norm_bias[0:1])
    *attended, ot, lse = attend_call(q, k, vt, imgq, imgk, lo, hi, row_count, local_rows)
    attended = send_pieces(attended, "row")
    attended_low = jnp.concatenate(attended, axis=1)
    w_out_here = jnp.concatenate([rows_of(w_out, p, features) for p in partners], axis=0)

    inputs_f32 = tokens[0].astype(f32)
    hidden = inputs_f32 + matmul(attended_low, w_out_here) + out_bias
    normed_two, back_two = jax.vjp(normalize, hidden, norm_gain[1], norm_bias[1])
    normed_two_low = normed_two.astype(bf16)
    gated, back_gate = jax.vjp(smooth, matmul(normed_two_low, w_up) + up_bias)
    gated_low = gated.astype(bf16)
    result = hidden + matmul(gated_low, w_down) + down_bias
    normed_three, back_three = jax.vjp(normalize, result, norm_gain[2], norm_bias[2])
    normed_three_low = normed_three.astype(bf16)
    inner, back_inner = jax.vjp(smooth, matmul(normed_three_low, learn_in) + learn_in_bias)
    inner_low = inner.astype(bf16)
    maps = jax.nn.sigmoid(matmul(inner_low, learn_out) + learn_out_bias)
    maps_low = maps.astype(bf16)
    result_low = result.astype(bf16)
    member = (image_here[:, None] == jnp.arange(IMGS, dtype=jnp.int32)[None, :]).astype(bf16)
    spread_maps = (member[:, :, None] * maps_low[:, None, :]).reshape(local_rows, IMGS * LT)
    partial_value = matmul(spread_maps.T, result_low)

    slot_rel = ((owner[0] // slots_here) ^ device) * slots_here + owner[0] % slots_here
    select = (slot_rel[:, None] == jnp.arange(IMGS, dtype=jnp.int32)[None, :]).astype(f32)
    scale = lax.rsqrt(group_counts.astype(f32))
    by_slot = jnp.dot(select.T, partial_value.reshape(IMGS, LT * width), precision=highest)
    by_slot = by_slot.astype(bf16).reshape(row_count, slots_here, LT * width)
    arrived = send_pieces([by_slot[d] for d in range(row_count)], "row")
    summed = sum(a.astype(f32) for a in arrived)
    scale_here = jnp.dot(scale, select, precision=highest)[:slots_here]
    learned = (summed * scale_here[:, None]).reshape(1, slots_here, LT, width)

    incoming = jnp.concatenate(grads_in, axis=0).astype(f32)
    grad_pooled = jnp.dot(select, incoming, precision=highest) * scale[:, None]
    grad_pooled_low = grad_pooled.reshape(IMGS * LT, width).astype(bf16)
    grad_result = matmul(spread_maps, grad_pooled_low)
    grad_spread = matmul(result_low, grad_pooled_low.T)
    grad_maps = jnp.sum(
        grad_spread.reshape(local_rows, IMGS, LT) * member.astype(f32)[:, :, None], axis=1
    )
    grad_logit = grad_maps * maps * (1.0 - maps)
    grad_learn_out_bias = jnp.sum(grad_logit, axis=0)
    grad_logit_low = grad_logit.astype(bf16)
    grad_learn_out = matmul(inner_low.T, grad_logit_low)
    (grad_learn_pre,) = back_inner(matmul(grad_logit_low, learn_out.T))
    grad_learn_in_bias = jnp.sum(grad_learn_pre, axis=0)
    grad_learn_low = grad_learn_pre.astype(bf16)
    grad_from_three, gain_three, shift_three = back_three(matmul(grad_learn_low, learn_in.T))
    grad_result = grad_result + grad_from_three
    grad_down_bias = jnp.sum(grad_result, axis=0)
    grad_result_low = grad_result.astype(bf16)
    grad_w_down = tn(gated_low, grad_result_low).astype(bf16)
    (grad_up_pre,) = back_gate(matmul(grad_result_low, w_down.T))
    grad_up_bias = jnp.sum(grad_up_pre, axis=0)
    grad_up_low = grad_up_pre.astype(bf16)
    grad_w_up = tn(normed_two_low, grad_up_low).astype(bf16)
    grad_from_two, gain_two, shift_two = back_two(matmul(grad_up_low, w_up.T))
    grad_hidden = grad_result + grad_from_two
    grad_out_bias = jnp.sum(grad_hidden, axis=0)
    grad_hidden_low = grad_hidden.astype(bf16)
    grad_attended = [
        nt(grad_hidden_low, w_out_here[d * features : (d + 1) * features]).astype(bf16)
        for d in range(row_count)
    ]
    grad_attended = send_pieces(grad_attended, "row")
    grad_learn_in = tn(normed_three_low, grad_learn_low).astype(bf16)
    grad_w_out = jnp.concatenate(
        [
            tn(a, grad_hidden_low)
            for a in [
                lax.dynamic_slice_in_dim(attended_low, (device ^ d) * features, features, 1)
                for d in range(row_count)
            ]
        ],
        axis=0,
    ).astype(bf16)

    share_down = reduce_weight(grad_w_down, True)
    share_up = reduce_weight(grad_w_up, False)
    share_learn = reduce_weight(grad_learn_in, True)
    share_out = reduce_weight(grad_w_out, False)
    early = jnp.concatenate(
        [
            grad_up_bias,
            grad_out_bias,
            grad_down_bias,
            gain_two,
            gain_three,
            shift_two,
            shift_three,
            grad_learn_in_bias,
            grad_learn_out.reshape(-1),
            grad_learn_out_bias,
        ]
    )
    early = all_sum(jnp.pad(early, (0, -early.shape[0] % 1024)).reshape(-1, 128), ("row", "img"))
    early = early.reshape(-1)

    dq, dk, dv, qv_sums = attend_back_call(
        grad_attended, q, k, v, kt, ot, lse, imgq, imgk, lo, hi
    )
    *back, grad_w_here, sums = qkv_back_call(
        pieces, dq, dk, dv, w_here, norm_gain[0:1], norm_bias[0:1]
    )
    grad_normed = reduce_pieces(back, "row").astype(f32)
    centred, rstd = norm_parts(inputs_f32)
    e = grad_normed * norm_gain[0]
    grad_tokens = (
        grad_hidden
        + (
            e
            - jnp.mean(e, axis=-1, keepdims=True)
            - centred * jnp.mean(e * centred, axis=-1, keepdims=True)
        )
        * rstd
    )[None]

    images_count = lax.axis_size("img")
    img_bits = bits_of(images_count)
    value = grad_w_here.reshape((2,) * len(img_bits) + (width // images_count, 3 * features))
    for bit in img_bits:
        value = halve(value, "img", bit, len(img_bits) - bit.bit_length())
    value = value.reshape(width // images_count, 3, features)
    for bit in bits_of(row_count):
        value = double(value, "row", bit, 2)
    share_qkv = value.reshape(width // images_count, 3 * width).astype(f32)

    spread_qv = lax.dynamic_update_slice(
        jnp.zeros((2, width), f32), qv_sums[0:2], (0, device * features)
    )
    late = all_sum(jnp.concatenate([spread_qv, sums[0:2]], axis=0), ("row", "img"))

    sizes = [up_bias.shape[0]] + [width] * 7 + [learn_out.size, learn_out.shape[1]]
    parts, at = [], 0
    for size in sizes:
        parts.append(early[at : at + size])
        at += size
    up_sum, out_sum, down_sum, gain_two, gain_three, shift_two, shift_three = parts[:7]
    learn_in_sum, learn_out_sum, learn_out_bias_sum = parts[7:]
    share_learn_out = rows_of(
        learn_out_sum.reshape(learn_out.shape), image_device, learn_out.shape[0] // images_count
    )
    return (
        learned,
        grad_tokens,
        share_qkv,
        late[0:2],
        share_out,
        out_sum,
        share_up,
        up_sum,
        share_down,
        down_sum,
        jnp.stack([late[2], gain_two, gain_three]),
        jnp.stack([late[3], shift_two, shift_three]),
        share_learn,
        learn_in_sum,
        share_learn_out,
        learn_out_bias_sum,
    )


def solution(mesh):
    by_image = P("img", None)
    in_specs = (
        (P("img", "row", None), by_image, by_image) + (P(),) * 14 + (P("img", "row", None, None),)
    )
    out_specs = (
        P("img", "row", None, None),
        P("img", "row", None),
        by_image,
        P(),
        by_image,
        P(),
        by_image,
        P(),
        by_image,
        P(),
        P(),
        P(),
        by_image,
        P(),
        by_image,
        P(),
    )
    return jax.shard_map(
        on_device, mesh=mesh, in_specs=in_specs, out_specs=out_specs, check_vma=False
    )
```

time: 2300 us -> 802 us (0.35)
  matrix products: 969 us -> 171 us
  waiting for transfers between devices: 769 us -> 228 us
  other arithmetic: 395 us -> 55 us
  Pallas kernels: 0 us -> 223 us
  blocking collectives: 54.5 us -> 0 us
  starting transfers between devices: 3.78 us -> 45.8 us
  local copies, waits for them, and re-layouts: 86.2 us -> 62.4 us
    dot_general x50 -> x25, matrix products: 968 us -> 170 us  [the longest x13 126 us: matmul(): return jnp.dot(left, right, preferred_element_type=f32)]
    reduce_scatter x5 -> x0, waiting for transfers between devices: 542 us -> none  [the longest x1 152 us: on_device(): lax.psum_scatter(matrices[2].astype(jnp.bfloat16), 'img', scatter_dimensi...]
    ppermute x0 -> x61, waiting for transfers between devices: none -> 228 us  [the longest x52 210 us: swap(): return lax.ppermute(value, axis, [(i, i ^ bit) for i in range(size)])]
    pallas_call x0 -> x4, Pallas kernels: none -> 223 us  [the longest x1 123 us: attend_back_call(): pl.pallas_call(functools.partial(attend_back_kernel, count, heads, local_...]
    convert_element_type x13 -> x27, other arithmetic: 231 us -> 31.5 us  [the longest x19 20.4 us: halve(): return (kept.astype(f32) + arrived.astype(f32)).astype(bf16)]
    unnamed x14 -> x0, waiting for transfers between devices: 116 us -> none
    reduce_sum x8 -> x4, other arithmetic: 99.7 us -> 8.92 us  [the longest x1 4.04 us: on_device(): jnp.mean(e, axis=-1, keepdims=True)]
    all_gather x2 -> x0, waiting for transfers between devices: 87.2 us -> none  [the longest x1 48.6 us: on_device(): lax.all_gather(value_rows, 'row', axis=0, tiled=True)]
  transfers between devices with their start and end apart: 12 -> 61, of which waited for: 11 -> 26; matrix products, arithmetic and copies ran while one was open for 6% -> 13% of each run, Pallas kernels for 0% -> 28%
where the time goes in v1:
time: 802 us; the launch traced here: 787 us
  waiting for transfers between devices  228 us (28%)
  Pallas kernels  223 us (28%)
  matrix products  171 us (21%)
  local copies, waits for them, and re-layouts  62.4 us (8%)
  other arithmetic  55 us (7%)
  starting transfers between devices  45.8 us (6%)
    ppermute x52, waiting for transfers between devices, swap(): return lax.ppermute(value, axis, [(i, i ^ bit) for i in range(size)])  210 us
    dot_general x13, matrix products, matmul(): return jnp.dot(left, right, preferred_element_type=f32)  126 us
    pallas_call x1, Pallas kernels, attend_back_call(): pl.pallas_call(functools.partial(attend_back_kernel, count, heads, local_...  123 us
    pallas_call x1, Pallas kernels, attend_call(): pl.pallas_call(functools.partial(attend_kernel, count, heads), grid_spec=...  55.3 us
    ppermute x52, starting transfers between devices, swap(): return lax.ppermute(value, axis, [(i, i ^ bit) for i in range(size)])  39.2 us
    dot_general x7, matrix products, tn(): lax.dot_general(left, right, (((0,), (0,)), ((), ())), preferred_element_...  36.8 us
    unnamed x149, local copies, waits for them, and re-layouts  25.6 us
    pallas_call x1, Pallas kernels, qkv_back_call(): pl.pallas_call(functools.partial(qkv_back_kernel, count, local_rows, feat...  24.7 us
  transfers between devices with their start and end apart: 61, of which 26 were waited for; matrix products, arithmetic and copies ran while one was open for 13% of the time, Pallas kernels for 28%

profile of v1, /device:TPU:0, one launch (start us, length us, event | category | flops | bytes accessed | tf_op | source)
XLA Modules:
  0.0 787.0 jit_solution(7937962389230283697)
XLA Ops:
  0.7 3.0 collective-permute-start.1
  6.7 8.6 %copy.50 = bf16[1024,3072]{0,1:T(8,128)(2,1)} copy(bf16[1024,3072]{1,0:T(8,128)(2,1)} %param.21) | data formatting | bytes 12582912 | tf_op args[3]
  15.7 2.7 constant_dynamic-slice_fusion.30
  18.3 31.3 %collective-permute-done.1.refs_2_ = bf16[1016,1024]{1,0:T(8,128)(2,1)} collective-permute-done((bf16[1016,1024]{1,0:T(8,128)(2,1)}, bf16[1016,1024]{1,0:T(8,128)(2,1)}, u32[]{:S(2)}, u32[]{:S(2)}) %collective-permute-start.1) | collective-permute-done | bytes 2080800 | tf_op jit(solution)/shard_map/ppermute | solution.py:56
  50.5 3.5 reshape_reshape.8.refs_4_.refs_11_
  54.1 2.6 copy.51.refs_4_.refs_7_
  58.9 1.9 convert_reduce_fusion
  61.5 2.3 fusion.16
  65.6 19.8 %shard_map.297 = (bf16[4096,256]{1,0:T(8,128)(2,1)}, bf16[4096,256]{1,0:T(8,128)(2,1)}, bf16[4096,256]{1,0:T(8,128)(2,1)}, bf16[16,256,256]{2,1,0:T(8,128)(2,1)}, bf16[16,256,256]{2,1,0:T(8,128)(2,1)}) custom-call(bf16[1016,1024]{1,0:T(8,128)(2,1)} %bitcast.146, bf16[1016,1024]{1,0:T(8,128)(2,1)} %collective-permute-done.refs_1_, ...), custom_call_target="tpu_custom_call" | custom-call | flops 6442450944 | bytes 18874368 | tf_op jit(solution)/shard_map/pallas_call | solution.py:185
  85.4 55.3 %shard_map.298 = (bf16[1016,256]{1,0:T(8,128)(2,1)}, bf16[1016,256]{1,0:T(8,128)(2,1)}, bf16[1016,256]{1,0:T(8,128)(2,1)}, bf16[1016,256]{1,0:T(8,128)(2,1)}, f3...) custom-call(s32[16]{0:T(128)} %get-tuple-element.101.lo_ref, s32[16]{0:T(128)} %get-tuple-element.100.hi_ref, ...), custom_call_target="tpu_custom_call" | custom-call | flops 8589934592 | bytes 16777216 | tf_op jit(solution)/shard_map/pallas_call | solution.py:260
  148.6 9.0 %collective-permute-done.4 = bf16[1016,256]{1,0:T(8,128)(2,1)} collective-permute-done((bf16[1016,256]{1,0:T(8,128)(2,1)}, bf16[1016,256]{1,0:T(8,128)(2,1)}, u32[]{:S(2)}, u32[]{:S(2)}) %collective-permute-start.4) | collective-permute-done | bytes 520224 | tf_op jit(solution)/shard_map/ppermute | solution.py:74
  158.7 9.1 %collective-permute-done.5 = bf16[1016,256]{1,0:T(8,128)(2,1)} collective-permute-done((bf16[1016,256]{1,0:T(8,128)(2,1)}, bf16[1016,256]{1,0:T(8,128)(2,1)}, u32[]{:S(2)}, u32[]{:S(2)}) %collective-permute-start.5) | collective-permute-done | bytes 520224 | tf_op jit(solution)/shard_map/ppermute | solution.py:74
  169.0 2.5 fusion.120
  172.2 52.3 %multiply_convert_fusion = (bf16[1016,4096]{1,0:T(8,128)(2,1)}, f32[1016,4096]{1,0:T(8,128)}, f32[1016,4096]{1,0:T(8,128)}) fusion(f32[4096]{0:T(1024)S(1)} %copy-done.56, bf16[1024,4096]{1,0:T(8,128)(2,1)} %param.25, f32[1016,1024]{1,0:T(8,128)S(1)} %get-tuple-element.149, f32[1024]{0:T(1024)S(1)} %bitcast.188, f32[1024]{0:T(1024)S(1)} %bitcast.173, ...), kind=kOutput, calls=%fused_computation.3 | convolution fusion | flops 8802689024 | bytes 54198208 | tf_op jit(solution)/shard_map/dot_general | solution.py:35
  224.5 11.8 %fusion.121 = (f32[1016]{0:T(1024)S(1)}, f32[1016,1024]{1,0:T(8,128)S(1)}) fusion(f32[1024]{0:T(1024)S(1)} %copy-done.58, f32[1016,1024]{1,0:T(8,128)S(1)} %get-tuple-element.149, bf16[1016,4096]{1,0:T(8,128)(2,1)} %get-tuple-element.111, bf16[4096,1024]{1,0:T(8,128)(2,1)S(1)} %copy-done.52), kind=kOutput, calls=%fused_computation.331 | convolution fusion | flops 8525945856 | bytes 25042912 | tf_op jit(solution)/shard_map/dot_general | solution.py:35
  238.1 11.0 %multiply_convert_fusion.1 = (bf16[1016,1024]{1,0:T(8,128)(2,1)S(1)}, f32[1016,1024]{1,0:T(8,128)S(1)}, f32[1016,1024]{1,0:T(8,128)S(1)}) fusion(f32[1024]{0:T(1024)S(1)} %copy-done.59, bf16[1024,1024]{1,0:T(8,128)(2,1)S(1)} %copy-done, f32[1016,1024]{1,0:T(8,128)S(1)} %get-tuple-element.152, f32[1024]{0:T(1024)S(1)} %bitcast.190, f32[1024]{0:T(1024)S(1)} %bitcast.177, ...), kind=kOutput, calls=%fused_computation.59 | convolution fusion | flops 2204573696 | bytes 16682944 | tf_op jit(solution)/shard_map/dot_general | solution.py:35
  251.0 2.4 fusion.123
  253.5 4.3 convolution_convert_fusion.3
  257.7 2.9 multiply_reduce_fusion
  264.7 11.9 %convolution_convert_fusion.1 = bf16[4096,1024]{1,0:T(8,128)(2,1)} fusion(bf16[1016,4096]{1,0:T(8,128)(2,1)S(1)} %bitcast.198, f32[1016,1024]{1,0:T(8,128)S(1)} %add_add_fusion.3), kind=kOutput, calls=%fused_computation.22 | convolution fusion | flops 8528060416 | bytes 20873216 | tf_op jit(solution)/shard_map/dot_general | solution.py:43
  276.6 23.9 %fusion.122 = (f32[4096]{0:T(1024)S(1)}, bf16[1016,4096]{1,0:T(8,128)(2,1)}) fusion(f32[1016,4096]{1,0:T(8,128)} %get-tuple-element.112, bf16[4096,1024]{1,0:T(8,128)(2,1)} %param.27, f32[1016,1024]{1,0:T(8,128)} %copy-done.8, f32[1016,4096]{1,0:T(8,128)} %get-tuple-element.150, f32[4096]{0:T(1024)S(1)} %copy-done.56), kind=kOutput, calls=%fused_computation.332 | convolution fusion | flops 8590446592 | bytes 54198272 | tf_op jit(solution)/shard_map/dot_general | solution.py:35
  300.5 15.4 %multiply_reduce_fusion.1 = (f32[1024]{0:T(1024)S(1)}, f32[1016]{0:T(1024)S(1)}, f32[1024]{0:T(1024)S(1)}, f32[1016,1024]{1,0:T(8,128)S(1)}) fusion(f32[1016,1024]{1,0:T(8,128)} %copy-done.6, f32[1016]{0:T(1024)S(1)} %fusion.96, f32[1016]{0:T(1024)S(1)} %broadcast_multiply_fusion.4, f32[1024]{0:T(1024)S(1)} %bitcast.174, bf16[1024,4096]{1,0:T(8,128)(2,1)} %param.25, ...), kind=kOutput, calls=%fused_computation.45 | convolution fusion | flops 8531145728 | bytes 25059232 | tf_op jit(solution)/shard_map/dot_general | solution.py:35
  316.0 15.1 %convolution_convert_fusion.2 = bf16[1024,4096]{1,0:T(8,128)(2,1)} fusion(bf16[1016,4096]{1,0:T(8,128)(2,1)} %get-tuple-element.158, f32[1016,1024]{1,0:T(8,128)S(1)} %copy-done.7, f32[1024]{0:T(1024)S(1)} %bitcast.189, f32[1024]{0:T(1024)S(1)} %bitcast.175, f32[1016]{0:T(1024)S(1)} %fusion.96, f32[1016]{0:T(1024)S(1)} %broadcast_multiply_fusion.4), kind=kOutput, calls=%fused_computation.23 | convolution fusion | flops 8532221952 | bytes 20889536 | tf_op jit(solution)/shard_map/dot_general | solution.py:43
  331.1 2.0 fusion.112
  350.9 4.8 constant_dynamic-slice_fusion.15
  355.7 4.5 constant_dynamic-slice_fusion.10
  362.1 14.1 %collective-permute-done.36 = f32[160,128]{1,0:T(8,128)S(1)} collective-permute-done((f32[160,128]{1,0:T(8,128)S(1)}, f32[160,128]{1,0:T(8,128)S(1)}, u32[]{:S(2)}, u32[]{:S(2)}) %collective-permute-start.36) | collective-permute-done | bytes 81952 | tf_op jit(solution)/shard_map/ppermute | solution.py:56
  377.8 2.9 collective-permute-done.37
  383.2 2.0 collective-permute-done.38
  385.3 1.8 collective-permute-start.7
  388.1 122.9 %shard_map.299 = (bf16[4096,256]{1,0:T(8,128)(2,1)}, bf16[4096,256]{1,0:T(8,128)(2,1)}, bf16[4096,256]{1,0:T(8,128)(2,1)}, f32[8,256]{1,0:T(8,128)}) custom-call(s32[16]{0:T(128)} %get-tuple-element.101.lo_ref, s32[16]{0:T(128)} %get-tuple-element.100.hi_ref, bf16[1016,256]{1,0:T(8,128)(2,1)} %convolution_convert_fusion.11.refs_0_, ...), custom_call_target="tpu_custom_call" | custom-call | flops 21474836480 | bytes 25165824 | tf_op jit(solution)/shard_map/pallas_call | solution.py:364
  511.0 24.7 %shard_map.300 = (bf16[1016,1024]{1,0:T(8,128)(2,1)}, bf16[1016,1024]{1,0:T(8,128)(2,1)}, bf16[1016,1024]{1,0:T(8,128)(2,1)}, bf16[1016,1024]{1,0:T(8,128)(2,1)}...) custom-call(bf16[1016,1024]{1,0:T(8,128)(2,1)} %bitcast.147, bf16[1016,1024]{1,0:T(8,128)(2,1)} %collective-permute-done.refs_1_, ...), custom_call_target="tpu_custom_call" | custom-call | flops 12884901888 | bytes 23068672 | tf_op jit(solution)/shard_map/pallas_call | solution.py:444
  537.6 2.6 collective-permute-start.39
  541.0 2.1 collective-permute-done.39
  548.3 2.0 collective-permute-start.25
  553.3 2.5 collective-permute-done.26
  557.4 2.6 constant_dynamic-slice_fusion.24
  561.5 2.3 copy.65
  567.0 1.8 add_convert_fusion.9
  572.1 9.6 %collective-permute-done.18 = bf16[2,2,1,128,768]{3,4,2,1,0:T(8,128)(2,1)S(1)} collective-permute-done((bf16[2,2,1,128,768]{3,4,2,1,0:T(8,128)(2,1)}, bf16[2,2,1,128,768]{3,4,2,1,0:T(8,128)(2,1)S(1)}, u32[]{:S(2)}, u32[]{:S(2)}) %collective-permute-start.18) | collective-permute-done | bytes 786464 | tf_op jit(solution)/shard_map/ppermute | solution.py:56
  583.5 10.2 %collective-permute-done.29 = bf16[2,2,1,128,512]{4,3,2,1,0:T(8,128)(2,1)S(1)} collective-permute-done((bf16[2,2,1,128,512]{4,3,2,1,0:T(8,128)(2,1)S(1)}, bf16[2,2,1,128,512]{4,3,2,1,0:T(8,128)(2,1)S(1)}, u32[]{:S(2)}, u32[]{:S(2)}) %collective-permute-start.29) | collective-permute-done | bytes 524320 | tf_op jit(solution)/shard_map/ppermute | solution.py:56
  595.5 4.6 collective-permute-done.56
  603.8 7.7 collective-permute-done.20
  611.7 7.0 collective-permute-done.31
  620.3 6.1 add_convert_fusion.1
  629.8 4.1 collective-permute-done.59
  634.3 3.9 collective-permute-done.33
  639.7 3.9 add_convert_fusion
  647.8 2.4 collective-permute-done.22
  650.4 3.9 add_convert_fusion.5
  654.3 17.0 %collective-permute-done.41 = bf16[2,2,1,128,2048]{4,3,2,1,0:T(8,128)(2,1)S(1)} collective-permute-done((bf16[2,2,1,128,2048]{4,3,2,1,0:T(8,128)(2,1)}, bf16[2,2,1,128,2048]{4,3,2,1,0:T(8,128)(2,1)S(1)}, u32[]{:S(2)}, u32[]{:S(2)}) %collective-permute-start.41) | collective-permute-done | bytes 2097184 | tf_op jit(solution)/shard_map/ppermute | solution.py:56
  675.2 3.0 copy.61
  678.3 17.0 %collective-permute-done.48 = bf16[2,2,2,512,256]{4,3,2,1,0:T(8,128)(2,1)} collective-permute-done((bf16[2,2,2,512,256]{4,3,2,1,0:T(8,128)(2,1)}, bf16[2,2,2,512,256]{4,3,2,1,0:T(8,128)(2,1)}, u32[]{:S(2)}, u32[]{:S(2)}) %collective-permute-start.48) | collective-permute-done | bytes 2097184 | tf_op jit(solution)/shard_map/ppermute | solution.py:56
  695.2 2.7 add_convert_fusion.2
  698.5 1.9 add_convert_fusion.11
  700.4 3.0 collective-permute-start.43
  703.4 36.1 %collective-permute-done.17 = bf16[1016,1024]{1,0:T(8,128)(2,1)} collective-permute-done((bf16[1016,1024]{1,0:T(8,128)(2,1)}, bf16[1016,1024]{1,0:T(8,128)(2,1)}, u32[]{:S(2)}, u32[]{:S(2)}) %collective-permute-start.17) | collective-permute-done | bytes 2080800 | tf_op jit(solution)/shard_map/ppermute | solution.py:56
  739.5 4.0 fusion.19
  743.9 2.9 collective-permute-start.50
  747.3 11.3 %collective-permute-done.50 = bf16[2,1,1,512,256]{4,3,2,1,0:T(8,128)(2,1)S(1)} collective-permute-done((bf16[2,1,1,512,256]{4,3,2,1,0:T(8,128)(2,1)S(1)}, bf16[2,1,1,512,256]{4,3,2,1,0:T(8,128)(2,1)S(1)}, u32[]{:S(2)}, u32[]{:S(2)}) %collective-permute-start.50) | collective-permute-done | bytes 524320 | tf_op jit(solution)/shard_map/ppermute | solution.py:56
  758.8 1.9 collective-permute-start.51
  761.0 11.8 %collective-permute-done.51 = bf16[1,1,1,512,256]{4,3,2,1,0:T(8,128)(2,1)S(1)} collective-permute-done((bf16[1,1,1,512,256]{4,3,2,1,0:T(8,128)(2,1)S(1)}, bf16[1,1,1,512,256]{4,3,2,1,0:T(8,128)(2,1)S(1)}, u32[]{:S(2)}, u32[]{:S(2)}) %collective-permute-start.51) | collective-permute-done | bytes 262176 | tf_op jit(solution)/shard_map/ppermute | solution.py:56
  773.2 7.0 collective-permute-done.52
  780.4 3.2 fusion.15
  (382 shorter events, 100.2 us)
Async XLA Ops:
  0.6 237.4 %copy-start = (bf16[1024,1024]{1,0:T(8,128)(2,1)S(1)}, bf16[1024,1024]{1,0:T(8,128)(2,1)}, u32[]{:S(2)}) copy-start(bf16[1024,1024]{1,0:T(8,128)(2,1)} %param.31) | copy-start | bytes 6291460
  0.7 49.0 %collective-permute-start.1 = (bf16[1016,1024]{1,0:T(8,128)(2,1)}, bf16[1016,1024]{1,0:T(8,128)(2,1)}, u32[]{:S(2)}, u32[]{:S(2)}) collective-permute-start(bf16[1016,1024]{1,0:T(8,128)(2,1)} %bitcast.144), channel_id=1, source_target_pairs={{0,2},{1,3},{2,0},{3,1},{4,6},{5,7},{6,4},{7,5},{8,10},{9,11},{10,... | collective-permute-start | bytes 6242312 | tf_op jit(solution)/shard_map/ppermute | solution.py:56
  4.5 137.9 %collective-permute-start.10 = (bf16[2,8192]{1,0:T(2,128)(2,1)S(1)}, bf16[2,8192]{1,0:T(2,128)(2,1)S(1)}, u32[]{:S(2)}, u32[]{:S(2)}) collective-permute-start(bf16[2,8192]{1,0:T(2,128)(2,1)S(1)} %bitcast.170), channel_id=1, source_target_pairs={{0,2},{1,3},{2,0},{3,1},{4,6},{5,7},{6,4},{7,5},{8,10},{9,11},{10,... | collective-permute-start | bytes 98312 | tf_op jit(solution)/shard_map/ppermute | solution.py:56
  4.8 140.4 %collective-permute-start.9 = (bf16[2,8192]{1,0:T(2,128)(2,1)S(1)}, bf16[2,8192]{1,0:T(2,128)(2,1)S(1)}, u32[]{:S(2)}, u32[]{:S(2)}) collective-permute-start(bf16[2,8192]{1,0:T(2,128)(2,1)S(1)} %bitcast.171), channel_id=1, source_target_pairs={{0,1},{1,0},{2,3},{3,2},{4,5},{5,4},{6,7},{7,6},{8,9},{9,8},{10,11... | collective-permute-start | bytes 98312 | tf_op jit(solution)/shard_map/ppermute | solution.py:56
  4.8 60.8 %collective-permute-start = (bf16[1016,1024]{1,0:T(8,128)(2,1)}, bf16[1016,1024]{1,0:T(8,128)(2,1)}, u32[]{:S(2)}, u32[]{:S(2)}) collective-permute-start(bf16[1016,1024]{1,0:T(8,128)(2,1)} %bitcast.145), channel_id=1, source_target_pairs={{0,1},{1,0},{2,3},{3,2},{4,5},{5,4},{6,7},{7,6},{8,9},{9,8},{10,11... | collective-permute-start | bytes 6242312 | tf_op jit(solution)/shard_map/ppermute | solution.py:56
  49.6 16.0 %collective-permute-start.2 = (bf16[1016,1024]{1,0:T(8,128)(2,1)}, bf16[1016,1024]{1,0:T(8,128)(2,1)}, u32[]{:S(2)}, u32[]{:S(2)}) collective-permute-start(bf16[1016,1024]{1,0:T(8,128)(2,1)} %collective-permute-done.1.refs_2_), channel_id=1, source_target_pairs={{0,1},{1,0},{2,3},{3,2},{4,5},{5,4},{6,7},{7,6},{8,9},{9,8},{10,11... | collective-permute-start | bytes 6242312 | tf_op jit(solution)/shard_map/ppermute | solution.py:56
  60.8 84.4 %copy-start.48 = (s32[8]{0:T(128)}, s32[8]{0:T(128)S(1)}, u32[]{:S(2)}) copy-start(s32[8]{0:T(128)S(1)} %fusion.102) | copy-start | bytes 100
  85.4 55.9 %copy-start.18 = (bf16[1024,1024]{1,0:T(8,128)(2,1)S(1)}, bf16[1024,1024]{1,0:T(8,128)(2,1)}, u32[]{:S(2)}) copy-start(bf16[1024,1024]{1,0:T(8,128)(2,1)} %param.23) | copy-start | bytes 6291460
  140.8 6.7 collective-permute-start.3
  142.5 2.7 collective-permute-start.11
  142.6 15.0 %collective-permute-start.4 = (bf16[1016,256]{1,0:T(8,128)(2,1)}, bf16[1016,256]{1,0:T(8,128)(2,1)}, u32[]{:S(2)}, u32[]{:S(2)}) collective-permute-start(bf16[1016,256]{1,0:T(8,128)(2,1)} %get-tuple-element.42), channel_id=1, source_target_pairs={{0,2},{1,3},{2,0},{3,1},{4,6},{5,7},{6,4},{7,5},{8,10},{9,11},{10,... | collective-permute-start | bytes 1560584 | tf_op jit(solution)/shard_map/ppermute | solution.py:74
  145.1 22.7 %collective-permute-start.5 = (bf16[1016,256]{1,0:T(8,128)(2,1)}, bf16[1016,256]{1,0:T(8,128)(2,1)}, u32[]{:S(2)}, u32[]{:S(2)}) collective-permute-start(bf16[1016,256]{1,0:T(8,128)(2,1)} %get-tuple-element.43), channel_id=1, source_target_pairs={{0,3},{1,2},{2,1},{3,0},{4,7},{5,6},{6,5},{7,4},{8,11},{9,10},{10,... | collective-permute-start | bytes 1560584 | tf_op jit(solution)/shard_map/ppermute | solution.py:74
  348.1 189.1 %collective-permute-start.6 = (bf16[2,8192]{1,0:T(2,128)(2,1)S(1)}, bf16[2,8192]{1,0:T(2,128)(2,1)S(1)}, u32[]{:S(2)}, u32[]{:S(2)}) collective-permute-start(bf16[2,8192]{1,0:T(2,128)(2,1)S(1)} %get-tuple-element.120), channel_id=1, source_target_pairs={{0,1},{1,0},{2,3},{3,2},{4,5},{5,4},{6,7},{7,6},{8,9},{9,8},{10,11... | collective-permute-start | bytes 98312 | tf_op jit(solution)/shard_map/ppermute | solution.py:74
  348.5 11.7 %collective-permute-start.35 = (f32[160,128]{1,0:T(8,128)S(1)}, f32[160,128]{1,0:T(8,128)S(1)}, u32[]{:S(2)}, u32[]{:S(2)}) collective-permute-start(f32[160,128]{1,0:T(8,128)S(1)} %pad_bitcast_fusion), channel_id=1, source_target_pairs={{0,1},{1,0},{2,3},{3,2},{4,5},{5,4},{6,7},{7,6},{8,9},{9,8},{10,11... | collective-permute-start | bytes 245768 | tf_op jit(solution)/shard_map/ppermute | solution.py:56
  348.8 36.4 %collective-permute-start.12 = (bf16[1016,256]{1,0:T(8,128)(2,1)}, bf16[1016,256]{1,0:T(8,128)(2,1)S(1)}, u32[]{:S(2)}, u32[]{:S(2)}) collective-permute-start(bf16[1016,256]{1,0:T(8,128)(2,1)} %convolution_convert_fusion.10), channel_id=1, source_target_pairs={{0,1},{1,0},{2,3},{3,2},{4,5},{5,4},{6,7},{7,6},{8,9},{9,8},{10,11... | collective-permute-start | bytes 1560584 | tf_op jit(solution)/shard_map/ppermute | solution.py:74
  349.1 38.0 %collective-permute-start.13 = (bf16[1016,256]{1,0:T(8,128)(2,1)}, bf16[1016,256]{1,0:T(8,128)(2,1)S(1)}, u32[]{:S(2)}, u32[]{:S(2)}) collective-permute-start(bf16[1016,256]{1,0:T(8,128)(2,1)} %convolution_convert_fusion.9), channel_id=1, source_target_pairs={{0,2},{1,3},{2,0},{3,1},{4,6},{5,7},{6,4},{7,5},{8,10},{9,11},{10,... | collective-permute-start | bytes 1560584 | tf_op jit(solution)/shard_map/ppermute | solution.py:74
  350.9 36.4 %collective-permute-start.14 = (bf16[1016,256]{1,0:T(8,128)(2,1)}, bf16[1016,256]{1,0:T(8,128)(2,1)S(1)}, u32[]{:S(2)}, u32[]{:S(2)}) collective-permute-start(bf16[1016,256]{1,0:T(8,128)(2,1)} %convolution_convert_fusion.8), channel_id=1, source_target_pairs={{0,3},{1,2},{2,1},{3,0},{4,7},{5,6},{6,5},{7,4},{8,11},{9,10},{10,... | collective-permute-start | bytes 1560584 | tf_op jit(solution)/shard_map/ppermute | solution.py:74
  360.3 16.0 %collective-permute-start.36 = (f32[160,128]{1,0:T(8,128)S(1)}, f32[160,128]{1,0:T(8,128)S(1)}, u32[]{:S(2)}, u32[]{:S(2)}) collective-permute-start(f32[160,128]{1,0:T(8,128)S(1)} %fusion.108), channel_id=1, source_target_pairs={{0,2},{1,3},{2,0},{3,1},{4,6},{5,7},{6,4},{7,5},{8,10},{9,11},{10,... | collective-permute-start | bytes 245768 | tf_op jit(solution)/shard_map/ppermute | solution.py:56
  376.2 4.5 collective-permute-start.37
  380.8 4.5 collective-permute-start.38
  385.3 152.3 %collective-permute-start.8 = (bf16[2,8192]{1,0:T(2,128)(2,1)S(1)}, bf16[2,8192]{1,0:T(2,128)(2,1)S(1)}, u32[]{:S(2)}, u32[]{:S(2)}) collective-permute-start(bf16[2,8192]{1,0:T(2,128)(2,1)S(1)} %get-tuple-element.121), channel_id=1, source_target_pairs={{0,3},{1,2},{2,1},{3,0},{4,7},{5,6},{6,5},{7,4},{8,11},{9,10},{10,... | collective-permute-start | bytes 98312 | tf_op jit(solution)/shard_map/ppermute | solution.py:74
  385.3 154.9 %collective-permute-start.7 = (bf16[2,8192]{1,0:T(2,128)(2,1)S(1)}, bf16[2,8192]{1,0:T(2,128)(2,1)S(1)}, u32[]{:S(2)}, u32[]{:S(2)}) collective-permute-start(bf16[2,8192]{1,0:T(2,128)(2,1)S(1)} %get-tuple-element.122), channel_id=1, source_target_pairs={{0,2},{1,3},{2,0},{3,1},{4,6},{5,7},{6,4},{7,5},{8,10},{9,11},{10,... | collective-permute-start | bytes 98312 | tf_op jit(solution)/shard_map/ppermute | solution.py:74
  387.1 179.9 %collective-permute-start.54 = (bf16[2,2,2,128,512]{4,3,2,1,0:T(8,128)(2,1)}, bf16[2,2,2,128,512]{4,3,2,1,0:T(8,128)(2,1)}, u32[]{:S(2)}, u32[]{:S(2)}) collective-permute-start(bf16[2,2,2,128,512]{4,3,2,1,0:T(8,128)(2,1)} %constant_dynamic-slice_fusion.5), channel_id=1, source_target_pairs={{0,1},{1,0},{2,3},{3,2},{4,5},{5,4},{6,7},{7,6},{8,9},{9,8},{10,11... | collective-permute-start | bytes 3145736 | tf_op jit(solution)/shard_map/ppermute | solution.py:56
  387.3 181.6 %collective-permute-start.28 = (bf16[2,2,2,128,512]{4,3,2,1,0:T(8,128)(2,1)}, bf16[2,2,2,128,512]{4,3,2,1,0:T(8,128)(2,1)}, u32[]{:S(2)}, u32[]{:S(2)}) collective-permute-start(bf16[2,2,2,128,512]{4,3,2,1,0:T(8,128)(2,1)} %constant_dynamic-slice_fusion.20), channel_id=1, source_target_pairs={{0,1},{1,0},{2,3},{3,2},{4,5},{5,4},{6,7},{7,6},{8,9},{9,8},{10,11... | collective-permute-start | bytes 3145736 | tf_op jit(solution)/shard_map/ppermute | solution.py:56
  537.2 81.6 %collective-permute-start.40 = (bf16[2,2,2,128,2048]{4,3,2,1,0:T(8,128)(2,1)}, bf16[2,2,2,128,2048]{4,3,2,1,0:T(8,128)(2,1)}, u32[]{:S(2)}, u32[]{:S(2)}) collective-permute-start(bf16[2,2,2,128,2048]{4,3,2,1,0:T(8,128)(2,1)} %constant_dynamic-slice_fusion.15), channel_id=1, source_target_pairs={{0,1},{1,0},{2,3},{3,2},{4,5},{5,4},{6,7},{7,6},{8,9},{9,8},{10,11... | collective-permute-start | bytes 12582920 | tf_op jit(solution)/shard_map/ppermute | solution.py:56
  537.6 5.6 collective-permute-start.39
  540.2 4.3 collective-permute-start.23
  543.2 96.2 %collective-permute-start.47 = (bf16[2,2,2,512,512]{4,3,2,1,0:T(8,128)(2,1)}, bf16[2,2,2,512,512]{4,3,2,1,0:T(8,128)(2,1)}, u32[]{:S(2)}, u32[]{:S(2)}) collective-permute-start(bf16[2,2,2,512,512]{4,3,2,1,0:T(8,128)(2,1)} %constant_dynamic-slice_fusion.10), channel_id=1, source_target_pairs={{0,1},{1,0},{2,3},{3,2},{4,5},{5,4},{6,7},{7,6},{8,9},{9,8},{10,11... | collective-permute-start | bytes 12582920 | tf_op jit(solution)/shard_map/ppermute | solution.py:56
  544.5 3.8 collective-permute-start.24
  548.3 3.7 collective-permute-start.25
  552.1 3.7 collective-permute-start.26
  555.8 8.0 %collective-permute-start.27 = (f32[4,1024]{1,0:T(4,128)S(1)}, f32[4,1024]{1,0:T(4,128)S(1)}, u32[]{:S(2)}, u32[]{:S(2)}) collective-permute-start(f32[4,1024]{1,0:T(4,128)S(1)} %add.507), channel_id=1, source_target_pairs={{0,16},{4,20},{8,24},{12,28},{16,0},{20,4},{24,8},{28,12},{1,17},{... | collective-permute-start | bytes 49160 | tf_op jit(solution)/shard_map/ppermute | solution.py:56
  563.8 17.9 %collective-permute-start.18 = (bf16[2,2,1,128,768]{3,4,2,1,0:T(8,128)(2,1)}, bf16[2,2,1,128,768]{3,4,2,1,0:T(8,128)(2,1)S(1)}, u32[]{:S(2)}, u32[]{:S(2)}) collective-permute-start(bf16[2,2,1,128,768]{3,4,2,1,0:T(8,128)(2,1)} %copy.65), channel_id=1, source_target_pairs={{0,4},{4,0},{8,12},{12,8},{16,20},{20,16},{24,28},{28,24},{1,5},{5... | collective-permute-start | bytes 2359304 | tf_op jit(solution)/shard_map/ppermute | solution.py:56
  567.0 83.5 %collective-permute-start.16 = (bf16[1016,1024]{1,0:T(8,128)(2,1)}, bf16[1016,1024]{1,0:T(8,128)(2,1)}, u32[]{:S(2)}, u32[]{:S(2)}) collective-permute-start(bf16[1016,1024]{1,0:T(8,128)(2,1)} %get-tuple-element.54), channel_id=1, source_target_pairs={{0,1},{1,0},{2,3},{3,2},{4,5},{5,4},{6,7},{7,6},{8,9},{9,8},{10,11... | collective-permute-start | bytes 6242312 | tf_op jit(solution)/shard_map/ppermute | solution.py:56
  568.9 14.4 %collective-permute-start.55 = (bf16[2,2,2,128,256]{4,3,2,1,0:T(8,128)(2,1)S(1)}, bf16[2,2,2,128,256]{4,3,2,1,0:T(8,128)(2,1)S(1)}, u32[]{:S(2)}, u32[]{:S(2)}) collective-permute-start(bf16[2,2,2,128,256]{4,3,2,1,0:T(8,128)(2,1)S(1)} %constant_dynamic-slice_fusion.4), channel_id=1, source_target_pairs={{0,2},{1,3},{2,0},{3,1},{4,6},{5,7},{6,4},{7,5},{8,10},{9,11},{10,... | collective-permute-start | bytes 1572872 | tf_op jit(solution)/shard_map/ppermute | solution.py:56
  581.7 12.1 %collective-permute-start.29 = (bf16[2,2,1,128,512]{4,3,2,1,0:T(8,128)(2,1)S(1)}, bf16[2,2,1,128,512]{4,3,2,1,0:T(8,128)(2,1)S(1)}, u32[]{:S(2)}, u32[]{:S(2)}) collective-permute-start(bf16[2,2,1,128,512]{4,3,2,1,0:T(8,128)(2,1)S(1)} %constant_dynamic-slice_fusion.19), channel_id=1, source_target_pairs={{0,4},{4,0},{8,12},{12,8},{16,20},{20,16},{24,28},{28,24},{1,5},{5... | collective-permute-start | bytes 1572872 | tf_op jit(solution)/shard_map/ppermute | solution.py:56
  583.3 12.0 %collective-permute-start.19 = (bf16[2,1,1,128,768]{3,4,2,1,0:T(8,128)(2,1)S(1)}, bf16[2,1,1,128,768]{3,4,2,1,0:T(8,128)(2,1)S(1)}, u32[]{:S(2)}, u32[]{:S(2)}) collective-permute-start(bf16[2,1,1,128,768]{3,4,2,1,0:T(8,128)(2,1)S(1)} %constant_dynamic-slice_fusion.22), channel_id=1, source_target_pairs={{0,8},{4,12},{8,0},{12,4},{16,24},{20,28},{24,16},{28,20},{1,9},{5... | collective-permute-start | bytes 1179656 | tf_op jit(solution)/shard_map/ppermute | solution.py:56
  593.8 6.4 collective-permute-start.56
  595.3 7.8 collective-permute-start.30
  600.2 11.3 %collective-permute-start.20 = (bf16[1,1,1,128,768]{3,4,2,1,0:T(8,128)(2,1)S(1)}, bf16[1,1,1,128,768]{3,4,2,1,0:T(8,128)(2,1)S(1)}, u32[]{:S(2)}, u32[]{:S(2)}) collective-permute-start(bf16[1,1,1,128,768]{3,4,2,1,0:T(8,128)(2,1)S(1)} %constant_dynamic-slice_fusion.21), channel_id=1, source_target_pairs={{0,16},{4,20},{8,24},{12,28},{16,0},{20,4},{24,8},{28,12},{1,17},{... | collective-permute-start | bytes 589832 | tf_op jit(solution)/shard_map/ppermute | solution.py:56
  603.1 8.5 %collective-permute-start.57 = (bf16[2,1,1,128,256]{4,3,2,1,0:T(8,128)(2,1)S(1)}, bf16[2,1,1,128,256]{4,3,2,1,0:T(8,128)(2,1)S(1)}, u32[]{:S(2)}, u32[]{:S(2)}) collective-permute-start(bf16[2,1,1,128,256]{4,3,2,1,0:T(8,128)(2,1)S(1)} %constant_dynamic-slice_fusion.2), channel_id=1, source_target_pairs={{0,8},{4,12},{8,0},{12,4},{16,24},{20,28},{24,16},{28,20},{1,9},{5... | collective-permute-start | bytes 393224 | tf_op jit(solution)/shard_map/ppermute | solution.py:56
  611.5 7.3 collective-permute-start.31
  611.5 22.6 %collective-permute-start.21 = (bf16[128,3,256]{0,2,1:T(8,128)(2,1)S(1)}, bf16[128,3,256]{0,2,1:T(8,128)(2,1)S(1)}, u32[]{:S(2)}, u32[]{:S(2)}) collective-permute-start(bf16[128,3,256]{0,2,1:T(8,128)(2,1)S(1)} %bitcast.161), channel_id=1, source_target_pairs={{0,1},{1,0},{2,3},{3,2},{4,5},{5,4},{6,7},{7,6},{8,9},{9,8},{10,11... | collective-permute-start | bytes 589832 | tf_op jit(solution)/shard_map/ppermute | solution.py:56
  618.7 9.1 %collective-permute-start.58 = (bf16[1,1,1,128,256]{4,3,2,1,0:T(8,128)(2,1)S(1)}, bf16[1,1,1,128,256]{4,3,2,1,0:T(8,128)(2,1)S(1)}, u32[]{:S(2)}, u32[]{:S(2)}) collective-permute-start(bf16[1,1,1,128,256]{4,3,2,1,0:T(8,128)(2,1)S(1)} %constant_dynamic-slice_fusion.1), channel_id=1, source_target_pairs={{0,16},{4,20},{8,24},{12,28},{16,0},{20,4},{24,8},{28,12},{1,17},{... | collective-permute-start | bytes 196616 | tf_op jit(solution)/shard_map/ppermute | solution.py:56
  618.8 10.7 %collective-permute-start.32 = (bf16[1,1,1,128,256]{4,3,2,1,0:T(8,128)(2,1)S(1)}, bf16[1,1,1,128,256]{4,3,2,1,0:T(8,128)(2,1)S(1)}, u32[]{:S(2)}, u32[]{:S(2)}) collective-permute-start(bf16[1,1,1,128,256]{4,3,2,1,0:T(8,128)(2,1)S(1)} %constant_dynamic-slice_fusion.16), channel_id=1, source_target_pairs={{0,2},{1,3},{2,0},{3,1},{4,6},{5,7},{6,4},{7,5},{8,10},{9,11},{10,... | collective-permute-start | bytes 196616 | tf_op jit(solution)/shard_map/ppermute | solution.py:56
  627.8 43.5 %collective-permute-start.41 = (bf16[2,2,1,128,2048]{4,3,2,1,0:T(8,128)(2,1)}, bf16[2,2,1,128,2048]{4,3,2,1,0:T(8,128)(2,1)S(1)}, u32[]{:S(2)}, u32[]{:S(2)}) collective-permute-start(bf16[2,2,1,128,2048]{4,3,2,1,0:T(8,128)(2,1)} %constant_dynamic-slice_fusion.14), channel_id=1, source_target_pairs={{0,4},{4,0},{8,12},{12,8},{16,20},{20,16},{24,28},{28,24},{1,5},{5... | collective-permute-start | bytes 6291464 | tf_op jit(solution)/shard_map/ppermute | solution.py:56
  629.6 4.3 collective-permute-start.59
  633.9 4.3 collective-permute-start.33
  634.1 4.1 collective-permute-start.60
  638.2 65.2 %collective-permute-start.15 = (bf16[1016,1024]{1,0:T(8,128)(2,1)}, bf16[1016,1024]{1,0:T(8,128)(2,1)}, u32[]{:S(2)}, u32[]{:S(2)}) collective-permute-start(bf16[1016,1024]{1,0:T(8,128)(2,1)} %get-tuple-element.52), channel_id=1, source_target_pairs={{0,1},{1,0},{2,3},{3,2},{4,5},{5,4},{6,7},{7,6},{8,9},{9,8},{10,11... | collective-permute-start | bytes 6242312 | tf_op jit(solution)/shard_map/ppermute | solution.py:56
  638.2 12.0 %collective-permute-start.22 = (bf16[128,3,512]{0,2,1:T(8,128)(2,1)S(1)}, bf16[128,3,512]{0,2,1:T(8,128)(2,1)S(1)}, u32[]{:S(2)}, u32[]{:S(2)}) collective-permute-start(bf16[128,3,512]{0,2,1:T(8,128)(2,1)S(1)} %maximum_select_fusion.5), channel_id=1, source_target_pairs={{0,2},{1,3},{2,0},{3,1},{4,6},{5,7},{6,4},{7,5},{8,10},{9,11},{10,... | collective-permute-start | bytes 1179656 | tf_op jit(solution)/shard_map/ppermute | solution.py:56
  639.4 5.8 collective-permute-start.34
  645.1 50.1 %collective-permute-start.48 = (bf16[2,2,2,512,256]{4,3,2,1,0:T(8,128)(2,1)}, bf16[2,2,2,512,256]{4,3,2,1,0:T(8,128)(2,1)}, u32[]{:S(2)}, u32[]{:S(2)}) collective-permute-start(bf16[2,2,2,512,256]{4,3,2,1,0:T(8,128)(2,1)} %constant_dynamic-slice_fusion.9), channel_id=1, source_target_pairs={{0,2},{1,3},{2,0},{3,1},{4,6},{5,7},{6,4},{7,5},{8,10},{9,11},{10,... | collective-permute-start | bytes 6291464 | tf_op jit(solution)/shard_map/ppermute | solution.py:56
  654.3 85.2 %collective-permute-start.17 = (bf16[1016,1024]{1,0:T(8,128)(2,1)}, bf16[1016,1024]{1,0:T(8,128)(2,1)}, u32[]{:S(2)}, u32[]{:S(2)}) collective-permute-start(bf16[1016,1024]{1,0:T(8,128)(2,1)} %add_convert_fusion.5), channel_id=1, source_target_pairs={{0,2},{1,3},{2,0},{3,1},{4,6},{5,7},{6,4},{7,5},{8,10},{9,11},{10,... | collective-permute-start | bytes 6242312 | tf_op jit(solution)/shard_map/ppermute | solution.py:56
  673.8 24.6 %collective-permute-start.42 = (bf16[2,1,1,128,2048]{4,3,2,1,0:T(8,128)(2,1)S(1)}, bf16[2,1,1,128,2048]{4,3,2,1,0:T(8,128)(2,1)}, u32[]{:S(2)}, u32[]{:S(2)}) collective-permute-start(bf16[2,1,1,128,2048]{4,3,2,1,0:T(8,128)(2,1)S(1)} %constant_dynamic-slice_fusion.13), channel_id=1, source_target_pairs={{0,8},{4,12},{8,0},{12,4},{16,24},{20,28},{24,16},{28,20},{1,9},{5... | collective-permute-start | bytes 3145736 | tf_op jit(solution)/shard_map/ppermute | solution.py:56
  698.1 45.4 %collective-permute-start.49 = (bf16[2,2,1,512,256]{4,3,2,1,0:T(8,128)(2,1)S(1)}, bf16[2,2,1,512,256]{4,3,2,1,0:T(8,128)(2,1)S(1)}, u32[]{:S(2)}, u32[]{:S(2)}) collective-permute-start(bf16[2,2,1,512,256]{4,3,2,1,0:T(8,128)(2,1)S(1)} %constant_dynamic-slice_fusion.8), channel_id=1, source_target_pairs={{0,4},{4,0},{8,12},{12,8},{16,20},{20,16},{24,28},{28,24},{1,5},{5... | collective-permute-start | bytes 3145736 | tf_op jit(solution)/shard_map/ppermute | solution.py:56
  700.4 46.4 %collective-permute-start.43 = (bf16[1,1,1,128,2048]{4,3,2,1,0:T(8,128)(2,1)S(1)}, bf16[1,1,1,128,2048]{4,3,2,1,0:T(8,128)(2,1)S(1)}, u32[]{:S(2)}, u32[]{:S(2)}) collective-permute-start(bf16[1,1,1,128,2048]{4,3,2,1,0:T(8,128)(2,1)S(1)} %constant_dynamic-slice_fusion.12), channel_id=1, source_target_pairs={{0,16},{4,20},{8,24},{12,28},{16,0},{20,4},{24,8},{28,12},{1,17},{... | collective-permute-start | bytes 1572872 | tf_op jit(solution)/shard_map/ppermute | solution.py:56
  743.9 14.7 %collective-permute-start.50 = (bf16[2,1,1,512,256]{4,3,2,1,0:T(8,128)(2,1)S(1)}, bf16[2,1,1,512,256]{4,3,2,1,0:T(8,128)(2,1)S(1)}, u32[]{:S(2)}, u32[]{:S(2)}) collective-permute-start(bf16[2,1,1,512,256]{4,3,2,1,0:T(8,128)(2,1)S(1)} %constant_dynamic-slice_fusion.7), channel_id=1, source_target_pairs={{0,8},{4,12},{8,0},{12,4},{16,24},{20,28},{24,16},{28,20},{1,9},{5... | collective-permute-start | bytes 1572872 | tf_op jit(solution)/shard_map/ppermute | solution.py:56
  747.0 13.7 %collective-permute-start.44 = (bf16[1,1,1,128,1024]{4,3,2,1,0:T(8,128)(2,1)S(1)}, bf16[1,1,1,128,1024]{4,3,2,1,0:T(8,128)(2,1)S(1)}, u32[]{:S(2)}, u32[]{:S(2)}) collective-permute-start(bf16[1,1,1,128,1024]{4,3,2,1,0:T(8,128)(2,1)S(1)} %constant_dynamic-slice_fusion.11), channel_id=1, source_target_pairs={{0,2},{1,3},{2,0},{3,1},{4,6},{5,7},{6,4},{7,5},{8,10},{9,11},{10,... | collective-permute-start | bytes 786440 | tf_op jit(solution)/shard_map/ppermute | solution.py:56
  758.8 13.9 %collective-permute-start.51 = (bf16[1,1,1,512,256]{4,3,2,1,0:T(8,128)(2,1)S(1)}, bf16[1,1,1,512,256]{4,3,2,1,0:T(8,128)(2,1)S(1)}, u32[]{:S(2)}, u32[]{:S(2)}) collective-permute-start(bf16[1,1,1,512,256]{4,3,2,1,0:T(8,128)(2,1)S(1)} %constant_dynamic-slice_fusion.6), channel_id=1, source_target_pairs={{0,16},{4,20},{8,24},{12,28},{16,0},{20,4},{24,8},{28,12},{1,17},{... | collective-permute-start | bytes 786440 | tf_op jit(solution)/shard_map/ppermute | solution.py:56
  760.8 12.2 %collective-permute-start.45 = (bf16[128,1024]{1,0:T(8,128)(2,1)S(1)}, bf16[128,1024]{1,0:T(8,128)(2,1)S(1)}, u32[]{:S(2)}, u32[]{:S(2)}) collective-permute-start(bf16[128,1024]{1,0:T(8,128)(2,1)S(1)} %fusion.67), channel_id=1, source_target_pairs={{0,2},{1,3},{2,0},{3,1},{4,6},{5,7},{6,4},{7,5},{8,10},{9,11},{10,... | collective-permute-start | bytes 786440 | tf_op jit(solution)/shard_map/ppermute | solution.py:56
  772.8 7.4 collective-permute-start.52
  773.1 10.5 %collective-permute-start.46 = (bf16[128,2048]{1,0:T(8,128)(2,1)S(1)}, bf16[128,2048]{1,0:T(8,128)(2,1)S(1)}, u32[]{:S(2)}, u32[]{:S(2)}) collective-permute-start(bf16[128,2048]{1,0:T(8,128)(2,1)S(1)} %maximum_select_fusion.3), channel_id=1, source_target_pairs={{0,1},{1,0},{2,3},{3,2},{4,5},{5,4},{6,7},{7,6},{8,9},{9,8},{10,11... | collective-permute-start | bytes 1572872 | tf_op jit(solution)/shard_map/ppermute | solution.py:56
  780.3 4.8 collective-permute-start.53
  (62 other events, 1016.8 us)

commit v2 on v1

v2 whole, which is shorter than its diff:
```python
import functools

import jax
import jax.numpy as jnp
from jax import lax
from jax.experimental import pallas as pl
from jax.experimental.pallas import tpu as pltpu
from jax.sharding import PartitionSpec as P

HEADS = 16
HEAD = 64
LT = 8
IMGS = 8
BLK = 256
NEG = -1e30
VMEM = 60 << 20
ROW_BLOCK = 256
GRAD_BLOCK = 512

highest = lax.Precision.HIGHEST
epsilon = 1e-06
f32 = jnp.float32
bf16 = jnp.bfloat16


def smooth_both(v):
    half = jnp.abs(v) * 0.7071067811865476
    t = 1.0 / (1.0 + 0.3275911 * half)
    bell = jnp.exp(-half * half)
    poly = t * (
        0.127414796
        + t * (-0.142248368 + t * (0.7107068705 + t * (-0.7265760135 + t * 0.5307027145)))
    )
    tail = poly * bell
    cdf = jnp.where(v >= 0.0, 1.0 - tail, tail)
    return v * cdf, cdf + v * (bell * 0.3989422804014327)


def matmul(left, right):
    return jnp.dot(left, right, preferred_element_type=f32)


def nt(left, right):
    return lax.dot_general(left, right, (((1,), (1,)), ((), ())), preferred_element_type=f32)


def tn(left, right):
    return lax.dot_general(left, right, (((0,), (0,)), ((), ())), preferred_element_type=f32)


def row_images(counts, device, local_rows, row_count):
    upper_end = counts * (device + 1) // row_count
    lower_end = counts * device // row_count
    run_ends = jnp.cumsum(upper_end - lower_end)
    positions = jnp.arange(local_rows, dtype=jnp.int32)
    return jnp.sum((positions[:, None] >= run_ends[None, :]).astype(jnp.int32), axis=1)


def bits_of(size):
    return [1 << i for i in range(size.bit_length() - 1)]


def jump(value, row_mask, img_mask=0):
    rows, imgs = lax.axis_size("row"), lax.axis_size("img")
    if img_mask == 0:
        return lax.ppermute(value, "row", [(i, i ^ row_mask) for i in range(rows)])
    if row_mask == 0:
        return lax.ppermute(value, "img", [(i, i ^ img_mask) for i in range(imgs)])
    mask = img_mask * rows + row_mask
    return lax.ppermute(value, ("img", "row"), [(i, i ^ mask) for i in range(rows * imgs)])


def masks_of(bits):
    masks = []
    for e in range(1 << len(bits)):
        masks.append(
            tuple(
                sum(bit for j, (axis, bit) in enumerate(bits) if axis == name and e >> j & 1)
                for name in ("row", "img")
            )
        )
    return masks


def gather_pieces(value):
    pieces = {0: value}
    order = sorted(range(1, lax.axis_size("row")), key=lambda d: (d & 1, d))
    for d in order:
        low = d & -d
        pieces[d] = jump(pieces[d ^ low], low)
    return [pieces[d] for d in range(lax.axis_size("row"))]


def send_pieces(pieces):
    far_first = sorted(range(1, len(pieces)), reverse=True)
    arrived = {d: jump(pieces[d], d) for d in far_first}
    return [pieces[0]] + [arrived[d] for d in range(1, len(pieces))]


def stages():
    row_bits = [("row", b) for b in bits_of(lax.axis_size("row"))]
    img_bits = [("img", b) for b in bits_of(lax.axis_size("img"))]
    return row_bits, img_bits


def tree(values):
    while len(values) > 1:
        values = [values[i] + values[i + 1] for i in range(0, len(values), 2)]
    return values[0]


def behind(value, after):
    return lax.optimization_barrier((value, *after))[0] if after else value


def reduce_stage(value, bits, img_count, after=()):
    mine = {"row": lax.axis_index("row"), "img": lax.axis_index("img")}

    def part(e):
        piece = value
        for j, (axis, bit) in enumerate(bits):
            want = (mine[axis] // bit) % 2 ^ (e >> j & 1)
            dim = value.ndim - 1 if axis == "row" else img_count - bit.bit_length()
            length = piece.shape[dim] // 2
            piece = lax.dynamic_slice_in_dim(piece, want * length, length, dim)
        return piece

    masks = masks_of(bits)
    arrived = {
        e: behind(jump(part(e), *masks[e]), after) for e in reversed(range(1, len(masks)))
    }
    arrived[0] = part(0)
    return tree([arrived[e].astype(f32) for e in range(len(masks))]).astype(bf16)


def spread_img(grad):
    rows, columns = grad.shape
    images = lax.axis_size("img")
    return grad.reshape((2,) * len(bits_of(images)) + (rows // images, columns))


def gather_columns(value, order, bits):
    masks = [row_mask for row_mask, _ in masks_of(bits)]
    device = lax.axis_index("row") % len(masks)
    stack = jnp.stack([value if m == 0 else jump(value, m) for m in masks])
    return [
        lax.dynamic_index_in_dim(stack, order(c) ^ device, 0, False) for c in range(len(masks))
    ]


def exchange_sum(value, bits):
    values = [value] + [jump(value, *mask) for mask in masks_of(bits)[1:]]
    return tree([v.astype(f32) for v in values]).astype(bf16)


def reversed_bits(index, size):
    width = size.bit_length() - 1
    return int(format(index, f"0{width}b")[::-1], 2) if width else 0


def finish_weight(value, bits):
    value = value.reshape(value.shape[-2:])
    count = 1 << len(bits)
    blocks = gather_columns(value, lambda c: reversed_bits(c, count), bits)
    return jnp.concatenate(blocks, axis=1).astype(f32)


def params(flags=("arbitrary",)):
    return pltpu.CompilerParams(dimension_semantics=flags, vmem_limit_bytes=VMEM)


ANYWHERE = pl.BlockSpec(memory_space=pl.ANY)


def own_columns(w_qkv, device, features, splits):
    width = w_qkv.shape[0]
    wide = features // splits

    def spec(s, part):
        def index(b, me):
            return 0, part * (width // wide) + me[0] * splits + s

        return pl.BlockSpec((width, wide), index, pipeline_mode=pl.Buffered(1))

    return [spec(s, part) for s in range(splits) for part in range(3)], [w_qkv] * (3 * splits)


def valid_rows(block, piece_rows, local_rows):
    position = lax.broadcasted_iota(jnp.int32, (BLK, 1), 0) % piece_rows + block * piece_rows
    return position < local_rows


def load_block(refs, block, piece_rows, local_rows):
    value = jnp.concatenate([ref[...] for ref in refs], axis=0).astype(f32)
    return jnp.where(valid_rows(block, piece_rows, local_rows), value, 0.0)


def norm_parts(value):
    centre = value - jnp.mean(value, axis=-1, keepdims=True)
    rstd = lax.rsqrt(jnp.mean(centre * centre, axis=-1, keepdims=True) + epsilon)
    return centre * rstd, rstd


def qkv_kernel(count, splits, local_rows, features, me_ref, *refs):
    n_w = 3 * splits
    pieces, columns = refs[:count], refs[count : count + n_w]
    bias_ref, gain_ref, shift_ref = refs[count + n_w : count + n_w + 3]
    n_ref, q_ref, k_ref, v_ref, kt_ref, vt_ref, w_ref = refs[count + n_w + 3 :]
    block = pl.program_id(0)
    wide = features // splits

    @pl.when(block == 0)
    def _():
        for i, ref in enumerate(columns):
            w_ref[:, i * wide : (i + 1) * wide] = ref[...]

    unit, _ = norm_parts(load_block(pieces, block, BLK // count, local_rows))
    normed = (unit * gain_ref[...] + shift_ref[...]).astype(bf16)
    n_ref[...] = normed.reshape(n_ref.shape)
    mixed = matmul(normed, w_ref[...])
    for s in range(splits):
        at = slice(s * wide, (s + 1) * wide)
        part = mixed[:, 3 * s * wide : 3 * (s + 1) * wide]
        keys = part[:, wide : 2 * wide]
        values = part[:, 2 * wide :] + bias_ref[1:2, at]
        q_ref[:, at] = ((part[:, :wide] + bias_ref[0:1, at]) * 0.125).astype(bf16)
        k_ref[:, at] = keys.astype(bf16)
        v_ref[:, at] = values.astype(bf16)
        kt_ref[0, at] = keys.T.astype(bf16)
        vt_ref[0, at] = values.T.astype(bf16)


def qkv_call(me, pieces, w_qkv, bias, gain, shift, splits):
    count, (local_rows, width) = len(pieces), pieces[0].shape
    features = width // count
    piece_rows = BLK // count
    blocks = pl.cdiv(local_rows, piece_rows)
    whole = lambda a: pl.BlockSpec(a.shape, lambda b, m: (0,) * a.ndim)
    flat = pl.BlockSpec((BLK, features), lambda b, m: (b, 0))
    turned = pl.BlockSpec((1, features, BLK), lambda b, m: (b, 0, 0))
    specs, operands = own_columns(w_qkv, me, features, splits)
    return pl.pallas_call(
        functools.partial(qkv_kernel, count, splits, local_rows, features),
        grid_spec=pltpu.PrefetchScalarGridSpec(
            num_scalar_prefetch=1,
            grid=(blocks,),
            in_specs=[pl.BlockSpec((piece_rows, width), lambda b, m: (b, 0))] * count
            + specs
            + [whole(bias), whole(gain), whole(shift)],
            out_specs=[
                pl.BlockSpec((count, piece_rows, width), lambda b, m: (0, b, 0)),
                flat,
                flat,
                flat,
                turned,
                turned,
            ],
            scratch_shapes=[pltpu.VMEM((width, 3 * features), bf16)],
        ),
        out_shape=[jax.ShapeDtypeStruct((count, blocks * piece_rows, width), bf16)]
        + [jax.ShapeDtypeStruct((blocks * BLK, features), bf16)] * 3
        + [jax.ShapeDtypeStruct((blocks, features, BLK), bf16)] * 2,
        compiler_params=params(),
        cost_estimate=pl.CostEstimate(
            flops=6 * blocks * BLK * width * 3 * features,
            bytes_accessed=2 * blocks * BLK * (2 * width + 5 * features),
            transcendentals=0,
        ),
    )(me, *pieces, *operands, bias, gain, shift)


def per_head(stack_ref, value, heads):
    lane = lax.broadcasted_iota(jnp.int32, value.shape, 1) // HEAD
    for h in range(heads):
        stack_ref[h] = jnp.where(lane == h, value, jnp.zeros_like(value))


def attend_kernel(count, heads, lo_ref, hi_ref, *refs):
    q_ref, k_ref, vt_ref, imgq_ref, imgk_ref = refs[:5]
    outs, (ot_ref, lse_ref) = refs[5 : 5 + count], refs[5 + count : 7 + count]
    s_ref, qs_ref, acc_ref = refs[7 + count :]
    block = pl.program_id(0)
    lo, hi = lo_ref[block], hi_ref[block]
    per_head(qs_ref, q_ref[...], heads)
    imgq = imgq_ref[...]

    def first(kb, tops):
        rows = pl.ds(pl.multiple_of(kb * BLK, BLK), BLK)
        keys = k_ref[rows, :]
        allowed = imgk_ref[rows, :] == imgq
        new = []
        for h in range(heads):
            s = jnp.where(allowed, nt(keys, qs_ref[h]), NEG)
            s_ref[kb - lo, h] = s
            new.append(jnp.maximum(tops[h], jnp.max(s.reshape(BLK // 8, 8, BLK), axis=0)))
        return tuple(new)

    tops = lax.fori_loop(lo, hi, first, (jnp.full((8, BLK), NEG, f32),) * heads)
    tops = [jnp.max(t, axis=0, keepdims=True) for t in tops]
    acc_ref[...] = jnp.zeros_like(acc_ref)

    def second(kb, sums):
        new = []
        for h in range(heads):
            p = jnp.exp(s_ref[kb - lo, h] - tops[h])
            new.append(sums[h] + jnp.sum(p.reshape(BLK // 8, 8, BLK), axis=0))
            rows = slice(h * HEAD, (h + 1) * HEAD)
            acc_ref[rows, :] += matmul(vt_ref[kb, rows, :], p.astype(bf16))
        return tuple(new)

    sums = lax.fori_loop(lo, hi, second, (jnp.zeros((8, BLK), f32),) * heads)
    sums = [jnp.sum(t, axis=0, keepdims=True) for t in sums]
    for h in range(heads):
        rows = slice(h * HEAD, (h + 1) * HEAD)
        acc_ref[rows, :] = acc_ref[rows, :] / sums[h]
    lse_ref[...] = jnp.concatenate(
        [t + jnp.log(s) for t, s in zip(tops, sums)] + [jnp.zeros((8 - heads, BLK), f32)], axis=0
    )
    ot_ref[0] = acc_ref[...]
    out = acc_ref[...].T.astype(bf16)
    for d in range(count):
        outs[d][...] = out[d * (BLK // count) : (d + 1) * (BLK // count)]


def attend_call(q, k, vt, imgq, imgk, lo, hi, count):
    blocks, features = vt.shape[0], q.shape[1]
    heads = features // HEAD
    piece_rows = BLK // count
    whole = lambda a: pl.BlockSpec(a.shape, lambda b, *_: (0,) * a.ndim)
    return pl.pallas_call(
        functools.partial(attend_kernel, count, heads),
        grid_spec=pltpu.PrefetchScalarGridSpec(
            num_scalar_prefetch=2,
            grid=(blocks,),
            in_specs=[
                pl.BlockSpec((BLK, features), lambda b, *_: (b, 0)),
                whole(k),
                whole(vt),
                pl.BlockSpec((1, BLK), lambda b, *_: (0, b)),
                whole(imgk),
            ],
            out_specs=[pl.BlockSpec((piece_rows, features), lambda b, *_: (b, 0))] * count
            + [
                pl.BlockSpec((1, features, BLK), lambda b, *_: (b, 0, 0)),
                pl.BlockSpec((8, BLK), lambda b, *_: (0, b)),
            ],
            scratch_shapes=[
                pltpu.VMEM((blocks, heads, BLK, BLK), f32),
                pltpu.VMEM((heads, BLK, features), bf16),
                pltpu.VMEM((features, BLK), f32),
            ],
        ),
        out_shape=[jax.ShapeDtypeStruct((blocks * piece_rows, features), bf16)] * count
        + [
            jax.ShapeDtypeStruct((blocks, features, BLK), f32),
            jax.ShapeDtypeStruct((8, blocks * BLK), f32),
        ],
        compiler_params=params(),
        cost_estimate=pl.CostEstimate(
            flops=10 * (blocks * BLK) ** 2 * features,
            bytes_accessed=2 * blocks * BLK * features * 8,
            transcendentals=0,
        ),
    )(lo, hi, q, k, vt, imgq, imgk)


def attend_back_kernel(count, heads, first, waits, lo_ref, hi_ref, *refs):
    pieces, refs = refs[:count], refs[:count] + refs[count + waits :]
    q_ref, k_ref, v_ref, kt_ref, ot_ref, lse_ref, imgq_ref, imgk_ref = refs[count : count + 8]
    groups = count // 2
    outs, sums_ref = refs[count + 8 : count + groups + 8], refs[count + groups + 8]
    qs_ref, dos_ref, p_ref, ds_ref, dqt_ref, dk_ref, dv_ref = refs[count + groups + 9 :]
    block = pl.program_id(0)
    lo, hi = lo_ref[block], hi_ref[block]
    piece_rows = BLK // count
    wide = heads * HEAD

    @pl.when(block == 0)
    def _():
        dk_ref[...] = jnp.zeros_like(dk_ref)
        dv_ref[...] = jnp.zeros_like(dv_ref)
        sums_ref[...] = jnp.zeros_like(sums_ref)

    grad = jnp.concatenate([ref[...] for ref in pieces], axis=0)
    query = q_ref[...]
    lane = lax.broadcasted_iota(jnp.int32, grad.shape, 1) // HEAD
    for h in range(heads):
        dos_ref[h * BLK : (h + 1) * BLK] = jnp.where(lane == h, grad, jnp.zeros_like(grad))
        qs_ref[h * BLK : (h + 1) * BLK] = jnp.where(lane == h, query, jnp.zeros_like(query))
    both = grad.astype(f32).T * ot_ref[0]
    delta = [
        jnp.sum(both[h * HEAD : (h + 1) * HEAD], axis=0, keepdims=True) for h in range(heads)
    ]
    logsum = [lse_ref[first + h : first + h + 1, :] for h in range(heads)]
    imgq = imgq_ref[...]
    dqt_ref[...] = jnp.zeros_like(dqt_ref)

    def step(kb, width):
        length = width * BLK
        rows = pl.ds(pl.multiple_of(kb * BLK, BLK), length)
        keys, values = k_ref[rows, :], v_ref[rows, :]
        allowed = imgk_ref[rows, :] == imgq
        s = nt(keys, qs_ref[...])
        dp = nt(values, dos_ref[...])
        for h in range(heads):
            cols = slice(h * BLK, (h + 1) * BLK)
            p = jnp.exp(jnp.where(allowed, s[:, cols] - logsum[h], NEG))
            p_ref[:length, cols] = p.astype(bf16)
            ds_ref[:length, cols] = (p * (dp[:, cols] - delta[h])).astype(bf16)
        dv_ref[rows, :] += matmul(p_ref[:length], dos_ref[...])
        dk_ref[rows, :] += matmul(ds_ref[:length], qs_ref[...])
        for h in range(heads):
            cols, feats = slice(h * BLK, (h + 1) * BLK), slice(h * HEAD, (h + 1) * HEAD)
            total = 0.0
            for j in range(width):
                ds = ds_ref[j * BLK : (j + 1) * BLK, cols]
                total = total + matmul(kt_ref[kb + j, feats, :], ds)
            dqt_ref[feats, :] += total

    def pair(i, _):
        step(lo + 2 * i, 2)
        return 0

    lax.fori_loop(0, (hi - lo) // 2, pair, 0)

    @pl.when((hi - lo) % 2 == 1)
    def _():
        step(hi - 1, 1)

    dq = dqt_ref[...].T * 0.125
    sums_ref[0:1, :] += jnp.sum(dq, axis=0, keepdims=True)
    here = pl.ds(pl.multiple_of(block * piece_rows, piece_rows), piece_rows)
    for d in range(count):
        outs[d // 2][d % 2, here, :wide] = dq[d * piece_rows : (d + 1) * piece_rows].astype(bf16)

    @pl.when(block == pl.num_programs(0) - 1)
    def _():
        sums_ref[1:2, :] = jnp.sum(dv_ref[...], axis=0, keepdims=True)

        def move(b, _):
            to = pl.ds(pl.multiple_of(b * piece_rows, piece_rows), piece_rows)
            for d in range(count):
                at = pl.ds(pl.multiple_of(b * BLK + d * piece_rows, piece_rows), piece_rows)
                outs[d // 2][d % 2, to, wide : 2 * wide] = dk_ref[at, :].astype(bf16)
                outs[d // 2][d % 2, to, 2 * wide :] = dv_ref[at, :].astype(bf16)
            return 0

        lax.fori_loop(0, pl.num_programs(0), move, 0)


def attend_back_call(pieces, q, k, v, kt, ot, lse, imgq, imgk, lo, hi, split, after):
    count, (rows, wide) = len(pieces), pieces[0].shape
    blocks = kt.shape[0]
    heads = wide // HEAD
    once = pl.Buffered(1)
    half = pl.BlockSpec((blocks * BLK, wide), lambda b, *_: (0, split), pipeline_mode=once)
    out = jax.ShapeDtypeStruct((2, rows, 3 * wide), bf16)
    return pl.pallas_call(
        functools.partial(attend_back_kernel, count, heads, split * heads, len(after)),
        grid_spec=pltpu.PrefetchScalarGridSpec(
            num_scalar_prefetch=2,
            grid=(blocks,),
            in_specs=[pl.BlockSpec((BLK // count, wide), lambda b, *_: (b, 0))] * count
            + [ANYWHERE] * len(after)
            + [
                pl.BlockSpec((BLK, wide), lambda b, *_: (b, split)),
                half,
                half,
                pl.BlockSpec((blocks, wide, BLK), lambda b, *_: (0, split, 0), pipeline_mode=once),
                pl.BlockSpec((1, wide, BLK), lambda b, *_: (b, split, 0)),
                pl.BlockSpec((8, BLK), lambda b, *_: (0, b)),
                pl.BlockSpec((1, BLK), lambda b, *_: (0, b)),
                pl.BlockSpec(imgk.shape, lambda b, *_: (0, 0), pipeline_mode=once),
            ],
            out_specs=[pl.BlockSpec(out.shape, lambda b, *_: (0, 0, 0), pipeline_mode=once)] * (count // 2)
            + [pl.BlockSpec((8, wide), lambda b, *_: (0, 0))],
            scratch_shapes=[
                pltpu.VMEM((heads * BLK, wide), bf16),
                pltpu.VMEM((heads * BLK, wide), bf16),
                pltpu.VMEM((2 * BLK, heads * BLK), bf16),
                pltpu.VMEM((2 * BLK, heads * BLK), bf16),
                pltpu.VMEM((wide, BLK), f32),
                pltpu.VMEM((blocks * BLK, wide), f32),
                pltpu.VMEM((blocks * BLK, wide), f32),
            ],
        ),
        out_shape=[out] * (count // 2) + [jax.ShapeDtypeStruct((8, wide), f32)],
        compiler_params=params(),
        cost_estimate=pl.CostEstimate(
            flops=16 * (blocks * BLK) ** 2 * wide,
            bytes_accessed=2 * blocks * BLK * wide * 12,
            transcendentals=0,
        ),
    )(lo, hi, *pieces, *after, q, k, v, kt, ot, lse, imgq, imgk)


def norm_back(grad, unit, rstd, gain):
    e = grad * gain
    mean = jnp.mean(e, axis=-1, keepdims=True)
    return (e - mean - unit * jnp.mean(e * unit, axis=-1, keepdims=True)) * rstd


def total(value):
    return jnp.sum(value, axis=0, keepdims=True)


def rows_kernel(count, splits, local_rows, *refs):
    (
        tok_ref,
        img_ref,
        w_out_ref,
        w_up_ref,
        w_down_ref,
        learn_in_ref,
        learn_out_ref,
        vec_ref,
        up_bias_ref,
        out_bias_ref,
        pooled_grad_ref,
    ) = refs[:11]
    attended = refs[11 : 11 + count]
    at = 11 + count
    (
        n2_ref,
        gated_ref,
        gup_ref,
        gres_ref,
        n3_ref,
        glearn_ref,
        inner_ref,
        glogit_ref,
        ghid_ref,
        ghid_f32_ref,
    ) = refs[at : at + 10]
    gatt = refs[at + 10 : at + 10 + count * splits]
    at += 10 + count * splits
    pooled_ref, vsum_ref, usum_ref, lsum_ref = refs[at : at + 4]
    hid_ref, res_ref, dgate_ref, up0_ref, up1_ref = refs[at + 4 :]
    step = pl.program_id(0)
    rows, width = tok_ref.shape
    hidden_units = w_up_ref.shape[1]
    chunk = up0_ref.shape[1]
    chunks = hidden_units // chunk

    @pl.when(step == 0)
    def _():
        for ref in (pooled_ref, vsum_ref, usum_ref, lsum_ref):
            ref[...] = jnp.zeros_like(ref)

    def vec(i):
        return vec_ref[i : i + 1, :]

    position = lax.broadcasted_iota(jnp.int32, (rows, 1), 0) + step * rows
    tok = jnp.where(position < local_rows, tok_ref[...].astype(f32), 0.0)
    low = jnp.concatenate([ref[...] for ref in attended], axis=1)
    hidden = tok + matmul(low, w_out_ref[...]) + vec(0)
    hid_ref[...] = hidden
    unit, _ = norm_parts(hidden)
    n2_ref[...] = (unit * vec(2) + vec(3)).astype(bf16)

    def columns(j):
        return pl.ds(pl.multiple_of(j * chunk, chunk), chunk)

    def up(ref, j):
        ref[...] = matmul(n2_ref[...], w_up_ref[:, columns(j)])

    def gate(ref, j):
        value, slope = smooth_both(ref[...] + up_bias_ref[:, columns(j)])
        gated_ref[:, columns(j)] = value.astype(bf16)
        dgate_ref[:, columns(j)] = slope

    up(up0_ref, 0)

    def pair(i, _):
        up(up1_ref, 2 * i + 1)
        gate(up0_ref, 2 * i)
        up(up0_ref, jnp.minimum(2 * i + 2, chunks - 1))
        gate(up1_ref, 2 * i + 1)
        return 0

    lax.fori_loop(0, chunks // 2, pair, 0)
    result = hid_ref[...] + matmul(gated_ref[...], w_down_ref[...]) + vec(1)
    res_ref[...] = result
    unit, rstd = norm_parts(result)
    n3_ref[...] = (unit * vec(4) + vec(5)).astype(bf16)
    inner, slope = smooth_both(matmul(n3_ref[...], learn_in_ref[...]) + vec(6))
    inner_ref[...] = inner.astype(bf16)
    maps = jax.nn.sigmoid(matmul(inner_ref[...], learn_out_ref[...]) + out_bias_ref[...])
    member = lax.broadcasted_iota(jnp.int32, maps.shape, 1) // LT == img_ref[...]
    spread = jnp.where(member, maps, 0.0).astype(bf16)
    result_low = res_ref[...].astype(bf16)
    pooled_ref[...] += tn(spread, result_low)
    grad_spread = nt(result_low, pooled_grad_ref[...])
    grad_logit = jnp.where(member, grad_spread * maps * (1.0 - maps), 0.0)
    lsum_ref[...] += total(grad_logit)
    glogit_ref[...] = grad_logit.astype(bf16)
    grad_pre = nt(glogit_ref[...], learn_out_ref[...]) * slope
    vsum_ref[6:7, :] += total(grad_pre)
    glearn_ref[...] = grad_pre.astype(bf16)
    back = nt(glearn_ref[...], learn_in_ref[...])
    unit, rstd = norm_parts(res_ref[...])
    vsum_ref[4:5, :] += total(back * unit)
    vsum_ref[5:6, :] += total(back)
    grad_result = matmul(spread, pooled_grad_ref[...]) + norm_back(back, unit, rstd, vec(4))
    vsum_ref[1:2, :] += total(grad_result)
    res_ref[...] = grad_result
    gres_ref[...] = grad_result.astype(bf16)

    def down_back(j, _):
        grad = nt(gres_ref[...], w_down_ref[columns(j), :]) * dgate_ref[:, columns(j)]
        usum_ref[:, columns(j)] += total(grad)
        gup_ref[:, columns(j)] = grad.astype(bf16)
        return 0

    lax.fori_loop(0, chunks, down_back, 0)
    back = nt(gup_ref[...], w_up_ref[...])
    unit, rstd = norm_parts(hid_ref[...])
    vsum_ref[2:3, :] += total(back * unit)
    vsum_ref[3:4, :] += total(back)
    grad_hidden = res_ref[...] + norm_back(back, unit, rstd, vec(2))
    vsum_ref[0:1, :] += total(grad_hidden)
    ghid_f32_ref[...] = grad_hidden
    ghid_ref[...] = grad_hidden.astype(bf16)
    grad = nt(ghid_ref[...], w_out_ref[...]).astype(bf16)
    wide = width // (count * splits)
    for i in range(count * splits):
        gatt[i][...] = grad[:, i * wide : (i + 1) * wide]


def rows_call(tok, img, attended, w_out, w_up, w_down, learn_in, learn_out, vecs, up_bias, out_bias, pooled_grad, splits):
    count, (rows, features) = len(attended), attended[0].shape
    local_rows, width = tok.shape
    hidden_units = w_up.shape[1]
    inner = learn_in.shape[1]
    spread = learn_out.shape[1]
    block = min(ROW_BLOCK, rows)
    chunk = 512
    wide = features // splits
    once = lambda a: pl.BlockSpec(a.shape, lambda i: (0,) * a.ndim, pipeline_mode=pl.Buffered(1))
    by_rows = lambda n: pl.BlockSpec((block, n), lambda i: (i, 0))
    kept = lambda a: pl.BlockSpec(a.shape, lambda i: (0, 0))
    low = lambda n: jax.ShapeDtypeStruct((rows, n), bf16)
    lows = [width, hidden_units, hidden_units, width, width, inner, inner, spread, width]
    sums = [
        jax.ShapeDtypeStruct((spread, width), f32),
        jax.ShapeDtypeStruct((8, width), f32),
        jax.ShapeDtypeStruct((1, hidden_units), f32),
        jax.ShapeDtypeStruct((1, spread), f32),
    ]
    resident = [w_out, w_up, w_down, learn_in, learn_out, vecs, up_bias, out_bias, pooled_grad]
    return pl.pallas_call(
        functools.partial(rows_kernel, count, splits, local_rows),
        grid=(rows // block,),
        in_specs=[by_rows(width), by_rows(1)]
        + [once(a) for a in resident]
        + [by_rows(features)] * count,
        out_specs=[by_rows(n) for n in lows]
        + [by_rows(width)]
        + [by_rows(wide)] * (count * splits)
        + [kept(a) for a in sums],
        out_shape=[low(n) for n in lows]
        + [jax.ShapeDtypeStruct((rows, width), f32)]
        + [low(wide)] * (count * splits)
        + sums,
        scratch_shapes=[
            pltpu.VMEM((block, width), f32),
            pltpu.VMEM((block, width), f32),
            pltpu.VMEM((block, hidden_units), f32),
            pltpu.VMEM((block, chunk), f32),
            pltpu.VMEM((block, chunk), f32),
        ],
        compiler_params=params(),
        cost_estimate=pl.CostEstimate(
            flops=4 * rows * width * (width + 2 * hidden_units + inner),
            bytes_accessed=2 * (rows * 20 * width + 2 * width * hidden_units),
            transcendentals=0,
        ),
    )(tok, img, *resident, *attended)


def grad_kernel(waits, left_ref, right_ref, *refs):
    refs[waits][...] = tn(left_ref[...], right_ref[...]).astype(bf16)


def grad_call(left, right, by_left, after=()):
    rows, m = left.shape
    n = right.shape[1]
    once = pl.Buffered(1)
    if by_left:
        grid, left_block, right_block, out_block = m // GRAD_BLOCK, GRAD_BLOCK, n, (GRAD_BLOCK, n)
        specs = [
            pl.BlockSpec((rows, left_block), lambda j: (0, j)),
            pl.BlockSpec((rows, right_block), lambda j: (0, 0), pipeline_mode=once),
        ]
        out_spec = pl.BlockSpec(out_block, lambda j: (j, 0))
    else:
        grid, left_block, right_block, out_block = n // GRAD_BLOCK, m, GRAD_BLOCK, (m, GRAD_BLOCK)
        specs = [
            pl.BlockSpec((rows, left_block), lambda j: (0, 0), pipeline_mode=once),
            pl.BlockSpec((rows, right_block), lambda j: (0, j)),
        ]
        out_spec = pl.BlockSpec(out_block, lambda j: (0, j))
    return pl.pallas_call(
        functools.partial(grad_kernel, len(after)),
        grid=(grid,),
        in_specs=specs + [ANYWHERE] * len(after),
        out_specs=out_spec,
        out_shape=jax.ShapeDtypeStruct((m, n), bf16),
        compiler_params=params(),
        cost_estimate=pl.CostEstimate(
            flops=3 * rows * m * n, bytes_accessed=4 * m * n, transcendentals=0
        ),
    )(left, right, *after)


def small_grad_kernel(count, waits, me_ref, *refs):
    n3_ref, glearn_ref, ghid_ref, inner_ref, glogit_ref = refs[:5]
    attended = refs[5 : 5 + count]
    out_ref, lout_ref = refs[5 + count + waits :]
    learn_columns = glearn_ref.shape[1]
    out_ref[:, :learn_columns] = tn(n3_ref[...], glearn_ref[...]).astype(bf16)
    lout_ref[...] = tn(inner_ref[...], glogit_ref[...])
    features = attended[0].shape[1]
    for d in range(count):
        owner = jnp.bitwise_xor(me_ref[0], d)
        to = pl.ds(pl.multiple_of(owner * features, features), features)
        out_ref[to, learn_columns:] = tn(attended[d][...], ghid_ref[...]).astype(bf16)


def small_grad_call(me, n3, glearn, ghid, inner, glogit, attended, after=()):
    rows, width = n3.shape
    operands = [n3, glearn, ghid, inner, glogit, *attended]
    out = jax.ShapeDtypeStruct((width, glearn.shape[1] + ghid.shape[1]), bf16)
    lout = jax.ShapeDtypeStruct((inner.shape[1], glogit.shape[1]), f32)
    once = lambda a: pl.BlockSpec(a.shape, lambda j, m: (0, 0), pipeline_mode=pl.Buffered(1))
    return pl.pallas_call(
        functools.partial(small_grad_kernel, len(attended), len(after)),
        grid_spec=pltpu.PrefetchScalarGridSpec(
            num_scalar_prefetch=1,
            grid=(1,),
            in_specs=[once(a) for a in operands] + [ANYWHERE] * len(after),
            out_specs=[once(out), once(lout)],
        ),
        out_shape=[out, lout],
        compiler_params=params(),
        cost_estimate=pl.CostEstimate(
            flops=6 * rows * width * width, bytes_accessed=20 * width * width, transcendentals=0
        ),
    )(me, *operands, *after)


def qkv_grad_kernel(groups, splits, waits, n_ref, *refs):
    parts = refs[: groups * splits]
    out_ref, acc_ref = refs[groups * splits + waits :]
    step = pl.program_id(0)
    columns = parts[0].shape[2]
    for d in range(2 * groups):

        @pl.when(step == d)
        def _():
            for s in range(splits):
                at = slice(s * columns, (s + 1) * columns)
                part = tn(n_ref[0], parts[s * groups + d // 2][d % 2])
                acc_ref[:, at] = part if d == 0 else acc_ref[:, at] + part

    @pl.when(step == 2 * groups - 1)
    def _():
        out_ref[...] = acc_ref[...].astype(bf16)


def qkv_grad_call(normed, parts, splits, after=()):
    count, rows, width = normed.shape
    columns = parts[0].shape[2] * splits
    once = lambda a: pl.BlockSpec(a.shape, lambda d: (0, 0, 0), pipeline_mode=pl.Buffered(1))
    return pl.pallas_call(
        functools.partial(qkv_grad_kernel, count // 2, splits, len(after)),
        grid=(count,),
        in_specs=[pl.BlockSpec((1, rows, width), lambda d: (d, 0, 0))]
        + [once(a) for a in parts]
        + [ANYWHERE] * len(after),
        out_specs=pl.BlockSpec((width, columns), lambda d: (0, 0)),
        out_shape=jax.ShapeDtypeStruct((width, columns), bf16),
        scratch_shapes=[pltpu.VMEM((width, columns), f32)],
        compiler_params=params(),
        cost_estimate=pl.CostEstimate(
            flops=3 * count * rows * width * columns,
            bytes_accessed=2 * count * rows * width,
            transcendentals=0,
        ),
    )(normed, *parts, *after)


def norm_sums_kernel(count, splits, local_rows, waits, me_ref, *refs):
    groups = count // 2
    pieces, parts = refs[:count], refs[count : count + groups * splits]
    at = count + groups * splits
    columns, (sums_ref, w_ref) = refs[at : at + 3 * splits], refs[at + 3 * splits + waits :]
    wide = columns[0].shape[1]
    block = pl.program_id(0)

    @pl.when(block == 0)
    def _():
        sums_ref[...] = jnp.zeros_like(sums_ref)
        for i, ref in enumerate(columns):
            w_ref[:, i * wide : (i + 1) * wide] = ref[...]

    unit, _ = norm_parts(load_block(pieces, block, BLK // count, local_rows))
    mixed = jnp.concatenate(
        [
            jnp.concatenate(
                [parts[s * groups + d // 2][d % 2] for d in range(count)], axis=0
            )
            for s in range(splits)
        ],
        axis=1,
    )
    back = nt(mixed, w_ref[...])
    sums_ref[0:1, :] += total(back * unit)
    sums_ref[1:2, :] += total(back)


def norm_sums_call(me, pieces, parts, w_qkv, after=()):
    count, (local_rows, width) = len(pieces), pieces[0].shape
    splits, columns = 2 * len(parts) // count, parts[0].shape[2]
    piece_rows = BLK // count
    blocks = parts[0].shape[1] // piece_rows
    specs, operands = own_columns(w_qkv, me, width // count, splits)
    return pl.pallas_call(
        functools.partial(norm_sums_kernel, count, splits, local_rows, len(after)),
        grid_spec=pltpu.PrefetchScalarGridSpec(
            num_scalar_prefetch=1,
            grid=(blocks,),
            in_specs=[pl.BlockSpec((piece_rows, width), lambda b, m: (b, 0))] * count
            + [pl.BlockSpec((2, piece_rows, columns), lambda b, m: (0, b, 0))] * len(parts)
            + specs
            + [ANYWHERE] * len(after),
            out_specs=pl.BlockSpec((8, width), lambda b, m: (0, 0)),
            scratch_shapes=[pltpu.VMEM((width, columns * splits), bf16)],
        ),
        out_shape=jax.ShapeDtypeStruct((8, width), f32),
        compiler_params=params(),
        cost_estimate=pl.CostEstimate(
            flops=4 * blocks * BLK * width * columns * splits,
            bytes_accessed=2 * blocks * BLK * width,
            transcendentals=0,
        ),
    )(me, *pieces, *parts, *operands, *after)


def tokens_kernel(groups, splits, me_ref, tok_ref, ghid_ref, w_ref, gain_ref, *refs):
    same, other = refs[: groups * splits], refs[groups * splits : groups * splits + splits]
    out_ref, mixed_ref = refs[groups * splits + splits :]
    width = tok_ref.shape[1]
    features = width // (2 * groups)
    wide = features // splits
    for d in range(2 * groups):
        owner = jnp.bitwise_xor(me_ref[0], d) * features
        for s in range(splits):
            for part in range(3):
                to = pl.ds(pl.multiple_of(part * width + owner + s * wide, wide), wide)
                at = slice(part * wide, (part + 1) * wide)
                if d % 2 == 0:
                    mixed_ref[:, to] = same[s * groups + d // 2][0, :, at]
                else:
                    mixed_ref[:, to] = other[s][d // 2, :, at]
    back = nt(mixed_ref[...], w_ref[...])
    unit, rstd = norm_parts(tok_ref[...].astype(f32))
    out_ref[0] = ghid_ref[...] + norm_back(back, unit, rstd, gain_ref[...])


def tokens_call(me, tok, ghid, w_qkv, gain, same, other, count):
    local_rows, width = tok.shape
    columns = same[0].shape[2]
    groups, splits = count // 2, len(other)
    block = 256
    by_rows = lambda n: pl.BlockSpec((block, n), lambda i, m: (i, 0))
    return pl.pallas_call(
        functools.partial(tokens_kernel, groups, splits),
        grid_spec=pltpu.PrefetchScalarGridSpec(
            num_scalar_prefetch=1,
            grid=(pl.cdiv(local_rows, block),),
            in_specs=[
                by_rows(width),
                by_rows(width),
                pl.BlockSpec(w_qkv.shape, lambda i, m: (0, 0), pipeline_mode=pl.Buffered(1)),
                pl.BlockSpec(gain.shape, lambda i, m: (0, 0)),
            ]
            + [pl.BlockSpec((1, block, columns), lambda i, m: (0, i, 0))] * len(same)
            + [pl.BlockSpec((groups, block, columns), lambda i, m: (0, i, 0))] * splits,
            out_specs=pl.BlockSpec((1, block, width), lambda i, m: (0, i, 0)),
            scratch_shapes=[pltpu.VMEM((block, 3 * width), bf16)],
        ),
        out_shape=jax.ShapeDtypeStruct((1, local_rows, width), f32),
        compiler_params=params(),
        cost_estimate=pl.CostEstimate(
            flops=12 * local_rows * width * width,
            bytes_accessed=local_rows * width * 16,
            transcendentals=0,
        ),
    )(me, tok, ghid, w_qkv, gain, *same, *other)


def flip(index, bit):
    return index + bit - 2 * bit * ((index // bit) % 2)


def vectors_kernel(count, row_bits, img_bits, vec_ref, slot_ref, out_ref, sum_ref, *scratch):
    recv, slot_recv, send_sem, recv_sem, slot_send, slot_got = scratch
    row, img = lax.axis_index("row"), lax.axis_index("img")

    def partner(row_mask, img_mask=0):
        r, g = row, img
        for bit in row_bits:
            r = flip(r, bit) if row_mask & bit else r
        for bit in img_bits:
            g = flip(g, bit) if img_mask & bit else g
        return (g, r)

    steps = [(bit, 0) for bit in row_bits] + [(0, bit) for bit in img_bits]
    everyone = sorted(set(steps) | {(d, 0) for d in range(1, count)})
    barrier = pltpu.get_barrier_semaphore()
    for masks in everyone:
        pl.semaphore_signal(
            barrier, inc=1, device_id=partner(*masks), device_id_type=pl.DeviceIdType.MESH
        )
    pl.semaphore_wait(barrier, len(everyone))
    slots = []
    for d in range(1, count):
        copy = pltpu.make_async_remote_copy(
            src_ref=slot_ref.at[d],
            dst_ref=slot_recv.at[d - 1],
            send_sem=slot_send.at[d - 1],
            recv_sem=slot_got.at[d - 1],
            device_id=partner(d),
            device_id_type=pl.DeviceIdType.MESH,
        )
        copy.start()
        slots.append(copy)
    out_ref[...] = vec_ref[...]
    for i, masks in enumerate(steps):
        copy = pltpu.make_async_remote_copy(
            src_ref=out_ref,
            dst_ref=recv.at[i],
            send_sem=send_sem.at[i],
            recv_sem=recv_sem.at[i],
            device_id=partner(*masks),
            device_id_type=pl.DeviceIdType.MESH,
        )
        copy.start()
        copy.wait()
        out_ref[...] = out_ref[...] + recv[i]
    for copy in slots:
        copy.wait()
    sum_ref[...] = tree(
        [slot_ref[0].astype(f32)] + [slot_recv[d - 1].astype(f32) for d in range(1, count)]
    )


def vectors_call(vec, slots):
    count = lax.axis_size("row")
    row_bits, img_bits = bits_of(count), bits_of(lax.axis_size("img"))
    steps = len(row_bits) + len(img_bits)
    whole = pl.BlockSpec(memory_space=pltpu.VMEM)
    return pl.pallas_call(
        functools.partial(vectors_kernel, count, row_bits, img_bits),
        in_specs=[whole, whole],
        out_specs=[whole, whole],
        out_shape=[
            jax.ShapeDtypeStruct(vec.shape, f32),
            jax.ShapeDtypeStruct(slots.shape[1:], f32),
        ],
        scratch_shapes=[
            pltpu.VMEM((steps,) + vec.shape, f32),
            pltpu.VMEM((count - 1,) + slots.shape[1:], bf16),
            pltpu.SemaphoreType.DMA((steps,)),
            pltpu.SemaphoreType.DMA((steps,)),
            pltpu.SemaphoreType.DMA((count - 1,)),
            pltpu.SemaphoreType.DMA((count - 1,)),
        ],
        compiler_params=pltpu.CompilerParams(
            collective_id=0, has_side_effects=True, vmem_limit_bytes=32 << 20
        ),
        cost_estimate=pl.CostEstimate(flops=1 << 33, bytes_accessed=1 << 20, transcendentals=0),
    )(vec, slots)


def rows_of(array, index, length):
    return lax.dynamic_slice_in_dim(array, index * length, length, 0)


def on_device(
    tokens,
    counts,
    owner,
    w_qkv,
    qv_bias,
    w_out,
    out_bias,
    w_up,
    up_bias,
    w_down,
    down_bias,
    norm_gain,
    norm_bias,
    learn_in,
    learn_in_bias,
    learn_out,
    learn_out_bias,
    cotangent,
):
    width = tokens.shape[2]
    local_rows = tokens.shape[1]
    row_count = lax.axis_size("row")
    images_count = lax.axis_size("img")
    device = lax.axis_index("row")
    image_device = lax.axis_index("img")
    features = width // row_count
    wide = min(features, 128)
    splits = features // wide
    slots_here = IMGS // row_count
    group_counts = counts[0]
    partners = [device ^ d for d in range(row_count)]
    row_bits, img_bits = stages()
    n_img = len(img_bits)

    pieces = gather_pieces(tokens[0])
    grads_in = gather_pieces(cotangent[0].reshape(slots_here, LT * width).astype(bf16))

    piece_rows = BLK // row_count
    blocks = pl.cdiv(local_rows, piece_rows)
    images = jnp.stack([row_images(group_counts, p, local_rows, row_count) for p in partners])
    extra = blocks * piece_rows - local_rows
    images = jnp.pad(images, ((0, 0), (0, extra)), constant_values=IMGS + 1)
    image_here = images[0].reshape(-1, 1)
    images = images.reshape(row_count, blocks, piece_rows).transpose(1, 0, 2).reshape(blocks, BLK)
    least, most = jnp.min(images, axis=1), jnp.max(images, axis=1)
    lo = jnp.sum((most[None, :] < least[:, None]).astype(jnp.int32), axis=1)
    hi = jnp.sum((least[None, :] <= most[:, None]).astype(jnp.int32), axis=1)
    imgq, imgk = images.reshape(1, -1), images.reshape(-1, 1)

    me = device.reshape(1)
    w_out_here = jnp.concatenate([rows_of(w_out, p, features) for p in partners], axis=0)
    bias_here = lax.dynamic_slice_in_dim(qv_bias, device * features, features, 1)

    normed, q, k, v, kt, vt = qkv_call(
        me, pieces, w_qkv, bias_here, norm_gain[0:1], norm_bias[0:1], splits
    )
    *attended, ot, lse = attend_call(q, k, vt, imgq, imgk, lo, hi, row_count)
    attended = send_pieces(attended)

    slot_rel = ((owner[0] // slots_here) ^ device) * slots_here + owner[0] % slots_here
    select = (slot_rel[:, None] == jnp.arange(IMGS, dtype=jnp.int32)[None, :]).astype(f32)
    scale = lax.rsqrt(group_counts.astype(f32))
    incoming = jnp.concatenate(grads_in, axis=0).astype(f32)
    grad_pooled = jnp.dot(select, incoming, precision=highest) * scale[:, None]
    grad_pooled_low = grad_pooled.reshape(IMGS * LT, width).astype(bf16)

    vecs = jnp.concatenate(
        [
            out_bias[None],
            down_bias[None],
            norm_gain[1:2],
            norm_bias[1:2],
            norm_gain[2:3],
            norm_bias[2:3],
            learn_in_bias[None],
            jnp.zeros((1, width), f32),
        ],
        axis=0,
    )
    out = rows_call(
        tokens[0],
        image_here,
        attended,
        w_out_here,
        w_up,
        w_down,
        learn_in,
        jnp.tile(learn_out, (1, IMGS)),
        vecs,
        up_bias[None],
        jnp.tile(learn_out_bias, IMGS)[None],
        grad_pooled_low,
        splits,
    )
    n2, gated, gup, gres, n3, glearn, inner, glogit, ghid, grad_hidden = out[:10]
    grad_attended = out[10 : 10 + row_count * splits]
    pooled, vec_sums, up_sums, logit_sums = out[10 + row_count * splits :]
    grad_attended = [send_pieces(grad_attended[s::splits]) for s in range(splits)]

    core, far_row = row_bits[:1], row_bits[1:]
    y_bits, z_bits = img_bits[:1], [[bit] for bit in img_bits[1:]]
    stage = lambda value, bits, after=(): reduce_stage(value, bits, n_img, after)
    stack_other = lambda groups: jump(jnp.stack([g[1] for g in groups]), 1)

    small, grad_learn_out = small_grad_call(me, n3, glearn, ghid, inner, glogit, attended)
    small = spread_img(small)
    grad_down = grad_call(gated, gres, True, [small])
    small = stage(small, core, [grad_down])
    grad_up = grad_call(n2, gup, False, [grad_down, small])
    down = stage(spread_img(grad_down), core, [grad_up])

    def back_call(s, after):
        *parts, sums = attend_back_call(
            grad_attended[s], q, k, v, kt, ot, lse, imgq, imgk, lo, hi, s, after
        )
        return parts, sums

    mixed, same, other, qkv_sums = [], [], [], []
    ups = spread_img(grad_up)
    for s in range(splits):
        parts, sums = back_call(s, [down, ups] if s == 0 else [small, ups, down])
        mixed += parts
        qkv_sums.append(sums[0:2])
        here = [parts[0]] + [jump(parts[g], 2 * g) for g in range(1, len(parts))]
        if s == 0:
            small = stage(small, y_bits, [sums])
            ups = stage(ups, core, [sums])
            down = stage(down, far_row, [sums])
            first = here
    if splits > 1:
        first = [first[0]] + [behind(h, [sums]) for h in first[1:]]
        same = first + here
    else:
        same = here
    ups = stage(ups, y_bits, [sums])
    down = stage(down, z_bits[0], [sums])
    small = stage(small, z_bits[0], [sums])
    other = [stack_other(first)]
    grad_qkv = qkv_grad_call(normed, mixed, splits, [down, ups, small])
    if splits > 1:
        other.append(stack_other([here[0]] + [behind(h, [grad_qkv]) for h in here[1:]]))
    norm_sums = norm_sums_call(me, pieces, mixed, w_qkv, [grad_qkv])
    down = stage(down, z_bits[1], [norm_sums])
    small = stage(small, z_bits[1], [norm_sums])
    ups = stage(ups, z_bits[0], [norm_sums])
    grad_qkv = stage(spread_img(grad_qkv), y_bits, [norm_sums])
    for bits in z_bits[1:]:
        ups = stage(ups, bits)
    for bits in z_bits[2:]:
        down = stage(down, bits)
        small = stage(small, bits)
    down = stage(down, y_bits)
    for bits in z_bits:
        grad_qkv = stage(grad_qkv, bits)
    grad_tokens = tokens_call(
        me, tokens[0], grad_hidden, w_qkv, norm_gain[0:1], same, other, row_count
    )

    by_slot = jnp.dot(select.T, pooled.reshape(IMGS, LT * width), precision=highest)
    by_slot = by_slot.astype(bf16).reshape(row_count, -1, 128)
    late = lax.dynamic_update_slice(
        jnp.zeros((2, width), f32), jnp.concatenate(qkv_sums, axis=1), (0, device * features)
    )
    vectors = jnp.concatenate(
        [
            up_sums.reshape(-1),
            vec_sums.reshape(-1),
            jnp.sum(grad_learn_out.reshape(-1, IMGS, LT), axis=1).reshape(-1),
            late.reshape(-1),
            norm_sums[0:2].reshape(-1),
            jnp.sum(logit_sums.reshape(IMGS, LT), axis=0),
        ]
    )
    vectors = jnp.pad(vectors, (0, -vectors.shape[0] % 1024)).reshape(-1, 128)
    vectors, learned = vectors_call(vectors, by_slot)
    vectors = vectors.reshape(-1)
    scale_here = jnp.dot(scale, select, precision=highest)[:slots_here]
    learned = learned.reshape(slots_here, LT * width) * scale_here[:, None]
    learned = learned.reshape(1, slots_here, LT, width)

    share_down = finish_weight(down, row_bits)
    share_small = finish_weight(exchange_sum(small, far_row), core)
    share_up = finish_weight(exchange_sum(ups, far_row), core)
    share_learn = share_small[:, : learn_in.shape[1]]
    share_out = share_small[:, learn_in.shape[1] :]
    shares = gather_columns(grad_qkv.reshape(grad_qkv.shape[-2:]), lambda c: c, row_bits)
    share_qkv = jnp.concatenate(
        [
            shares[c][:, (3 * s + part) * wide : (3 * s + part + 1) * wide]
            for part in range(3)
            for c in range(row_count)
            for s in range(splits)
        ],
        axis=1,
    ).astype(f32)

    at = up_bias.shape[0]
    up_sum, vec_sums = vectors[:at], vectors[at : at + 8 * width].reshape(8, width)
    at += 8 * width
    learn_out_sum = vectors[at : at + learn_out.size].reshape(learn_out.shape)
    at += learn_out.size
    late = vectors[at : at + 4 * width].reshape(4, width)
    at += 4 * width
    out_sum, down_sum, gain_two, shift_two, gain_three, shift_three, learn_in_sum = vec_sums[:7]
    share_learn_out = rows_of(learn_out_sum, image_device, learn_out.shape[0] // images_count)
    return (
        learned,
        grad_tokens,
        share_qkv,
        late[0:2],
        share_out,
        out_sum,
        share_up,
        up_sum,
        share_down,
        down_sum,
        jnp.stack([late[2], gain_two, gain_three]),
        jnp.stack([late[3], shift_two, shift_three]),
        share_learn,
        learn_in_sum,
        share_learn_out,
        vectors[at : at + learn_out.shape[1]],
    )


def solution(mesh):
    by_image = P("img", None)
    in_specs = (
        (P("img", "row", None), by_image, by_image) + (P(),) * 14 + (P("img", "row", None, None),)
    )
    out_specs = (
        P("img", "row", None, None),
        P("img", "row", None),
        by_image,
        P(),
        by_image,
        P(),
        by_image,
        P(),
        by_image,
        P(),
        P(),
        P(),
        by_image,
        P(),
        by_image,
        P(),
    )
    return jax.shard_map(
        on_device, mesh=mesh, in_specs=in_specs, out_specs=out_specs, check_vma=False
    )
```

time: 802 us -> 659 us (0.82); the launches traced: 787 us -> 654 us
  matrix products: 171 us -> 0.84 us
  Pallas kernels: 223 us -> 353 us
  waiting for transfers between devices: 228 us -> 152 us
  other arithmetic: 55 us -> 43.6 us
    dot_general x25 -> x1, matrix products: 170 us -> 0.39 us  [on_device(): jnp.dot(select.T, pooled.reshape(IMGS, LT * width), precision=highest)]
    pallas_call x3 -> x11, Pallas kernels: 167 us -> 302 us  [the longest x1 92.8 us: rows_call(): pl.pallas_call(functools.partial(rows_kernel, count, splits, local_rows),...]
    ppermute x61 -> x45, waiting for transfers between devices: 228 us -> 152 us  [the longest x33 97.5 us: jump(): return lax.ppermute(value, 'row', [(i, i ^ row_mask) for i in range(rows)])]
    reduce_sum x8 -> x2, other arithmetic: 13.7 us -> 0.04 us  [the longest x1 0.02 us: on_device(): jnp.sum(logit_sums.reshape(IMGS, LT), axis=0)]
    unnamed x149 -> x129, local copies, waits for them, and re-layouts: 25.6 us -> 14.4 us
    dynamic_slice x24 -> x16, local copies, waits for them, and re-layouts: 20.5 us -> 19 us  [part(): piece = lax.dynamic_slice_in_dim(piece, want * length, length, dim)]
    ppermute x61 -> x45, starting transfers between devices: 45.8 us -> 45 us  [the longest x12 24.1 us: jump(): return lax.ppermute(value, 'img', [(i, i ^ img_mask) for i in range(imgs)])]
    convert_element_type x27 -> x18, other arithmetic: 31.5 us -> 31.1 us  [the longest x14 26.6 us: reduce_stage(): tree([arrived[e].astype(f32) for e in range(len(masks))]).astype(bf16)]
  transfers between devices with their start and end apart: 61 -> 45, of which waited for: 26 -> 13; matrix products, arithmetic and copies ran while one was open for 13% -> 13% of each run, Pallas kernels for 28% -> 36%
where the time goes in v2:
time: 659 us; the launch traced here: 654 us
  Pallas kernels  353 us (54%)
  waiting for transfers between devices  152 us (23%)
  local copies, waits for them, and re-layouts  57.4 us (9%)
  starting transfers between devices  45 us (7%)
  other arithmetic  43.6 us (7%)
    ppermute x33, waiting for transfers between devices, jump(): return lax.ppermute(value, 'row', [(i, i ^ row_mask) for i in range(rows)])  97.5 us
    pallas_call x1, Pallas kernels, rows_call(): pl.pallas_call(functools.partial(rows_kernel, count, splits, local_rows),...  92.8 us
    pallas_call x2, Pallas kernels, attend_back_call(): pl.pallas_call(functools.partial(attend_back_kernel, count, heads, split...  75.9 us
    ppermute x12, waiting for transfers between devices, jump(): return lax.ppermute(value, 'img', [(i, i ^ img_mask) for i in range(imgs)])  54.9 us
    pallas_call x1, Pallas kernels, attend_call(): pl.pallas_call(functools.partial(attend_kernel, count, heads), grid_spec=...  50.9 us
    pallas_call x2, Pallas kernels, grad_call(): pl.pallas_call(functools.partial(grad_kernel, len(after)), grid=(grid,),...  28.8 us
    convert_element_type x14, other arithmetic, reduce_stage(): tree([arrived[e].astype(f32) for e in range(len(masks))]).astype(bf16)  26.6 us
    ppermute x12, starting transfers between devices, jump(): return lax.ppermute(value, 'img', [(i, i ^ img_mask) for i in range(imgs)])  24.1 us
  transfers between devices with their start and end apart: 45, of which 13 were waited for; matrix products, arithmetic and copies ran while one was open for 13% of the time, Pallas kernels for 36%

profile of v2, /device:TPU:0, one launch (start us, length us, event | category | flops | bytes accessed | tf_op | source)
XLA Modules:
  0.0 654.1 jit_solution(17010293503648710240)
XLA Ops:
  0.7 3.0 collective-permute-start.4
  5.3 44.3 %collective-permute-done.4.refs_2_ = bf16[1016,1024]{1,0:T(8,128)(2,1)} collective-permute-done((bf16[1016,1024]{1,0:T(8,128)(2,1)}, bf16[1016,1024]{1,0:T(8,128)(2,1)}, u32[]{:S(2)}, u32[]{:S(2)}) %collective-permute-start.4) | collective-permute-done | bytes 2080800 | tf_op jit(solution)/shard_map/ppermute | solution.py:66
  52.3 3.4 reshape_reshape.8.refs_4_.refs_13_.refs_14_
  56.1 1.3 constant_dynamic-slice_fusion.17.refs_10_
  59.8 22.7 %shard_map.297 = (bf16[4,1024,1024]{2,1,0:T(8,128)(2,1)}, bf16[4096,256]{1,0:T(8,128)(2,1)}, bf16[4096,256]{1,0:T(8,128)(2,1)}, bf16[4096,256]{1,0:T(8,128)(2,1)...) custom-call(s32[1]{0:T(128)} %bitcast.21.me_ref, bf16[1016,1024]{1,0:T(8,128)(2,1)} %bitcast.148, ...), custom_call_target="tpu_custom_call" | custom-call | flops 19327352832 | bytes 27262976 | tf_op jit(solution)/shard_map/pallas_call | solution.py:242
  82.5 50.9 %shard_map.298 = (bf16[1024,256]{1,0:T(8,128)(2,1)}, bf16[1024,256]{1,0:T(8,128)(2,1)}, bf16[1024,256]{1,0:T(8,128)(2,1)}, bf16[1024,256]{1,0:T(8,128)(2,1)}, f3...) custom-call(s32[16]{0:T(128)} %get-tuple-element.183.lo_ref, s32[16]{0:T(128)} %get-tuple-element.182.hi_ref, ...), custom_call_target="tpu_custom_call" | custom-call | flops 42949672960 | bytes 16777216 | tf_op jit(solution)/shard_map/pallas_call | solution.py:330
  134.0 1.7 collective-permute-start.7
  135.8 1.5 pad_maximum_fusion.refs_2_
  141.9 7.2 %collective-permute-done.7.refs_13_.refs_7_ = bf16[1024,256]{1,0:T(8,128)(2,1)S(1)} collective-permute-done((bf16[1024,256]{1,0:T(8,128)(2,1)}, bf16[1024,256]{1,0:T(8,128)(2,1)S(1)}, u32[]{:S(2)}, u32[]{:S(2)}) %collective-permute-start.7) | collective-permute-done | bytes 524320 | tf_op jit(solution)/shard_map/ppermute | solution.py:66
  149.0 9.7 %collective-permute-done.8.refs_14_.refs_8_ = bf16[1024,256]{1,0:T(8,128)(2,1)} collective-permute-done((bf16[1024,256]{1,0:T(8,128)(2,1)}, bf16[1024,256]{1,0:T(8,128)(2,1)}, u32[]{:S(2)}, u32[]{:S(2)}) %collective-permute-start.8) | collective-permute-done | bytes 524320 | tf_op jit(solution)/shard_map/ppermute | solution.py:66
  158.7 92.8 %shard_map.299 = (bf16[1024,1024]{1,0:T(8,128)(2,1)}, bf16[1024,4096]{1,0:T(8,128)(2,1)}, bf16[1024,4096]{1,0:T(8,128)(2,1)}, bf16[1024,1024]{1,0:T(8,128)(2,1)}...) custom-call(bf16[1016,1024]{1,0:T(8,128)(2,1)} %bitcast.149, ...), custom_call_target="tpu_custom_call" | custom-call | flops 42949672960 | bytes 58720256 | tf_op jit(solution)/shard_map/pallas_call | solution.py:651
  251.6 11.2 %shard_map.300 = (bf16[1024,2048]{1,0:T(8,128)(2,1)}, f32[1024,64]{1,0:T(8,128)}) custom-call(s32[1]{0:T(128)} %bitcast.21.me_ref, bf16[1024,1024]{1,0:T(8,128)(2,1)} %get-tuple-element.83.refs_0_, bf16[1024,1024]{1,0:T(8,128)(2,1)} %get-tuple-element.84.refs_1_, bf16[1024,1024]{1,0:T(8,128)(2,1)} %get-tuple-element.85.refs_2_, ...), custom_call_target="tpu_custom_call" | custom-call | flops 6442450944 | bytes 20971520 | tf_op jit(solution)/shard_map/pallas_call | solution.py:736
  262.7 14.4 %shard_map.301.refs_0_ = bf16[4096,1024]{1,0:T(8,128)(2,1)} custom-call(bf16[1024,4096]{1,0:T(8,128)(2,1)} %get-tuple-element.93.left_ref, bf16[1024,1024]{1,0:T(8,128)(2,1)} %get-tuple-element.94.right_ref, bf16[2,2,2,128,2048]{4,3,2,1,0:T(8,128)(2,1)} %bitcast.143), custom_call_target="tpu_custom_call" | custom-call | flops 12884901888 | bytes 16777216 | tf_op jit(solution)/shard_map/pallas_call | solution.py:703
  277.1 4.7 constant_dynamic-slice_fusion.16
  282.3 1.5 constant_dynamic-slice_fusion.15
  286.4 1.7 collective-permute-start.10
  288.9 3.8 collective-permute-done.13
  292.7 1.3 copy-done.21
  294.4 3.2 add_convert_fusion.4.refs_1_
  297.7 1.2 copy-done.9
  299.0 14.4 %shard_map.302 = bf16[1024,4096]{1,0:T(8,128)(2,1)} custom-call(bf16[1024,1024]{1,0:T(8,128)(2,1)} %get-tuple-element.96.left_ref, bf16[1024,4096]{1,0:T(8,128)(2,1)} %get-tuple-element.97.right_ref, bf16[4096,1024]{1,0:T(8,128)(2,1)} %shard_map.301.refs_0_, bf16[2,2,2,128,1024]{4,3,2,1,0:T(8,128)(2,1)} %copy-done.9), custom_call_target="tpu_custom_call" | custom-call | flops 12884901888 | bytes 16777216 | tf_op jit(solution)/shard_map/pallas_call | solution.py:703
  313.4 4.8 constant_dynamic-slice_fusion.13
  318.4 4.7 add_convert_fusion.1.refs_4_
  323.1 1.6 constant_dynamic-slice_fusion.12
  325.7 1.7 collective-permute-start.15
  327.4 6.7 %collective-permute-start.17 = (bf16[2,2,1,128,1024]{4,3,2,1,0:T(8,128)(2,1)S(1)}, bf16[2,2,1,128,1024]{4,3,2,1,0:T(8,128)(2,1)}, u32[]{:S(2)}, u32[]{:S(2)}) collective-permute-start(bf16[2,2,1,128,1024]{4,3,2,1,0:T(8,128)(2,1)S(1)} %constant_dynamic-slice_fusion.14), channel_id=1, source_target_pairs={{0,4},{4,0},{8,12},{12,8},{16,20},{20,16},{24,28},{28,24},{1,5},{5... | collective-permute-start | bytes 3145736 | tf_op jit(solution)/shard_map/ppermute | solution.py:68
  334.7 38.0 %shard_map.303 = (bf16[2,1024,384]{2,1,0:T(8,128)(2,1)}, bf16[2,1024,384]{2,1,0:T(8,128)(2,1)}, f32[8,128]{1,0:T(8,128)}) custom-call(s32[16]{0:T(128)} %get-tuple-element.183.lo_ref, s32[16]{0:T(128)} %get-tuple-element.182.hi_ref, bf16[1024,128]{1,0:T(8,128)(2,1)} %get-tuple-element.89.refs_0_, bf16[1024,128]{1,0:T(8,128)(2,1)} %collective-permute-done.9.refs_1_, ...), custom_call_target="tpu_custom_call" | custom-call | flops 34359738368 | bytes 12582912 | tf_op jit(solution)/shard_map/pallas_call | solution.py:458
  374.0 2.1 slice.190
  376.1 1.6 add_convert_fusion.7.refs_4_
  378.7 6.1 collective-permute-start.22
  384.8 5.4 add_convert_fusion.refs_5_
  390.2 1.5 constant_dynamic-slice_fusion.10
  391.7 1.6 copy-done.2
  394.6 2.1 add_convert_fusion.3.refs_6_
  397.8 3.5 collective-permute-start.21
  402.0 37.9 %shard_map.304 = (bf16[2,1024,384]{2,1,0:T(8,128)(2,1)}, bf16[2,1024,384]{2,1,0:T(8,128)(2,1)}, f32[8,128]{1,0:T(8,128)}) custom-call(s32[16]{0:T(128)} %get-tuple-element.183.lo_ref, s32[16]{0:T(128)} %get-tuple-element.182.hi_ref, bf16[1024,128]{1,0:T(8,128)(2,1)} %get-tuple-element.105.refs_0_, bf16[1024,128]{1,0:T(8,128)(2,1)} %collective-permute-done.14.refs_1_, ...), custom_call_target="tpu_custom_call" | custom-call | flops 34359738368 | bytes 12582912 | tf_op jit(solution)/shard_map/pallas_call | solution.py:458
  441.0 4.6 collective-permute-start.33
  445.6 1.2 slice.191
  448.7 1.3 pad_maximum_fusion.1
  450.0 1.7 add_convert_fusion.6.refs_4_
  452.5 3.7 add_convert_fusion.2.refs_5_
  456.2 14.6 %shard_map.305.refs_14_ = bf16[1024,768]{1,0:T(8,128)(2,1)} custom-call(bf16[4,1024,1024]{2,1,0:T(8,128)(2,1)} %get-tuple-element.117.n_ref, bf16[2,1024,384]{2,1,0:T(8,128)(2,1)} %get-tuple-element.113.refs_0_.refs_4_, bf16[2,1024,384]{2,1,0:T(8,128)(2,1)} %get-tuple-element.114.refs_1_.refs_5_, bf16[2,1024,384]{2,1,0:T(8,128)(2,1)} %get-tuple-element.115.refs_2_.refs_6_, ...), custom_call_target="tpu_custom_call" | custom-call | flops 9663676416 | bytes 8388608 | tf_op jit(solution)/shard_map/pallas_call | solution.py:775
  470.8 18.0 %shard_map.306 = f32[8,1024]{1,0:T(8,128)} custom-call(s32[1]{0:T(128)} %bitcast.21.me_ref, bf16[1016,1024]{1,0:T(8,128)(2,1)} %bitcast.150, bf16[1016,1024]{1,0:T(8,128)(2,1)} %collective-permute-done.3.refs_1_, bf16[1016,1024]{1,0:T(8,128)(2,1)} %collective-permute-done.4.refs_2_, bf16[1016,1024]{1,0:T(8,128)(2,1)} %collective-permute-done.5.refs_3_, ...), custom_call_target="tpu_custom_call" | custom-call | flops 12884901888 | bytes 8388608 | tf_op jit(solution)/shard_map/pallas_call | solution.py:828
  490.4 22.8 %shard_map.307 = (f32[200,128]{1,0:T(8,128)S(1)}, f32[128,128]{1,0:T(8,128)S(1)}) custom-call(f32[200,128]{1,0:T(8,128)S(1)} %pad_bitcast_fusion.vec_ref, bf16[4,128,128]{2,1,0:T(8,128)(2,1)S(1)} %reshape.477.slot_ref), custom_call_target="tpu_custom_call" | custom-call | flops 8589934592 | bytes 1048576 | tf_op jit(solution)/shard_map/pallas_call | solution.py:964
  513.2 1.3 add_convert_fusion.9
  516.1 1.8 add_convert_fusion.16
  526.0 1.5 copy.64
  527.5 1.2 slice.193
  528.7 2.1 collective-permute-start.27
  533.2 1.2 collective-permute-start.44
  536.2 5.2 collective-permute-done.44
  541.4 6.1 collective-permute-done.43
  547.9 1.2 copy-done.12
  549.4 1.6 maximum_convert_fusion.1
  552.0 15.3 %collective-permute-done.36 = bf16[2,1,1,128,2048]{4,3,2,1,0:T(8,128)(2,1)S(1)} collective-permute-done((bf16[2,1,1,128,2048]{4,3,2,1,0:T(8,128)(2,1)S(1)}, bf16[2,1,1,128,2048]{4,3,2,1,0:T(8,128)(2,1)S(1)}, u32[]{:S(2)}, u32[]{:S(2)}) %collective-permute-start.36) | collective-permute-done | bytes 1048608 | tf_op jit(solution)/shard_map/ppermute | solution.py:68
  567.3 8.4 %collective-permute-done.28 = bf16[2,1,1,128,768]{4,3,2,1,0:T(8,128)(2,1)S(1)} collective-permute-done((bf16[2,1,1,128,768]{4,3,2,1,0:T(8,128)(2,1)S(1)}, bf16[2,1,1,128,768]{4,3,2,1,0:T(8,128)(2,1)S(1)}, u32[]{:S(2)}, u32[]{:S(2)}) %collective-permute-start.28) | collective-permute-done | bytes 393248 | tf_op jit(solution)/shard_map/ppermute | solution.py:68
  577.0 10.3 %collective-permute-done.29 = bf16[1,1,1,128,768]{4,3,2,1,0:T(8,128)(2,1)S(1)} collective-permute-done((bf16[1,1,1,128,768]{4,3,2,1,0:T(8,128)(2,1)S(1)}, bf16[1,1,1,128,768]{4,3,2,1,0:T(8,128)(2,1)S(1)}, u32[]{:S(2)}, u32[]{:S(2)}) %collective-permute-start.29) | collective-permute-done | bytes 196640 | tf_op jit(solution)/shard_map/ppermute | solution.py:68
  589.3 5.1 collective-permute-done.32
  594.4 4.4 collective-permute-done.31
  599.4 20.8 %collective-permute-done.37 = bf16[1,1,1,128,2048]{4,3,2,1,0:T(8,128)(2,1)S(1)} collective-permute-done((bf16[1,1,1,128,2048]{4,3,2,1,0:T(8,128)(2,1)S(1)}, bf16[1,1,1,128,2048]{4,3,2,1,0:T(8,128)(2,1)S(1)}, u32[]{:S(2)}, u32[]{:S(2)}) %collective-permute-start.37) | collective-permute-done | bytes 524320 | tf_op jit(solution)/shard_map/ppermute | solution.py:68
  621.3 1.3 convert_element_type.263
  622.6 11.7 %collective-permute-done.38 = bf16[1,1,1,128,2048]{4,3,2,1,0:T(8,128)(2,1)S(1)} collective-permute-done((bf16[1,1,1,128,2048]{4,3,2,1,0:T(8,128)(2,1)S(1)}, bf16[1,1,1,128,2048]{4,3,2,1,0:T(8,128)(2,1)S(1)}, u32[]{:S(2)}, u32[]{:S(2)}) %collective-permute-start.38) | collective-permute-done | bytes 524320 | tf_op jit(solution)/shard_map/ppermute | solution.py:66
  636.8 15.2 %shard_map.308 = f32[1,1016,1024]{2,1,0:T(8,128)} custom-call(s32[1]{0:T(128)} %bitcast.21.me_ref, bf16[1016,1024]{1,0:T(8,128)(2,1)} %bitcast.151, f32[1024,1024]{1,0:T(8,128)} %get-tuple-element.124.ghid_ref, bf16[1024,3072]{1,0:T(8,128)(2,1)} %w_ref.1, f32[1,1024]{1,0:T(1,128)} %get-tuple-element.232.refs_11_.gain_ref, ...), custom_call_target="tpu_custom_call" | custom-call | flops 12784238592 | bytes 16646144 | tf_op jit(solution)/shard_map/pallas_call | solution.py:877
  652.4 1.5 maximum_convert_fusion
  (286 shorter events, 51.6 us)
Async XLA Ops:
  0.6 59.1 %copy-start = (bf16[1024,8]{0,1:T(8,128)(2,1)S(1)}, bf16[1024,8]{0,1:T(8,128)(2,1)}, u32[]{:S(2)}) copy-start(bf16[1024,8]{0,1:T(8,128)(2,1)} %param.33) | copy-start | bytes 49156
  0.7 57.4 %copy-start.25 = (bf16[1024,1024]{1,0:T(8,128)(2,1)S(1)}, bf16[1024,1024]{1,0:T(8,128)(2,1)}, u32[]{:S(2)}) copy-start(bf16[1024,1024]{1,0:T(8,128)(2,1)} %param.23) | copy-start | bytes 6291460
  0.7 49.0 %collective-permute-start.4 = (bf16[1016,1024]{1,0:T(8,128)(2,1)}, bf16[1016,1024]{1,0:T(8,128)(2,1)}, u32[]{:S(2)}, u32[]{:S(2)}) collective-permute-start(bf16[1016,1024]{1,0:T(8,128)(2,1)} %bitcast.146), channel_id=1, source_target_pairs={{0,2},{1,3},{2,0},{3,1},{4,6},{5,7},{6,4},{7,5},{8,10},{9,11},{10,... | collective-permute-start | bytes 6242312 | tf_op jit(solution)/shard_map/ppermute | solution.py:66
  4.6 132.7 %collective-permute-start.1 = (bf16[2,8192]{1,0:T(2,128)(2,1)S(1)}, bf16[2,8192]{1,0:T(2,128)(2,1)S(1)}, u32[]{:S(2)}, u32[]{:S(2)}) collective-permute-start(bf16[2,8192]{1,0:T(2,128)(2,1)S(1)} %bitcast.162), channel_id=1, source_target_pairs={{0,2},{1,3},{2,0},{3,1},{4,6},{5,7},{6,4},{7,5},{8,10},{9,11},{10,... | collective-permute-start | bytes 98312 | tf_op jit(solution)/shard_map/ppermute | solution.py:66
  4.8 136.1 %collective-permute-start = (bf16[2,8192]{1,0:T(2,128)(2,1)S(1)}, bf16[2,8192]{1,0:T(2,128)(2,1)S(1)}, u32[]{:S(2)}, u32[]{:S(2)}) collective-permute-start(bf16[2,8192]{1,0:T(2,128)(2,1)S(1)} %bitcast.163), channel_id=1, source_target_pairs={{0,1},{1,0},{2,3},{3,2},{4,5},{5,4},{6,7},{7,6},{8,9},{9,8},{10,11... | collective-permute-start | bytes 98312 | tf_op jit(solution)/shard_map/ppermute | solution.py:66
  4.8 55.0 %collective-permute-start.3 = (bf16[1016,1024]{1,0:T(8,128)(2,1)}, bf16[1016,1024]{1,0:T(8,128)(2,1)}, u32[]{:S(2)}, u32[]{:S(2)}) collective-permute-start(bf16[1016,1024]{1,0:T(8,128)(2,1)} %bitcast.147), channel_id=1, source_target_pairs={{0,1},{1,0},{2,3},{3,2},{4,5},{5,4},{6,7},{7,6},{8,9},{9,8},{10,11... | collective-permute-start | bytes 6242312 | tf_op jit(solution)/shard_map/ppermute | solution.py:66
  49.6 10.2 %collective-permute-start.5 = (bf16[1016,1024]{1,0:T(8,128)(2,1)}, bf16[1016,1024]{1,0:T(8,128)(2,1)}, u32[]{:S(2)}, u32[]{:S(2)}) collective-permute-start(bf16[1016,1024]{1,0:T(8,128)(2,1)} %collective-permute-done.4.refs_2_), channel_id=1, source_target_pairs={{0,1},{1,0},{2,3},{3,2},{4,5},{5,4},{6,7},{7,6},{8,9},{9,8},{10,11... | collective-permute-start | bytes 6242312 | tf_op jit(solution)/shard_map/ppermute | solution.py:66
  82.5 53.2 %copy-start.26 = (bf16[256,1024]{1,0:T(8,128)(2,1)S(1)}, bf16[256,1024]{1,0:T(8,128)(2,1)}, u32[]{:S(2)}) copy-start(bf16[256,1024]{1,0:T(8,128)(2,1)} %get-tuple-element.187) | copy-start | bytes 1572868
  133.5 8.4 %collective-permute-start.6 = (bf16[1024,256]{1,0:T(8,128)(2,1)}, bf16[1024,256]{1,0:T(8,128)(2,1)S(1)}, u32[]{:S(2)}, u32[]{:S(2)}) collective-permute-start(bf16[1024,256]{1,0:T(8,128)(2,1)} %get-tuple-element.78), channel_id=1, source_target_pairs={{0,1},{1,0},{2,3},{3,2},{4,5},{5,4},{6,7},{7,6},{8,9},{9,8},{10,11... | collective-permute-start | bytes 1572872 | tf_op jit(solution)/shard_map/ppermute | solution.py:66
  134.0 15.0 %collective-permute-start.7 = (bf16[1024,256]{1,0:T(8,128)(2,1)}, bf16[1024,256]{1,0:T(8,128)(2,1)S(1)}, u32[]{:S(2)}, u32[]{:S(2)}) collective-permute-start(bf16[1024,256]{1,0:T(8,128)(2,1)} %get-tuple-element.79), channel_id=1, source_target_pairs={{0,2},{1,3},{2,0},{3,1},{4,6},{5,7},{6,4},{7,5},{8,10},{9,11},{10,... | collective-permute-start | bytes 1572872 | tf_op jit(solution)/shard_map/ppermute | solution.py:66
  135.8 23.0 %collective-permute-start.8 = (bf16[1024,256]{1,0:T(8,128)(2,1)}, bf16[1024,256]{1,0:T(8,128)(2,1)}, u32[]{:S(2)}, u32[]{:S(2)}) collective-permute-start(bf16[1024,256]{1,0:T(8,128)(2,1)} %get-tuple-element.80), channel_id=1, source_target_pairs={{0,3},{1,2},{2,1},{3,0},{4,7},{5,6},{6,5},{7,4},{8,11},{9,10},{10,... | collective-permute-start | bytes 1572872 | tf_op jit(solution)/shard_map/ppermute | solution.py:66
  137.3 3.6 collective-permute-start.2
  141.9 16.9 %copy-start.44 = (bf16[1024,256]{1,0:T(8,128)(2,1)}, bf16[1024,256]{1,0:T(8,128)(2,1)S(1)}, u32[]{:S(2)}) copy-start(bf16[1024,256]{1,0:T(8,128)(2,1)S(1)} %collective-permute-done.6.refs_12_.refs_6_) | copy-start | bytes 1572868
  149.0 9.7 %copy-start.45 = (bf16[1024,256]{1,0:T(8,128)(2,1)}, bf16[1024,256]{1,0:T(8,128)(2,1)S(1)}, u32[]{:S(2)}) copy-start(bf16[1024,256]{1,0:T(8,128)(2,1)S(1)} %collective-permute-done.7.refs_13_.refs_7_) | copy-start | bytes 1572868
  281.8 6.4 copy-start.29
  281.8 36.5 %collective-permute-start.12 = (bf16[2,2,2,512,512]{4,3,2,1,0:T(8,128)(2,1)}, bf16[2,2,2,512,512]{4,3,2,1,0:T(8,128)(2,1)}, u32[]{:S(2)}, u32[]{:S(2)}) collective-permute-start(bf16[2,2,2,512,512]{4,3,2,1,0:T(8,128)(2,1)} %constant_dynamic-slice_fusion.16), channel_id=1, source_target_pairs={{0,1},{1,0},{2,3},{3,2},{4,5},{5,4},{6,7},{7,6},{8,9},{9,8},{10,11... | collective-permute-start | bytes 12582920 | tf_op jit(solution)/shard_map/ppermute | solution.py:66
  283.8 8.9 %collective-permute-start.13 = (bf16[2,2,2,128,1024]{4,3,2,1,0:T(8,128)(2,1)}, bf16[2,2,2,128,1024]{4,3,2,1,0:T(8,128)(2,1)S(1)}, u32[]{:S(2)}, u32[]{:S(2)}) collective-permute-start(bf16[2,2,2,128,1024]{4,3,2,1,0:T(8,128)(2,1)} %constant_dynamic-slice_fusion.15), channel_id=1, source_target_pairs={{0,1},{1,0},{2,3},{3,2},{4,5},{5,4},{6,7},{7,6},{8,9},{9,8},{10,11... | collective-permute-start | bytes 6291464 | tf_op jit(solution)/shard_map/ppermute | solution.py:66
  285.9 39.8 %collective-permute-start.9 = (bf16[1024,128]{1,0:T(8,128)(2,1)}, bf16[1024,128]{1,0:T(8,128)(2,1)}, u32[]{:S(2)}, u32[]{:S(2)}) collective-permute-start(bf16[1024,128]{1,0:T(8,128)(2,1)} %get-tuple-element.90), channel_id=1, source_target_pairs={{0,1},{1,0},{2,3},{3,2},{4,5},{5,4},{6,7},{7,6},{8,9},{9,8},{10,11... | collective-permute-start | bytes 786440 | tf_op jit(solution)/shard_map/ppermute | solution.py:66
  286.4 41.0 %collective-permute-start.10 = (bf16[1024,128]{1,0:T(8,128)(2,1)}, bf16[1024,128]{1,0:T(8,128)(2,1)}, u32[]{:S(2)}, u32[]{:S(2)}) collective-permute-start(bf16[1024,128]{1,0:T(8,128)(2,1)} %get-tuple-element.91), channel_id=1, source_target_pairs={{0,2},{1,3},{2,0},{3,1},{4,6},{5,7},{6,4},{7,5},{8,10},{9,11},{10,... | collective-permute-start | bytes 786440 | tf_op jit(solution)/shard_map/ppermute | solution.py:66
  288.1 46.0 %collective-permute-start.11 = (bf16[1024,128]{1,0:T(8,128)(2,1)}, bf16[1024,128]{1,0:T(8,128)(2,1)}, u32[]{:S(2)}, u32[]{:S(2)}) collective-permute-start(bf16[1024,128]{1,0:T(8,128)(2,1)} %get-tuple-element.92), channel_id=1, source_target_pairs={{0,3},{1,2},{2,1},{3,0},{4,7},{5,6},{6,5},{7,4},{8,11},{9,10},{10,... | collective-permute-start | bytes 786440 | tf_op jit(solution)/shard_map/ppermute | solution.py:66
  294.0 103.8 %collective-permute-start.14 = (bf16[1024,128]{1,0:T(8,128)(2,1)}, bf16[1024,128]{1,0:T(8,128)(2,1)}, u32[]{:S(2)}, u32[]{:S(2)}) collective-permute-start(bf16[1024,128]{1,0:T(8,128)(2,1)} %get-tuple-element.106), channel_id=1, source_target_pairs={{0,1},{1,0},{2,3},{3,2},{4,5},{5,4},{6,7},{7,6},{8,9},{9,8},{10,11... | collective-permute-start | bytes 786440 | tf_op jit(solution)/shard_map/ppermute | solution.py:66
  318.2 60.4 %collective-permute-start.18 = (bf16[2,2,2,128,2048]{4,3,2,1,0:T(8,128)(2,1)}, bf16[2,2,2,128,2048]{4,3,2,1,0:T(8,128)(2,1)}, u32[]{:S(2)}, u32[]{:S(2)}) collective-permute-start(bf16[2,2,2,128,2048]{4,3,2,1,0:T(8,128)(2,1)} %constant_dynamic-slice_fusion.13), channel_id=1, source_target_pairs={{0,1},{1,0},{2,3},{3,2},{4,5},{5,4},{6,7},{7,6},{8,9},{9,8},{10,11... | collective-permute-start | bytes 12582920 | tf_op jit(solution)/shard_map/ppermute | solution.py:66
  325.7 75.7 %collective-permute-start.15 = (bf16[1024,128]{1,0:T(8,128)(2,1)}, bf16[1024,128]{1,0:T(8,128)(2,1)}, u32[]{:S(2)}, u32[]{:S(2)}) collective-permute-start(bf16[1024,128]{1,0:T(8,128)(2,1)} %get-tuple-element.107), channel_id=1, source_target_pairs={{0,2},{1,3},{2,0},{3,1},{4,6},{5,7},{6,4},{7,5},{8,10},{9,11},{10,... | collective-permute-start | bytes 786440 | tf_op jit(solution)/shard_map/ppermute | solution.py:66
  327.4 46.0 %collective-permute-start.17 = (bf16[2,2,1,128,1024]{4,3,2,1,0:T(8,128)(2,1)S(1)}, bf16[2,2,1,128,1024]{4,3,2,1,0:T(8,128)(2,1)}, u32[]{:S(2)}, u32[]{:S(2)}) collective-permute-start(bf16[2,2,1,128,1024]{4,3,2,1,0:T(8,128)(2,1)S(1)} %constant_dynamic-slice_fusion.14), channel_id=1, source_target_pairs={{0,4},{4,0},{8,12},{12,8},{16,20},{20,16},{24,28},{28,24},{1,5},{5... | collective-permute-start | bytes 3145736 | tf_op jit(solution)/shard_map/ppermute | solution.py:68
  334.1 59.2 %collective-permute-start.19 = (bf16[2,2,2,512,256]{4,3,2,1,0:T(8,128)(2,1)}, bf16[2,2,2,512,256]{4,3,2,1,0:T(8,128)(2,1)}, u32[]{:S(2)}, u32[]{:S(2)}) collective-permute-start(bf16[2,2,2,512,256]{4,3,2,1,0:T(8,128)(2,1)} %constant_dynamic-slice_fusion.12), channel_id=1, source_target_pairs={{0,2},{1,3},{2,0},{3,1},{4,6},{5,7},{6,4},{7,5},{8,10},{9,11},{10,... | collective-permute-start | bytes 6291464 | tf_op jit(solution)/shard_map/ppermute | solution.py:66
  334.7 41.5 %copy-start.10 = (bf16[2,2,2,128,1024]{4,3,2,1,0:T(8,128)(2,1)S(1)}, bf16[2,2,2,128,1024]{4,3,2,1,0:T(8,128)(2,1)}, u32[]{:S(2)}) copy-start(bf16[2,2,2,128,1024]{4,3,2,1,0:T(8,128)(2,1)} %copy-done.9) | copy-start | bytes 6291460
  373.4 27.9 %collective-permute-start.16 = (bf16[1024,128]{1,0:T(8,128)(2,1)}, bf16[1024,128]{1,0:T(8,128)(2,1)S(1)}, u32[]{:S(2)}, u32[]{:S(2)}) collective-permute-start(bf16[1024,128]{1,0:T(8,128)(2,1)} %get-tuple-element.108), channel_id=1, source_target_pairs={{0,3},{1,2},{2,1},{3,0},{4,7},{5,6},{6,5},{7,4},{8,11},{9,10},{10,... | collective-permute-start | bytes 786440 | tf_op jit(solution)/shard_map/ppermute | solution.py:66
  377.7 12.4 %copy-start.14 = (bf16[2,2,1,128,1024]{4,3,2,1,0:T(8,128)(2,1)}, bf16[2,2,1,128,1024]{4,3,2,1,0:T(8,128)(2,1)S(1)}, u32[]{:S(2)}) copy-start(bf16[2,2,1,128,1024]{4,3,2,1,0:T(8,128)(2,1)S(1)} %add_convert_fusion.7.refs_4_) | copy-start | bytes 3145732
  378.7 62.1 %collective-permute-start.22 = (bf16[2,1,1,128,1024]{4,3,2,1,0:T(8,128)(2,1)}, bf16[2,1,1,128,1024]{4,3,2,1,0:T(8,128)(2,1)S(1)}, u32[]{:S(2)}, u32[]{:S(2)}) collective-permute-start(bf16[2,1,1,128,1024]{4,3,2,1,0:T(8,128)(2,1)} %constant_dynamic-slice_fusion.9), channel_id=1, source_target_pairs={{0,8},{4,12},{8,0},{12,4},{16,24},{20,28},{24,16},{28,20},{1,9},{5... | collective-permute-start | bytes 1572872 | tf_op jit(solution)/shard_map/ppermute | solution.py:68
  393.3 47.4 %collective-permute-start.23 = (bf16[2,1024,384]{2,1,0:T(8,128)(2,1)}, bf16[2,1024,384]{2,1,0:T(8,128)(2,1)}, u32[]{:S(2)}, u32[]{:S(2)}) collective-permute-start(bf16[2,1024,384]{2,1,0:T(8,128)(2,1)} %get-tuple-element.114.refs_1_.refs_5_), channel_id=1, source_target_pairs={{0,2},{1,3},{2,0},{3,1},{4,6},{5,7},{6,4},{7,5},{8,10},{9,11},{10,... | collective-permute-start | bytes 4718600 | tf_op jit(solution)/shard_map/ppermute | solution.py:66
  396.7 5.3 copy-start.7
  397.8 54.3 %collective-permute-start.21 = (bf16[2,2,1,128,2048]{4,3,2,1,0:T(8,128)(2,1)}, bf16[2,2,1,128,2048]{4,3,2,1,0:T(8,128)(2,1)}, u32[]{:S(2)}, u32[]{:S(2)}) collective-permute-start(bf16[2,2,1,128,2048]{4,3,2,1,0:T(8,128)(2,1)} %constant_dynamic-slice_fusion.10), channel_id=1, source_target_pairs={{0,4},{4,0},{8,12},{12,8},{16,20},{20,16},{24,28},{28,24},{1,5},{5... | collective-permute-start | bytes 6291464 | tf_op jit(solution)/shard_map/ppermute | solution.py:68
  401.3 48.7 %collective-permute-start.20 = (bf16[2,1,2,512,256]{4,3,2,1,0:T(8,128)(2,1)}, bf16[2,1,2,512,256]{4,3,2,1,0:T(8,128)(2,1)}, u32[]{:S(2)}, u32[]{:S(2)}) collective-permute-start(bf16[2,1,2,512,256]{4,3,2,1,0:T(8,128)(2,1)} %constant_dynamic-slice_fusion.11), channel_id=1, source_target_pairs={{0,8},{4,12},{8,0},{12,4},{16,24},{20,28},{24,16},{28,20},{1,9},{5... | collective-permute-start | bytes 3145736 | tf_op jit(solution)/shard_map/ppermute | solution.py:68
  402.0 38.7 %copy-start.15 = (bf16[2,2,1,128,1024]{4,3,2,1,0:T(8,128)(2,1)S(1)}, bf16[2,2,1,128,1024]{4,3,2,1,0:T(8,128)(2,1)}, u32[]{:S(2)}) copy-start(bf16[2,2,1,128,1024]{4,3,2,1,0:T(8,128)(2,1)} %copy-done.14) | copy-start | bytes 3145732
  439.9 6.9 %copy-start.18 = (bf16[2,1024,384]{2,1,0:T(8,128)(2,1)S(1)}, bf16[2,1024,384]{2,1,0:T(8,128)(2,1)}, u32[]{:S(2)}) copy-start(bf16[2,1024,384]{2,1,0:T(8,128)(2,1)} %get-tuple-element.115.refs_2_.refs_6_) | copy-start | bytes 4718596
  441.0 9.0 %copy-start.22 = (bf16[2,1,1,128,1024]{4,3,2,1,0:T(8,128)(2,1)}, bf16[2,1,1,128,1024]{4,3,2,1,0:T(8,128)(2,1)S(1)}, u32[]{:S(2)}) copy-start(bf16[2,1,1,128,1024]{4,3,2,1,0:T(8,128)(2,1)S(1)} %add_convert_fusion.12.refs_6_) | copy-start | bytes 1572868
  441.0 7.7 %copy-start.20 = (bf16[1,1024,384]{2,1,0:T(8,128)(2,1)S(1)}, bf16[1,1024,384]{2,1,0:T(8,128)(2,1)}, u32[]{:S(2)}) copy-start(bf16[1,1024,384]{2,1,0:T(8,128)(2,1)} %slice.190) | copy-start | bytes 2359300
  441.0 48.7 %collective-permute-start.33 = (bf16[1,1,1,128,1024]{4,3,2,1,0:T(8,128)(2,1)S(1)}, bf16[1,1,1,128,1024]{4,3,2,1,0:T(8,128)(2,1)S(1)}, u32[]{:S(2)}, u32[]{:S(2)}) collective-permute-start(bf16[1,1,1,128,1024]{4,3,2,1,0:T(8,128)(2,1)S(1)} %constant_dynamic-slice_fusion.5), channel_id=1, source_target_pairs={{0,16},{4,20},{8,24},{12,28},{16,0},{20,4},{24,8},{28,12},{1,17},{... | collective-permute-start | bytes 786440 | tf_op jit(solution)/shard_map/ppermute | solution.py:68
  447.8 77.1 %collective-permute-start.24 = (bf16[2,1024,384]{2,1,0:T(8,128)(2,1)}, bf16[2,1024,384]{2,1,0:T(8,128)(2,1)}, u32[]{:S(2)}, u32[]{:S(2)}) collective-permute-start(bf16[2,1024,384]{2,1,0:T(8,128)(2,1)} %get-tuple-element.116.refs_3_.refs_7_), channel_id=1, source_target_pairs={{0,2},{1,3},{2,0},{3,1},{4,6},{5,7},{6,4},{7,5},{8,10},{9,11},{10,... | collective-permute-start | bytes 4718600 | tf_op jit(solution)/shard_map/ppermute | solution.py:66
  451.8 37.1 %collective-permute-start.40 = (bf16[1,1,2,512,256]{4,3,2,1,0:T(8,128)(2,1)S(1)}, bf16[1,1,2,512,256]{4,3,2,1,0:T(8,128)(2,1)S(1)}, u32[]{:S(2)}, u32[]{:S(2)}) collective-permute-start(bf16[1,1,2,512,256]{4,3,2,1,0:T(8,128)(2,1)S(1)} %constant_dynamic-slice_fusion.2), channel_id=1, source_target_pairs={{0,16},{4,20},{8,24},{12,28},{16,0},{20,4},{24,8},{28,12},{1,17},{... | collective-permute-start | bytes 1572872 | tf_op jit(solution)/shard_map/ppermute | solution.py:68
  488.9 24.3 %copy-start.30 = (bf16[1,1,2,512,256]{4,3,2,1,0:T(8,128)(2,1)}, bf16[1,1,2,512,256]{4,3,2,1,0:T(8,128)(2,1)S(1)}, u32[]{:S(2)}) copy-start(bf16[1,1,2,512,256]{4,3,2,1,0:T(8,128)(2,1)S(1)} %collective-permute-done.40) | copy-start | bytes 1572868
  490.4 22.8 %copy-start.17 = (bf16[2,1,2,512,256]{4,3,2,1,0:T(8,128)(2,1)S(1)}, bf16[2,1,2,512,256]{4,3,2,1,0:T(8,128)(2,1)}, u32[]{:S(2)}) copy-start(bf16[2,1,2,512,256]{4,3,2,1,0:T(8,128)(2,1)} %copy-done.16) | copy-start | bytes 3145732
  513.2 8.5 %copy-start.6 = (bf16[2,2,1,128,2048]{4,3,2,1,0:T(8,128)(2,1)S(1)}, bf16[2,2,1,128,2048]{4,3,2,1,0:T(8,128)(2,1)}, u32[]{:S(2)}) copy-start(bf16[2,2,1,128,2048]{4,3,2,1,0:T(8,128)(2,1)} %add_convert_fusion.2.refs_5_) | copy-start | bytes 6291460
  516.1 15.9 %collective-permute-start.41 = (bf16[1,1,1,512,256]{4,3,2,1,0:T(8,128)(2,1)}, bf16[1,1,1,512,256]{4,3,2,1,0:T(8,128)(2,1)}, u32[]{:S(2)}, u32[]{:S(2)}) collective-permute-start(bf16[1,1,1,512,256]{4,3,2,1,0:T(8,128)(2,1)} %constant_dynamic-slice_fusion.1), channel_id=1, source_target_pairs={{0,4},{4,0},{8,12},{12,8},{16,20},{20,16},{24,28},{28,24},{1,5},{5... | collective-permute-start | bytes 786440 | tf_op jit(solution)/shard_map/ppermute | solution.py:68
  517.9 12.9 %collective-permute-start.34 = (bf16[1,1,1,128,1024]{4,3,2,1,0:T(8,128)(2,1)}, bf16[1,1,1,128,1024]{4,3,2,1,0:T(8,128)(2,1)}, u32[]{:S(2)}, u32[]{:S(2)}) collective-permute-start(bf16[1,1,1,128,1024]{4,3,2,1,0:T(8,128)(2,1)} %add_convert_fusion.16), channel_id=1, source_target_pairs={{0,2},{1,3},{2,0},{3,1},{4,6},{5,7},{6,4},{7,5},{8,10},{9,11},{10,... | collective-permute-start | bytes 786440 | tf_op jit(solution)/shard_map/ppermute | solution.py:66
  523.3 8.7 %copy-start.24 = (bf16[1,1,2,512,256]{4,3,2,1,0:T(8,128)(2,1)S(1)}, bf16[1,1,2,512,256]{4,3,2,1,0:T(8,128)(2,1)}, u32[]{:S(2)}) copy-start(bf16[1,1,2,512,256]{4,3,2,1,0:T(8,128)(2,1)} %copy-done.23) | copy-start | bytes 1572868
  524.3 11.0 %copy-start.19 = (bf16[1,1024,384]{2,1,0:T(8,128)(2,1)S(1)}, bf16[1,1024,384]{2,1,0:T(8,128)(2,1)}, u32[]{:S(2)}) copy-start(bf16[1,1024,384]{2,1,0:T(8,128)(2,1)} %slice.192) | copy-start | bytes 2359300
  528.7 19.1 %collective-permute-start.27 = (bf16[2,2,1,128,768]{4,3,2,1,0:T(8,128)(2,1)}, bf16[2,2,1,128,768]{4,3,2,1,0:T(8,128)(2,1)S(1)}, u32[]{:S(2)}, u32[]{:S(2)}) collective-permute-start(bf16[2,2,1,128,768]{4,3,2,1,0:T(8,128)(2,1)} %constant_dynamic-slice_fusion.8), channel_id=1, source_target_pairs={{0,4},{4,0},{8,12},{12,8},{16,20},{20,16},{24,28},{28,24},{1,5},{5... | collective-permute-start | bytes 2359304 | tf_op jit(solution)/shard_map/ppermute | solution.py:68
  531.9 3.5 collective-permute-start.35
  533.2 8.2 %copy-start.28 = (bf16[2,1,1,128,2048]{4,3,2,1,0:T(8,128)(2,1)S(1)}, bf16[2,1,1,128,2048]{4,3,2,1,0:T(8,128)(2,1)}, u32[]{:S(2)}) copy-start(bf16[2,1,1,128,2048]{4,3,2,1,0:T(8,128)(2,1)} %constant_dynamic-slice_fusion.4) | copy-start | bytes 3145732
  533.2 8.2 %collective-permute-start.44 = (bf16[512,256]{1,0:T(8,128)(2,1)S(1)}, bf16[512,256]{1,0:T(8,128)(2,1)S(1)}, u32[]{:S(2)}, u32[]{:S(2)}) collective-permute-start(bf16[512,256]{1,0:T(8,128)(2,1)S(1)} %get-tuple-element.199), channel_id=1, source_target_pairs={{0,3},{1,2},{2,1},{3,0},{4,7},{5,6},{6,5},{7,4},{8,11},{9,10},{10,... | collective-permute-start | bytes 786440 | tf_op jit(solution)/shard_map/ppermute | solution.py:66
  534.4 13.1 %collective-permute-start.43 = (bf16[512,256]{1,0:T(8,128)(2,1)S(1)}, bf16[512,256]{1,0:T(8,128)(2,1)S(1)}, u32[]{:S(2)}, u32[]{:S(2)}) collective-permute-start(bf16[512,256]{1,0:T(8,128)(2,1)S(1)} %get-tuple-element.199), channel_id=1, source_target_pairs={{0,2},{1,3},{2,0},{3,1},{4,6},{5,7},{6,4},{7,5},{8,10},{9,11},{10,... | collective-permute-start | bytes 786440 | tf_op jit(solution)/shard_map/ppermute | solution.py:66
  535.3 12.2 %collective-permute-start.42 = (bf16[512,256]{1,0:T(8,128)(2,1)S(1)}, bf16[512,256]{1,0:T(8,128)(2,1)S(1)}, u32[]{:S(2)}, u32[]{:S(2)}) collective-permute-start(bf16[512,256]{1,0:T(8,128)(2,1)S(1)} %get-tuple-element.199), channel_id=1, source_target_pairs={{0,1},{1,0},{2,3},{3,2},{4,5},{5,4},{6,7},{7,6},{8,9},{9,8},{10,11... | collective-permute-start | bytes 786440 | tf_op jit(solution)/shard_map/ppermute | solution.py:66
  535.5 99.0 %collective-permute-start.25 = (bf16[2,1024,384]{2,1,0:T(8,128)(2,1)S(1)}, bf16[2,1024,384]{2,1,0:T(8,128)(2,1)S(1)}, u32[]{:S(2)}, u32[]{:S(2)}) collective-permute-start(bf16[2,1024,384]{2,1,0:T(8,128)(2,1)S(1)} %copy-done.27), channel_id=1, source_target_pairs={{0,1},{1,0},{2,3},{3,2},{4,5},{5,4},{6,7},{7,6},{8,9},{9,8},{10,11... | collective-permute-start | bytes 4718600 | tf_op jit(solution)/shard_map/ppermute | solution.py:66
  541.4 25.9 %collective-permute-start.36 = (bf16[2,1,1,128,2048]{4,3,2,1,0:T(8,128)(2,1)S(1)}, bf16[2,1,1,128,2048]{4,3,2,1,0:T(8,128)(2,1)S(1)}, u32[]{:S(2)}, u32[]{:S(2)}) collective-permute-start(bf16[2,1,1,128,2048]{4,3,2,1,0:T(8,128)(2,1)S(1)} %copy-done.28), channel_id=1, source_target_pairs={{0,8},{4,12},{8,0},{12,4},{16,24},{20,28},{24,16},{28,20},{1,9},{5... | collective-permute-start | bytes 3145736 | tf_op jit(solution)/shard_map/ppermute | solution.py:68
  547.5 87.0 %collective-permute-start.26 = (bf16[2,1024,384]{2,1,0:T(8,128)(2,1)S(1)}, bf16[2,1024,384]{2,1,0:T(8,128)(2,1)S(1)}, u32[]{:S(2)}, u32[]{:S(2)}) collective-permute-start(bf16[2,1024,384]{2,1,0:T(8,128)(2,1)S(1)} %pad_maximum_fusion.2), channel_id=1, source_target_pairs={{0,1},{1,0},{2,3},{3,2},{4,5},{5,4},{6,7},{7,6},{8,9},{9,8},{10,11... | collective-permute-start | bytes 4718600 | tf_op jit(solution)/shard_map/ppermute | solution.py:66
  549.3 26.5 %collective-permute-start.28 = (bf16[2,1,1,128,768]{4,3,2,1,0:T(8,128)(2,1)S(1)}, bf16[2,1,1,128,768]{4,3,2,1,0:T(8,128)(2,1)S(1)}, u32[]{:S(2)}, u32[]{:S(2)}) collective-permute-start(bf16[2,1,1,128,768]{4,3,2,1,0:T(8,128)(2,1)S(1)} %constant_dynamic-slice_fusion.7), channel_id=1, source_target_pairs={{0,8},{4,12},{8,0},{12,4},{16,24},{20,28},{24,16},{28,20},{1,9},{5... | collective-permute-start | bytes 1179656 | tf_op jit(solution)/shard_map/ppermute | solution.py:68
  575.9 11.3 %collective-permute-start.29 = (bf16[1,1,1,128,768]{4,3,2,1,0:T(8,128)(2,1)S(1)}, bf16[1,1,1,128,768]{4,3,2,1,0:T(8,128)(2,1)S(1)}, u32[]{:S(2)}, u32[]{:S(2)}) collective-permute-start(bf16[1,1,1,128,768]{4,3,2,1,0:T(8,128)(2,1)S(1)} %constant_dynamic-slice_fusion.6), channel_id=1, source_target_pairs={{0,16},{4,20},{8,24},{12,28},{16,0},{20,4},{24,8},{28,12},{1,17},{... | collective-permute-start | bytes 589832 | tf_op jit(solution)/shard_map/ppermute | solution.py:68
  587.3 7.1 %collective-permute-start.32 = (bf16[128,768]{1,0:T(8,128)(2,1)S(1)}, bf16[128,768]{1,0:T(8,128)(2,1)S(1)}, u32[]{:S(2)}, u32[]{:S(2)}) collective-permute-start(bf16[128,768]{1,0:T(8,128)(2,1)S(1)} %get-tuple-element.205), channel_id=1, source_target_pairs={{0,3},{1,2},{2,1},{3,0},{4,7},{5,6},{6,5},{7,4},{8,11},{9,10},{10,... | collective-permute-start | bytes 589832 | tf_op jit(solution)/shard_map/ppermute | solution.py:66
  588.2 10.6 %collective-permute-start.31 = (bf16[128,768]{1,0:T(8,128)(2,1)S(1)}, bf16[128,768]{1,0:T(8,128)(2,1)S(1)}, u32[]{:S(2)}, u32[]{:S(2)}) collective-permute-start(bf16[128,768]{1,0:T(8,128)(2,1)S(1)} %get-tuple-element.205), channel_id=1, source_target_pairs={{0,2},{1,3},{2,0},{3,1},{4,6},{5,7},{6,4},{7,5},{8,10},{9,11},{10,... | collective-permute-start | bytes 589832 | tf_op jit(solution)/shard_map/ppermute | solution.py:66
  589.0 9.8 %collective-permute-start.30 = (bf16[128,768]{1,0:T(8,128)(2,1)S(1)}, bf16[128,768]{1,0:T(8,128)(2,1)S(1)}, u32[]{:S(2)}, u32[]{:S(2)}) collective-permute-start(bf16[128,768]{1,0:T(8,128)(2,1)S(1)} %get-tuple-element.205), channel_id=1, source_target_pairs={{0,1},{1,0},{2,3},{3,2},{4,5},{5,4},{6,7},{7,6},{8,9},{9,8},{10,11... | collective-permute-start | bytes 589832 | tf_op jit(solution)/shard_map/ppermute | solution.py:66
  594.4 25.8 %collective-permute-start.37 = (bf16[1,1,1,128,2048]{4,3,2,1,0:T(8,128)(2,1)S(1)}, bf16[1,1,1,128,2048]{4,3,2,1,0:T(8,128)(2,1)S(1)}, u32[]{:S(2)}, u32[]{:S(2)}) collective-permute-start(bf16[1,1,1,128,2048]{4,3,2,1,0:T(8,128)(2,1)S(1)} %constant_dynamic-slice_fusion.3), channel_id=1, source_target_pairs={{0,16},{4,20},{8,24},{12,28},{16,0},{20,4},{24,8},{28,12},{1,17},{... | collective-permute-start | bytes 1572872 | tf_op jit(solution)/shard_map/ppermute | solution.py:68
  620.3 13.9 %collective-permute-start.38 = (bf16[1,1,1,128,2048]{4,3,2,1,0:T(8,128)(2,1)S(1)}, bf16[1,1,1,128,2048]{4,3,2,1,0:T(8,128)(2,1)S(1)}, u32[]{:S(2)}, u32[]{:S(2)}) collective-permute-start(bf16[1,1,1,128,2048]{4,3,2,1,0:T(8,128)(2,1)S(1)} %add_convert_fusion.11), channel_id=1, source_target_pairs={{0,2},{1,3},{2,0},{3,1},{4,6},{5,7},{6,4},{7,5},{8,10},{9,11},{10,... | collective-permute-start | bytes 1572872 | tf_op jit(solution)/shard_map/ppermute | solution.py:66
  634.4 17.6 %collective-permute-start.39 = (bf16[128,2048]{1,0:T(8,128)(2,1)S(1)}, bf16[128,2048]{1,0:T(8,128)(2,1)S(1)}, u32[]{:S(2)}, u32[]{:S(2)}) collective-permute-start(bf16[128,2048]{1,0:T(8,128)(2,1)S(1)} %get-tuple-element.196), channel_id=1, source_target_pairs={{0,1},{1,0},{2,3},{3,2},{4,5},{5,4},{6,7},{7,6},{8,9},{9,8},{10,11... | collective-permute-start | bytes 1572872 | tf_op jit(solution)/shard_map/ppermute | solution.py:66
  (30 other events, 79.6 us)

commit v3 on v2

--- a/solution.py
+++ b/solution.py
@@ -15,7 +15,8 @@
 NEG = -1e30
 VMEM = 60 << 20
 ROW_BLOCK = 256
-GRAD_BLOCK = 512
+UP_BLOCK = 1024
+GRAD_BLOCK = 1024
 
 highest = lax.Precision.HIGHEST
 epsilon = 1e-06
@@ -82,12 +83,14 @@
     return masks
 
 
-def gather_pieces(value):
+def gather_pieces(value, after=()):
     pieces = {0: value}
     order = sorted(range(1, lax.axis_size("row")), key=lambda d: (d & 1, d))
     for d in order:
         low = d & -d
         pieces[d] = jump(pieces[d ^ low], low)
+        if d % 2 == 0:
+            pieces[d] = behind(pieces[d], after)
     return [pieces[d] for d in range(lax.axis_size("row"))]
 
 
@@ -139,17 +142,17 @@
     return grad.reshape((2,) * len(bits_of(images)) + (rows // images, columns))
 
 
-def gather_columns(value, order, bits):
+def gather_columns(value, order, bits, after=()):
     masks = [row_mask for row_mask, _ in masks_of(bits)]
     device = lax.axis_index("row") % len(masks)
-    stack = jnp.stack([value if m == 0 else jump(value, m) for m in masks])
+    stack = jnp.stack([value if m == 0 else behind(jump(value, m), after) for m in masks])
     return [
         lax.dynamic_index_in_dim(stack, order(c) ^ device, 0, False) for c in range(len(masks))
     ]
 
 
-def exchange_sum(value, bits):
-    values = [value] + [jump(value, *mask) for mask in masks_of(bits)[1:]]
+def exchange_sum(value, bits, after=()):
+    values = [value] + [behind(jump(value, *mask), after) for mask in masks_of(bits)[1:]]
     return tree([v.astype(f32) for v in values]).astype(bf16)
 
 
@@ -158,10 +161,10 @@
     return int(format(index, f"0{width}b")[::-1], 2) if width else 0
 
 
-def finish_weight(value, bits):
+def finish_weight(value, bits, after=()):
     value = value.reshape(value.shape[-2:])
     count = 1 << len(bits)
-    blocks = gather_columns(value, lambda c: reversed_bits(c, count), bits)
+    blocks = gather_columns(value, lambda c: reversed_bits(c, count), bits, after)
     return jnp.concatenate(blocks, axis=1).astype(f32)
 
 
@@ -172,7 +175,7 @@
 ANYWHERE = pl.BlockSpec(memory_space=pl.ANY)
 
 
-def own_columns(w_qkv, device, features, splits):
+def own_columns(w_qkv, features, splits, chosen):
     width = w_qkv.shape[0]
     wide = features // splits
 
@@ -182,7 +185,7 @@
 
         return pl.BlockSpec((width, wide), index, pipeline_mode=pl.Buffered(1))
 
-    return [spec(s, part) for s in range(splits) for part in range(3)], [w_qkv] * (3 * splits)
+    return [spec(s, part) for s in chosen for part in range(3)], [w_qkv] * (3 * len(chosen))
 
 
 def valid_rows(block, piece_rows, local_rows):
@@ -216,7 +219,7 @@
 
     unit, _ = norm_parts(load_block(pieces, block, BLK // count, local_rows))
     normed = (unit * gain_ref[...] + shift_ref[...]).astype(bf16)
-    n_ref[...] = normed.reshape(n_ref.shape)
+    n_ref[...] = unit.astype(bf16).reshape(n_ref.shape)
     mixed = matmul(normed, w_ref[...])
     for s in range(splits):
         at = slice(s * wide, (s + 1) * wide)
@@ -238,7 +241,7 @@
     whole = lambda a: pl.BlockSpec(a.shape, lambda b, m: (0,) * a.ndim)
     flat = pl.BlockSpec((BLK, features), lambda b, m: (b, 0))
     turned = pl.BlockSpec((1, features, BLK), lambda b, m: (b, 0, 0))
-    specs, operands = own_columns(w_qkv, me, features, splits)
+    specs, operands = own_columns(w_qkv, features, splits, range(splits))
     return pl.pallas_call(
         functools.partial(qkv_kernel, count, splits, local_rows, features),
         grid_spec=pltpu.PrefetchScalarGridSpec(
@@ -272,7 +275,13 @@
 def per_head(stack_ref, value, heads):
     lane = lax.broadcasted_iota(jnp.int32, value.shape, 1) // HEAD
     for h in range(heads):
-        stack_ref[h] = jnp.where(lane == h, value, jnp.zeros_like(value))
+        stack_ref[h * BLK : (h + 1) * BLK] = jnp.where(lane == h, value, jnp.zeros_like(value))
+
+
+def in_pairs(lo, hi, step, carry):
+    pairs = (hi - lo) // 2
+    carry = lax.fori_loop(0, pairs, lambda i, c: step(lo + 2 * i, 2, c), carry)
+    return lax.fori_loop(lo + 2 * pairs, hi, lambda kb, c: step(kb, 1, c), carry)
 
 
 def attend_kernel(count, heads, lo_ref, hi_ref, *refs):
@@ -284,31 +293,38 @@
     per_head(qs_ref, q_ref[...], heads)
     imgq = imgq_ref[...]
 
-    def first(kb, tops):
-        rows = pl.ds(pl.multiple_of(kb * BLK, BLK), BLK)
-        keys = k_ref[rows, :]
+    def first(kb, width, tops):
+        rows = pl.ds(pl.multiple_of(kb * BLK, BLK), width * BLK)
         allowed = imgk_ref[rows, :] == imgq
+        s = nt(k_ref[rows, :], qs_ref[...])
         new = []
         for h in range(heads):
-            s = jnp.where(allowed, nt(keys, qs_ref[h]), NEG)
-            s_ref[kb - lo, h] = s
-            new.append(jnp.maximum(tops[h], jnp.max(s.reshape(BLK // 8, 8, BLK), axis=0)))
+            cols = slice(h * BLK, (h + 1) * BLK)
+            part = jnp.where(allowed, s[:, cols], NEG)
+            for j in range(width):
+                s_ref[kb - lo + j, :, cols] = part[j * BLK : (j + 1) * BLK]
+            high = jnp.max(part.reshape(width * BLK // 8, 8, BLK), axis=0)
+            new.append(jnp.maximum(tops[h], high))
         return tuple(new)
 
-    tops = lax.fori_loop(lo, hi, first, (jnp.full((8, BLK), NEG, f32),) * heads)
+    tops = in_pairs(lo, hi, first, (jnp.full((8, BLK), NEG, f32),) * heads)
     tops = [jnp.max(t, axis=0, keepdims=True) for t in tops]
     acc_ref[...] = jnp.zeros_like(acc_ref)
 
-    def second(kb, sums):
+    def second(kb, width, sums):
         new = []
         for h in range(heads):
-            p = jnp.exp(s_ref[kb - lo, h] - tops[h])
-            new.append(sums[h] + jnp.sum(p.reshape(BLK // 8, 8, BLK), axis=0))
-            rows = slice(h * HEAD, (h + 1) * HEAD)
-            acc_ref[rows, :] += matmul(vt_ref[kb, rows, :], p.astype(bf16))
+            rows, cols = slice(h * HEAD, (h + 1) * HEAD), slice(h * BLK, (h + 1) * BLK)
+            part, weights = 0.0, sums[h]
+            for j in range(width):
+                p = jnp.exp(s_ref[kb - lo + j, :, cols] - tops[h])
+                weights = weights + jnp.sum(p.reshape(BLK // 8, 8, BLK), axis=0)
+                part = part + matmul(vt_ref[kb + j, rows, :], p.astype(bf16))
+            new.append(weights)
+            acc_ref[rows, :] += part
         return tuple(new)
 
-    sums = lax.fori_loop(lo, hi, second, (jnp.zeros((8, BLK), f32),) * heads)
+    sums = in_pairs(lo, hi, second, (jnp.zeros((8, BLK), f32),) * heads)
     sums = [jnp.sum(t, axis=0, keepdims=True) for t in sums]
     for h in range(heads):
         rows = slice(h * HEAD, (h + 1) * HEAD)
@@ -326,7 +342,9 @@
     blocks, features = vt.shape[0], q.shape[1]
     heads = features // HEAD
     piece_rows = BLK // count
-    whole = lambda a: pl.BlockSpec(a.shape, lambda b, *_: (0,) * a.ndim)
+    whole = lambda a: pl.BlockSpec(
+        a.shape, lambda b, *_: (0,) * a.ndim, pipeline_mode=pl.Buffered(1)
+    )
     return pl.pallas_call(
         functools.partial(attend_kernel, count, heads),
         grid_spec=pltpu.PrefetchScalarGridSpec(
@@ -345,8 +363,8 @@
                 pl.BlockSpec((8, BLK), lambda b, *_: (0, b)),
             ],
             scratch_shapes=[
-                pltpu.VMEM((blocks, heads, BLK, BLK), f32),
-                pltpu.VMEM((heads, BLK, features), bf16),
+                pltpu.VMEM((blocks, BLK, heads * BLK), f32),
+                pltpu.VMEM((heads * BLK, features), bf16),
                 pltpu.VMEM((features, BLK), f32),
             ],
         ),
@@ -634,7 +652,7 @@
     inner = learn_in.shape[1]
     spread = learn_out.shape[1]
     block = min(ROW_BLOCK, rows)
-    chunk = 512
+    chunk = UP_BLOCK
     wide = features // splits
     once = lambda a: pl.BlockSpec(a.shape, lambda i: (0,) * a.ndim, pipeline_mode=pl.Buffered(1))
     by_rows = lambda n: pl.BlockSpec((block, n), lambda i: (i, 0))
@@ -678,173 +696,187 @@
     )(tok, img, *resident, *attended)
 
 
-def grad_kernel(waits, left_ref, right_ref, *refs):
-    refs[waits][...] = tn(left_ref[...], right_ref[...]).astype(bf16)
-
-
-def grad_call(left, right, by_left, after=()):
+def part_halves(me_ref, value, keep_ref, send_ref, whole_ref):
+    half = value.shape[1] // 2
+    core = me_ref[0] % 2
+    whole_ref[...] = value
+    keep_ref[...] = whole_ref[:, pl.ds(pl.multiple_of(core * half, half), half)]
+    send_ref[...] = whole_ref[:, pl.ds(pl.multiple_of((1 - core) * half, half), half)]
+
+
+def down_grad_kernel(waits, me_ref, left_ref, right_ref, *refs):
+    part_halves(me_ref, tn(left_ref[...], right_ref[...]).astype(bf16), *refs[waits:])
+
+
+def down_grad_call(me, left, right, after=()):
     rows, m = left.shape
     n = right.shape[1]
-    once = pl.Buffered(1)
-    if by_left:
-        grid, left_block, right_block, out_block = m // GRAD_BLOCK, GRAD_BLOCK, n, (GRAD_BLOCK, n)
-        specs = [
-            pl.BlockSpec((rows, left_block), lambda j: (0, j)),
-            pl.BlockSpec((rows, right_block), lambda j: (0, 0), pipeline_mode=once),
-        ]
-        out_spec = pl.BlockSpec(out_block, lambda j: (j, 0))
-    else:
-        grid, left_block, right_block, out_block = n // GRAD_BLOCK, m, GRAD_BLOCK, (m, GRAD_BLOCK)
-        specs = [
-            pl.BlockSpec((rows, left_block), lambda j: (0, 0), pipeline_mode=once),
-            pl.BlockSpec((rows, right_block), lambda j: (0, j)),
-        ]
-        out_spec = pl.BlockSpec(out_block, lambda j: (0, j))
+    out = pl.BlockSpec((GRAD_BLOCK, n // 2), lambda j, m: (j, 0))
     return pl.pallas_call(
-        functools.partial(grad_kernel, len(after)),
-        grid=(grid,),
-        in_specs=specs + [ANYWHERE] * len(after),
-        out_specs=out_spec,
-        out_shape=jax.ShapeDtypeStruct((m, n), bf16),
+        functools.partial(down_grad_kernel, len(after)),
+        grid_spec=pltpu.PrefetchScalarGridSpec(
+            num_scalar_prefetch=1,
+            grid=(m // GRAD_BLOCK,),
+            in_specs=[
+                pl.BlockSpec((rows, GRAD_BLOCK), lambda j, m: (0, j)),
+                pl.BlockSpec((rows, n), lambda j, m: (0, 0), pipeline_mode=pl.Buffered(1)),
+            ]
+            + [ANYWHERE] * len(after),
+            out_specs=[out, out],
+            scratch_shapes=[pltpu.VMEM((GRAD_BLOCK, n), bf16)],
+        ),
+        out_shape=[jax.ShapeDtypeStruct((m, n // 2), bf16)] * 2,
         compiler_params=params(),
         cost_estimate=pl.CostEstimate(
             flops=3 * rows * m * n, bytes_accessed=4 * m * n, transcendentals=0
         ),
-    )(left, right, *after)
-
-
-def small_grad_kernel(count, waits, me_ref, *refs):
+    )(me, left, right, *after)
+
+
+def up_grad_kernel(half, waits, me_ref, left_ref, right_ref, *refs):
+    keep_ref, send_ref = refs[waits:]
+    value = tn(left_ref[...], right_ref[...]).astype(bf16)
+
+    @pl.when(pl.program_id(0) < half)
+    def _():
+        send_ref[...] = value
+
+    @pl.when(pl.program_id(0) >= half)
+    def _():
+        keep_ref[...] = value
+
+
+def up_grad_call(me, left, right, after=()):
+    rows, m = left.shape
+    n = right.shape[1]
+    half = n // GRAD_BLOCK // 2
+
+    def column(j, core):
+        return jnp.where(j < half, (1 - core) * half + j, core * half + j - half)
+
+    return pl.pallas_call(
+        functools.partial(up_grad_kernel, half, len(after)),
+        grid_spec=pltpu.PrefetchScalarGridSpec(
+            num_scalar_prefetch=1,
+            grid=(2 * half,),
+            in_specs=[
+                pl.BlockSpec((rows, m), lambda j, me: (0, 0), pipeline_mode=pl.Buffered(1)),
+                pl.BlockSpec((rows, GRAD_BLOCK), lambda j, me: (0, column(j, me[0] % 2))),
+            ]
+            + [ANYWHERE] * len(after),
+            out_specs=[
+                pl.BlockSpec((m, GRAD_BLOCK), lambda j, me: (0, jnp.maximum(j - half, 0))),
+                pl.BlockSpec((m, GRAD_BLOCK), lambda j, me: (0, jnp.minimum(j, half - 1))),
+            ],
+        ),
+        out_shape=[jax.ShapeDtypeStruct((m, n // 2), bf16)] * 2,
+        compiler_params=params(),
+        cost_estimate=pl.CostEstimate(
+            flops=3 * rows * m * n, bytes_accessed=4 * m * n, transcendentals=0
+        ),
+    )(me, left, right, *after)
+
+
+def small_grad_kernel(count, me_ref, *refs):
     n3_ref, glearn_ref, ghid_ref, inner_ref, glogit_ref = refs[:5]
     attended = refs[5 : 5 + count]
-    out_ref, lout_ref = refs[5 + count + waits :]
-    learn_columns = glearn_ref.shape[1]
-    out_ref[:, :learn_columns] = tn(n3_ref[...], glearn_ref[...]).astype(bf16)
+    keep_ref, send_ref, lout_ref, learn_ref, wout_ref = refs[5 + count :]
+    learn_ref[...] = tn(n3_ref[...], glearn_ref[...]).astype(bf16)
     lout_ref[...] = tn(inner_ref[...], glogit_ref[...])
     features = attended[0].shape[1]
     for d in range(count):
         owner = jnp.bitwise_xor(me_ref[0], d)
         to = pl.ds(pl.multiple_of(owner * features, features), features)
-        out_ref[to, learn_columns:] = tn(attended[d][...], ghid_ref[...]).astype(bf16)
-
-
-def small_grad_call(me, n3, glearn, ghid, inner, glogit, attended, after=()):
+        wout_ref[to, :] = tn(attended[d][...], ghid_ref[...]).astype(bf16)
+    first = me_ref[0] % 2 == 0
+
+    @pl.when(first)
+    def _():
+        keep_ref[...] = learn_ref[...]
+        send_ref[...] = wout_ref[...]
+
+    @pl.when(jnp.logical_not(first))
+    def _():
+        keep_ref[...] = wout_ref[...]
+        send_ref[...] = learn_ref[...]
+
+
+def small_grad_call(me, n3, glearn, ghid, inner, glogit, attended):
     rows, width = n3.shape
     operands = [n3, glearn, ghid, inner, glogit, *attended]
-    out = jax.ShapeDtypeStruct((width, glearn.shape[1] + ghid.shape[1]), bf16)
+    out = jax.ShapeDtypeStruct((width, ghid.shape[1]), bf16)
     lout = jax.ShapeDtypeStruct((inner.shape[1], glogit.shape[1]), f32)
     once = lambda a: pl.BlockSpec(a.shape, lambda j, m: (0, 0), pipeline_mode=pl.Buffered(1))
     return pl.pallas_call(
-        functools.partial(small_grad_kernel, len(attended), len(after)),
+        functools.partial(small_grad_kernel, len(attended)),
         grid_spec=pltpu.PrefetchScalarGridSpec(
             num_scalar_prefetch=1,
             grid=(1,),
-            in_specs=[once(a) for a in operands] + [ANYWHERE] * len(after),
-            out_specs=[once(out), once(lout)],
-        ),
-        out_shape=[out, lout],
+            in_specs=[once(a) for a in operands],
+            out_specs=[once(out), once(out), once(lout)],
+            scratch_shapes=[pltpu.VMEM(out.shape, bf16), pltpu.VMEM(out.shape, bf16)],
+        ),
+        out_shape=[out, out, lout],
         compiler_params=params(),
         cost_estimate=pl.CostEstimate(
             flops=6 * rows * width * width, bytes_accessed=20 * width * width, transcendentals=0
         ),
-    )(me, *operands, *after)
-
-
-def qkv_grad_kernel(groups, splits, waits, n_ref, *refs):
-    parts = refs[: groups * splits]
-    out_ref, acc_ref = refs[groups * splits + waits :]
+    )(me, *operands)
+
+
+def qkv_grad_kernel(groups, waits, me_ref, n_ref, gain_ref, shift_ref, *refs):
+    parts, weights = refs[:groups], refs[groups : groups + 3]
+    out_ref, sums_ref, acc_ref, sum_ref = refs[groups + 3 + waits :]
     step = pl.program_id(0)
-    columns = parts[0].shape[2]
+    wide = weights[0].shape[1]
     for d in range(2 * groups):
 
         @pl.when(step == d)
         def _():
-            for s in range(splits):
-                at = slice(s * columns, (s + 1) * columns)
-                part = tn(n_ref[0], parts[s * groups + d // 2][d % 2])
-                acc_ref[:, at] = part if d == 0 else acc_ref[:, at] + part
+            mixed = parts[d // 2][d % 2]
+            part = tn(n_ref[0], mixed)
+            column = total(mixed.astype(f32))
+            acc_ref[...] = part if d == 0 else acc_ref[...] + part
+            sum_ref[...] = column if d == 0 else sum_ref[...] + column
 
     @pl.when(step == 2 * groups - 1)
     def _():
-        out_ref[...] = acc_ref[...].astype(bf16)
-
-
-def qkv_grad_call(normed, parts, splits, after=()):
-    count, rows, width = normed.shape
-    columns = parts[0].shape[2] * splits
-    once = lambda a: pl.BlockSpec(a.shape, lambda d: (0, 0, 0), pipeline_mode=pl.Buffered(1))
+        by_unit, column = acc_ref[...], sum_ref[...]
+        out_ref[...] = (by_unit * gain_ref[...] + shift_ref[...] * column).astype(bf16)
+        weight = jnp.concatenate([ref[...].astype(f32) for ref in weights], axis=1)
+        sums_ref[:, 0:1] = jnp.sum(by_unit * weight, axis=1, keepdims=True)
+        sums_ref[:, 1:2] = jnp.sum(weight * column, axis=1, keepdims=True)
+
+
+def qkv_grad_call(me, unit, parts, w_qkv, gain, shift, split, splits, after=()):
+    count, rows, width = unit.shape
+    columns = parts[0].shape[2]
+    once = lambda a: pl.BlockSpec(
+        a.shape, lambda d, m: (0,) * len(a.shape), pipeline_mode=pl.Buffered(1)
+    )
+    specs, operands = own_columns(w_qkv, width // count, splits, [split])
     return pl.pallas_call(
-        functools.partial(qkv_grad_kernel, count // 2, splits, len(after)),
-        grid=(count,),
-        in_specs=[pl.BlockSpec((1, rows, width), lambda d: (d, 0, 0))]
-        + [once(a) for a in parts]
-        + [ANYWHERE] * len(after),
-        out_specs=pl.BlockSpec((width, columns), lambda d: (0, 0)),
-        out_shape=jax.ShapeDtypeStruct((width, columns), bf16),
-        scratch_shapes=[pltpu.VMEM((width, columns), f32)],
-        compiler_params=params(),
-        cost_estimate=pl.CostEstimate(
-            flops=3 * count * rows * width * columns,
-            bytes_accessed=2 * count * rows * width,
-            transcendentals=0,
-        ),
-    )(normed, *parts, *after)
-
-
-def norm_sums_kernel(count, splits, local_rows, waits, me_ref, *refs):
-    groups = count // 2
-    pieces, parts = refs[:count], refs[count : count + groups * splits]
-    at = count + groups * splits
-    columns, (sums_ref, w_ref) = refs[at : at + 3 * splits], refs[at + 3 * splits + waits :]
-    wide = columns[0].shape[1]
-    block = pl.program_id(0)
-
-    @pl.when(block == 0)
-    def _():
-        sums_ref[...] = jnp.zeros_like(sums_ref)
-        for i, ref in enumerate(columns):
-            w_ref[:, i * wide : (i + 1) * wide] = ref[...]
-
-    unit, _ = norm_parts(load_block(pieces, block, BLK // count, local_rows))
-    mixed = jnp.concatenate(
-        [
-            jnp.concatenate(
-                [parts[s * groups + d // 2][d % 2] for d in range(count)], axis=0
-            )
-            for s in range(splits)
-        ],
-        axis=1,
-    )
-    back = nt(mixed, w_ref[...])
-    sums_ref[0:1, :] += total(back * unit)
-    sums_ref[1:2, :] += total(back)
-
-
-def norm_sums_call(me, pieces, parts, w_qkv, after=()):
-    count, (local_rows, width) = len(pieces), pieces[0].shape
-    splits, columns = 2 * len(parts) // count, parts[0].shape[2]
-    piece_rows = BLK // count
-    blocks = parts[0].shape[1] // piece_rows
-    specs, operands = own_columns(w_qkv, me, width // count, splits)
-    return pl.pallas_call(
-        functools.partial(norm_sums_kernel, count, splits, local_rows, len(after)),
+        functools.partial(qkv_grad_kernel, count // 2, len(after)),
         grid_spec=pltpu.PrefetchScalarGridSpec(
             num_scalar_prefetch=1,
-            grid=(blocks,),
-            in_specs=[pl.BlockSpec((piece_rows, width), lambda b, m: (b, 0))] * count
-            + [pl.BlockSpec((2, piece_rows, columns), lambda b, m: (0, b, 0))] * len(parts)
+            grid=(count,),
+            in_specs=[pl.BlockSpec((1, rows, width), lambda d, m: (d, 0, 0)), once(gain), once(shift)]
+            + [once(a) for a in parts]
             + specs
             + [ANYWHERE] * len(after),
-            out_specs=pl.BlockSpec((8, width), lambda b, m: (0, 0)),
-            scratch_shapes=[pltpu.VMEM((width, columns * splits), bf16)],
-        ),
-        out_shape=jax.ShapeDtypeStruct((8, width), f32),
+            out_specs=[
+                pl.BlockSpec((width, columns), lambda d, m: (0, 0)),
+                pl.BlockSpec((width, 2), lambda d, m: (0, 0)),
+            ],
+            scratch_shapes=[pltpu.VMEM((width, columns), f32), pltpu.VMEM((1, columns), f32)],
+        ),
+        out_shape=[
+            jax.ShapeDtypeStruct((width, columns), bf16),
+            jax.ShapeDtypeStruct((width, 2), f32),
+        ],
         compiler_params=params(),
-        cost_estimate=pl.CostEstimate(
-            flops=4 * blocks * BLK * width * columns * splits,
-            bytes_accessed=2 * blocks * BLK * width,
-            transcendentals=0,
-        ),
-    )(me, *pieces, *parts, *operands, *after)
+        cost_estimate=pl.CostEstimate(flops=1 << 20, bytes_accessed=1 << 10, transcendentals=0),
+    )(me, unit, gain, shift, *parts, *operands, *after)
 
 
 def tokens_kernel(groups, splits, me_ref, tok_ref, ghid_ref, w_ref, gain_ref, *refs):
@@ -892,11 +924,7 @@
         ),
         out_shape=jax.ShapeDtypeStruct((1, local_rows, width), f32),
         compiler_params=params(),
-        cost_estimate=pl.CostEstimate(
-            flops=12 * local_rows * width * width,
-            bytes_accessed=local_rows * width * 16,
-            transcendentals=0,
-        ),
+        cost_estimate=pl.CostEstimate(flops=1 << 20, bytes_accessed=1 << 10, transcendentals=0),
     )(me, tok, ghid, w_qkv, gain, *same, *other)
 
 
@@ -980,7 +1008,7 @@
         compiler_params=pltpu.CompilerParams(
             collective_id=0, has_side_effects=True, vmem_limit_bytes=32 << 20
         ),
-        cost_estimate=pl.CostEstimate(flops=1 << 33, bytes_accessed=1 << 20, transcendentals=0),
+        cost_estimate=pl.CostEstimate(flops=1 << 20, bytes_accessed=1 << 10, transcendentals=0),
     )(vec, slots)
 
 
@@ -1023,9 +1051,6 @@
     row_bits, img_bits = stages()
     n_img = len(img_bits)
 
-    pieces = gather_pieces(tokens[0])
-    grads_in = gather_pieces(cotangent[0].reshape(slots_here, LT * width).astype(bf16))
-
     piece_rows = BLK // row_count
     blocks = pl.cdiv(local_rows, piece_rows)
     images = jnp.stack([row_images(group_counts, p, local_rows, row_count) for p in partners])
@@ -1041,8 +1066,12 @@
     me = device.reshape(1)
     w_out_here = jnp.concatenate([rows_of(w_out, p, features) for p in partners], axis=0)
     bias_here = lax.dynamic_slice_in_dim(qv_bias, device * features, features, 1)
-
-    normed, q, k, v, kt, vt = qkv_call(
+    grads_in = gather_pieces(cotangent[0].reshape(slots_here, LT * width).astype(bf16))
+    pieces = gather_pieces(
+        tokens[0], [imgq, imgk, lo, hi, image_here, w_out_here, bias_here, grads_in[-1]]
+    )
+
+    unit, q, k, v, kt, vt = qkv_call(
         me, pieces, w_qkv, bias_here, norm_gain[0:1], norm_bias[0:1], splits
     )
     *attended, ot, lse = attend_call(q, k, vt, imgq, imgk, lo, hi, row_count)
@@ -1093,12 +1122,17 @@
     stage = lambda value, bits, after=(): reduce_stage(value, bits, n_img, after)
     stack_other = lambda groups: jump(jnp.stack([g[1] for g in groups]), 1)
 
-    small, grad_learn_out = small_grad_call(me, n3, glearn, ghid, inner, glogit, attended)
-    small = spread_img(small)
-    grad_down = grad_call(gated, gres, True, [small])
-    small = stage(small, core, [grad_down])
-    grad_up = grad_call(n2, gup, False, [grad_down, small])
-    down = stage(spread_img(grad_down), core, [grad_up])
+    def core_sum(keep, send, after):
+        arrived = behind(jump(send, 1), after)
+        return spread_img((keep.astype(f32) + arrived.astype(f32)).astype(bf16))
+
+    keep_small, send_small, grad_learn_out = small_grad_call(
+        me, n3, glearn, ghid, inner, glogit, attended
+    )
+    keep_down, send_down = down_grad_call(me, gated, gres, [send_small])
+    small = core_sum(keep_small, send_small, [send_down])
+    keep_up, send_up = up_grad_call(me, n2, gup, [send_down, small])
+    down = core_sum(keep_down, send_down, [send_up])
 
     def back_call(s, after):
         *parts, sums = attend_back_call(
@@ -1106,47 +1140,36 @@
         )
         return parts, sums
 
-    mixed, same, other, qkv_sums = [], [], [], []
-    ups = spread_img(grad_up)
+    def grad_qkv_call(s, parts, after):
+        turned = [norm_gain[0].reshape(-1, 1), norm_bias[0].reshape(-1, 1)]
+        return qkv_grad_call(me, unit, parts, w_qkv, *turned, s, splits, after)
+
+    def far_sent(parts):
+        return [parts[0]] + [jump(parts[g], 2 * g) for g in range(1, len(parts))]
+
+    same, qkv_sums, norm_sums, grad_qkv = [], [], [], []
+    after = [down, send_up]
     for s in range(splits):
-        parts, sums = back_call(s, [down, ups] if s == 0 else [small, ups, down])
-        mixed += parts
+        parts, sums = back_call(s, after)
+        here = far_sent(parts)
         qkv_sums.append(sums[0:2])
-        here = [parts[0]] + [jump(parts[g], 2 * g) for g in range(1, len(parts))]
+        last = s == splits - 1
         if s == 0:
             small = stage(small, y_bits, [sums])
-            ups = stage(ups, core, [sums])
+            ups = core_sum(keep_up, send_up, [sums])
             down = stage(down, far_row, [sums])
-            first = here
-    if splits > 1:
-        first = [first[0]] + [behind(h, [sums]) for h in first[1:]]
-        same = first + here
-    else:
-        same = here
-    ups = stage(ups, y_bits, [sums])
-    down = stage(down, z_bits[0], [sums])
-    small = stage(small, z_bits[0], [sums])
-    other = [stack_other(first)]
-    grad_qkv = qkv_grad_call(normed, mixed, splits, [down, ups, small])
-    if splits > 1:
-        other.append(stack_other([here[0]] + [behind(h, [grad_qkv]) for h in here[1:]]))
-    norm_sums = norm_sums_call(me, pieces, mixed, w_qkv, [grad_qkv])
-    down = stage(down, z_bits[1], [norm_sums])
-    small = stage(small, z_bits[1], [norm_sums])
-    ups = stage(ups, z_bits[0], [norm_sums])
-    grad_qkv = stage(spread_img(grad_qkv), y_bits, [norm_sums])
-    for bits in z_bits[1:]:
-        ups = stage(ups, bits)
-    for bits in z_bits[2:]:
-        down = stage(down, bits)
-        small = stage(small, bits)
-    down = stage(down, y_bits)
-    for bits in z_bits:
-        grad_qkv = stage(grad_qkv, bits)
-    grad_tokens = tokens_call(
-        me, tokens[0], grad_hidden, w_qkv, norm_gain[0:1], same, other, row_count
-    )
-
+        if last:
+            ups = stage(ups, y_bits, [sums])
+            down = stage(down, z_bits[0], [sums])
+            small = stage(small, z_bits[1], [sums])
+            same = [behind(h, [sums]) for h in same]
+        grad, norm_sum = grad_qkv_call(s, parts, [ups, down])
+        norm_sums.append(norm_sum)
+        grad_qkv.append(spread_img(grad))
+        same += here
+        if s == 0:
+            small = stage(small, z_bits[0], [norm_sum])
+            after = [small, grad]
     by_slot = jnp.dot(select.T, pooled.reshape(IMGS, LT * width), precision=highest)
     by_slot = by_slot.astype(bf16).reshape(row_count, -1, 128)
     late = lax.dynamic_update_slice(
@@ -1158,20 +1181,51 @@
             vec_sums.reshape(-1),
             jnp.sum(grad_learn_out.reshape(-1, IMGS, LT), axis=1).reshape(-1),
             late.reshape(-1),
-            norm_sums[0:2].reshape(-1),
+            sum(norm_sums).T.reshape(-1),
             jnp.sum(logit_sums.reshape(IMGS, LT), axis=0),
         ]
     )
     vectors = jnp.pad(vectors, (0, -vectors.shape[0] % 1024)).reshape(-1, 128)
     vectors, learned = vectors_call(vectors, by_slot)
+
+    here = [behind(h, [vectors]) for h in same[-row_count // 2 + 1 :]]
+    same = same[: len(same) - len(here)] + here
+    groups = row_count // 2
+    others = jnp.stack([p[1] for p in same])
+    others = jump(others, 1)
+    other = [others[s * groups : (s + 1) * groups] for s in range(splits)]
+    ups = stage(ups, z_bits[0], [vectors])
+    down = stage(down, z_bits[1], [vectors])
+    grad_qkv = stage(jnp.concatenate(grad_qkv, axis=-1), y_bits, [vectors])
+    for bits in z_bits[2:]:
+        down = stage(down, bits)
+        small = stage(small, bits)
+    grad_tokens = tokens_call(
+        me,
+        tokens[0],
+        behind(grad_hidden, [ups, down, grad_qkv]),
+        w_qkv,
+        norm_gain[0:1],
+        same,
+        other,
+        row_count,
+    )
+    small = exchange_sum(small, far_row, [grad_tokens])
+    grad_qkv = stage(grad_qkv, z_bits[0], [grad_tokens])
+    for bits in z_bits[1:]:
+        ups = stage(ups, bits, [grad_tokens])
+    down = stage(down, y_bits, [grad_tokens])
+    ups = exchange_sum(ups, far_row)
+    for bits in z_bits[1:]:
+        grad_qkv = stage(grad_qkv, bits)
     vectors = vectors.reshape(-1)
     scale_here = jnp.dot(scale, select, precision=highest)[:slots_here]
     learned = learned.reshape(slots_here, LT * width) * scale_here[:, None]
     learned = learned.reshape(1, slots_here, LT, width)
 
     share_down = finish_weight(down, row_bits)
-    share_small = finish_weight(exchange_sum(small, far_row), core)
-    share_up = finish_weight(exchange_sum(ups, far_row), core)
+    share_small = finish_weight(small, core, [grad_tokens])
+    share_up = finish_weight(ups, core)
     share_learn = share_small[:, : learn_in.shape[1]]
     share_out = share_small[:, learn_in.shape[1] :]
     shares = gather_columns(grad_qkv.reshape(grad_qkv.shape[-2:]), lambda c: c, row_bits)

time: 659 us -> 585 us (0.89)
  waiting for transfers between devices: 152 us -> 102 us
  Pallas kernels: 353 us -> 334 us
  local copies, waits for them, and re-layouts: 57.4 us -> 47 us
  other arithmetic: 43.6 us -> 50.3 us
    ppermute x12, waiting for transfers between devices: 54.9 us -> 25.1 us  [jump(): return lax.ppermute(value, 'img', [(i, i ^ img_mask) for i in range(imgs)])]
    ppermute x33 -> x32, waiting for transfers between devices: 97.5 us -> 77 us  [jump(): return lax.ppermute(value, 'row', [(i, i ^ row_mask) for i in range(rows)])]
    pallas_call x5, Pallas kernels: 72.6 us -> 60.6 us  [the longest x2 20.2 us: qkv_grad_call(): pl.pallas_call(functools.partial(qkv_grad_kernel, count // 2, len(after))...]
    convert_element_type x0 -> x3, other arithmetic: none -> 11.9 us  [core_sum(): return spread_img((keep.astype(f32) + arrived.astype(f32)).astype(bf16))]
    dynamic_slice x16 -> x12, local copies, waits for them, and re-layouts: 19 us -> 9.41 us  [part(): piece = lax.dynamic_slice_in_dim(piece, want * length, length, dim)]
    pallas_call x1, Pallas kernels: 50.9 us -> 41.5 us  [attend_call(): pl.pallas_call(functools.partial(attend_kernel, count, heads), grid_spec=...]
    convert_element_type x14 -> x11, other arithmetic: 26.6 us -> 17.7 us  [reduce_stage(): tree([arrived[e].astype(f32) for e in range(len(masks))]).astype(bf16)]
    unnamed x129 -> x116, local copies, waits for them, and re-layouts: 14.4 us -> 7.36 us
  transfers between devices with their start and end apart: 45 -> 44, of which waited for: 13 -> 12; matrix products, arithmetic and copies ran while one was open for 13% -> 15% of each run, Pallas kernels for 36% -> 38%
where the time goes in v3:
time: 585 us; the launch traced here: 579 us
  Pallas kernels  334 us (57%)
  waiting for transfers between devices  102 us (17%)
  other arithmetic  50.3 us (9%)
  local copies, waits for them, and re-layouts  47 us (8%)
  starting transfers between devices  43.2 us (7%)
    pallas_call x1, Pallas kernels, rows_call(): pl.pallas_call(functools.partial(rows_kernel, count, splits, local_rows),...  89 us
    ppermute x32, waiting for transfers between devices, jump(): return lax.ppermute(value, 'row', [(i, i ^ row_mask) for i in range(rows)])  77 us
    pallas_call x2, Pallas kernels, attend_back_call(): pl.pallas_call(functools.partial(attend_back_kernel, count, heads, split...  76.5 us
    pallas_call x1, Pallas kernels, attend_call(): pl.pallas_call(functools.partial(attend_kernel, count, heads), grid_spec=...  41.5 us
    pallas_call x1, Pallas kernels, vectors_call(): pl.pallas_call(functools.partial(vectors_kernel, count, row_bits, img_bit...  28.2 us
    ppermute x12, waiting for transfers between devices, jump(): return lax.ppermute(value, 'img', [(i, i ^ img_mask) for i in range(imgs)])  25.1 us
    pallas_call x1, Pallas kernels, qkv_call(): pl.pallas_call(functools.partial(qkv_kernel, count, splits, local_rows, f...  22.6 us
    ppermute x32, starting transfers between devices, jump(): return lax.ppermute(value, 'row', [(i, i ^ row_mask) for i in range(rows)])  21.9 us
  transfers between devices with their start and end apart: 44, of which 12 were waited for; matrix products, arithmetic and copies ran while one was open for 15% of the time, Pallas kernels for 38%

profile of v3, /device:TPU:0, one launch (start us, length us, event | category | flops | bytes accessed | tf_op | source)
XLA Modules:
  0.0 579.1 jit_solution(18243056846219978242)
XLA Ops:
  0.7 3.0 collective-permute-start.4
  7.6 1.7 constant_dynamic-slice_fusion.17
  9.3 1.5 pad_maximum_fusion.1.refs_2_
  10.8 39.1 %collective-permute-done.1 = bf16[2,8192]{1,0:T(2,128)(2,1)S(1)} collective-permute-done((bf16[2,8192]{1,0:T(2,128)(2,1)S(1)}, bf16[2,8192]{1,0:T(2,128)(2,1)S(1)}, u32[]{:S(2)}, u32[]{:S(2)}) %collective-permute-start.1) | collective-permute-done | bytes 32800 | tf_op jit(solution)/shard_map/ppermute | solution.py:67
  49.9 1.3 constant_dynamic-slice_fusion.13.refs_10_
  52.7 2.0 copy.67.refs_4_.refs_13_
  55.3 1.2 collective-permute-done.5.refs_3_
  56.6 22.6 %shard_map.297 = (bf16[4,1024,1024]{2,1,0:T(8,128)(2,1)}, bf16[4096,256]{1,0:T(8,128)(2,1)}, bf16[4096,256]{1,0:T(8,128)(2,1)}, bf16[4096,256]{1,0:T(8,128)(2,1)...) custom-call(s32[1]{0:T(128)} %bitcast.21.me_ref, bf16[1016,1024]{1,0:T(8,128)(2,1)} %bitcast.157, ...), custom_call_target="tpu_custom_call" | custom-call | flops 19327352832 | bytes 27262976 | tf_op jit(solution)/shard_map/pallas_call | solution.py:245
  79.3 41.5 %shard_map.298 = (bf16[1024,256]{1,0:T(8,128)(2,1)}, bf16[1024,256]{1,0:T(8,128)(2,1)}, bf16[1024,256]{1,0:T(8,128)(2,1)}, bf16[1024,256]{1,0:T(8,128)(2,1)}, f3...) custom-call(s32[16]{0:T(128)} %get-tuple-element.217.lo_ref, s32[16]{0:T(128)} %get-tuple-element.216.hi_ref, ...), custom_call_target="tpu_custom_call" | custom-call | flops 42949672960 | bytes 16777216 | tf_op jit(solution)/shard_map/pallas_call | solution.py:348
  121.2 1.7 collective-permute-start.7
  127.1 9.0 %collective-permute-done.7.refs_13_.refs_7_ = bf16[1024,256]{1,0:T(8,128)(2,1)S(1)} collective-permute-done((bf16[1024,256]{1,0:T(8,128)(2,1)}, bf16[1024,256]{1,0:T(8,128)(2,1)S(1)}, u32[]{:S(2)}, u32[]{:S(2)}) %collective-permute-start.7) | collective-permute-done | bytes 524320 | tf_op jit(solution)/shard_map/ppermute | solution.py:67
  136.2 9.8 %collective-permute-done.8.refs_14_.refs_8_ = bf16[1024,256]{1,0:T(8,128)(2,1)S(1)} collective-permute-done((bf16[1024,256]{1,0:T(8,128)(2,1)}, bf16[1024,256]{1,0:T(8,128)(2,1)S(1)}, u32[]{:S(2)}, u32[]{:S(2)}) %collective-permute-start.8) | collective-permute-done | bytes 524320 | tf_op jit(solution)/shard_map/ppermute | solution.py:67
  146.8 89.0 %shard_map.299 = (bf16[1024,1024]{1,0:T(8,128)(2,1)}, bf16[1024,4096]{1,0:T(8,128)(2,1)}, bf16[1024,4096]{1,0:T(8,128)(2,1)}, bf16[1024,1024]{1,0:T(8,128)(2,1)}...) custom-call(bf16[1016,1024]{1,0:T(8,128)(2,1)} %bitcast.158, ...), custom_call_target="tpu_custom_call" | custom-call | flops 42949672960 | bytes 58720256 | tf_op jit(solution)/shard_map/pallas_call | solution.py:669
  235.8 11.5 %shard_map.300 = (bf16[1024,1024]{1,0:T(8,128)(2,1)}, bf16[1024,1024]{1,0:T(8,128)(2,1)}, f32[1024,64]{1,0:T(8,128)}) custom-call(s32[1]{0:T(128)} %bitcast.21.me_ref, bf16[1024,1024]{1,0:T(8,128)(2,1)} %get-tuple-element.101.refs_0_, bf16[1024,1024]{1,0:T(8,128)(2,1)} %get-tuple-element.102.refs_1_, bf16[1024,1024]{1,0:T(8,128)(2,1)} %get-tuple-element.103.refs_2_, ...), custom_call_target="tpu_custom_call" | custom-call | flops 6442450944 | bytes 20971520 | tf_op jit(solution)/shard_map/pallas_call | solution.py:810
  247.4 14.0 %shard_map.301 = (bf16[4096,512]{1,0:T(8,128)(2,1)}, bf16[4096,512]{1,0:T(8,128)(2,1)}) custom-call(s32[1]{0:T(128)} %bitcast.21.me_ref, bf16[1024,4096]{1,0:T(8,128)(2,1)} %get-tuple-element.111.left_ref, bf16[1024,1024]{1,0:T(8,128)(2,1)} %get-tuple-element.112.right_ref, bf16[1024,1024]{1,0:T(8,128)(2,1)} %get-tuple-element.113.refs_0_), custom_call_target="tpu_custom_call" | custom-call | flops 12884901888 | bytes 16777216 | tf_op jit(solution)/shard_map/pallas_call | solution.py:715
  264.0 1.6 collective-permute-start.10
  268.7 2.9 collective-permute-done.13
  271.9 3.2 add_convert_fusion.4
  275.2 1.2 copy-done.13
  276.4 14.8 %shard_map.302 = (bf16[1024,2048]{1,0:T(8,128)(2,1)}, bf16[1024,2048]{1,0:T(8,128)(2,1)}) custom-call(s32[1]{0:T(128)} %bitcast.21.me_ref, bf16[1024,1024]{1,0:T(8,128)(2,1)} %get-tuple-element.116.left_ref, bf16[1024,4096]{1,0:T(8,128)(2,1)} %get-tuple-element.117.right_ref, bf16[4096,512]{1,0:T(8,128)(2,1)} %get-tuple-element.115.refs_0_, ...), custom_call_target="tpu_custom_call" | custom-call | flops 12884901888 | bytes 16777216 | tf_op jit(solution)/shard_map/pallas_call | solution.py:757
  291.4 4.7 add_convert_fusion.1
  296.1 1.6 constant_dynamic-slice_fusion.10
  298.7 2.1 collective-permute-start.15
  300.8 4.0 collective-permute-start.17
  305.4 38.2 %shard_map.303 = (bf16[2,1024,384]{2,1,0:T(8,128)(2,1)}, bf16[2,1024,384]{2,1,0:T(8,128)(2,1)}, f32[8,128]{1,0:T(8,128)}) custom-call(s32[16]{0:T(128)} %get-tuple-element.217.lo_ref, s32[16]{0:T(128)} %get-tuple-element.216.hi_ref, bf16[1024,128]{1,0:T(8,128)(2,1)} %get-tuple-element.107.refs_0_, bf16[1024,128]{1,0:T(8,128)(2,1)} %collective-permute-done.9.refs_1_, ...), custom_call_target="tpu_custom_call" | custom-call | flops 34359738368 | bytes 12582912 | tf_op jit(solution)/shard_map/pallas_call | solution.py:476
  344.6 1.8 add_convert_fusion.7
  347.3 6.3 %collective-permute-start.18 = (bf16[2,1,1,128,1024]{4,3,2,1,0:T(8,128)(2,1)}, bf16[2,1,1,128,1024]{4,3,2,1,0:T(8,128)(2,1)S(1)}, u32[]{:S(2)}, u32[]{:S(2)}) collective-permute-start(bf16[2,1,1,128,1024]{4,3,2,1,0:T(8,128)(2,1)} %constant_dynamic-slice_fusion.11), channel_id=1, source_target_pairs={{0,8},{4,12},{8,0},{12,4},{16,24},{20,28},{24,16},{28,20},{1,9},{5... | collective-permute-start | bytes 1572872 | tf_op jit(solution)/shard_map/ppermute | solution.py:69
  353.5 4.1 add_convert_fusion
  357.7 1.5 constant_dynamic-slice_fusion.9
  359.2 1.6 copy-done.2
  362.1 2.2 add_convert_fusion.3.refs_6_
  365.9 10.0 %shard_map.304 = (bf16[1024,384]{1,0:T(8,128)(2,1)}, f32[1024,2]{1,0:T(8,128)}) custom-call(s32[1]{0:T(128)} %bitcast.21.me_ref, bf16[4,1024,1024]{2,1,0:T(8,128)(2,1)} %get-tuple-element.132.n_ref, f32[1024,1]{1,0:T(8,128)} %copy.73.gain_ref, f32[1024,1]{1,0:T(8,128)} %copy.74.shift_ref, bf16[2,1024,384]{2,1,0:T(8,128)(2,1)} %get-tuple-element.157.refs_0_, ...), custom_call_target="tpu_custom_call" | custom-call | flops 1048576 | bytes 1024 | tf_op jit(solution)/shard_map/pallas_call | solution.py:858
  375.9 1.3 collective-permute-start.21
  378.2 38.3 %shard_map.305 = (bf16[2,1024,384]{2,1,0:T(8,128)(2,1)}, bf16[2,1024,384]{2,1,0:T(8,128)(2,1)}, f32[8,128]{1,0:T(8,128)}) custom-call(s32[16]{0:T(128)} %get-tuple-element.217.lo_ref, s32[16]{0:T(128)} %get-tuple-element.216.hi_ref, bf16[1024,128]{1,0:T(8,128)(2,1)} %get-tuple-element.127.refs_0_, bf16[1024,128]{1,0:T(8,128)(2,1)} %collective-permute-done.14.refs_1_, ...), custom_call_target="tpu_custom_call" | custom-call | flops 34359738368 | bytes 12582912 | tf_op jit(solution)/shard_map/pallas_call | solution.py:476
  418.1 2.1 slice.197
  422.9 7.5 %collective-permute-start.34 = (bf16[1,1,1,128,1024]{4,3,2,1,0:T(8,128)(2,1)}, bf16[1,1,1,128,1024]{4,3,2,1,0:T(8,128)(2,1)}, u32[]{:S(2)}, u32[]{:S(2)}) collective-permute-start(bf16[1,1,1,128,1024]{4,3,2,1,0:T(8,128)(2,1)} %constant_dynamic-slice_fusion.3), channel_id=1, source_target_pairs={{0,16},{4,20},{8,24},{12,28},{16,0},{20,4},{24,8},{28,12},{1,17},{... | collective-permute-start | bytes 786440 | tf_op jit(solution)/shard_map/ppermute | solution.py:69
  430.5 1.7 add_convert_fusion.6.refs_6_
  433.1 3.7 add_convert_fusion.2.refs_5_
  436.8 10.2 %shard_map.306 = (bf16[1024,384]{1,0:T(8,128)(2,1)}, f32[1024,2]{1,0:T(8,128)}) custom-call(s32[1]{0:T(128)} %bitcast.21.me_ref, bf16[4,1024,1024]{2,1,0:T(8,128)(2,1)} %get-tuple-element.132.n_ref, f32[1024,1]{1,0:T(8,128)} %copy.73.gain_ref, f32[1024,1]{1,0:T(8,128)} %copy.74.shift_ref, bf16[2,1024,384]{2,1,0:T(8,128)(2,1)} %get-tuple-element.142.refs_0_.refs_2_, ...), custom_call_target="tpu_custom_call" | custom-call | flops 1048576 | bytes 1024 | tf_op jit(solution)/shard_map/pallas_call | solution.py:858
  447.0 1.2 add_bitcast_fusion
  448.5 28.2 %shard_map.307 = (f32[200,128]{1,0:T(8,128)S(1)}, f32[128,128]{1,0:T(8,128)S(1)}) custom-call(f32[200,128]{1,0:T(8,128)S(1)} %pad_bitcast_fusion.vec_ref, bf16[4,128,128]{2,1,0:T(8,128)(2,1)S(1)} %reshape.480.slot_ref), custom_call_target="tpu_custom_call" | custom-call | flops 1048576 | bytes 1024 | tf_op jit(solution)/shard_map/pallas_call | solution.py:992
  476.7 1.2 slice.199
  478.0 1.9 pad_maximum_fusion
  480.1 1.9 add_convert_fusion.16
  482.6 2.1 fusion.1
  485.8 1.8 collective-permute-start.23
  487.6 1.2 add_convert_fusion.11
  497.4 8.0 %collective-permute-done.25 = bf16[2,2,1,128,768]{4,3,2,1,0:T(8,128)(2,1)} collective-permute-done((bf16[2,2,1,128,768]{4,3,2,1,0:T(8,128)(2,1)}, bf16[2,2,1,128,768]{4,3,2,1,0:T(8,128)(2,1)}, u32[]{:S(2)}, u32[]{:S(2)}) %collective-permute-start.25) | collective-permute-done | bytes 786464 | tf_op jit(solution)/shard_map/ppermute | solution.py:69
  505.4 1.4 add_convert_fusion.8
  507.6 4.5 collective-permute-done.23
  512.1 1.6 add_convert_fusion.5
  513.9 3.9 fusion.33
  517.7 15.4 %shard_map.308 = f32[1,1016,1024]{2,1,0:T(8,128)} custom-call(s32[1]{0:T(128)} %bitcast.21.me_ref, bf16[1016,1024]{1,0:T(8,128)(2,1)} %bitcast.159, f32[1024,1024]{1,0:T(8,128)} %get-tuple-element.156.ghid_ref, bf16[1024,3072]{1,0:T(8,128)(2,1)} %w_ref.1, f32[1,1024]{1,0:T(1,128)} %get-tuple-element.269.refs_11_.gain_ref, ...), custom_call_target="tpu_custom_call" | custom-call | flops 1048576 | bytes 1024 | tf_op jit(solution)/shard_map/pallas_call | solution.py:909
  534.3 1.5 collective-permute-start.42
  535.8 2.4 collective-permute-done.37
  539.3 1.6 collective-permute-start.36
  542.3 10.1 %collective-permute-done.30 = bf16[1,1,1,128,768]{4,3,2,1,0:T(8,128)(2,1)S(1)} collective-permute-done((bf16[1,1,1,128,768]{4,3,2,1,0:T(8,128)(2,1)S(1)}, bf16[1,1,1,128,768]{4,3,2,1,0:T(8,128)(2,1)S(1)}, u32[]{:S(2)}, u32[]{:S(2)}) %collective-permute-start.30) | collective-permute-done | bytes 196640 | tf_op jit(solution)/shard_map/ppermute | solution.py:69
  552.5 1.4 collective-permute-start.38
  556.1 1.2 collective-permute-start.33
  557.5 1.6 maximum_convert_fusion.1
  559.1 12.4 %collective-permute-done.32 = bf16[128,768]{1,0:T(8,128)(2,1)S(1)} collective-permute-done((bf16[128,768]{1,0:T(8,128)(2,1)S(1)}, bf16[128,768]{1,0:T(8,128)(2,1)S(1)}, u32[]{:S(2)}, u32[]{:S(2)}) %collective-permute-start.32) | collective-permute-done | bytes 196640 | tf_op jit(solution)/shard_map/ppermute | solution.py:67
  571.5 2.3 collective-permute-done.33
  575.4 1.3 convert_element_type.269
  577.3 1.5 maximum_convert_fusion
  (273 shorter events, 49.9 us)
Async XLA Ops:
  0.6 54.7 %copy-start = (bf16[1024,8]{0,1:T(8,128)(2,1)S(1)}, bf16[1024,8]{0,1:T(8,128)(2,1)}, u32[]{:S(2)}) copy-start(bf16[1024,8]{0,1:T(8,128)(2,1)} %param.33) | copy-start | bytes 49156
  0.7 51.4 %collective-permute-start.4 = (bf16[1016,1024]{1,0:T(8,128)(2,1)}, bf16[1016,1024]{1,0:T(8,128)(2,1)S(1)}, u32[]{:S(2)}, u32[]{:S(2)}) collective-permute-start(bf16[1016,1024]{1,0:T(8,128)(2,1)} %bitcast.155), channel_id=1, source_target_pairs={{0,2},{1,3},{2,0},{3,1},{4,6},{5,7},{6,4},{7,5},{8,10},{9,11},{10,... | collective-permute-start | bytes 6242312 | tf_op jit(solution)/shard_map/ppermute | solution.py:67
  3.7 51.6 %collective-permute-start.3 = (bf16[1016,1024]{1,0:T(8,128)(2,1)}, bf16[1016,1024]{1,0:T(8,128)(2,1)}, u32[]{:S(2)}, u32[]{:S(2)}) collective-permute-start(bf16[1016,1024]{1,0:T(8,128)(2,1)} %bitcast.156), channel_id=1, source_target_pairs={{0,1},{1,0},{2,3},{3,2},{4,5},{5,4},{6,7},{7,6},{8,9},{9,8},{10,11... | collective-permute-start | bytes 6242312 | tf_op jit(solution)/shard_map/ppermute | solution.py:67
  4.6 45.3 %collective-permute-start.1 = (bf16[2,8192]{1,0:T(2,128)(2,1)S(1)}, bf16[2,8192]{1,0:T(2,128)(2,1)S(1)}, u32[]{:S(2)}, u32[]{:S(2)}) collective-permute-start(bf16[2,8192]{1,0:T(2,128)(2,1)S(1)} %bitcast.171), channel_id=1, source_target_pairs={{0,2},{1,3},{2,0},{3,1},{4,6},{5,7},{6,4},{7,5},{8,10},{9,11},{10,... | collective-permute-start | bytes 98312 | tf_op jit(solution)/shard_map/ppermute | solution.py:67
  10.8 43.9 %copy-start.28 = (f32[3,1024]{1,0:T(4,128)S(1)}, f32[3,1024]{1,0:T(4,128)}, u32[]{:S(2)}) copy-start(f32[3,1024]{1,0:T(4,128)} %param.30) | copy-start | bytes 36868
  10.8 43.9 %copy-start.29 = (f32[3,1024]{1,0:T(4,128)S(1)}, f32[3,1024]{1,0:T(4,128)}, u32[]{:S(2)}) copy-start(f32[3,1024]{1,0:T(4,128)} %param.29) | copy-start | bytes 36868
  49.9 2.2 collective-permute-start.2
  52.1 4.5 collective-permute-start.5
  52.6 73.5 %collective-permute-start = (bf16[2,8192]{1,0:T(2,128)(2,1)S(1)}, bf16[2,8192]{1,0:T(2,128)(2,1)S(1)}, u32[]{:S(2)}, u32[]{:S(2)}) collective-permute-start(bf16[2,8192]{1,0:T(2,128)(2,1)S(1)} %bitcast.172), channel_id=1, source_target_pairs={{0,1},{1,0},{2,3},{3,2},{4,5},{5,4},{6,7},{7,6},{8,9},{9,8},{10,11... | collective-permute-start | bytes 98312 | tf_op jit(solution)/shard_map/ppermute | solution.py:67
  79.2 43.7 %copy-start.34 = (s32[1,8]{1,0:T(1,128)S(1)}, s32[1,8]{1,0:T(1,128)}, u32[]{:S(2)}) copy-start(s32[1,8]{1,0:T(1,128)} %param.19) | copy-start | bytes 100
  79.2 43.7 %copy-start.41 = (s32[1,8]{1,0:T(1,128)S(1)}, s32[1,8]{1,0:T(1,128)}, u32[]{:S(2)}) copy-start(s32[1,8]{1,0:T(1,128)} %param.20) | copy-start | bytes 100
  79.2 45.6 %copy-start.33 = (f32[8]{0:T(128)S(1)}, f32[8]{0:T(128)}, u32[]{:S(2)}) copy-start(f32[8]{0:T(128)} %param.34) | copy-start | bytes 100
  79.3 46.2 %copy-start.30 = (f32[1024]{0:T(1024)S(1)}, f32[1024]{0:T(1024)}, u32[]{:S(2)}) copy-start(f32[1024]{0:T(1024)} %param.24) | copy-start | bytes 12292
  79.3 46.2 %copy-start.31 = (f32[1024]{0:T(1024)S(1)}, f32[1024]{0:T(1024)}, u32[]{:S(2)}) copy-start(f32[1024]{0:T(1024)} %param.28) | copy-start | bytes 12292
  79.3 46.2 %copy-start.32 = (f32[1024]{0:T(1024)S(1)}, f32[1024]{0:T(1024)}, u32[]{:S(2)}) copy-start(f32[1024]{0:T(1024)} %param.32) | copy-start | bytes 12292
  120.8 6.4 %collective-permute-start.6 = (bf16[1024,256]{1,0:T(8,128)(2,1)}, bf16[1024,256]{1,0:T(8,128)(2,1)S(1)}, u32[]{:S(2)}, u32[]{:S(2)}) collective-permute-start(bf16[1024,256]{1,0:T(8,128)(2,1)} %get-tuple-element.96), channel_id=1, source_target_pairs={{0,1},{1,0},{2,3},{3,2},{4,5},{5,4},{6,7},{7,6},{8,9},{9,8},{10,11... | collective-permute-start | bytes 1572872 | tf_op jit(solution)/shard_map/ppermute | solution.py:67
  121.2 15.0 %collective-permute-start.7 = (bf16[1024,256]{1,0:T(8,128)(2,1)}, bf16[1024,256]{1,0:T(8,128)(2,1)S(1)}, u32[]{:S(2)}, u32[]{:S(2)}) collective-permute-start(bf16[1024,256]{1,0:T(8,128)(2,1)} %get-tuple-element.97), channel_id=1, source_target_pairs={{0,2},{1,3},{2,0},{3,1},{4,6},{5,7},{6,4},{7,5},{8,10},{9,11},{10,... | collective-permute-start | bytes 1572872 | tf_op jit(solution)/shard_map/ppermute | solution.py:67
  122.9 23.1 %collective-permute-start.8 = (bf16[1024,256]{1,0:T(8,128)(2,1)}, bf16[1024,256]{1,0:T(8,128)(2,1)S(1)}, u32[]{:S(2)}, u32[]{:S(2)}) collective-permute-start(bf16[1024,256]{1,0:T(8,128)(2,1)} %get-tuple-element.98), channel_id=1, source_target_pairs={{0,3},{1,2},{2,1},{3,0},{4,7},{5,6},{6,5},{7,4},{8,11},{9,10},{10,... | collective-permute-start | bytes 1572872 | tf_op jit(solution)/shard_map/ppermute | solution.py:67
  127.1 18.8 %copy-start.38 = (bf16[1024,256]{1,0:T(8,128)(2,1)}, bf16[1024,256]{1,0:T(8,128)(2,1)S(1)}, u32[]{:S(2)}) copy-start(bf16[1024,256]{1,0:T(8,128)(2,1)S(1)} %collective-permute-done.6.refs_12_.refs_6_) | copy-start | bytes 1572868
  247.4 14.2 %copy-start.36 = (bf16[1024,1024]{1,0:T(8,128)(2,1)S(1)}, bf16[1024,1024]{1,0:T(8,128)(2,1)}, u32[]{:S(2)}) copy-start(bf16[1024,1024]{1,0:T(8,128)(2,1)} %get-tuple-element.113.refs_0_) | copy-start | bytes 6291460
  247.4 18.7 %copy-start.24 = (f32[1024,64]{1,0:T(8,128)S(1)}, f32[1024,64]{1,0:T(8,128)}, u32[]{:S(2)}) copy-start(f32[1024,64]{1,0:T(8,128)} %get-tuple-element.106) | copy-start | bytes 786436
  261.4 29.8 %collective-permute-start.12 = (bf16[4096,512]{1,0:T(8,128)(2,1)}, bf16[4096,512]{1,0:T(8,128)(2,1)}, u32[]{:S(2)}, u32[]{:S(2)}) collective-permute-start(bf16[4096,512]{1,0:T(8,128)(2,1)} %get-tuple-element.115.refs_0_), channel_id=1, source_target_pairs={{0,1},{1,0},{2,3},{3,2},{4,5},{5,4},{6,7},{7,6},{8,9},{9,8},{10,11... | collective-permute-start | bytes 12582920 | tf_op jit(solution)/shard_map/ppermute | solution.py:67
  261.6 9.9 %collective-permute-start.13 = (bf16[1024,1024]{1,0:T(8,128)(2,1)S(1)}, bf16[1024,1024]{1,0:T(8,128)(2,1)}, u32[]{:S(2)}, u32[]{:S(2)}) collective-permute-start(bf16[1024,1024]{1,0:T(8,128)(2,1)S(1)} %copy-done.36), channel_id=1, source_target_pairs={{0,1},{1,0},{2,3},{3,2},{4,5},{5,4},{6,7},{7,6},{8,9},{9,8},{10,11... | collective-permute-start | bytes 6291464 | tf_op jit(solution)/shard_map/ppermute | solution.py:67
  264.0 34.7 %collective-permute-start.10 = (bf16[1024,128]{1,0:T(8,128)(2,1)}, bf16[1024,128]{1,0:T(8,128)(2,1)}, u32[]{:S(2)}, u32[]{:S(2)}) collective-permute-start(bf16[1024,128]{1,0:T(8,128)(2,1)} %get-tuple-element.109), channel_id=1, source_target_pairs={{0,2},{1,3},{2,0},{3,1},{4,6},{5,7},{6,4},{7,5},{8,10},{9,11},{10,... | collective-permute-start | bytes 786440 | tf_op jit(solution)/shard_map/ppermute | solution.py:67
  265.6 35.2 %collective-permute-start.11 = (bf16[1024,128]{1,0:T(8,128)(2,1)}, bf16[1024,128]{1,0:T(8,128)(2,1)}, u32[]{:S(2)}, u32[]{:S(2)}) collective-permute-start(bf16[1024,128]{1,0:T(8,128)(2,1)} %get-tuple-element.110), channel_id=1, source_target_pairs={{0,3},{1,2},{2,1},{3,0},{4,7},{5,6},{6,5},{7,4},{8,11},{9,10},{10,... | collective-permute-start | bytes 786440 | tf_op jit(solution)/shard_map/ppermute | solution.py:67
  265.6 39.2 %collective-permute-start.9 = (bf16[1024,128]{1,0:T(8,128)(2,1)}, bf16[1024,128]{1,0:T(8,128)(2,1)}, u32[]{:S(2)}, u32[]{:S(2)}) collective-permute-start(bf16[1024,128]{1,0:T(8,128)(2,1)} %get-tuple-element.108), channel_id=1, source_target_pairs={{0,1},{1,0},{2,3},{3,2},{4,5},{5,4},{6,7},{7,6},{8,9},{9,8},{10,11... | collective-permute-start | bytes 786440 | tf_op jit(solution)/shard_map/ppermute | solution.py:67
  271.5 106.6 %collective-permute-start.14 = (bf16[1024,128]{1,0:T(8,128)(2,1)}, bf16[1024,128]{1,0:T(8,128)(2,1)}, u32[]{:S(2)}, u32[]{:S(2)}) collective-permute-start(bf16[1024,128]{1,0:T(8,128)(2,1)} %get-tuple-element.128), channel_id=1, source_target_pairs={{0,1},{1,0},{2,3},{3,2},{4,5},{5,4},{6,7},{7,6},{8,9},{9,8},{10,11... | collective-permute-start | bytes 786440 | tf_op jit(solution)/shard_map/ppermute | solution.py:67
  291.3 56.0 %collective-permute-start.19 = (bf16[1024,2048]{1,0:T(8,128)(2,1)}, bf16[1024,2048]{1,0:T(8,128)(2,1)}, u32[]{:S(2)}, u32[]{:S(2)}) collective-permute-start(bf16[1024,2048]{1,0:T(8,128)(2,1)} %get-tuple-element.120.refs_5_), channel_id=1, source_target_pairs={{0,1},{1,0},{2,3},{3,2},{4,5},{5,4},{6,7},{7,6},{8,9},{9,8},{10,11... | collective-permute-start | bytes 12582920 | tf_op jit(solution)/shard_map/ppermute | solution.py:67
  298.7 79.5 %collective-permute-start.15 = (bf16[1024,128]{1,0:T(8,128)(2,1)}, bf16[1024,128]{1,0:T(8,128)(2,1)}, u32[]{:S(2)}, u32[]{:S(2)}) collective-permute-start(bf16[1024,128]{1,0:T(8,128)(2,1)} %get-tuple-element.129), channel_id=1, source_target_pairs={{0,2},{1,3},{2,0},{3,1},{4,6},{5,7},{6,4},{7,5},{8,10},{9,11},{10,... | collective-permute-start | bytes 786440 | tf_op jit(solution)/shard_map/ppermute | solution.py:67
  300.8 43.5 %collective-permute-start.17 = (bf16[2,2,1,128,1024]{4,3,2,1,0:T(8,128)(2,1)S(1)}, bf16[2,2,1,128,1024]{4,3,2,1,0:T(8,128)(2,1)}, u32[]{:S(2)}, u32[]{:S(2)}) collective-permute-start(bf16[2,2,1,128,1024]{4,3,2,1,0:T(8,128)(2,1)S(1)} %constant_dynamic-slice_fusion.12), channel_id=1, source_target_pairs={{0,4},{4,0},{8,12},{12,8},{16,20},{20,16},{24,28},{28,24},{1,5},{5... | collective-permute-start | bytes 3145736 | tf_op jit(solution)/shard_map/ppermute | solution.py:69
  304.8 56.0 %collective-permute-start.20 = (bf16[2,2,2,512,256]{4,3,2,1,0:T(8,128)(2,1)}, bf16[2,2,2,512,256]{4,3,2,1,0:T(8,128)(2,1)}, u32[]{:S(2)}, u32[]{:S(2)}) collective-permute-start(bf16[2,2,2,512,256]{4,3,2,1,0:T(8,128)(2,1)} %constant_dynamic-slice_fusion.10), channel_id=1, source_target_pairs={{0,2},{1,3},{2,0},{3,1},{4,6},{5,7},{6,4},{7,5},{8,10},{9,11},{10,... | collective-permute-start | bytes 6291464 | tf_op jit(solution)/shard_map/ppermute | solution.py:67
  305.4 39.2 %copy-start.14 = (bf16[1024,1024]{1,0:T(8,128)(2,1)S(1)}, bf16[1024,1024]{1,0:T(8,128)(2,1)}, u32[]{:S(2)}) copy-start(bf16[1024,1024]{1,0:T(8,128)(2,1)} %copy-done.13) | copy-start | bytes 6291460
  344.3 33.9 %collective-permute-start.16 = (bf16[1024,128]{1,0:T(8,128)(2,1)}, bf16[1024,128]{1,0:T(8,128)(2,1)}, u32[]{:S(2)}, u32[]{:S(2)}) collective-permute-start(bf16[1024,128]{1,0:T(8,128)(2,1)} %get-tuple-element.130), channel_id=1, source_target_pairs={{0,3},{1,2},{2,1},{3,0},{4,7},{5,6},{6,5},{7,4},{8,11},{9,10},{10,... | collective-permute-start | bytes 786440 | tf_op jit(solution)/shard_map/ppermute | solution.py:67
  347.3 28.7 %collective-permute-start.18 = (bf16[2,1,1,128,1024]{4,3,2,1,0:T(8,128)(2,1)}, bf16[2,1,1,128,1024]{4,3,2,1,0:T(8,128)(2,1)S(1)}, u32[]{:S(2)}, u32[]{:S(2)}) collective-permute-start(bf16[2,1,1,128,1024]{4,3,2,1,0:T(8,128)(2,1)} %constant_dynamic-slice_fusion.11), channel_id=1, source_target_pairs={{0,8},{4,12},{8,0},{12,4},{16,24},{20,28},{24,16},{28,20},{1,9},{5... | collective-permute-start | bytes 1572872 | tf_op jit(solution)/shard_map/ppermute | solution.py:69
  360.8 57.3 %collective-permute-start.26 = (bf16[2,1024,384]{2,1,0:T(8,128)(2,1)}, bf16[2,1024,384]{2,1,0:T(8,128)(2,1)}, u32[]{:S(2)}, u32[]{:S(2)}) collective-permute-start(bf16[2,1024,384]{2,1,0:T(8,128)(2,1)} %get-tuple-element.134.refs_1_), channel_id=1, source_target_pairs={{0,2},{1,3},{2,0},{3,1},{4,6},{5,7},{6,4},{7,5},{8,10},{9,11},{10,... | collective-permute-start | bytes 4718600 | tf_op jit(solution)/shard_map/ppermute | solution.py:67
  375.9 57.2 %collective-permute-start.21 = (bf16[2,2,1,128,2048]{4,3,2,1,0:T(8,128)(2,1)}, bf16[2,2,1,128,2048]{4,3,2,1,0:T(8,128)(2,1)}, u32[]{:S(2)}, u32[]{:S(2)}) collective-permute-start(bf16[2,2,1,128,2048]{4,3,2,1,0:T(8,128)(2,1)} %constant_dynamic-slice_fusion.9), channel_id=1, source_target_pairs={{0,4},{4,0},{8,12},{12,8},{16,20},{20,16},{24,28},{28,24},{1,5},{5... | collective-permute-start | bytes 6291464 | tf_op jit(solution)/shard_map/ppermute | solution.py:69
  378.2 52.3 %collective-permute-start.22 = (bf16[2,1,2,512,256]{4,3,2,1,0:T(8,128)(2,1)}, bf16[2,1,2,512,256]{4,3,2,1,0:T(8,128)(2,1)}, u32[]{:S(2)}, u32[]{:S(2)}) collective-permute-start(bf16[2,1,2,512,256]{4,3,2,1,0:T(8,128)(2,1)} %constant_dynamic-slice_fusion.8), channel_id=1, source_target_pairs={{0,8},{4,12},{8,0},{12,4},{16,24},{20,28},{24,16},{28,20},{1,9},{5... | collective-permute-start | bytes 3145736 | tf_op jit(solution)/shard_map/ppermute | solution.py:69
  378.2 43.9 %copy-start.20 = (bf16[2,1,1,128,1024]{4,3,2,1,0:T(8,128)(2,1)S(1)}, bf16[2,1,1,128,1024]{4,3,2,1,0:T(8,128)(2,1)}, u32[]{:S(2)}) copy-start(bf16[2,1,1,128,1024]{4,3,2,1,0:T(8,128)(2,1)} %add_convert_fusion.12.refs_4_) | copy-start | bytes 1572868
  417.4 59.3 %collective-permute-start.27 = (bf16[2,1024,384]{2,1,0:T(8,128)(2,1)}, bf16[2,1024,384]{2,1,0:T(8,128)(2,1)}, u32[]{:S(2)}, u32[]{:S(2)}) collective-permute-start(bf16[2,1024,384]{2,1,0:T(8,128)(2,1)} %get-tuple-element.143.refs_1_), channel_id=1, source_target_pairs={{0,2},{1,3},{2,0},{3,1},{4,6},{5,7},{6,4},{7,5},{8,10},{9,11},{10,... | collective-permute-start | bytes 4718600 | tf_op jit(solution)/shard_map/ppermute | solution.py:67
  420.2 10.3 %copy-start.6 = (bf16[2,2,2,512,256]{4,3,2,1,0:T(8,128)(2,1)S(1)}, bf16[2,2,2,512,256]{4,3,2,1,0:T(8,128)(2,1)}, u32[]{:S(2)}) copy-start(bf16[2,2,2,512,256]{4,3,2,1,0:T(8,128)(2,1)} %copy-done.5) | copy-start | bytes 6291460
  422.9 57.2 %collective-permute-start.34 = (bf16[1,1,1,128,1024]{4,3,2,1,0:T(8,128)(2,1)}, bf16[1,1,1,128,1024]{4,3,2,1,0:T(8,128)(2,1)}, u32[]{:S(2)}, u32[]{:S(2)}) collective-permute-start(bf16[1,1,1,128,1024]{4,3,2,1,0:T(8,128)(2,1)} %constant_dynamic-slice_fusion.3), channel_id=1, source_target_pairs={{0,16},{4,20},{8,24},{12,28},{16,0},{20,4},{24,8},{28,12},{1,17},{... | collective-permute-start | bytes 786440 | tf_op jit(solution)/shard_map/ppermute | solution.py:69
  433.1 51.6 %collective-permute-start.24 = (bf16[1,1,2,512,256]{4,3,2,1,0:T(8,128)(2,1)}, bf16[1,1,2,512,256]{4,3,2,1,0:T(8,128)(2,1)}, u32[]{:S(2)}, u32[]{:S(2)}) collective-permute-start(bf16[1,1,2,512,256]{4,3,2,1,0:T(8,128)(2,1)} %constant_dynamic-slice_fusion.6), channel_id=1, source_target_pairs={{0,16},{4,20},{8,24},{12,28},{16,0},{20,4},{24,8},{28,12},{1,17},{... | collective-permute-start | bytes 1572872 | tf_op jit(solution)/shard_map/ppermute | solution.py:69
  436.8 10.2 %copy-start.23 = (f32[1024,2]{1,0:T(8,128)S(1)}, f32[1024,2]{1,0:T(8,128)}, u32[]{:S(2)}) copy-start(f32[1024,2]{1,0:T(8,128)} %get-tuple-element.138) | copy-start | bytes 24580
  447.0 31.0 %copy-start.16 = (bf16[1,1024,384]{2,1,0:T(8,128)(2,1)S(1)}, bf16[1,1024,384]{2,1,0:T(8,128)(2,1)}, u32[]{:S(2)}) copy-start(bf16[1,1024,384]{2,1,0:T(8,128)(2,1)} %slice.197) | copy-start | bytes 2359300
  447.0 31.0 %copy-start.17 = (bf16[1,1024,384]{2,1,0:T(8,128)(2,1)S(1)}, bf16[1,1024,384]{2,1,0:T(8,128)(2,1)}, u32[]{:S(2)}) copy-start(bf16[1,1024,384]{2,1,0:T(8,128)(2,1)} %slice.196) | copy-start | bytes 2359300
  447.0 31.0 %copy-start.18 = (bf16[1,1024,384]{2,1,0:T(8,128)(2,1)S(1)}, bf16[1,1024,384]{2,1,0:T(8,128)(2,1)}, u32[]{:S(2)}) copy-start(bf16[1,1024,384]{2,1,0:T(8,128)(2,1)} %slice.198) | copy-start | bytes 2359300
  479.9 33.9 %collective-permute-start.28 = (bf16[4,1024,384]{2,1,0:T(8,128)(2,1)}, bf16[4,1024,384]{2,1,0:T(8,128)(2,1)}, u32[]{:S(2)}, u32[]{:S(2)}) collective-permute-start(bf16[4,1024,384]{2,1,0:T(8,128)(2,1)} %pad_maximum_fusion), channel_id=1, source_target_pairs={{0,1},{1,0},{2,3},{3,2},{4,5},{5,4},{6,7},{7,6},{8,9},{9,8},{10,11... | collective-permute-start | bytes 9437192 | tf_op jit(solution)/shard_map/ppermute | solution.py:67
  482.0 56.2 %collective-permute-start.35 = (bf16[1,1,1,128,1024]{4,3,2,1,0:T(8,128)(2,1)}, bf16[1,1,1,128,1024]{4,3,2,1,0:T(8,128)(2,1)}, u32[]{:S(2)}, u32[]{:S(2)}) collective-permute-start(bf16[1,1,1,128,1024]{4,3,2,1,0:T(8,128)(2,1)} %add_convert_fusion.16), channel_id=1, source_target_pairs={{0,2},{1,3},{2,0},{3,1},{4,6},{5,7},{6,4},{7,5},{8,10},{9,11},{10,... | collective-permute-start | bytes 786440 | tf_op jit(solution)/shard_map/ppermute | solution.py:67
  484.7 20.7 %collective-permute-start.25 = (bf16[2,2,1,128,768]{4,3,2,1,0:T(8,128)(2,1)}, bf16[2,2,1,128,768]{4,3,2,1,0:T(8,128)(2,1)}, u32[]{:S(2)}, u32[]{:S(2)}) collective-permute-start(bf16[2,2,1,128,768]{4,3,2,1,0:T(8,128)(2,1)} %fusion.1), channel_id=1, source_target_pairs={{0,4},{4,0},{8,12},{12,8},{16,20},{20,16},{24,28},{28,24},{1,5},{5... | collective-permute-start | bytes 2359304 | tf_op jit(solution)/shard_map/ppermute | solution.py:69
  485.8 26.3 %collective-permute-start.23 = (bf16[2,1,1,128,2048]{4,3,2,1,0:T(8,128)(2,1)}, bf16[2,1,1,128,2048]{4,3,2,1,0:T(8,128)(2,1)}, u32[]{:S(2)}, u32[]{:S(2)}) collective-permute-start(bf16[2,1,1,128,2048]{4,3,2,1,0:T(8,128)(2,1)} %constant_dynamic-slice_fusion.7), channel_id=1, source_target_pairs={{0,8},{4,12},{8,0},{12,4},{16,24},{20,28},{24,16},{28,20},{1,9},{5... | collective-permute-start | bytes 3145736 | tf_op jit(solution)/shard_map/ppermute | solution.py:69
  490.3 42.9 %collective-permute-start.40 = (bf16[1,1,1,512,256]{4,3,2,1,0:T(8,128)(2,1)}, bf16[1,1,1,512,256]{4,3,2,1,0:T(8,128)(2,1)}, u32[]{:S(2)}, u32[]{:S(2)}) collective-permute-start(bf16[1,1,1,512,256]{4,3,2,1,0:T(8,128)(2,1)} %constant_dynamic-slice_fusion.1), channel_id=1, source_target_pairs={{0,4},{4,0},{8,12},{12,8},{16,20},{20,16},{24,28},{28,24},{1,5},{5... | collective-permute-start | bytes 786440 | tf_op jit(solution)/shard_map/ppermute | solution.py:69
  507.6 33.4 %collective-permute-start.29 = (bf16[2,1,1,128,768]{4,3,2,1,0:T(8,128)(2,1)}, bf16[2,1,1,128,768]{4,3,2,1,0:T(8,128)(2,1)}, u32[]{:S(2)}, u32[]{:S(2)}) collective-permute-start(bf16[2,1,1,128,768]{4,3,2,1,0:T(8,128)(2,1)} %constant_dynamic-slice_fusion.5), channel_id=1, source_target_pairs={{0,8},{4,12},{8,0},{12,4},{16,24},{20,28},{24,16},{28,20},{1,9},{5... | collective-permute-start | bytes 1179656 | tf_op jit(solution)/shard_map/ppermute | solution.py:69
  513.8 24.5 %collective-permute-start.37 = (bf16[1,1,1,128,2048]{4,3,2,1,0:T(8,128)(2,1)S(1)}, bf16[1,1,1,128,2048]{4,3,2,1,0:T(8,128)(2,1)S(1)}, u32[]{:S(2)}, u32[]{:S(2)}) collective-permute-start(bf16[1,1,1,128,2048]{4,3,2,1,0:T(8,128)(2,1)S(1)} %constant_dynamic-slice_fusion.2), channel_id=1, source_target_pairs={{0,16},{4,20},{8,24},{12,28},{16,0},{20,4},{24,8},{28,12},{1,17},{... | collective-permute-start | bytes 1572872 | tf_op jit(solution)/shard_map/ppermute | solution.py:69
  517.7 15.4 %copy-start.22 = (bf16[1,1,2,512,256]{4,3,2,1,0:T(8,128)(2,1)S(1)}, bf16[1,1,2,512,256]{4,3,2,1,0:T(8,128)(2,1)}, u32[]{:S(2)}) copy-start(bf16[1,1,2,512,256]{4,3,2,1,0:T(8,128)(2,1)} %copy-done.21) | copy-start | bytes 1572868
  534.2 21.2 %collective-permute-start.41 = (bf16[512,256]{1,0:T(8,128)(2,1)S(1)}, bf16[512,256]{1,0:T(8,128)(2,1)S(1)}, u32[]{:S(2)}, u32[]{:S(2)}) collective-permute-start(bf16[512,256]{1,0:T(8,128)(2,1)S(1)} %get-tuple-element.235), channel_id=1, source_target_pairs={{0,1},{1,0},{2,3},{3,2},{4,5},{5,4},{6,7},{7,6},{8,9},{9,8},{10,11... | collective-permute-start | bytes 786440 | tf_op jit(solution)/shard_map/ppermute | solution.py:67
  534.3 21.8 %collective-permute-start.42 = (bf16[512,256]{1,0:T(8,128)(2,1)S(1)}, bf16[512,256]{1,0:T(8,128)(2,1)S(1)}, u32[]{:S(2)}, u32[]{:S(2)}) collective-permute-start(bf16[512,256]{1,0:T(8,128)(2,1)S(1)} %get-tuple-element.235), channel_id=1, source_target_pairs={{0,2},{1,3},{2,0},{3,1},{4,6},{5,7},{6,4},{7,5},{8,10},{9,11},{10,... | collective-permute-start | bytes 786440 | tf_op jit(solution)/shard_map/ppermute | solution.py:67
  538.2 19.0 %collective-permute-start.43 = (bf16[512,256]{1,0:T(8,128)(2,1)S(1)}, bf16[512,256]{1,0:T(8,128)(2,1)S(1)}, u32[]{:S(2)}, u32[]{:S(2)}) collective-permute-start(bf16[512,256]{1,0:T(8,128)(2,1)S(1)} %get-tuple-element.235), channel_id=1, source_target_pairs={{0,3},{1,2},{2,1},{3,0},{4,7},{5,6},{6,5},{7,4},{8,11},{9,10},{10,... | collective-permute-start | bytes 786440 | tf_op jit(solution)/shard_map/ppermute | solution.py:67
  539.3 14.6 %collective-permute-start.36 = (bf16[128,1024]{1,0:T(8,128)(2,1)S(1)}, bf16[128,1024]{1,0:T(8,128)(2,1)S(1)}, u32[]{:S(2)}, u32[]{:S(2)}) collective-permute-start(bf16[128,1024]{1,0:T(8,128)(2,1)S(1)} %get-tuple-element.244), channel_id=1, source_target_pairs={{0,1},{1,0},{2,3},{3,2},{4,5},{5,4},{6,7},{7,6},{8,9},{9,8},{10,11... | collective-permute-start | bytes 786440 | tf_op jit(solution)/shard_map/ppermute | solution.py:67
  542.1 10.4 %collective-permute-start.30 = (bf16[1,1,1,128,768]{4,3,2,1,0:T(8,128)(2,1)S(1)}, bf16[1,1,1,128,768]{4,3,2,1,0:T(8,128)(2,1)S(1)}, u32[]{:S(2)}, u32[]{:S(2)}) collective-permute-start(bf16[1,1,1,128,768]{4,3,2,1,0:T(8,128)(2,1)S(1)} %constant_dynamic-slice_fusion.4), channel_id=1, source_target_pairs={{0,16},{4,20},{8,24},{12,28},{16,0},{20,4},{24,8},{28,12},{1,17},{... | collective-permute-start | bytes 589832 | tf_op jit(solution)/shard_map/ppermute | solution.py:69
  552.5 21.9 %collective-permute-start.38 = (bf16[1,1,1,128,2048]{4,3,2,1,0:T(8,128)(2,1)S(1)}, bf16[1,1,1,128,2048]{4,3,2,1,0:T(8,128)(2,1)S(1)}, u32[]{:S(2)}, u32[]{:S(2)}) collective-permute-start(bf16[1,1,1,128,2048]{4,3,2,1,0:T(8,128)(2,1)S(1)} %add_convert_fusion.10), channel_id=1, source_target_pairs={{0,2},{1,3},{2,0},{3,1},{4,6},{5,7},{6,4},{7,5},{8,10},{9,11},{10,... | collective-permute-start | bytes 1572872 | tf_op jit(solution)/shard_map/ppermute | solution.py:67
  553.9 5.1 collective-permute-start.31
  555.4 16.1 %collective-permute-start.32 = (bf16[128,768]{1,0:T(8,128)(2,1)S(1)}, bf16[128,768]{1,0:T(8,128)(2,1)S(1)}, u32[]{:S(2)}, u32[]{:S(2)}) collective-permute-start(bf16[128,768]{1,0:T(8,128)(2,1)S(1)} %get-tuple-element.241), channel_id=1, source_target_pairs={{0,2},{1,3},{2,0},{3,1},{4,6},{5,7},{6,4},{7,5},{8,10},{9,11},{10,... | collective-permute-start | bytes 589832 | tf_op jit(solution)/shard_map/ppermute | solution.py:67
  556.1 17.8 %collective-permute-start.33 = (bf16[128,768]{1,0:T(8,128)(2,1)S(1)}, bf16[128,768]{1,0:T(8,128)(2,1)S(1)}, u32[]{:S(2)}, u32[]{:S(2)}) collective-permute-start(bf16[128,768]{1,0:T(8,128)(2,1)S(1)} %get-tuple-element.241), channel_id=1, source_target_pairs={{0,3},{1,2},{2,1},{3,0},{4,7},{5,6},{6,5},{7,4},{8,11},{9,10},{10,... | collective-permute-start | bytes 589832 | tf_op jit(solution)/shard_map/ppermute | solution.py:67
  574.6 2.4 collective-permute-start.39
  (23 other events, 96.1 us)

commit v4 on v3

--- a/solution.py
+++ b/solution.py
@@ -113,27 +113,55 @@
 
 
 def behind(value, after):
-    return lax.optimization_barrier((value, *after))[0] if after else value
-
-
-def reduce_stage(value, bits, img_count, after=()):
-    mine = {"row": lax.axis_index("row"), "img": lax.axis_index("img")}
-
-    def part(e):
-        piece = value
-        for j, (axis, bit) in enumerate(bits):
-            want = (mine[axis] // bit) % 2 ^ (e >> j & 1)
-            dim = value.ndim - 1 if axis == "row" else img_count - bit.bit_length()
-            length = piece.shape[dim] // 2
-            piece = lax.dynamic_slice_in_dim(piece, want * length, length, dim)
-        return piece
-
-    masks = masks_of(bits)
-    arrived = {
-        e: behind(jump(part(e), *masks[e]), after) for e in reversed(range(1, len(masks)))
-    }
-    arrived[0] = part(0)
-    return tree([arrived[e].astype(f32) for e in range(len(masks))]).astype(bf16)
+    return lax.optimization_barrier((value, tuple(after)))[0] if after else value
+
+
+class Halving:
+    def __init__(self, value, bits, img_count):
+        mine = {"row": lax.axis_index("row"), "img": lax.axis_index("img")}
+
+        def part(e):
+            piece = value
+            for j, (axis, bit) in enumerate(bits):
+                want = (mine[axis] // bit) % 2 ^ (e >> j & 1)
+                dim = value.ndim - 1 if axis == "row" else img_count - bit.bit_length()
+                length = piece.shape[dim] // 2
+                piece = lax.dynamic_slice_in_dim(piece, want * length, length, dim)
+            return piece
+
+        masks = masks_of(bits)
+        self.kept = part(0)
+        self.moved = [jump(part(e), *masks[e]) for e in range(1, len(masks))]
+
+    def finish(self):
+        values = [self.kept, *self.moved]
+        return tree([v.astype(f32) for v in values]).astype(bf16)
+
+
+class Exchange(Halving):
+    def __init__(self, value, bits):
+        self.kept = value
+        self.moved = [jump(value, *mask) for mask in masks_of(bits)[1:]]
+
+
+class Moved(Halving):
+    def __init__(self, values, masks):
+        self.moved = [jump(v, *mask) for v, mask in zip(values, masks)]
+
+    def finish(self):
+        return self.moved
+
+
+def arrive(flights, after=()):
+    return arrive_with(flights, tuple(after))[0]
+
+
+def arrive_with(flights, beside):
+    flat = [m for flight in flights for m in flight.moved]
+    flat, beside = lax.optimization_barrier((flat, beside))
+    for flight in flights:
+        flight.moved, flat = flat[: len(flight.moved)], flat[len(flight.moved) :]
+    return [flight.finish() for flight in flights], beside
 
 
 def spread_img(grad):
@@ -149,11 +177,6 @@
     return [
         lax.dynamic_index_in_dim(stack, order(c) ^ device, 0, False) for c in range(len(masks))
     ]
-
-
-def exchange_sum(value, bits, after=()):
-    values = [value] + [behind(jump(value, *mask), after) for mask in masks_of(bits)[1:]]
-    return tree([v.astype(f32) for v in values]).astype(bf16)
 
 
 def reversed_bits(index, size):
@@ -875,7 +898,7 @@
             jax.ShapeDtypeStruct((width, 2), f32),
         ],
         compiler_params=params(),
-        cost_estimate=pl.CostEstimate(flops=1 << 20, bytes_accessed=1 << 10, transcendentals=0),
+        cost_estimate=pl.CostEstimate(flops=1 << 34, bytes_accessed=1 << 10, transcendentals=0),
     )(me, unit, gain, shift, *parts, *operands, *after)
 
 
@@ -924,7 +947,7 @@
         ),
         out_shape=jax.ShapeDtypeStruct((1, local_rows, width), f32),
         compiler_params=params(),
-        cost_estimate=pl.CostEstimate(flops=1 << 20, bytes_accessed=1 << 10, transcendentals=0),
+        cost_estimate=pl.CostEstimate(flops=1 << 34, bytes_accessed=1 << 10, transcendentals=0),
     )(me, tok, ghid, w_qkv, gain, *same, *other)
 
 
@@ -1008,7 +1031,7 @@
         compiler_params=pltpu.CompilerParams(
             collective_id=0, has_side_effects=True, vmem_limit_bytes=32 << 20
         ),
-        cost_estimate=pl.CostEstimate(flops=1 << 20, bytes_accessed=1 << 10, transcendentals=0),
+        cost_estimate=pl.CostEstimate(flops=1 << 34, bytes_accessed=1 << 10, transcendentals=0),
     )(vec, slots)
 
 
@@ -1119,20 +1142,22 @@
 
     core, far_row = row_bits[:1], row_bits[1:]
     y_bits, z_bits = img_bits[:1], [[bit] for bit in img_bits[1:]]
-    stage = lambda value, bits, after=(): reduce_stage(value, bits, n_img, after)
-    stack_other = lambda groups: jump(jnp.stack([g[1] for g in groups]), 1)
-
-    def core_sum(keep, send, after):
-        arrived = behind(jump(send, 1), after)
-        return spread_img((keep.astype(f32) + arrived.astype(f32)).astype(bf16))
+    half = lambda value, bits: Halving(value, bits, n_img)
+
+    def core_flight(keep, send):
+        flight = Exchange(keep, [])
+        flight.moved = [jump(send, 1)]
+        return flight
 
     keep_small, send_small, grad_learn_out = small_grad_call(
         me, n3, glearn, ghid, inner, glogit, attended
     )
     keep_down, send_down = down_grad_call(me, gated, gres, [send_small])
-    small = core_sum(keep_small, send_small, [send_down])
-    keep_up, send_up = up_grad_call(me, n2, gup, [send_down, small])
-    down = core_sum(keep_down, send_down, [send_up])
+    keep_up, send_up = up_grad_call(me, n2, gup, [send_down])
+    small, down = arrive(
+        [core_flight(keep_small, send_small), core_flight(keep_down, send_down)], [send_up]
+    )
+    small, down = spread_img(small), spread_img(down)
 
     def back_call(s, after):
         *parts, sums = attend_back_call(
@@ -1144,32 +1169,40 @@
         turned = [norm_gain[0].reshape(-1, 1), norm_bias[0].reshape(-1, 1)]
         return qkv_grad_call(me, unit, parts, w_qkv, *turned, s, splits, after)
 
-    def far_sent(parts):
-        return [parts[0]] + [jump(parts[g], 2 * g) for g in range(1, len(parts))]
-
+    groups = row_count // 2
+    far_masks = [(2 * g, 0) for g in range(1, groups)]
     same, qkv_sums, norm_sums, grad_qkv = [], [], [], []
-    after = [down, send_up]
+    after, far = [small, down, send_up], None
     for s in range(splits):
         parts, sums = back_call(s, after)
-        here = far_sent(parts)
         qkv_sums.append(sums[0:2])
-        last = s == splits - 1
         if s == 0:
-            small = stage(small, y_bits, [sums])
-            ups = core_sum(keep_up, send_up, [sums])
-            down = stage(down, far_row, [sums])
-        if last:
-            ups = stage(ups, y_bits, [sums])
-            down = stage(down, z_bits[0], [sums])
-            small = stage(small, z_bits[1], [sums])
-            same = [behind(h, [sums]) for h in same]
+            small, down, ups = arrive(
+                [half(small, y_bits), half(down, z_bits[0]), core_flight(keep_up, send_up)], [sums]
+            )
+            ups = spread_img(ups)
+        if s == splits - 1:
+            flights = [half(ups, y_bits), half(down, z_bits[1]), half(small, z_bits[0])]
+            if far is not None:
+                flights.append(far)
+            ups, down, small, *arrived = arrive(flights, [sums])
+            for pieces_far in arrived:
+                same += pieces_far
+        same.append(parts[0])
+        far = Moved(parts[1:], far_masks)
         grad, norm_sum = grad_qkv_call(s, parts, [ups, down])
+        if s == splits - 1:
+            (ups, arrived, down, small), (grad, norm_sum) = arrive_with(
+                [half(ups, z_bits[0]), far, half(down, y_bits), half(small, z_bits[1])],
+                (grad, norm_sum),
+            )
+            same += arrived
         norm_sums.append(norm_sum)
         grad_qkv.append(spread_img(grad))
-        same += here
-        if s == 0:
-            small = stage(small, z_bits[0], [norm_sum])
-            after = [small, grad]
+        after = [grad]
+    grad_qkv = jnp.concatenate(grad_qkv, axis=-1)
+    near = Moved([jnp.stack([p[1] for p in same])], [(1, 0)])
+
     by_slot = jnp.dot(select.T, pooled.reshape(IMGS, LT * width), precision=highest)
     by_slot = by_slot.astype(bf16).reshape(row_count, -1, 128)
     late = lax.dynamic_update_slice(
@@ -1186,38 +1219,38 @@
         ]
     )
     vectors = jnp.pad(vectors, (0, -vectors.shape[0] % 1024)).reshape(-1, 128)
-    vectors, learned = vectors_call(vectors, by_slot)
-
-    here = [behind(h, [vectors]) for h in same[-row_count // 2 + 1 :]]
-    same = same[: len(same) - len(here)] + here
-    groups = row_count // 2
-    others = jnp.stack([p[1] for p in same])
-    others = jump(others, 1)
+    made = vectors_call(vectors, by_slot)
+
+    for bits in z_bits[2:]:
+        down, small = arrive([half(down, bits), half(small, bits)])
+    ((others,), grad_qkv, ups, down, small), (vectors, learned) = arrive_with(
+        [
+            near,
+            half(grad_qkv, y_bits),
+            half(ups, z_bits[1]),
+            half(down, far_row),
+            Exchange(small, far_row),
+        ],
+        tuple(made),
+    )
+    for bits in z_bits[2:]:
+        ups, grad_qkv = arrive([half(ups, bits), half(grad_qkv, bits)])
     other = [others[s * groups : (s + 1) * groups] for s in range(splits)]
-    ups = stage(ups, z_bits[0], [vectors])
-    down = stage(down, z_bits[1], [vectors])
-    grad_qkv = stage(jnp.concatenate(grad_qkv, axis=-1), y_bits, [vectors])
-    for bits in z_bits[2:]:
-        down = stage(down, bits)
-        small = stage(small, bits)
     grad_tokens = tokens_call(
         me,
         tokens[0],
-        behind(grad_hidden, [ups, down, grad_qkv]),
+        behind(grad_hidden, [ups, grad_qkv, down, small]),
         w_qkv,
         norm_gain[0:1],
         same,
         other,
         row_count,
     )
-    small = exchange_sum(small, far_row, [grad_tokens])
-    grad_qkv = stage(grad_qkv, z_bits[0], [grad_tokens])
-    for bits in z_bits[1:]:
-        ups = stage(ups, bits, [grad_tokens])
-    down = stage(down, y_bits, [grad_tokens])
-    ups = exchange_sum(ups, far_row)
-    for bits in z_bits[1:]:
-        grad_qkv = stage(grad_qkv, bits)
+    (grad_qkv, ups), grad_tokens = arrive_with(
+        [half(grad_qkv, z_bits[0]), Exchange(ups, far_row)], grad_tokens
+    )
+    (grad_qkv,) = arrive([half(grad_qkv, z_bits[1])])
+    vectors, learned = behind((vectors, learned), [grad_tokens])
     vectors = vectors.reshape(-1)
     scale_here = jnp.dot(scale, select, precision=highest)[:slots_here]
     learned = learned.reshape(slots_here, LT * width) * scale_here[:, None]

time: 585 us -> 567 us (0.969)
  Pallas kernels: 334 us -> 351 us
  starting transfers between devices: 43.2 us -> 27.7 us
  other arithmetic: 50.3 us -> 40.3 us
  waiting for transfers between devices: 102 us -> 94.9 us
    ppermute x12, starting transfers between devices: 21.3 us -> 7.76 us  [jump(): return lax.ppermute(value, 'img', [(i, i ^ img_mask) for i in range(imgs)])]
    ppermute x12, waiting for transfers between devices: 25.1 us -> 13 us  [jump(): return lax.ppermute(value, 'img', [(i, i ^ img_mask) for i in range(imgs)])]
    pallas_call x2, Pallas kernels: 76.5 us -> 85.2 us  [attend_back_call(): pl.pallas_call(functools.partial(attend_back_kernel, count, heads, split...]
    convert_element_type x14 -> x16, other arithmetic: 29.6 us -> 23.8 us  [finish(): return tree([v.astype(f32) for v in values]).astype(bf16)]
    pallas_call x1, Pallas kernels: 41.5 us -> 47.3 us  [attend_call(): pl.pallas_call(functools.partial(attend_kernel, count, heads), grid_spec=...]
  transfers between devices with their start and end apart: 44 -> 44, of which waited for: 12 -> 11; matrix products, arithmetic and copies ran while one was open for 15% -> 13% of each run, Pallas kernels for 38% -> 42%
where the time goes in v4:
time: 567 us; the launch traced here: 559 us
  Pallas kernels  351 us (62%)
  waiting for transfers between devices  94.9 us (17%)
  local copies, waits for them, and re-layouts  42.1 us (7%)
  other arithmetic  40.3 us (7%)
  starting transfers between devices  27.7 us (5%)
    pallas_call x1, Pallas kernels, rows_call(): pl.pallas_call(functools.partial(rows_kernel, count, splits, local_rows),...  89.1 us
    pallas_call x2, Pallas kernels, attend_back_call(): pl.pallas_call(functools.partial(attend_back_kernel, count, heads, split...  85.2 us
    ppermute x32, waiting for transfers between devices, jump(): return lax.ppermute(value, 'row', [(i, i ^ row_mask) for i in range(rows)])  81.9 us
    pallas_call x1, Pallas kernels, attend_call(): pl.pallas_call(functools.partial(attend_kernel, count, heads), grid_spec=...  47.3 us
    pallas_call x1, Pallas kernels, vectors_call(): pl.pallas_call(functools.partial(vectors_kernel, count, row_bits, img_bit...  30.6 us
    convert_element_type x16, other arithmetic, finish(): return tree([v.astype(f32) for v in values]).astype(bf16)  23.8 us
    pallas_call x1, Pallas kernels, qkv_call(): pl.pallas_call(functools.partial(qkv_kernel, count, splits, local_rows, f...  22.7 us
    pallas_call x2, Pallas kernels, qkv_grad_call(): pl.pallas_call(functools.partial(qkv_grad_kernel, count // 2, len(after))...  20.1 us
  transfers between devices with their start and end apart: 44, of which 11 were waited for; matrix products, arithmetic and copies ran while one was open for 13% of the time, Pallas kernels for 42%

profile of v4, /device:TPU:0, one launch (start us, length us, event | category | flops | bytes accessed | tf_op | source)
XLA Modules:
  0.0 558.9 jit_solution(17105052274225236591)
XLA Ops:
  0.7 3.0 collective-permute-start.4
  7.6 1.7 constant_dynamic-slice_fusion.17
  9.3 1.5 pad_maximum_fusion.1.refs_2_
  10.8 39.1 %collective-permute-done.1 = bf16[2,8192]{1,0:T(2,128)(2,1)S(1)} collective-permute-done((bf16[2,8192]{1,0:T(2,128)(2,1)S(1)}, bf16[2,8192]{1,0:T(2,128)(2,1)S(1)}, u32[]{:S(2)}, u32[]{:S(2)}) %collective-permute-start.1) | collective-permute-done | bytes 32800 | tf_op jit(solution)/shard_map/ppermute | solution.py:67
  49.9 1.3 constant_dynamic-slice_fusion.13.refs_10_
  52.7 2.0 copy.67.refs_4_.refs_14_.refs_12_
  55.3 1.2 collective-permute-done.5.refs_3_
  56.6 22.7 %shard_map.297 = (bf16[4,1024,1024]{2,1,0:T(8,128)(2,1)}, bf16[4096,256]{1,0:T(8,128)(2,1)}, bf16[4096,256]{1,0:T(8,128)(2,1)}, bf16[4096,256]{1,0:T(8,128)(2,1)...) custom-call(s32[1]{0:T(128)} %bitcast.21.me_ref, bf16[1016,1024]{1,0:T(8,128)(2,1)} %bitcast.192, ...), custom_call_target="tpu_custom_call" | custom-call | flops 19327352832 | bytes 27262976 | tf_op jit(solution)/shard_map/pallas_call | solution.py:268
  79.3 47.3 %shard_map.298 = (bf16[1024,256]{1,0:T(8,128)(2,1)}, bf16[1024,256]{1,0:T(8,128)(2,1)}, bf16[1024,256]{1,0:T(8,128)(2,1)}, bf16[1024,256]{1,0:T(8,128)(2,1)}, f3...) custom-call(s32[16]{0:T(128)} %get-tuple-element.233.lo_ref, s32[16]{0:T(128)} %get-tuple-element.232.hi_ref, ...), custom_call_target="tpu_custom_call" | custom-call | flops 42949672960 | bytes 16777216 | tf_op jit(solution)/shard_map/pallas_call | solution.py:371
  127.1 1.8 collective-permute-start.7
  128.9 1.0 copy.68.refs_1_
  133.0 9.0 %collective-permute-done.7.refs_13_.refs_7_ = bf16[1024,256]{1,0:T(8,128)(2,1)S(1)} collective-permute-done((bf16[1024,256]{1,0:T(8,128)(2,1)}, bf16[1024,256]{1,0:T(8,128)(2,1)S(1)}, u32[]{:S(2)}, u32[]{:S(2)}) %collective-permute-start.7) | collective-permute-done | bytes 524320 | tf_op jit(solution)/shard_map/ppermute | solution.py:67
  142.1 9.8 %collective-permute-done.8.refs_14_.refs_8_ = bf16[1024,256]{1,0:T(8,128)(2,1)S(1)} collective-permute-done((bf16[1024,256]{1,0:T(8,128)(2,1)}, bf16[1024,256]{1,0:T(8,128)(2,1)S(1)}, u32[]{:S(2)}, u32[]{:S(2)}) %collective-permute-start.8) | collective-permute-done | bytes 524320 | tf_op jit(solution)/shard_map/ppermute | solution.py:67
  152.7 89.1 %shard_map.299 = (bf16[1024,1024]{1,0:T(8,128)(2,1)}, bf16[1024,4096]{1,0:T(8,128)(2,1)}, bf16[1024,4096]{1,0:T(8,128)(2,1)}, bf16[1024,1024]{1,0:T(8,128)(2,1)}...) custom-call(bf16[1016,1024]{1,0:T(8,128)(2,1)} %bitcast.193, ...), custom_call_target="tpu_custom_call" | custom-call | flops 42949672960 | bytes 58720256 | tf_op jit(solution)/shard_map/pallas_call | solution.py:692
  241.8 11.5 %shard_map.300 = (bf16[1024,1024]{1,0:T(8,128)(2,1)}, bf16[1024,1024]{1,0:T(8,128)(2,1)}, f32[1024,64]{1,0:T(8,128)}) custom-call(s32[1]{0:T(128)} %bitcast.21.me_ref, bf16[1024,1024]{1,0:T(8,128)(2,1)} %get-tuple-element.111.refs_0_, bf16[1024,1024]{1,0:T(8,128)(2,1)} %get-tuple-element.112.refs_1_, bf16[1024,1024]{1,0:T(8,128)(2,1)} %get-tuple-element.113.refs_2_, ...), custom_call_target="tpu_custom_call" | custom-call | flops 6442450944 | bytes 20971520 | tf_op jit(solution)/shard_map/pallas_call | solution.py:833
  253.4 13.9 %shard_map.301 = (bf16[4096,512]{1,0:T(8,128)(2,1)}, bf16[4096,512]{1,0:T(8,128)(2,1)}) custom-call(s32[1]{0:T(128)} %bitcast.21.me_ref, bf16[1024,4096]{1,0:T(8,128)(2,1)} %get-tuple-element.118.left_ref, bf16[1024,1024]{1,0:T(8,128)(2,1)} %get-tuple-element.119.right_ref, bf16[1024,1024]{1,0:T(8,128)(2,1)} %get-tuple-element.117.refs_0_), custom_call_target="tpu_custom_call" | custom-call | flops 12884901888 | bytes 16777216 | tf_op jit(solution)/shard_map/pallas_call | solution.py:738
  267.5 1.0 copy.71.gain_ref
  268.5 1.0 copy.72.shift_ref
  270.5 1.7 collective-permute-start.10
  275.7 14.7 %shard_map.302 = (bf16[1024,2048]{1,0:T(8,128)(2,1)}, bf16[1024,2048]{1,0:T(8,128)(2,1)}) custom-call(s32[1]{0:T(128)} %bitcast.21.me_ref, bf16[1024,1024]{1,0:T(8,128)(2,1)} %get-tuple-element.121.left_ref, bf16[1024,4096]{1,0:T(8,128)(2,1)} %get-tuple-element.122.right_ref, bf16[4096,512]{1,0:T(8,128)(2,1)} %get-tuple-element.120.refs_0_), custom_call_target="tpu_custom_call" | custom-call | flops 12884901888 | bytes 16777216 | tf_op jit(solution)/shard_map/pallas_call | solution.py:780
  290.9 4.8 add_convert_fusion.1
  297.6 1.4 constant_dynamic-slice_fusion.11
  299.1 1.7 collective-permute-start.22
  300.8 42.7 %shard_map.303 = (bf16[2,1024,384]{2,1,0:T(8,128)(2,1)}, bf16[2,1024,384]{2,1,0:T(8,128)(2,1)}, f32[8,128]{1,0:T(8,128)}) custom-call(s32[16]{0:T(128)} %get-tuple-element.233.lo_ref, s32[16]{0:T(128)} %get-tuple-element.232.hi_ref, bf16[1024,128]{1,0:T(8,128)(2,1)} %get-tuple-element.107.refs_0_, bf16[1024,128]{1,0:T(8,128)(2,1)} %collective-permute-done.9.refs_1_, ...), custom_call_target="tpu_custom_call" | custom-call | flops 34359738368 | bytes 12582912 | tf_op jit(solution)/shard_map/pallas_call | solution.py:499
  344.2 2.1 slice.193
  346.3 1.4 collective-permute-start.20
  348.4 1.6 add_convert_fusion.7
  351.1 2.3 add_convert_fusion.3.refs_6_
  353.7 6.6 %add_convert_fusion = bf16[1024,2048]{1,0:T(8,128)(2,1)} fusion(bf16[1024,2048]{1,0:T(8,128)(2,1)} %collective-permute-done.16, bf16[1024,2048]{1,0:T(8,128)(2,1)S(1)} %copy-done.10), kind=kLoop, calls=%fused_computation.3 | loop fusion | flops 8388608 | bytes 12582912 | tf_op jit(solution)/shard_map/convert_element_type | solution.py:138
  360.3 1.1 constant_dynamic-slice_fusion.9
  361.3 10.0 %shard_map.304 = (bf16[1024,384]{1,0:T(8,128)(2,1)}, f32[1024,2]{1,0:T(8,128)}) custom-call(s32[1]{0:T(128)} %bitcast.21.me_ref, bf16[4,1024,1024]{2,1,0:T(8,128)(2,1)} %get-tuple-element.142.n_ref, f32[1024,1]{1,0:T(8,128)} %copy.71.gain_ref, f32[1024,1]{1,0:T(8,128)} %copy.72.shift_ref, bf16[2,1024,384]{2,1,0:T(8,128)(2,1)} %get-tuple-element.131.refs_0_, ...), custom_call_target="tpu_custom_call" | custom-call | flops 17179869184 | bytes 1024 | tf_op jit(solution)/shard_map/pallas_call | solution.py:881
  371.4 3.2 constant_dynamic-slice_fusion.10
  374.6 2.4 collective-permute-start.18
  377.0 1.5 collective-permute-start.17
  378.5 42.6 %shard_map.305 = (bf16[2,1024,384]{2,1,0:T(8,128)(2,1)}, bf16[2,1024,384]{2,1,0:T(8,128)(2,1)}, f32[8,128]{1,0:T(8,128)}) custom-call(s32[16]{0:T(128)} %get-tuple-element.233.lo_ref, s32[16]{0:T(128)} %get-tuple-element.232.hi_ref, bf16[1024,128]{1,0:T(8,128)(2,1)} %get-tuple-element.138.refs_0_, bf16[1024,128]{1,0:T(8,128)(2,1)} %collective-permute-done.21.refs_1_, ...), custom_call_target="tpu_custom_call" | custom-call | flops 34359738368 | bytes 12582912 | tf_op jit(solution)/shard_map/pallas_call | solution.py:499
  422.4 2.2 slice.195
  425.3 2.4 add_convert_fusion.2.refs_5_
  428.0 2.0 copy-done.5
  430.0 1.5 add_convert_fusion.6.refs_6_
  432.9 10.0 %shard_map.306 = (bf16[1024,384]{1,0:T(8,128)(2,1)}, f32[1024,2]{1,0:T(8,128)}) custom-call(s32[1]{0:T(128)} %bitcast.21.me_ref, bf16[4,1024,1024]{2,1,0:T(8,128)(2,1)} %get-tuple-element.142.n_ref, f32[1024,1]{1,0:T(8,128)} %copy.71.gain_ref, f32[1024,1]{1,0:T(8,128)} %copy.72.shift_ref, bf16[2,1024,384]{2,1,0:T(8,128)(2,1)} %get-tuple-element.146.refs_0_.refs_2_, ...), custom_call_target="tpu_custom_call" | custom-call | flops 17179869184 | bytes 1024 | tf_op jit(solution)/shard_map/pallas_call | solution.py:881
  442.9 1.2 slice.194
  444.1 12.2 %collective-permute-done.25.refs_3_ = bf16[2,1024,384]{2,1,0:T(8,128)(2,1)} collective-permute-done((bf16[2,1024,384]{2,1,0:T(8,128)(2,1)}, bf16[2,1024,384]{2,1,0:T(8,128)(2,1)}, u32[]{:S(2)}, u32[]{:S(2)}) %collective-permute-start.25) | collective-permute-done | bytes 1572896 | tf_op jit(solution)/shard_map/ppermute | solution.py:67
  456.3 5.4 collective-permute-done.24
  461.7 1.2 add_bitcast_fusion
  463.1 1.0 add_convert_fusion.16
  464.1 1.4 collective-permute-start.32
  465.6 1.2 slice.196
  469.1 1.6 add_convert_fusion.5
  471.0 1.4 collective-permute-start.29
  472.4 30.6 %shard_map.307 = (f32[200,128]{1,0:T(8,128)S(1)}, f32[128,128]{1,0:T(8,128)S(1)}) custom-call(f32[200,128]{1,0:T(8,128)S(1)} %pad_bitcast_fusion.vec_ref, bf16[4,128,128]{2,1,0:T(8,128)(2,1)S(1)} %reshape.482.slot_ref), custom_call_target="tpu_custom_call" | custom-call | flops 17179869184 | bytes 1024 | tf_op jit(solution)/shard_map/pallas_call | solution.py:1015
  504.1 1.1 collective-permute-start.43
  506.4 2.0 fusion.29
  508.7 15.4 %shard_map.308 = f32[1,1016,1024]{2,1,0:T(8,128)} custom-call(s32[1]{0:T(128)} %bitcast.21.me_ref, bf16[1016,1024]{1,0:T(8,128)(2,1)} %bitcast.194, f32[1024,1024]{1,0:T(8,128)} %get-tuple-element.174.ghid_ref, bf16[1024,3072]{1,0:T(8,128)(2,1)} %w_ref.1, f32[1,1024]{1,0:T(1,128)} %get-tuple-element.281.refs_11_.gain_ref, ...), custom_call_target="tpu_custom_call" | custom-call | flops 17179869184 | bytes 1024 | tf_op jit(solution)/shard_map/pallas_call | solution.py:932
  524.2 1.1 pad_maximum_fusion.2
  525.4 1.6 maximum_convert_fusion.1
  526.9 1.9 collective-permute-done.34
  530.0 1.1 fusion.30
  531.2 1.2 collective-permute-start.35
  536.6 7.0 %collective-permute-done.35 = bf16[1,1,1,128,768]{4,3,2,1,0:T(8,128)(2,1)S(1)} collective-permute-done((bf16[1,1,1,128,768]{4,3,2,1,0:T(8,128)(2,1)S(1)}, bf16[1,1,1,128,768]{4,3,2,1,0:T(8,128)(2,1)S(1)}, u32[]{:S(2)}, u32[]{:S(2)}) %collective-permute-start.35) | collective-permute-done | bytes 196640 | tf_op jit(solution)/shard_map/ppermute | solution.py:69
  544.5 1.0 collective-permute-start.38
  546.1 5.3 collective-permute-done.37
  551.4 3.3 collective-permute-done.38
  555.4 1.3 convert_element_type.281
  557.1 1.5 maximum_convert_fusion
  (271 shorter events, 37.0 us)
Async XLA Ops:
  0.6 54.7 %copy-start = (bf16[1024,8]{0,1:T(8,128)(2,1)S(1)}, bf16[1024,8]{0,1:T(8,128)(2,1)}, u32[]{:S(2)}) copy-start(bf16[1024,8]{0,1:T(8,128)(2,1)} %param.33) | copy-start | bytes 49156
  0.7 51.4 %collective-permute-start.4 = (bf16[1016,1024]{1,0:T(8,128)(2,1)}, bf16[1016,1024]{1,0:T(8,128)(2,1)S(1)}, u32[]{:S(2)}, u32[]{:S(2)}) collective-permute-start(bf16[1016,1024]{1,0:T(8,128)(2,1)} %bitcast.190), channel_id=1, source_target_pairs={{0,2},{1,3},{2,0},{3,1},{4,6},{5,7},{6,4},{7,5},{8,10},{9,11},{10,... | collective-permute-start | bytes 6242312 | tf_op jit(solution)/shard_map/ppermute | solution.py:67
  3.7 51.6 %collective-permute-start.3 = (bf16[1016,1024]{1,0:T(8,128)(2,1)}, bf16[1016,1024]{1,0:T(8,128)(2,1)}, u32[]{:S(2)}, u32[]{:S(2)}) collective-permute-start(bf16[1016,1024]{1,0:T(8,128)(2,1)} %bitcast.191), channel_id=1, source_target_pairs={{0,1},{1,0},{2,3},{3,2},{4,5},{5,4},{6,7},{7,6},{8,9},{9,8},{10,11... | collective-permute-start | bytes 6242312 | tf_op jit(solution)/shard_map/ppermute | solution.py:67
  4.6 45.3 %collective-permute-start.1 = (bf16[2,8192]{1,0:T(2,128)(2,1)S(1)}, bf16[2,8192]{1,0:T(2,128)(2,1)S(1)}, u32[]{:S(2)}, u32[]{:S(2)}) collective-permute-start(bf16[2,8192]{1,0:T(2,128)(2,1)S(1)} %bitcast.167), channel_id=1, source_target_pairs={{0,2},{1,3},{2,0},{3,1},{4,6},{5,7},{6,4},{7,5},{8,10},{9,11},{10,... | collective-permute-start | bytes 98312 | tf_op jit(solution)/shard_map/ppermute | solution.py:67
  10.8 43.9 %copy-start.27 = (f32[3,1024]{1,0:T(4,128)S(1)}, f32[3,1024]{1,0:T(4,128)}, u32[]{:S(2)}) copy-start(f32[3,1024]{1,0:T(4,128)} %param.30) | copy-start | bytes 36868
  10.8 43.9 %copy-start.28 = (f32[3,1024]{1,0:T(4,128)S(1)}, f32[3,1024]{1,0:T(4,128)}, u32[]{:S(2)}) copy-start(f32[3,1024]{1,0:T(4,128)} %param.29) | copy-start | bytes 36868
  49.9 2.2 collective-permute-start.2
  52.1 4.5 collective-permute-start.5
  52.6 79.4 %collective-permute-start = (bf16[2,8192]{1,0:T(2,128)(2,1)S(1)}, bf16[2,8192]{1,0:T(2,128)(2,1)S(1)}, u32[]{:S(2)}, u32[]{:S(2)}) collective-permute-start(bf16[2,8192]{1,0:T(2,128)(2,1)S(1)} %bitcast.168), channel_id=1, source_target_pairs={{0,1},{1,0},{2,3},{3,2},{4,5},{5,4},{6,7},{7,6},{8,9},{9,8},{10,11... | collective-permute-start | bytes 98312 | tf_op jit(solution)/shard_map/ppermute | solution.py:67
  79.2 49.6 %copy-start.35 = (s32[1,8]{1,0:T(1,128)S(1)}, s32[1,8]{1,0:T(1,128)}, u32[]{:S(2)}) copy-start(s32[1,8]{1,0:T(1,128)} %param.19) | copy-start | bytes 100
  79.2 49.6 %copy-start.40 = (s32[1,8]{1,0:T(1,128)S(1)}, s32[1,8]{1,0:T(1,128)}, u32[]{:S(2)}) copy-start(s32[1,8]{1,0:T(1,128)} %param.20) | copy-start | bytes 100
  79.3 51.5 %copy-start.33 = (f32[8]{0:T(128)S(1)}, f32[8]{0:T(128)}, u32[]{:S(2)}) copy-start(f32[8]{0:T(128)} %param.34) | copy-start | bytes 100
  79.3 52.1 %copy-start.29 = (f32[1024]{0:T(1024)S(1)}, f32[1024]{0:T(1024)}, u32[]{:S(2)}) copy-start(f32[1024]{0:T(1024)} %param.24) | copy-start | bytes 12292
  79.3 52.1 %copy-start.30 = (f32[1024]{0:T(1024)S(1)}, f32[1024]{0:T(1024)}, u32[]{:S(2)}) copy-start(f32[1024]{0:T(1024)} %param.28) | copy-start | bytes 12292
  79.3 52.1 %copy-start.31 = (f32[1024]{0:T(1024)S(1)}, f32[1024]{0:T(1024)}, u32[]{:S(2)}) copy-start(f32[1024]{0:T(1024)} %param.32) | copy-start | bytes 12292
  126.6 6.4 %collective-permute-start.6 = (bf16[1024,256]{1,0:T(8,128)(2,1)}, bf16[1024,256]{1,0:T(8,128)(2,1)S(1)}, u32[]{:S(2)}, u32[]{:S(2)}) collective-permute-start(bf16[1024,256]{1,0:T(8,128)(2,1)} %get-tuple-element.104), channel_id=1, source_target_pairs={{0,1},{1,0},{2,3},{3,2},{4,5},{5,4},{6,7},{7,6},{8,9},{9,8},{10,11... | collective-permute-start | bytes 1572872 | tf_op jit(solution)/shard_map/ppermute | solution.py:67
  127.1 15.0 %collective-permute-start.7 = (bf16[1024,256]{1,0:T(8,128)(2,1)}, bf16[1024,256]{1,0:T(8,128)(2,1)S(1)}, u32[]{:S(2)}, u32[]{:S(2)}) collective-permute-start(bf16[1024,256]{1,0:T(8,128)(2,1)} %get-tuple-element.105), channel_id=1, source_target_pairs={{0,2},{1,3},{2,0},{3,1},{4,6},{5,7},{6,4},{7,5},{8,10},{9,11},{10,... | collective-permute-start | bytes 1572872 | tf_op jit(solution)/shard_map/ppermute | solution.py:67
  128.8 23.0 %collective-permute-start.8 = (bf16[1024,256]{1,0:T(8,128)(2,1)}, bf16[1024,256]{1,0:T(8,128)(2,1)S(1)}, u32[]{:S(2)}, u32[]{:S(2)}) collective-permute-start(bf16[1024,256]{1,0:T(8,128)(2,1)} %get-tuple-element.106), channel_id=1, source_target_pairs={{0,3},{1,2},{2,1},{3,0},{4,7},{5,6},{6,5},{7,4},{8,11},{9,10},{10,... | collective-permute-start | bytes 1572872 | tf_op jit(solution)/shard_map/ppermute | solution.py:67
  133.0 18.8 %copy-start.37 = (bf16[1024,256]{1,0:T(8,128)(2,1)}, bf16[1024,256]{1,0:T(8,128)(2,1)S(1)}, u32[]{:S(2)}) copy-start(bf16[1024,256]{1,0:T(8,128)(2,1)S(1)} %collective-permute-done.6.refs_12_.refs_6_) | copy-start | bytes 1572868
  142.1 9.8 %copy-start.38 = (bf16[1024,256]{1,0:T(8,128)(2,1)}, bf16[1024,256]{1,0:T(8,128)(2,1)S(1)}, u32[]{:S(2)}) copy-start(bf16[1024,256]{1,0:T(8,128)(2,1)S(1)} %collective-permute-done.7.refs_13_.refs_7_) | copy-start | bytes 1572868
  253.4 19.3 %copy-start.19 = (f32[1024,64]{1,0:T(8,128)S(1)}, f32[1024,64]{1,0:T(8,128)}, u32[]{:S(2)}) copy-start(f32[1024,64]{1,0:T(8,128)} %get-tuple-element.160) | copy-start | bytes 786436
  267.2 6.6 %copy-start.41 = (f32[1,64]{1,0:T(1,128)S(1)}, f32[1,64]{1,0:T(1,128)}, u32[]{:S(2)}) copy-start(f32[1,64]{1,0:T(1,128)} %get-tuple-element.163) | copy-start | bytes 772
  267.2 7.9 %copy-start.22 = (f32[64,1024]{1,0:T(8,128)S(1)}, f32[64,1024]{1,0:T(8,128)}, u32[]{:S(2)}) copy-start(f32[64,1024]{1,0:T(8,128)} %get-tuple-element.164) | copy-start | bytes 786436
  267.2 23.2 %collective-permute-start.13 = (bf16[4096,512]{1,0:T(8,128)(2,1)}, bf16[4096,512]{1,0:T(8,128)(2,1)}, u32[]{:S(2)}, u32[]{:S(2)}) collective-permute-start(bf16[4096,512]{1,0:T(8,128)(2,1)} %get-tuple-element.120.refs_0_), channel_id=1, source_target_pairs={{0,1},{1,0},{2,3},{3,2},{4,5},{5,4},{6,7},{7,6},{8,9},{9,8},{10,11... | collective-permute-start | bytes 12582920 | tf_op jit(solution)/shard_map/ppermute | solution.py:67
  268.5 7.1 %copy-start.26 = (f32[1,4096]{1,0:T(1,128)S(1)}, f32[1,4096]{1,0:T(1,128)}, u32[]{:S(2)}) copy-start(f32[1,4096]{1,0:T(1,128)} %get-tuple-element.158) | copy-start | bytes 49156
  268.5 7.1 %copy-start.25 = (f32[8,1024]{1,0:T(8,128)S(1)}, f32[8,1024]{1,0:T(8,128)}, u32[]{:S(2)}) copy-start(f32[8,1024]{1,0:T(8,128)} %get-tuple-element.159) | copy-start | bytes 98308
  269.5 20.8 %collective-permute-start.12 = (bf16[1024,1024]{1,0:T(8,128)(2,1)}, bf16[1024,1024]{1,0:T(8,128)(2,1)S(1)}, u32[]{:S(2)}, u32[]{:S(2)}) collective-permute-start(bf16[1024,1024]{1,0:T(8,128)(2,1)} %get-tuple-element.117.refs_0_), channel_id=1, source_target_pairs={{0,1},{1,0},{2,3},{3,2},{4,5},{5,4},{6,7},{7,6},{8,9},{9,8},{10,11... | collective-permute-start | bytes 6291464 | tf_op jit(solution)/shard_map/ppermute | solution.py:67
  270.5 28.6 %collective-permute-start.10 = (bf16[1024,128]{1,0:T(8,128)(2,1)}, bf16[1024,128]{1,0:T(8,128)(2,1)}, u32[]{:S(2)}, u32[]{:S(2)}) collective-permute-start(bf16[1024,128]{1,0:T(8,128)(2,1)} %get-tuple-element.109), channel_id=1, source_target_pairs={{0,2},{1,3},{2,0},{3,1},{4,6},{5,7},{6,4},{7,5},{8,10},{9,11},{10,... | collective-permute-start | bytes 786440 | tf_op jit(solution)/shard_map/ppermute | solution.py:67
  272.1 28.6 %collective-permute-start.11 = (bf16[1024,128]{1,0:T(8,128)(2,1)}, bf16[1024,128]{1,0:T(8,128)(2,1)}, u32[]{:S(2)}, u32[]{:S(2)}) collective-permute-start(bf16[1024,128]{1,0:T(8,128)(2,1)} %get-tuple-element.110), channel_id=1, source_target_pairs={{0,3},{1,2},{2,1},{3,0},{4,7},{5,6},{6,5},{7,4},{8,11},{9,10},{10,... | collective-permute-start | bytes 786440 | tf_op jit(solution)/shard_map/ppermute | solution.py:67
  272.1 28.6 %collective-permute-start.9 = (bf16[1024,128]{1,0:T(8,128)(2,1)}, bf16[1024,128]{1,0:T(8,128)(2,1)}, u32[]{:S(2)}, u32[]{:S(2)}) collective-permute-start(bf16[1024,128]{1,0:T(8,128)(2,1)} %get-tuple-element.108), channel_id=1, source_target_pairs={{0,1},{1,0},{2,3},{3,2},{4,5},{5,4},{6,7},{7,6},{8,9},{9,8},{10,11... | collective-permute-start | bytes 786440 | tf_op jit(solution)/shard_map/ppermute | solution.py:67
  290.4 55.9 %collective-permute-start.16 = (bf16[1024,2048]{1,0:T(8,128)(2,1)}, bf16[1024,2048]{1,0:T(8,128)(2,1)}, u32[]{:S(2)}, u32[]{:S(2)}) collective-permute-start(bf16[1024,2048]{1,0:T(8,128)(2,1)} %get-tuple-element.123.refs_6_), channel_id=1, source_target_pairs={{0,1},{1,0},{2,3},{3,2},{4,5},{5,4},{6,7},{7,6},{8,9},{9,8},{10,11... | collective-permute-start | bytes 12582920 | tf_op jit(solution)/shard_map/ppermute | solution.py:67
  290.4 84.2 %collective-permute-start.21 = (bf16[1024,128]{1,0:T(8,128)(2,1)}, bf16[1024,128]{1,0:T(8,128)(2,1)}, u32[]{:S(2)}, u32[]{:S(2)}) collective-permute-start(bf16[1024,128]{1,0:T(8,128)(2,1)} %get-tuple-element.139), channel_id=1, source_target_pairs={{0,1},{1,0},{2,3},{3,2},{4,5},{5,4},{6,7},{7,6},{8,9},{9,8},{10,11... | collective-permute-start | bytes 786440 | tf_op jit(solution)/shard_map/ppermute | solution.py:67
  299.1 77.9 %collective-permute-start.22 = (bf16[1024,128]{1,0:T(8,128)(2,1)}, bf16[1024,128]{1,0:T(8,128)(2,1)}, u32[]{:S(2)}, u32[]{:S(2)}) collective-permute-start(bf16[1024,128]{1,0:T(8,128)(2,1)} %get-tuple-element.140), channel_id=1, source_target_pairs={{0,2},{1,3},{2,0},{3,1},{4,6},{5,7},{6,4},{7,5},{8,10},{9,11},{10,... | collective-permute-start | bytes 786440 | tf_op jit(solution)/shard_map/ppermute | solution.py:67
  300.7 47.7 %collective-permute-start.15 = (bf16[2,1,2,512,512]{4,3,2,1,0:T(8,128)(2,1)}, bf16[2,1,2,512,512]{4,3,2,1,0:T(8,128)(2,1)}, u32[]{:S(2)}, u32[]{:S(2)}) collective-permute-start(bf16[2,1,2,512,512]{4,3,2,1,0:T(8,128)(2,1)} %constant_dynamic-slice_fusion.11), channel_id=1, source_target_pairs={{0,8},{4,12},{8,0},{12,4},{16,24},{20,28},{24,16},{28,20},{1,9},{5... | collective-permute-start | bytes 6291464 | tf_op jit(solution)/shard_map/ppermute | solution.py:69
  300.7 45.6 %collective-permute-start.14 = (bf16[2,2,1,128,1024]{4,3,2,1,0:T(8,128)(2,1)S(1)}, bf16[2,2,1,128,1024]{4,3,2,1,0:T(8,128)(2,1)}, u32[]{:S(2)}, u32[]{:S(2)}) collective-permute-start(bf16[2,2,1,128,1024]{4,3,2,1,0:T(8,128)(2,1)S(1)} %constant_dynamic-slice_fusion.12), channel_id=1, source_target_pairs={{0,4},{4,0},{8,12},{12,8},{16,20},{20,16},{24,28},{28,24},{1,5},{5... | collective-permute-start | bytes 3145736 | tf_op jit(solution)/shard_map/ppermute | solution.py:69
  300.8 47.6 %copy-start.9 = (bf16[1024,1024]{1,0:T(8,128)(2,1)S(1)}, bf16[1024,1024]{1,0:T(8,128)(2,1)}, u32[]{:S(2)}) copy-start(bf16[1024,1024]{1,0:T(8,128)(2,1)} %copy-done.8) | copy-start | bytes 6291460
  346.3 32.2 %collective-permute-start.23 = (bf16[1024,128]{1,0:T(8,128)(2,1)}, bf16[1024,128]{1,0:T(8,128)(2,1)}, u32[]{:S(2)}, u32[]{:S(2)}) collective-permute-start(bf16[1024,128]{1,0:T(8,128)(2,1)} %get-tuple-element.141), channel_id=1, source_target_pairs={{0,3},{1,2},{2,1},{3,0},{4,7},{5,6},{6,5},{7,4},{8,11},{9,10},{10,... | collective-permute-start | bytes 786440 | tf_op jit(solution)/shard_map/ppermute | solution.py:67
  346.3 78.3 %collective-permute-start.20 = (bf16[2,1024,384]{2,1,0:T(8,128)(2,1)}, bf16[2,1024,384]{2,1,0:T(8,128)(2,1)}, u32[]{:S(2)}, u32[]{:S(2)}) collective-permute-start(bf16[2,1024,384]{2,1,0:T(8,128)(2,1)} %get-tuple-element.137.refs_1_), channel_id=1, source_target_pairs={{0,2},{1,3},{2,0},{3,1},{4,6},{5,7},{6,4},{7,5},{8,10},{9,11},{10,... | collective-permute-start | bytes 4718600 | tf_op jit(solution)/shard_map/ppermute | solution.py:67
  350.8 73.8 %collective-permute-start.19 = (bf16[2,1,1,128,1024]{4,3,2,1,0:T(8,128)(2,1)}, bf16[2,1,1,128,1024]{4,3,2,1,0:T(8,128)(2,1)S(1)}, u32[]{:S(2)}, u32[]{:S(2)}) collective-permute-start(bf16[2,1,1,128,1024]{4,3,2,1,0:T(8,128)(2,1)} %constant_dynamic-slice_fusion.8), channel_id=1, source_target_pairs={{0,8},{4,12},{8,0},{12,4},{16,24},{20,28},{24,16},{28,20},{1,9},{5... | collective-permute-start | bytes 1572872 | tf_op jit(solution)/shard_map/ppermute | solution.py:69
  353.5 6.8 %copy-start.4 = (bf16[2,1,2,512,512]{4,3,2,1,0:T(8,128)(2,1)}, bf16[2,1,2,512,512]{4,3,2,1,0:T(8,128)(2,1)S(1)}, u32[]{:S(2)}) copy-start(bf16[2,1,2,512,512]{4,3,2,1,0:T(8,128)(2,1)S(1)} %add_convert_fusion.3.refs_6_) | copy-start | bytes 6291460
  374.6 50.1 %collective-permute-start.18 = (bf16[1,1,2,512,512]{4,3,2,1,0:T(8,128)(2,1)}, bf16[1,1,2,512,512]{4,3,2,1,0:T(8,128)(2,1)}, u32[]{:S(2)}, u32[]{:S(2)}) collective-permute-start(bf16[1,1,2,512,512]{4,3,2,1,0:T(8,128)(2,1)} %constant_dynamic-slice_fusion.9), channel_id=1, source_target_pairs={{0,16},{4,20},{8,24},{12,28},{16,0},{20,4},{24,8},{28,12},{1,17},{... | collective-permute-start | bytes 3145736 | tf_op jit(solution)/shard_map/ppermute | solution.py:69
  377.0 47.6 %collective-permute-start.17 = (bf16[2,2,1,128,2048]{4,3,2,1,0:T(8,128)(2,1)}, bf16[2,2,1,128,2048]{4,3,2,1,0:T(8,128)(2,1)S(1)}, u32[]{:S(2)}, u32[]{:S(2)}) collective-permute-start(bf16[2,2,1,128,2048]{4,3,2,1,0:T(8,128)(2,1)} %constant_dynamic-slice_fusion.10), channel_id=1, source_target_pairs={{0,4},{4,0},{8,12},{12,8},{16,20},{20,16},{24,28},{28,24},{1,5},{5... | collective-permute-start | bytes 6291464 | tf_op jit(solution)/shard_map/ppermute | solution.py:69
  421.1 35.2 %collective-permute-start.25 = (bf16[2,1024,384]{2,1,0:T(8,128)(2,1)}, bf16[2,1024,384]{2,1,0:T(8,128)(2,1)}, u32[]{:S(2)}, u32[]{:S(2)}) collective-permute-start(bf16[2,1024,384]{2,1,0:T(8,128)(2,1)} %get-tuple-element.148.refs_1_), channel_id=1, source_target_pairs={{0,2},{1,3},{2,0},{3,1},{4,6},{5,7},{6,4},{7,5},{8,10},{9,11},{10,... | collective-permute-start | bytes 4718600 | tf_op jit(solution)/shard_map/ppermute | solution.py:67
  427.9 28.4 %collective-permute-start.27 = (bf16[1,1,1,128,1024]{4,3,2,1,0:T(8,128)(2,1)S(1)}, bf16[1,1,1,128,1024]{4,3,2,1,0:T(8,128)(2,1)}, u32[]{:S(2)}, u32[]{:S(2)}) collective-permute-start(bf16[1,1,1,128,1024]{4,3,2,1,0:T(8,128)(2,1)S(1)} %constant_dynamic-slice_fusion.5), channel_id=1, source_target_pairs={{0,16},{4,20},{8,24},{12,28},{16,0},{20,4},{24,8},{28,12},{1,17},{... | collective-permute-start | bytes 786440 | tf_op jit(solution)/shard_map/ppermute | solution.py:69
  432.4 23.9 %collective-permute-start.26 = (bf16[1,1,1,512,512]{4,3,2,1,0:T(8,128)(2,1)}, bf16[1,1,1,512,512]{4,3,2,1,0:T(8,128)(2,1)S(1)}, u32[]{:S(2)}, u32[]{:S(2)}) collective-permute-start(bf16[1,1,1,512,512]{4,3,2,1,0:T(8,128)(2,1)} %constant_dynamic-slice_fusion.6), channel_id=1, source_target_pairs={{0,4},{4,0},{8,12},{12,8},{16,20},{20,16},{24,28},{28,24},{1,5},{5... | collective-permute-start | bytes 1572872 | tf_op jit(solution)/shard_map/ppermute | solution.py:69
  432.6 29.1 %copy-start.18 = (f32[1024,2]{1,0:T(8,128)S(1)}, f32[1024,2]{1,0:T(8,128)}, u32[]{:S(2)}) copy-start(f32[1024,2]{1,0:T(8,128)} %get-tuple-element.161) | copy-start | bytes 24580
  432.6 29.1 %collective-permute-start.24 = (bf16[2,1,1,128,2048]{4,3,2,1,0:T(8,128)(2,1)S(1)}, bf16[2,1,1,128,2048]{4,3,2,1,0:T(8,128)(2,1)}, u32[]{:S(2)}, u32[]{:S(2)}) collective-permute-start(bf16[2,1,1,128,2048]{4,3,2,1,0:T(8,128)(2,1)S(1)} %constant_dynamic-slice_fusion.7), channel_id=1, source_target_pairs={{0,8},{4,12},{8,0},{12,4},{16,24},{20,28},{24,16},{28,20},{1,9},{5... | collective-permute-start | bytes 3145736 | tf_op jit(solution)/shard_map/ppermute | solution.py:69
  464.1 38.9 %collective-permute-start.32 = (bf16[1,1,1,128,1024]{4,3,2,1,0:T(8,128)(2,1)S(1)}, bf16[1,1,1,128,1024]{4,3,2,1,0:T(8,128)(2,1)S(1)}, u32[]{:S(2)}, u32[]{:S(2)}) collective-permute-start(bf16[1,1,1,128,1024]{4,3,2,1,0:T(8,128)(2,1)S(1)} %add_convert_fusion.16), channel_id=1, source_target_pairs={{0,2},{1,3},{2,0},{3,1},{4,6},{5,7},{6,4},{7,5},{8,10},{9,11},{10,... | collective-permute-start | bytes 786440 | tf_op jit(solution)/shard_map/ppermute | solution.py:67
  467.4 35.7 %collective-permute-start.28 = (bf16[4,1024,384]{2,1,0:T(8,128)(2,1)S(1)}, bf16[4,1024,384]{2,1,0:T(8,128)(2,1)S(1)}, u32[]{:S(2)}, u32[]{:S(2)}) collective-permute-start(bf16[4,1024,384]{2,1,0:T(8,128)(2,1)S(1)} %pad_maximum_fusion), channel_id=1, source_target_pairs={{0,1},{1,0},{2,3},{3,2},{4,5},{5,4},{6,7},{7,6},{8,9},{9,8},{10,11... | collective-permute-start | bytes 9437192 | tf_op jit(solution)/shard_map/ppermute | solution.py:67
  468.4 34.7 %collective-permute-start.31 = (bf16[1,1,1,512,256]{4,3,2,1,0:T(8,128)(2,1)S(1)}, bf16[1,1,1,512,256]{4,3,2,1,0:T(8,128)(2,1)S(1)}, u32[]{:S(2)}, u32[]{:S(2)}) collective-permute-start(bf16[1,1,1,512,256]{4,3,2,1,0:T(8,128)(2,1)S(1)} %constant_dynamic-slice_fusion.3), channel_id=1, source_target_pairs={{0,2},{1,3},{2,0},{3,1},{4,6},{5,7},{6,4},{7,5},{8,10},{9,11},{10,... | collective-permute-start | bytes 786440 | tf_op jit(solution)/shard_map/ppermute | solution.py:67
  470.8 32.3 %collective-permute-start.30 = (bf16[1,1,1,128,2048]{4,3,2,1,0:T(8,128)(2,1)S(1)}, bf16[1,1,1,128,2048]{4,3,2,1,0:T(8,128)(2,1)S(1)}, u32[]{:S(2)}, u32[]{:S(2)}) collective-permute-start(bf16[1,1,1,128,2048]{4,3,2,1,0:T(8,128)(2,1)S(1)} %constant_dynamic-slice_fusion.4), channel_id=1, source_target_pairs={{0,16},{4,20},{8,24},{12,28},{16,0},{20,4},{24,8},{28,12},{1,17},{... | collective-permute-start | bytes 1572872 | tf_op jit(solution)/shard_map/ppermute | solution.py:69
  471.0 32.1 %collective-permute-start.29 = (bf16[2,2,1,128,768]{4,3,2,1,0:T(8,128)(2,1)S(1)}, bf16[2,2,1,128,768]{4,3,2,1,0:T(8,128)(2,1)S(1)}, u32[]{:S(2)}, u32[]{:S(2)}) collective-permute-start(bf16[2,2,1,128,768]{4,3,2,1,0:T(8,128)(2,1)S(1)} %fusion.2), channel_id=1, source_target_pairs={{0,4},{4,0},{8,12},{12,8},{16,20},{20,16},{24,28},{28,24},{1,5},{5... | collective-permute-start | bytes 2359304 | tf_op jit(solution)/shard_map/ppermute | solution.py:69
  503.2 20.9 %collective-permute-start.41 = (bf16[512,256]{1,0:T(8,128)(2,1)S(1)}, bf16[512,256]{1,0:T(8,128)(2,1)S(1)}, u32[]{:S(2)}, u32[]{:S(2)}) collective-permute-start(bf16[512,256]{1,0:T(8,128)(2,1)S(1)} %bitcast.153), channel_id=1, source_target_pairs={{0,1},{1,0},{2,3},{3,2},{4,5},{5,4},{6,7},{7,6},{8,9},{9,8},{10,11... | collective-permute-start | bytes 786440 | tf_op jit(solution)/shard_map/ppermute | solution.py:67
  503.3 20.9 %collective-permute-start.42 = (bf16[512,256]{1,0:T(8,128)(2,1)S(1)}, bf16[512,256]{1,0:T(8,128)(2,1)S(1)}, u32[]{:S(2)}, u32[]{:S(2)}) collective-permute-start(bf16[512,256]{1,0:T(8,128)(2,1)S(1)} %bitcast.154), channel_id=1, source_target_pairs={{0,2},{1,3},{2,0},{3,1},{4,6},{5,7},{6,4},{7,5},{8,10},{9,11},{10,... | collective-permute-start | bytes 786440 | tf_op jit(solution)/shard_map/ppermute | solution.py:67
  504.1 20.1 %collective-permute-start.43 = (bf16[512,256]{1,0:T(8,128)(2,1)S(1)}, bf16[512,256]{1,0:T(8,128)(2,1)}, u32[]{:S(2)}, u32[]{:S(2)}) collective-permute-start(bf16[512,256]{1,0:T(8,128)(2,1)S(1)} %bitcast.155), channel_id=1, source_target_pairs={{0,3},{1,2},{2,1},{3,0},{4,7},{5,6},{6,5},{7,4},{8,11},{9,10},{10,... | collective-permute-start | bytes 786440 | tf_op jit(solution)/shard_map/ppermute | solution.py:67
  505.5 23.3 %collective-permute-start.34 = (bf16[1,1,1,128,2048]{4,3,2,1,0:T(8,128)(2,1)S(1)}, bf16[1,1,1,128,2048]{4,3,2,1,0:T(8,128)(2,1)S(1)}, u32[]{:S(2)}, u32[]{:S(2)}) collective-permute-start(bf16[1,1,1,128,2048]{4,3,2,1,0:T(8,128)(2,1)S(1)} %add_convert_fusion.10), channel_id=1, source_target_pairs={{0,2},{1,3},{2,0},{3,1},{4,6},{5,7},{6,4},{7,5},{8,10},{9,11},{10,... | collective-permute-start | bytes 1572872 | tf_op jit(solution)/shard_map/ppermute | solution.py:67
  508.4 18.6 %collective-permute-start.33 = (bf16[2,1,1,128,768]{4,3,2,1,0:T(8,128)(2,1)S(1)}, bf16[2,1,1,128,768]{4,3,2,1,0:T(8,128)(2,1)S(1)}, u32[]{:S(2)}, u32[]{:S(2)}) collective-permute-start(bf16[2,1,1,128,768]{4,3,2,1,0:T(8,128)(2,1)S(1)} %constant_dynamic-slice_fusion.2), channel_id=1, source_target_pairs={{0,8},{4,12},{8,0},{12,4},{16,24},{20,28},{24,16},{28,20},{1,9},{5... | collective-permute-start | bytes 1179656 | tf_op jit(solution)/shard_map/ppermute | solution.py:69
  524.1 5.6 %collective-permute-start.39 = (bf16[128,1024]{1,0:T(8,128)(2,1)S(1)}, bf16[128,1024]{1,0:T(8,128)(2,1)S(1)}, u32[]{:S(2)}, u32[]{:S(2)}) collective-permute-start(bf16[128,1024]{1,0:T(8,128)(2,1)S(1)} %bitcast.151), channel_id=1, source_target_pairs={{0,1},{1,0},{2,3},{3,2},{4,5},{5,4},{6,7},{7,6},{8,9},{9,8},{10,11... | collective-permute-start | bytes 786440 | tf_op jit(solution)/shard_map/ppermute | solution.py:67
  529.0 27.6 %collective-permute-start.40 = (bf16[128,2048]{1,0:T(8,128)(2,1)S(1)}, bf16[128,2048]{1,0:T(8,128)(2,1)S(1)}, u32[]{:S(2)}, u32[]{:S(2)}) collective-permute-start(bf16[128,2048]{1,0:T(8,128)(2,1)S(1)} %get-tuple-element.248), channel_id=1, source_target_pairs={{0,1},{1,0},{2,3},{3,2},{4,5},{5,4},{6,7},{7,6},{8,9},{9,8},{10,11... | collective-permute-start | bytes 1572872 | tf_op jit(solution)/shard_map/ppermute | solution.py:67
  530.0 5.8 %copy-start.32 = (f32[8]{0:T(128)S(1)}, f32[8]{0:T(128)}, u32[]{:S(2)}) copy-start(f32[8]{0:T(128)} %convolution_bitcast_fusion) | copy-start | bytes 100
  531.2 12.3 %collective-permute-start.35 = (bf16[1,1,1,128,768]{4,3,2,1,0:T(8,128)(2,1)S(1)}, bf16[1,1,1,128,768]{4,3,2,1,0:T(8,128)(2,1)S(1)}, u32[]{:S(2)}, u32[]{:S(2)}) collective-permute-start(bf16[1,1,1,128,768]{4,3,2,1,0:T(8,128)(2,1)S(1)} %constant_dynamic-slice_fusion.1), channel_id=1, source_target_pairs={{0,16},{4,20},{8,24},{12,28},{16,0},{20,4},{24,8},{28,12},{1,17},{... | collective-permute-start | bytes 589832 | tf_op jit(solution)/shard_map/ppermute | solution.py:69
  543.6 2.6 collective-permute-start.36
  543.7 7.7 %collective-permute-start.37 = (bf16[128,768]{1,0:T(8,128)(2,1)S(1)}, bf16[128,768]{1,0:T(8,128)(2,1)S(1)}, u32[]{:S(2)}, u32[]{:S(2)}) collective-permute-start(bf16[128,768]{1,0:T(8,128)(2,1)S(1)} %get-tuple-element.255), channel_id=1, source_target_pairs={{0,2},{1,3},{2,0},{3,1},{4,6},{5,7},{6,4},{7,5},{8,10},{9,11},{10,... | collective-permute-start | bytes 589832 | tf_op jit(solution)/shard_map/ppermute | solution.py:67
  544.5 10.3 %collective-permute-start.38 = (bf16[128,768]{1,0:T(8,128)(2,1)S(1)}, bf16[128,768]{1,0:T(8,128)(2,1)S(1)}, u32[]{:S(2)}, u32[]{:S(2)}) collective-permute-start(bf16[128,768]{1,0:T(8,128)(2,1)S(1)} %get-tuple-element.255), channel_id=1, source_target_pairs={{0,3},{1,2},{2,1},{3,0},{4,7},{5,6},{6,5},{7,4},{8,11},{9,10},{10,... | collective-permute-start | bytes 589832 | tf_op jit(solution)/shard_map/ppermute | solution.py:67
  (22 other events, 61.6 us)

commit v5 on v4

--- a/solution.py
+++ b/solution.py
@@ -83,15 +83,13 @@
     return masks
 
 
-def gather_pieces(value, after=()):
+def gather_pieces(value, count):
     pieces = {0: value}
-    order = sorted(range(1, lax.axis_size("row")), key=lambda d: (d & 1, d))
+    order = sorted(range(1, count), key=lambda d: (d & 1, d))
     for d in order:
         low = d & -d
         pieces[d] = jump(pieces[d ^ low], low)
-        if d % 2 == 0:
-            pieces[d] = behind(pieces[d], after)
-    return [pieces[d] for d in range(lax.axis_size("row"))]
+    return [pieces[d] for d in range(count)]
 
 
 def send_pieces(pieces):
@@ -227,54 +225,71 @@
     return centre * rstd, rstd
 
 
-def qkv_kernel(count, splits, local_rows, features, me_ref, *refs):
+def qkv_kernel(count, splits, local_rows, features, held, me_ref, *refs):
     n_w = 3 * splits
     pieces, columns = refs[:count], refs[count : count + n_w]
     bias_ref, gain_ref, shift_ref = refs[count + n_w : count + n_w + 3]
-    n_ref, q_ref, k_ref, v_ref, kt_ref, vt_ref, w_ref = refs[count + n_w + 3 :]
-    block = pl.program_id(0)
+    n_ref, q_ref, k_ref, v_ref, kt_ref, vt_ref, w_ref = refs[count + n_w + 3 + held :]
+    step = pl.program_id(0)
     wide = features // splits
-
-    @pl.when(block == 0)
+    half = BLK // 2
+    rows = half // count
+
+    @pl.when(step == 0)
     def _():
         for i, ref in enumerate(columns):
             w_ref[:, i * wide : (i + 1) * wide] = ref[...]
 
-    unit, _ = norm_parts(load_block(pieces, block, BLK // count, local_rows))
+    places = [(b, d) for b in range(2) for d in range(count)]
+    value = jnp.concatenate(
+        [pieces[d][b * rows : (b + 1) * rows, :] for b, d in places], axis=0
+    ).astype(f32)
+    row = lax.broadcasted_iota(jnp.int32, (BLK, 1), 0)
+    position = (2 * step + row // half) * rows + row % rows
+    unit, _ = norm_parts(jnp.where(position < local_rows, value, 0.0))
     normed = (unit * gain_ref[...] + shift_ref[...]).astype(bf16)
-    n_ref[...] = unit.astype(bf16).reshape(n_ref.shape)
+    low = unit.astype(bf16)
+    for i, (b, d) in enumerate(places):
+        n_ref[d, b * rows : (b + 1) * rows, :] = low[i * rows : (i + 1) * rows]
     mixed = matmul(normed, w_ref[...])
     for s in range(splits):
         at = slice(s * wide, (s + 1) * wide)
         part = mixed[:, 3 * s * wide : 3 * (s + 1) * wide]
+        queries = ((part[:, :wide] + bias_ref[0:1, at]) * 0.125).astype(bf16)
         keys = part[:, wide : 2 * wide]
         values = part[:, 2 * wide :] + bias_ref[1:2, at]
-        q_ref[:, at] = ((part[:, :wide] + bias_ref[0:1, at]) * 0.125).astype(bf16)
-        k_ref[:, at] = keys.astype(bf16)
-        v_ref[:, at] = values.astype(bf16)
-        kt_ref[0, at] = keys.T.astype(bf16)
-        vt_ref[0, at] = values.T.astype(bf16)
-
-
-def qkv_call(me, pieces, w_qkv, bias, gain, shift, splits):
+        keys_low, values_low = keys.astype(bf16), values.astype(bf16)
+        keys_turned, values_turned = keys.T.astype(bf16), values.T.astype(bf16)
+        for b in range(2):
+            here = slice(b * half, (b + 1) * half)
+            q_ref[b, 0, :, at] = queries[here]
+            k_ref[b, 0, :, at] = keys_low[here]
+            v_ref[b, 0, :, at] = values_low[here]
+            kt_ref[b, at, :] = keys_turned[:, here]
+            vt_ref[b, at, :] = values_turned[:, here]
+
+
+def qkv_call(me, pieces, part, w_qkv, bias, gain, shift, splits, held=()):
     count, (local_rows, width) = len(pieces), pieces[0].shape
-    features = width // count
-    piece_rows = BLK // count
-    blocks = pl.cdiv(local_rows, piece_rows)
+    features = width // (2 * count)
+    rows = BLK // 2 // count
+    blocks = pl.cdiv(local_rows, rows)
     whole = lambda a: pl.BlockSpec(a.shape, lambda b, m: (0,) * a.ndim)
-    flat = pl.BlockSpec((BLK, features), lambda b, m: (b, 0))
-    turned = pl.BlockSpec((1, features, BLK), lambda b, m: (b, 0, 0))
+    flat = pl.BlockSpec((2, 1, BLK // 2, features), lambda b, m: (b, part, 0, 0))
+    turned = pl.BlockSpec((2, features, BLK // 2), lambda b, m: (b, 0, part))
     specs, operands = own_columns(w_qkv, features, splits, range(splits))
+    at = 1 + count + 3 * splits + 3
     return pl.pallas_call(
-        functools.partial(qkv_kernel, count, splits, local_rows, features),
+        functools.partial(qkv_kernel, count, splits, local_rows, features, len(held)),
         grid_spec=pltpu.PrefetchScalarGridSpec(
             num_scalar_prefetch=1,
-            grid=(blocks,),
-            in_specs=[pl.BlockSpec((piece_rows, width), lambda b, m: (b, 0))] * count
+            grid=(blocks // 2,),
+            in_specs=[pl.BlockSpec((2 * rows, width), lambda b, m: (b, 0))] * count
             + specs
-            + [whole(bias), whole(gain), whole(shift)],
+            + [whole(bias), whole(gain), whole(shift)]
+            + [ANYWHERE] * len(held),
             out_specs=[
-                pl.BlockSpec((count, piece_rows, width), lambda b, m: (0, b, 0)),
+                pl.BlockSpec((count, 2 * rows, width), lambda b, m: (part, b, 0)),
                 flat,
                 flat,
                 flat,
@@ -283,16 +298,17 @@
             ],
             scratch_shapes=[pltpu.VMEM((width, 3 * features), bf16)],
         ),
-        out_shape=[jax.ShapeDtypeStruct((count, blocks * piece_rows, width), bf16)]
-        + [jax.ShapeDtypeStruct((blocks * BLK, features), bf16)] * 3
+        out_shape=[jax.ShapeDtypeStruct((2 * count, blocks * rows, width), bf16)]
+        + [jax.ShapeDtypeStruct((blocks, 2, BLK // 2, features), bf16)] * 3
         + [jax.ShapeDtypeStruct((blocks, features, BLK), bf16)] * 2,
+        input_output_aliases={at + i: i for i in range(len(held))},
         compiler_params=params(),
         cost_estimate=pl.CostEstimate(
             flops=6 * blocks * BLK * width * 3 * features,
-            bytes_accessed=2 * blocks * BLK * (2 * width + 5 * features),
+            bytes_accessed=blocks * BLK * (2 * width + 5 * features),
             transcendentals=0,
         ),
-    )(me, *pieces, *operands, bias, gain, shift)
+    )(me, *pieces, *operands, bias, gain, shift, *held)
 
 
 def per_head(stack_ref, value, heads):
@@ -1089,14 +1105,19 @@
     me = device.reshape(1)
     w_out_here = jnp.concatenate([rows_of(w_out, p, features) for p in partners], axis=0)
     bias_here = lax.dynamic_slice_in_dim(qv_bias, device * features, features, 1)
-    grads_in = gather_pieces(cotangent[0].reshape(slots_here, LT * width).astype(bf16))
-    pieces = gather_pieces(
-        tokens[0], [imgq, imgk, lo, hi, image_here, w_out_here, bias_here, grads_in[-1]]
-    )
-
-    unit, q, k, v, kt, vt = qkv_call(
-        me, pieces, w_qkv, bias_here, norm_gain[0:1], norm_bias[0:1], splits
-    )
+    half_count = row_count // 2
+    first_norm = (w_qkv, bias_here, norm_gain[0:1], norm_bias[0:1], splits)
+    far_tokens = jump(tokens[0], half_count)
+    pieces = gather_pieces(tokens[0], half_count)
+    filled = qkv_call(me, pieces, 0, *first_norm)
+    tables = (imgq, imgk, lo, hi, image_here, w_out_here)
+    far_tokens, filled, tables = lax.optimization_barrier((far_tokens, filled, tables))
+    imgq, imgk, lo, hi, image_here, w_out_here = tables
+    pieces = gather_pieces(far_tokens, half_count)
+    unit, q, k, v, kt, vt = qkv_call(me, pieces, 1, *first_norm, filled)
+    q, k, v = (a.reshape(-1, features) for a in (q, k, v))
+    slot_grads = behind(cotangent[0].reshape(slots_here, LT * width).astype(bf16), [lo, unit])
+    grads_in = gather_pieces(slot_grads, row_count)
     *attended, ot, lse = attend_call(q, k, vt, imgq, imgk, lo, hi, row_count)
     attended = send_pieces(attended)
 

time: 567 us -> 565 us (level)
  starting transfers between devices: 27.7 us -> 38.4 us
  waiting for transfers between devices: 94.9 us -> 89.1 us
    ppermute x32, waiting for transfers between devices: 81.9 us -> 68.9 us  [jump(): return lax.ppermute(value, 'row', [(i, i ^ row_mask) for i in range(rows)])]
    ppermute x12, starting transfers between devices: 7.76 us -> 17.9 us  [jump(): return lax.ppermute(value, 'img', [(i, i ^ img_mask) for i in range(imgs)])]
    ppermute x12, waiting for transfers between devices: 13 us -> 20.1 us  [jump(): return lax.ppermute(value, 'img', [(i, i ^ img_mask) for i in range(imgs)])]
    pallas_call x1 -> x2, Pallas kernels: 22.7 us -> 24.9 us  [qkv_call(): pl.pallas_call(functools.partial(qkv_kernel, count, splits, local_rows, f...]
  transfers between devices with their start and end apart: 44 -> 44, of which waited for: 11 -> 12; matrix products, arithmetic and copies ran while one was open for 13% -> 13% of each run, Pallas kernels for 42% -> 31%
where the time goes in v5:
time: 565 us; the launch traced here: 557 us
  Pallas kernels  346 us (61%)
  waiting for transfers between devices  89.1 us (16%)
  local copies, waits for them, and re-layouts  40.7 us (7%)
  other arithmetic  39.5 us (7%)
  starting transfers between devices  38.4 us (7%)
    pallas_call x1, Pallas kernels, rows_call(): pl.pallas_call(functools.partial(rows_kernel, count, splits, local_rows),...  89.1 us
    pallas_call x2, Pallas kernels, attend_back_call(): pl.pallas_call(functools.partial(attend_back_kernel, count, heads, split...  80.6 us
    ppermute x32, waiting for transfers between devices, jump(): return lax.ppermute(value, 'row', [(i, i ^ row_mask) for i in range(rows)])  68.9 us
    pallas_call x1, Pallas kernels, attend_call(): pl.pallas_call(functools.partial(attend_kernel, count, heads), grid_spec=...  44.1 us
    pallas_call x1, Pallas kernels, vectors_call(): pl.pallas_call(functools.partial(vectors_kernel, count, row_bits, img_bit...  31.9 us
    pallas_call x2, Pallas kernels, qkv_call(): pl.pallas_call(functools.partial(qkv_kernel, count, splits, local_rows, f...  24.9 us
    convert_element_type x16, other arithmetic, finish(): return tree([v.astype(f32) for v in values]).astype(bf16)  23.8 us
    ppermute x32, starting transfers between devices, jump(): return lax.ppermute(value, 'row', [(i, i ^ row_mask) for i in range(rows)])  20.5 us
  transfers between devices with their start and end apart: 44, of which 12 were waited for; matrix products, arithmetic and copies ran while one was open for 13% of the time, Pallas kernels for 31%

profile of v5, /device:TPU:0, one launch (start us, length us, event | category | flops | bytes accessed | tf_op | source)
XLA Modules:
  0.0 557.1 jit_solution(167874995254405432)
XLA Ops:
  1.2 2.6 collective-permute-start
  6.6 1.7 constant_dynamic-slice_fusion.16
  8.4 1.5 pad_maximum_fusion.1.refs_2_
  9.9 1.3 constant_dynamic-slice_fusion.17.refs_8_
  12.7 12.5 %shard_map.297 = (bf16[4,1024,1024]{2,1,0:T(8,128)(2,1)}, bf16[16,2,128,256]{3,2,1,0:T(8,128)(2,1)}, bf16[16,2,128,256]{3,2,1,0:T(8,128)(2,1)}, bf16[16,2,128,25...) custom-call(s32[1]{0:T(128)} %bitcast.1.me_ref, bf16[1016,1024]{1,0:T(8,128)(2,1)} %bitcast.195, ...), custom_call_target="tpu_custom_call" | custom-call | flops 19327352832 | bytes 13631488 | tf_op jit(solution)/shard_map/pallas_call | solution.py:282
  25.1 24.7 %collective-permute-done.refs_0_ = bf16[1016,1024]{1,0:T(8,128)(2,1)S(1)} collective-permute-done((bf16[1016,1024]{1,0:T(8,128)(2,1)}, bf16[1016,1024]{1,0:T(8,128)(2,1)S(1)}, u32[]{:S(2)}, u32[]{:S(2)}) %collective-permute-start) | collective-permute-done | bytes 2080800 | tf_op jit(solution)/shard_map/ppermute | solution.py:67
  49.9 2.0 copy.73.refs_4_.refs_14_.refs_12_
  51.9 2.2 collective-permute-done.2.refs_1_
  54.1 12.5 %shard_map.298 = (bf16[4,1024,1024]{2,1,0:T(8,128)(2,1)}, bf16[16,2,128,256]{3,2,1,0:T(8,128)(2,1)}, bf16[16,2,128,256]{3,2,1,0:T(8,128)(2,1)}, bf16[16,2,128,25...) custom-call(s32[1]{0:T(128)} %bitcast.1.me_ref, ...), custom_call_target="tpu_custom_call", output_to_operand_aliasing={{0}: (12, {}), {1}: (13, {}), {2}: (14, {}), {3}: (15, {}),... | custom-call | flops 19327352832 | bytes 13631488 | tf_op jit(solution)/shard_map/pallas_call | solution.py:282
  66.6 44.1 %shard_map.299 = (bf16[1024,256]{1,0:T(8,128)(2,1)}, bf16[1024,256]{1,0:T(8,128)(2,1)}, bf16[1024,256]{1,0:T(8,128)(2,1)}, bf16[1024,256]{1,0:T(8,128)(2,1)}, f3...) custom-call(s32[16]{0:T(128)} %get-tuple-element.124.lo_ref, s32[16]{0:T(128)} %get-tuple-element.125.hi_ref, ...), custom_call_target="tpu_custom_call" | custom-call | flops 42949672960 | bytes 16777216 | tf_op jit(solution)/shard_map/pallas_call | solution.py:387
  110.9 1.8 collective-permute-start.7
  112.7 1.8 collective-permute-start.4
  114.6 22.7 %collective-permute-done.4 = bf16[2,8192]{1,0:T(2,128)(2,1)S(1)} collective-permute-done((bf16[2,8192]{1,0:T(2,128)(2,1)S(1)}, bf16[2,8192]{1,0:T(2,128)(2,1)S(1)}, u32[]{:S(2)}, u32[]{:S(2)}) %collective-permute-start.4) | collective-permute-done | bytes 32800 | tf_op jit(solution)/shard_map/ppermute | solution.py:67
  142.6 89.1 %shard_map.300 = (bf16[1024,1024]{1,0:T(8,128)(2,1)}, bf16[1024,4096]{1,0:T(8,128)(2,1)}, bf16[1024,4096]{1,0:T(8,128)(2,1)}, bf16[1024,1024]{1,0:T(8,128)(2,1)}...) custom-call(bf16[1016,1024]{1,0:T(8,128)(2,1)} %bitcast.196, ...), custom_call_target="tpu_custom_call" | custom-call | flops 42949672960 | bytes 58720256 | tf_op jit(solution)/shard_map/pallas_call | solution.py:708
  231.7 11.6 %shard_map.301 = (bf16[1024,1024]{1,0:T(8,128)(2,1)}, bf16[1024,1024]{1,0:T(8,128)(2,1)}, f32[1024,64]{1,0:T(8,128)}) custom-call(s32[1]{0:T(128)} %bitcast.1.me_ref, bf16[1024,1024]{1,0:T(8,128)(2,1)} %get-tuple-element.150.refs_0_, bf16[1024,1024]{1,0:T(8,128)(2,1)} %get-tuple-element.151.refs_1_, bf16[1024,1024]{1,0:T(8,128)(2,1)} %get-tuple-element.152.refs_2_, ...), custom_call_target="tpu_custom_call" | custom-call | flops 6442450944 | bytes 20971520 | tf_op jit(solution)/shard_map/pallas_call | solution.py:849
  243.3 13.8 %shard_map.302 = (bf16[4096,512]{1,0:T(8,128)(2,1)}, bf16[4096,512]{1,0:T(8,128)(2,1)}) custom-call(s32[1]{0:T(128)} %bitcast.1.me_ref, bf16[1024,4096]{1,0:T(8,128)(2,1)} %get-tuple-element.157.left_ref, bf16[1024,1024]{1,0:T(8,128)(2,1)} %get-tuple-element.158.right_ref, bf16[1024,1024]{1,0:T(8,128)(2,1)} %get-tuple-element.156.refs_0_), custom_call_target="tpu_custom_call" | custom-call | flops 12884901888 | bytes 16777216 | tf_op jit(solution)/shard_map/pallas_call | solution.py:754
  260.4 1.7 collective-permute-start.10
  265.6 14.7 %shard_map.303 = (bf16[1024,2048]{1,0:T(8,128)(2,1)}, bf16[1024,2048]{1,0:T(8,128)(2,1)}) custom-call(s32[1]{0:T(128)} %bitcast.1.me_ref, bf16[1024,1024]{1,0:T(8,128)(2,1)} %get-tuple-element.160.left_ref, bf16[1024,4096]{1,0:T(8,128)(2,1)} %get-tuple-element.161.right_ref, bf16[4096,512]{1,0:T(8,128)(2,1)} %get-tuple-element.159.refs_0_), custom_call_target="tpu_custom_call" | custom-call | flops 12884901888 | bytes 16777216 | tf_op jit(solution)/shard_map/pallas_call | solution.py:796
  280.8 4.8 add_convert_fusion.1
  287.6 1.4 constant_dynamic-slice_fusion.11
  289.0 1.7 collective-permute-start.22
  290.8 2.8 collective-permute-start.14
  293.6 40.4 %shard_map.304 = (bf16[2,1024,384]{2,1,0:T(8,128)(2,1)}, bf16[2,1024,384]{2,1,0:T(8,128)(2,1)}, f32[8,128]{1,0:T(8,128)}) custom-call(s32[16]{0:T(128)} %get-tuple-element.124.lo_ref, s32[16]{0:T(128)} %get-tuple-element.125.hi_ref, bf16[1024,128]{1,0:T(8,128)(2,1)} %get-tuple-element.146.refs_0_, bf16[1024,128]{1,0:T(8,128)(2,1)} %collective-permute-done.9.refs_1_, ...), custom_call_target="tpu_custom_call" | custom-call | flops 34359738368 | bytes 12582912 | tf_op jit(solution)/shard_map/pallas_call | solution.py:515
  334.7 2.1 slice.193
  338.4 1.6 add_convert_fusion.7
  341.2 2.3 add_convert_fusion.3.refs_6_
  343.7 6.6 %add_convert_fusion = bf16[1024,2048]{1,0:T(8,128)(2,1)} fusion(bf16[1024,2048]{1,0:T(8,128)(2,1)} %collective-permute-done.16, bf16[1024,2048]{1,0:T(8,128)(2,1)S(1)} %copy-done.10), kind=kLoop, calls=%fused_computation.3 | loop fusion | flops 8388608 | bytes 12582912 | tf_op jit(solution)/shard_map/convert_element_type | solution.py:136
  350.4 1.1 constant_dynamic-slice_fusion.9
  351.4 10.0 %shard_map.305 = (bf16[1024,384]{1,0:T(8,128)(2,1)}, f32[1024,2]{1,0:T(8,128)}) custom-call(s32[1]{0:T(128)} %bitcast.1.me_ref, bf16[4,1024,1024]{2,1,0:T(8,128)(2,1)} %get-tuple-element.135.n_ref, f32[1024,1]{1,0:T(8,128)} %copy.77.gain_ref, f32[1024,1]{1,0:T(8,128)} %copy.78.shift_ref, bf16[2,1024,384]{2,1,0:T(8,128)(2,1)} %get-tuple-element.170.refs_0_, ...), custom_call_target="tpu_custom_call" | custom-call | flops 17179869184 | bytes 1024 | tf_op jit(solution)/shard_map/pallas_call | solution.py:897
  361.4 3.2 constant_dynamic-slice_fusion.10
  364.6 8.1 %collective-permute-start.18 = (bf16[1,1,2,512,512]{4,3,2,1,0:T(8,128)(2,1)}, bf16[1,1,2,512,512]{4,3,2,1,0:T(8,128)(2,1)}, u32[]{:S(2)}, u32[]{:S(2)}) collective-permute-start(bf16[1,1,2,512,512]{4,3,2,1,0:T(8,128)(2,1)} %constant_dynamic-slice_fusion.9), channel_id=1, source_target_pairs={{0,16},{4,20},{8,24},{12,28},{16,0},{20,4},{24,8},{28,12},{1,17},{... | collective-permute-start | bytes 3145736 | tf_op jit(solution)/shard_map/ppermute | solution.py:69
  373.0 40.3 %shard_map.306 = (bf16[2,1024,384]{2,1,0:T(8,128)(2,1)}, bf16[2,1024,384]{2,1,0:T(8,128)(2,1)}, f32[8,128]{1,0:T(8,128)}) custom-call(s32[16]{0:T(128)} %get-tuple-element.124.lo_ref, s32[16]{0:T(128)} %get-tuple-element.125.hi_ref, bf16[1024,128]{1,0:T(8,128)(2,1)} %get-tuple-element.177.refs_0_, bf16[1024,128]{1,0:T(8,128)(2,1)} %collective-permute-done.21.refs_1_, ...), custom_call_target="tpu_custom_call" | custom-call | flops 34359738368 | bytes 12582912 | tf_op jit(solution)/shard_map/pallas_call | solution.py:515
  414.9 2.2 slice.195
  417.1 2.1 collective-permute-done.18
  419.3 1.4 collective-permute-done.17
  420.6 2.4 add_convert_fusion.2.refs_5_
  423.3 1.2 collective-permute-start.27
  425.4 1.5 add_convert_fusion.6.refs_6_
  428.2 1.7 collective-permute-start.24
  429.9 10.0 %shard_map.307 = (bf16[1024,384]{1,0:T(8,128)(2,1)}, f32[1024,2]{1,0:T(8,128)}) custom-call(s32[1]{0:T(128)} %bitcast.1.me_ref, bf16[4,1024,1024]{2,1,0:T(8,128)(2,1)} %get-tuple-element.135.n_ref, f32[1024,1]{1,0:T(8,128)} %copy.77.gain_ref, f32[1024,1]{1,0:T(8,128)} %copy.78.shift_ref, bf16[2,1024,384]{2,1,0:T(8,128)(2,1)} %get-tuple-element.184.refs_0_.refs_2_, ...), custom_call_target="tpu_custom_call" | custom-call | flops 17179869184 | bytes 1024 | tf_op jit(solution)/shard_map/pallas_call | solution.py:897
  439.9 1.2 slice.194
  441.1 8.7 %collective-permute-done.25.refs_3_ = bf16[2,1024,384]{2,1,0:T(8,128)(2,1)} collective-permute-done((bf16[2,1024,384]{2,1,0:T(8,128)(2,1)}, bf16[2,1024,384]{2,1,0:T(8,128)(2,1)}, u32[]{:S(2)}, u32[]{:S(2)}) %collective-permute-start.25) | collective-permute-done | bytes 1572896 | tf_op jit(solution)/shard_map/ppermute | solution.py:67
  449.9 7.6 %collective-permute-done.24 = bf16[2,1,1,128,2048]{4,3,2,1,0:T(8,128)(2,1)} collective-permute-done((bf16[2,1,1,128,2048]{4,3,2,1,0:T(8,128)(2,1)S(1)}, bf16[2,1,1,128,2048]{4,3,2,1,0:T(8,128)(2,1)}, u32[]{:S(2)}, u32[]{:S(2)}) %collective-permute-start.24) | collective-permute-done | bytes 1048608 | tf_op jit(solution)/shard_map/ppermute | solution.py:69
  457.4 1.2 add_bitcast_fusion
  458.8 1.0 add_convert_fusion.16
  460.3 1.2 slice.196
  463.1 1.7 collective-permute-start.31
  464.8 1.6 add_convert_fusion.5
  466.5 1.5 collective-permute-start.30
  468.1 1.1 collective-permute-start.29
  469.2 31.9 %shard_map.308 = (f32[200,128]{1,0:T(8,128)S(1)}, f32[128,128]{1,0:T(8,128)S(1)}) custom-call(f32[200,128]{1,0:T(8,128)S(1)} %pad_bitcast_fusion.vec_ref, bf16[4,128,128]{2,1,0:T(8,128)(2,1)S(1)} %reshape.494.slot_ref), custom_call_target="tpu_custom_call" | custom-call | flops 17179869184 | bytes 1024 | tf_op jit(solution)/shard_map/pallas_call | solution.py:1031
  501.9 1.3 collective-permute-start.43
  504.2 2.0 fusion.29
  506.7 15.4 %shard_map.309 = f32[1,1016,1024]{2,1,0:T(8,128)} custom-call(s32[1]{0:T(128)} %bitcast.1.me_ref, bf16[1016,1024]{1,0:T(8,128)(2,1)} %bitcast.197, f32[1024,1024]{1,0:T(8,128)} %get-tuple-element.212.ghid_ref, bf16[1024,3072]{1,0:T(8,128)(2,1)} %w_ref.1, f32[1,1024]{1,0:T(1,128)} %get-tuple-element.320.refs_9_.gain_ref, ...), custom_call_target="tpu_custom_call" | custom-call | flops 17179869184 | bytes 1024 | tf_op jit(solution)/shard_map/pallas_call | solution.py:948
  522.3 1.1 pad_maximum_fusion.2
  523.4 1.6 maximum_convert_fusion.1
  525.0 1.9 collective-permute-done.34
  528.1 1.1 fusion.30
  533.5 8.3 %collective-permute-done.35 = bf16[1,1,1,128,768]{4,3,2,1,0:T(8,128)(2,1)S(1)} collective-permute-done((bf16[1,1,1,128,768]{4,3,2,1,0:T(8,128)(2,1)S(1)}, bf16[1,1,1,128,768]{4,3,2,1,0:T(8,128)(2,1)S(1)}, u32[]{:S(2)}, u32[]{:S(2)}) %collective-permute-start.35) | collective-permute-done | bytes 196640 | tf_op jit(solution)/shard_map/ppermute | solution.py:69
  542.5 1.2 collective-permute-start.38
  544.4 5.3 collective-permute-done.37
  549.6 3.3 collective-permute-done.38
  553.6 1.3 convert_element_type.281
  555.3 1.5 maximum_convert_fusion
  (278 shorter events, 40.1 us)
Async XLA Ops:
  0.6 49.3 %copy-start = (bf16[1024,8]{0,1:T(8,128)(2,1)S(1)}, bf16[1024,8]{0,1:T(8,128)(2,1)}, u32[]{:S(2)}) copy-start(bf16[1024,8]{0,1:T(8,128)(2,1)} %param.33) | copy-start | bytes 49156
  0.7 12.0 %collective-permute-start.1 = (bf16[1016,1024]{1,0:T(8,128)(2,1)}, bf16[1016,1024]{1,0:T(8,128)(2,1)}, u32[]{:S(2)}, u32[]{:S(2)}) collective-permute-start(bf16[1016,1024]{1,0:T(8,128)(2,1)} %bitcast.193), channel_id=1, source_target_pairs={{0,1},{1,0},{2,3},{3,2},{4,5},{5,4},{6,7},{7,6},{8,9},{9,8},{10,11... | collective-permute-start | bytes 6242312 | tf_op jit(solution)/shard_map/ppermute | solution.py:67
  1.2 48.6 %collective-permute-start = (bf16[1016,1024]{1,0:T(8,128)(2,1)}, bf16[1016,1024]{1,0:T(8,128)(2,1)S(1)}, u32[]{:S(2)}, u32[]{:S(2)}) collective-permute-start(bf16[1016,1024]{1,0:T(8,128)(2,1)} %bitcast.194), channel_id=1, source_target_pairs={{0,2},{1,3},{2,0},{3,1},{4,6},{5,7},{6,4},{7,5},{8,10},{9,11},{10,... | collective-permute-start | bytes 6242312 | tf_op jit(solution)/shard_map/ppermute | solution.py:67
  12.7 37.2 %copy-start.25 = (f32[1,2,8,1024]{3,2,1,0:T(8,128)S(1)}, f32[1,2,8,1024]{3,2,1,0:T(8,128)}, u32[]{:S(2)}) copy-start(f32[1,2,8,1024]{3,2,1,0:T(8,128)} %param.35) | copy-start | bytes 196612
  49.8 4.3 collective-permute-start.2
  66.6 47.9 %copy-start.38 = (s32[1,8]{1,0:T(1,128)S(1)}, s32[1,8]{1,0:T(1,128)}, u32[]{:S(2)}) copy-start(s32[1,8]{1,0:T(1,128)} %param.19) | copy-start | bytes 100
  66.6 70.7 %copy-start.43 = (s32[1,8]{1,0:T(1,128)S(1)}, s32[1,8]{1,0:T(1,128)}, u32[]{:S(2)}) copy-start(s32[1,8]{1,0:T(1,128)} %param.20) | copy-start | bytes 100
  66.6 71.6 %copy-start.36 = (f32[8]{0:T(128)S(1)}, f32[8]{0:T(128)}, u32[]{:S(2)}) copy-start(f32[8]{0:T(128)} %param.34) | copy-start | bytes 100
  66.6 72.1 %copy-start.32 = (f32[1024]{0:T(1024)S(1)}, f32[1024]{0:T(1024)}, u32[]{:S(2)}) copy-start(f32[1024]{0:T(1024)} %param.24) | copy-start | bytes 12292
  66.6 72.1 %copy-start.33 = (f32[1024]{0:T(1024)S(1)}, f32[1024]{0:T(1024)}, u32[]{:S(2)}) copy-start(f32[1024]{0:T(1024)} %param.28) | copy-start | bytes 12292
  66.6 72.1 %copy-start.34 = (f32[1024]{0:T(1024)S(1)}, f32[1024]{0:T(1024)}, u32[]{:S(2)}) copy-start(f32[1024]{0:T(1024)} %param.32) | copy-start | bytes 12292
  110.7 30.8 %collective-permute-start.6 = (bf16[1024,256]{1,0:T(8,128)(2,1)}, bf16[1024,256]{1,0:T(8,128)(2,1)S(1)}, u32[]{:S(2)}, u32[]{:S(2)}) collective-permute-start(bf16[1024,256]{1,0:T(8,128)(2,1)} %get-tuple-element.143), channel_id=1, source_target_pairs={{0,1},{1,0},{2,3},{3,2},{4,5},{5,4},{6,7},{7,6},{8,9},{9,8},{10,11... | collective-permute-start | bytes 1572872 | tf_op jit(solution)/shard_map/ppermute | solution.py:67
  110.9 30.6 %collective-permute-start.7 = (bf16[1024,256]{1,0:T(8,128)(2,1)}, bf16[1024,256]{1,0:T(8,128)(2,1)S(1)}, u32[]{:S(2)}, u32[]{:S(2)}) collective-permute-start(bf16[1024,256]{1,0:T(8,128)(2,1)} %get-tuple-element.144), channel_id=1, source_target_pairs={{0,2},{1,3},{2,0},{3,1},{4,6},{5,7},{6,4},{7,5},{8,10},{9,11},{10,... | collective-permute-start | bytes 1572872 | tf_op jit(solution)/shard_map/ppermute | solution.py:67
  112.7 28.8 %collective-permute-start.8 = (bf16[1024,256]{1,0:T(8,128)(2,1)}, bf16[1024,256]{1,0:T(8,128)(2,1)S(1)}, u32[]{:S(2)}, u32[]{:S(2)}) collective-permute-start(bf16[1024,256]{1,0:T(8,128)(2,1)} %get-tuple-element.145), channel_id=1, source_target_pairs={{0,3},{1,2},{2,1},{3,0},{4,7},{5,6},{6,5},{7,4},{8,11},{9,10},{10,... | collective-permute-start | bytes 1572872 | tf_op jit(solution)/shard_map/ppermute | solution.py:67
  112.7 24.6 %collective-permute-start.4 = (bf16[2,8192]{1,0:T(2,128)(2,1)S(1)}, bf16[2,8192]{1,0:T(2,128)(2,1)S(1)}, u32[]{:S(2)}, u32[]{:S(2)}) collective-permute-start(bf16[2,8192]{1,0:T(2,128)(2,1)S(1)} %bitcast.170), channel_id=1, source_target_pairs={{0,2},{1,3},{2,0},{3,1},{4,6},{5,7},{6,4},{7,5},{8,10},{9,11},{10,... | collective-permute-start | bytes 98312 | tf_op jit(solution)/shard_map/ppermute | solution.py:67
  114.5 26.0 %collective-permute-start.3 = (bf16[2,8192]{1,0:T(2,128)(2,1)S(1)}, bf16[2,8192]{1,0:T(2,128)(2,1)S(1)}, u32[]{:S(2)}, u32[]{:S(2)}) collective-permute-start(bf16[2,8192]{1,0:T(2,128)(2,1)S(1)} %bitcast.171), channel_id=1, source_target_pairs={{0,1},{1,0},{2,3},{3,2},{4,5},{5,4},{6,7},{7,6},{8,9},{9,8},{10,11... | collective-permute-start | bytes 98312 | tf_op jit(solution)/shard_map/ppermute | solution.py:67
  137.3 3.2 collective-permute-start.5
  243.3 14.2 %copy-start.28 = (f32[1024,1]{0,1:T(1,128)S(1)}, f32[1024,1]{0,1:T(1,128)}, u32[]{:S(2)}) copy-start(f32[1024,1]{0,1:T(1,128)} %get-tuple-element.321) | copy-start | bytes 12292
  243.3 15.2 %copy-start.27 = (f32[1024,1]{0,1:T(1,128)S(1)}, f32[1024,1]{0,1:T(1,128)}, u32[]{:S(2)}) copy-start(f32[1024,1]{0,1:T(1,128)} %get-tuple-element.305) | copy-start | bytes 12292
  243.3 19.3 %copy-start.19 = (f32[1024,64]{1,0:T(8,128)S(1)}, f32[1024,64]{1,0:T(8,128)}, u32[]{:S(2)}) copy-start(f32[1024,64]{1,0:T(8,128)} %get-tuple-element.198) | copy-start | bytes 786436
  257.1 6.6 %copy-start.44 = (f32[1,64]{1,0:T(1,128)S(1)}, f32[1,64]{1,0:T(1,128)}, u32[]{:S(2)}) copy-start(f32[1,64]{1,0:T(1,128)} %get-tuple-element.201) | copy-start | bytes 772
  257.1 7.9 %copy-start.22 = (f32[64,1024]{1,0:T(8,128)S(1)}, f32[64,1024]{1,0:T(8,128)}, u32[]{:S(2)}) copy-start(f32[64,1024]{1,0:T(8,128)} %get-tuple-element.202) | copy-start | bytes 786436
  257.1 23.3 %collective-permute-start.13 = (bf16[4096,512]{1,0:T(8,128)(2,1)}, bf16[4096,512]{1,0:T(8,128)(2,1)}, u32[]{:S(2)}, u32[]{:S(2)}) collective-permute-start(bf16[4096,512]{1,0:T(8,128)(2,1)} %get-tuple-element.159.refs_0_), channel_id=1, source_target_pairs={{0,1},{1,0},{2,3},{3,2},{4,5},{5,4},{6,7},{7,6},{8,9},{9,8},{10,11... | collective-permute-start | bytes 12582920 | tf_op jit(solution)/shard_map/ppermute | solution.py:67
  258.5 7.1 %copy-start.29 = (f32[1,4096]{1,0:T(1,128)S(1)}, f32[1,4096]{1,0:T(1,128)}, u32[]{:S(2)}) copy-start(f32[1,4096]{1,0:T(1,128)} %get-tuple-element.196) | copy-start | bytes 49156
  258.5 7.1 %copy-start.26 = (f32[8,1024]{1,0:T(8,128)S(1)}, f32[8,1024]{1,0:T(8,128)}, u32[]{:S(2)}) copy-start(f32[8,1024]{1,0:T(8,128)} %get-tuple-element.197) | copy-start | bytes 98308
  259.5 20.8 %collective-permute-start.12 = (bf16[1024,1024]{1,0:T(8,128)(2,1)}, bf16[1024,1024]{1,0:T(8,128)(2,1)S(1)}, u32[]{:S(2)}, u32[]{:S(2)}) collective-permute-start(bf16[1024,1024]{1,0:T(8,128)(2,1)} %get-tuple-element.156.refs_0_), channel_id=1, source_target_pairs={{0,1},{1,0},{2,3},{3,2},{4,5},{5,4},{6,7},{7,6},{8,9},{9,8},{10,11... | collective-permute-start | bytes 6291464 | tf_op jit(solution)/shard_map/ppermute | solution.py:67
  260.4 28.6 %collective-permute-start.10 = (bf16[1024,128]{1,0:T(8,128)(2,1)}, bf16[1024,128]{1,0:T(8,128)(2,1)}, u32[]{:S(2)}, u32[]{:S(2)}) collective-permute-start(bf16[1024,128]{1,0:T(8,128)(2,1)} %get-tuple-element.148), channel_id=1, source_target_pairs={{0,2},{1,3},{2,0},{3,1},{4,6},{5,7},{6,4},{7,5},{8,10},{9,11},{10,... | collective-permute-start | bytes 786440 | tf_op jit(solution)/shard_map/ppermute | solution.py:67
  262.1 28.7 %collective-permute-start.11 = (bf16[1024,128]{1,0:T(8,128)(2,1)}, bf16[1024,128]{1,0:T(8,128)(2,1)}, u32[]{:S(2)}, u32[]{:S(2)}) collective-permute-start(bf16[1024,128]{1,0:T(8,128)(2,1)} %get-tuple-element.149), channel_id=1, source_target_pairs={{0,3},{1,2},{2,1},{3,0},{4,7},{5,6},{6,5},{7,4},{8,11},{9,10},{10,... | collective-permute-start | bytes 786440 | tf_op jit(solution)/shard_map/ppermute | solution.py:67
  262.1 28.7 %collective-permute-start.9 = (bf16[1024,128]{1,0:T(8,128)(2,1)}, bf16[1024,128]{1,0:T(8,128)(2,1)}, u32[]{:S(2)}, u32[]{:S(2)}) collective-permute-start(bf16[1024,128]{1,0:T(8,128)(2,1)} %get-tuple-element.147), channel_id=1, source_target_pairs={{0,1},{1,0},{2,3},{3,2},{4,5},{5,4},{6,7},{7,6},{8,9},{9,8},{10,11... | collective-permute-start | bytes 786440 | tf_op jit(solution)/shard_map/ppermute | solution.py:67
  280.3 56.5 %collective-permute-start.16 = (bf16[1024,2048]{1,0:T(8,128)(2,1)}, bf16[1024,2048]{1,0:T(8,128)(2,1)}, u32[]{:S(2)}, u32[]{:S(2)}) collective-permute-start(bf16[1024,2048]{1,0:T(8,128)(2,1)} %get-tuple-element.162.refs_6_), channel_id=1, source_target_pairs={{0,1},{1,0},{2,3},{3,2},{4,5},{5,4},{6,7},{7,6},{8,9},{9,8},{10,11... | collective-permute-start | bytes 12582920 | tf_op jit(solution)/shard_map/ppermute | solution.py:67
  280.4 84.2 %collective-permute-start.21 = (bf16[1024,128]{1,0:T(8,128)(2,1)}, bf16[1024,128]{1,0:T(8,128)(2,1)}, u32[]{:S(2)}, u32[]{:S(2)}) collective-permute-start(bf16[1024,128]{1,0:T(8,128)(2,1)} %get-tuple-element.178), channel_id=1, source_target_pairs={{0,1},{1,0},{2,3},{3,2},{4,5},{5,4},{6,7},{7,6},{8,9},{9,8},{10,11... | collective-permute-start | bytes 786440 | tf_op jit(solution)/shard_map/ppermute | solution.py:67
  289.0 83.7 %collective-permute-start.22 = (bf16[1024,128]{1,0:T(8,128)(2,1)}, bf16[1024,128]{1,0:T(8,128)(2,1)}, u32[]{:S(2)}, u32[]{:S(2)}) collective-permute-start(bf16[1024,128]{1,0:T(8,128)(2,1)} %get-tuple-element.179), channel_id=1, source_target_pairs={{0,2},{1,3},{2,0},{3,1},{4,6},{5,7},{6,4},{7,5},{8,10},{9,11},{10,... | collective-permute-start | bytes 786440 | tf_op jit(solution)/shard_map/ppermute | solution.py:67
  290.8 47.7 %collective-permute-start.15 = (bf16[2,1,2,512,512]{4,3,2,1,0:T(8,128)(2,1)}, bf16[2,1,2,512,512]{4,3,2,1,0:T(8,128)(2,1)}, u32[]{:S(2)}, u32[]{:S(2)}) collective-permute-start(bf16[2,1,2,512,512]{4,3,2,1,0:T(8,128)(2,1)} %constant_dynamic-slice_fusion.11), channel_id=1, source_target_pairs={{0,8},{4,12},{8,0},{12,4},{16,24},{20,28},{24,16},{28,20},{1,9},{5... | collective-permute-start | bytes 6291464 | tf_op jit(solution)/shard_map/ppermute | solution.py:69
  290.8 46.0 %collective-permute-start.14 = (bf16[2,2,1,128,1024]{4,3,2,1,0:T(8,128)(2,1)S(1)}, bf16[2,2,1,128,1024]{4,3,2,1,0:T(8,128)(2,1)}, u32[]{:S(2)}, u32[]{:S(2)}) collective-permute-start(bf16[2,2,1,128,1024]{4,3,2,1,0:T(8,128)(2,1)S(1)} %constant_dynamic-slice_fusion.12), channel_id=1, source_target_pairs={{0,4},{4,0},{8,12},{12,8},{16,20},{20,16},{24,28},{28,24},{1,5},{5... | collective-permute-start | bytes 3145736 | tf_op jit(solution)/shard_map/ppermute | solution.py:69
  293.6 44.8 %copy-start.9 = (bf16[1024,1024]{1,0:T(8,128)(2,1)S(1)}, bf16[1024,1024]{1,0:T(8,128)(2,1)}, u32[]{:S(2)}) copy-start(bf16[1024,1024]{1,0:T(8,128)(2,1)} %copy-done.8) | copy-start | bytes 6291460
  336.8 36.2 %collective-permute-start.23 = (bf16[1024,128]{1,0:T(8,128)(2,1)}, bf16[1024,128]{1,0:T(8,128)(2,1)}, u32[]{:S(2)}, u32[]{:S(2)}) collective-permute-start(bf16[1024,128]{1,0:T(8,128)(2,1)} %get-tuple-element.180), channel_id=1, source_target_pairs={{0,3},{1,2},{2,1},{3,0},{4,7},{5,6},{6,5},{7,4},{8,11},{9,10},{10,... | collective-permute-start | bytes 786440 | tf_op jit(solution)/shard_map/ppermute | solution.py:67
  336.8 80.3 %collective-permute-start.20 = (bf16[2,1024,384]{2,1,0:T(8,128)(2,1)}, bf16[2,1024,384]{2,1,0:T(8,128)(2,1)}, u32[]{:S(2)}, u32[]{:S(2)}) collective-permute-start(bf16[2,1024,384]{2,1,0:T(8,128)(2,1)} %get-tuple-element.176.refs_1_), channel_id=1, source_target_pairs={{0,2},{1,3},{2,0},{3,1},{4,6},{5,7},{6,4},{7,5},{8,10},{9,11},{10,... | collective-permute-start | bytes 4718600 | tf_op jit(solution)/shard_map/ppermute | solution.py:67
  340.9 76.2 %collective-permute-start.19 = (bf16[2,1,1,128,1024]{4,3,2,1,0:T(8,128)(2,1)}, bf16[2,1,1,128,1024]{4,3,2,1,0:T(8,128)(2,1)S(1)}, u32[]{:S(2)}, u32[]{:S(2)}) collective-permute-start(bf16[2,1,1,128,1024]{4,3,2,1,0:T(8,128)(2,1)} %constant_dynamic-slice_fusion.8), channel_id=1, source_target_pairs={{0,8},{4,12},{8,0},{12,4},{16,24},{20,28},{24,16},{28,20},{1,9},{5... | collective-permute-start | bytes 1572872 | tf_op jit(solution)/shard_map/ppermute | solution.py:69
  343.5 6.8 %copy-start.4 = (bf16[2,1,2,512,512]{4,3,2,1,0:T(8,128)(2,1)}, bf16[2,1,2,512,512]{4,3,2,1,0:T(8,128)(2,1)S(1)}, u32[]{:S(2)}) copy-start(bf16[2,1,2,512,512]{4,3,2,1,0:T(8,128)(2,1)S(1)} %add_convert_fusion.3.refs_6_) | copy-start | bytes 6291460
  364.6 54.7 %collective-permute-start.18 = (bf16[1,1,2,512,512]{4,3,2,1,0:T(8,128)(2,1)}, bf16[1,1,2,512,512]{4,3,2,1,0:T(8,128)(2,1)}, u32[]{:S(2)}, u32[]{:S(2)}) collective-permute-start(bf16[1,1,2,512,512]{4,3,2,1,0:T(8,128)(2,1)} %constant_dynamic-slice_fusion.9), channel_id=1, source_target_pairs={{0,16},{4,20},{8,24},{12,28},{16,0},{20,4},{24,8},{28,12},{1,17},{... | collective-permute-start | bytes 3145736 | tf_op jit(solution)/shard_map/ppermute | solution.py:69
  372.7 47.9 %collective-permute-start.17 = (bf16[2,2,1,128,2048]{4,3,2,1,0:T(8,128)(2,1)}, bf16[2,2,1,128,2048]{4,3,2,1,0:T(8,128)(2,1)S(1)}, u32[]{:S(2)}, u32[]{:S(2)}) collective-permute-start(bf16[2,2,1,128,2048]{4,3,2,1,0:T(8,128)(2,1)} %constant_dynamic-slice_fusion.10), channel_id=1, source_target_pairs={{0,4},{4,0},{8,12},{12,8},{16,20},{20,16},{24,28},{28,24},{1,5},{5... | collective-permute-start | bytes 6291464 | tf_op jit(solution)/shard_map/ppermute | solution.py:69
  413.3 36.6 %collective-permute-start.25 = (bf16[2,1024,384]{2,1,0:T(8,128)(2,1)}, bf16[2,1024,384]{2,1,0:T(8,128)(2,1)}, u32[]{:S(2)}, u32[]{:S(2)}) collective-permute-start(bf16[2,1024,384]{2,1,0:T(8,128)(2,1)} %get-tuple-element.186.refs_1_), channel_id=1, source_target_pairs={{0,2},{1,3},{2,0},{3,1},{4,6},{5,7},{6,4},{7,5},{8,10},{9,11},{10,... | collective-permute-start | bytes 4718600 | tf_op jit(solution)/shard_map/ppermute | solution.py:67
  423.0 5.1 copy-start.6
  423.3 26.6 %collective-permute-start.27 = (bf16[1,1,1,128,1024]{4,3,2,1,0:T(8,128)(2,1)S(1)}, bf16[1,1,1,128,1024]{4,3,2,1,0:T(8,128)(2,1)}, u32[]{:S(2)}, u32[]{:S(2)}) collective-permute-start(bf16[1,1,1,128,1024]{4,3,2,1,0:T(8,128)(2,1)S(1)} %constant_dynamic-slice_fusion.5), channel_id=1, source_target_pairs={{0,16},{4,20},{8,24},{12,28},{16,0},{20,4},{24,8},{28,12},{1,17},{... | collective-permute-start | bytes 786440 | tf_op jit(solution)/shard_map/ppermute | solution.py:69
  427.8 22.1 %collective-permute-start.26 = (bf16[1,1,1,512,512]{4,3,2,1,0:T(8,128)(2,1)}, bf16[1,1,1,512,512]{4,3,2,1,0:T(8,128)(2,1)S(1)}, u32[]{:S(2)}, u32[]{:S(2)}) collective-permute-start(bf16[1,1,1,512,512]{4,3,2,1,0:T(8,128)(2,1)} %constant_dynamic-slice_fusion.6), channel_id=1, source_target_pairs={{0,4},{4,0},{8,12},{12,8},{16,20},{20,16},{24,28},{28,24},{1,5},{5... | collective-permute-start | bytes 1572872 | tf_op jit(solution)/shard_map/ppermute | solution.py:69
  428.2 29.2 %copy-start.18 = (f32[1024,2]{1,0:T(8,128)S(1)}, f32[1024,2]{1,0:T(8,128)}, u32[]{:S(2)}) copy-start(f32[1024,2]{1,0:T(8,128)} %get-tuple-element.199) | copy-start | bytes 24580
  428.2 29.2 %collective-permute-start.24 = (bf16[2,1,1,128,2048]{4,3,2,1,0:T(8,128)(2,1)S(1)}, bf16[2,1,1,128,2048]{4,3,2,1,0:T(8,128)(2,1)}, u32[]{:S(2)}, u32[]{:S(2)}) collective-permute-start(bf16[2,1,1,128,2048]{4,3,2,1,0:T(8,128)(2,1)S(1)} %constant_dynamic-slice_fusion.7), channel_id=1, source_target_pairs={{0,8},{4,12},{8,0},{12,4},{16,24},{20,28},{24,16},{28,20},{1,9},{5... | collective-permute-start | bytes 3145736 | tf_op jit(solution)/shard_map/ppermute | solution.py:69
  449.9 7.6 %copy-start.20 = (bf16[1,1,1,512,512]{4,3,2,1,0:T(8,128)(2,1)}, bf16[1,1,1,512,512]{4,3,2,1,0:T(8,128)(2,1)S(1)}, u32[]{:S(2)}) copy-start(bf16[1,1,1,512,512]{4,3,2,1,0:T(8,128)(2,1)S(1)} %collective-permute-done.26) | copy-start | bytes 1572868
  459.9 41.2 %collective-permute-start.32 = (bf16[1,1,1,128,1024]{4,3,2,1,0:T(8,128)(2,1)S(1)}, bf16[1,1,1,128,1024]{4,3,2,1,0:T(8,128)(2,1)S(1)}, u32[]{:S(2)}, u32[]{:S(2)}) collective-permute-start(bf16[1,1,1,128,1024]{4,3,2,1,0:T(8,128)(2,1)S(1)} %add_convert_fusion.16), channel_id=1, source_target_pairs={{0,2},{1,3},{2,0},{3,1},{4,6},{5,7},{6,4},{7,5},{8,10},{9,11},{10,... | collective-permute-start | bytes 786440 | tf_op jit(solution)/shard_map/ppermute | solution.py:67
  462.2 39.0 %collective-permute-start.28 = (bf16[4,1024,384]{2,1,0:T(8,128)(2,1)S(1)}, bf16[4,1024,384]{2,1,0:T(8,128)(2,1)S(1)}, u32[]{:S(2)}, u32[]{:S(2)}) collective-permute-start(bf16[4,1024,384]{2,1,0:T(8,128)(2,1)S(1)} %pad_maximum_fusion), channel_id=1, source_target_pairs={{0,1},{1,0},{2,3},{3,2},{4,5},{5,4},{6,7},{7,6},{8,9},{9,8},{10,11... | collective-permute-start | bytes 9437192 | tf_op jit(solution)/shard_map/ppermute | solution.py:67
  463.1 38.0 %collective-permute-start.31 = (bf16[1,1,1,512,256]{4,3,2,1,0:T(8,128)(2,1)S(1)}, bf16[1,1,1,512,256]{4,3,2,1,0:T(8,128)(2,1)S(1)}, u32[]{:S(2)}, u32[]{:S(2)}) collective-permute-start(bf16[1,1,1,512,256]{4,3,2,1,0:T(8,128)(2,1)S(1)} %constant_dynamic-slice_fusion.3), channel_id=1, source_target_pairs={{0,2},{1,3},{2,0},{3,1},{4,6},{5,7},{6,4},{7,5},{8,10},{9,11},{10,... | collective-permute-start | bytes 786440 | tf_op jit(solution)/shard_map/ppermute | solution.py:67
  466.5 34.6 %collective-permute-start.30 = (bf16[1,1,1,128,2048]{4,3,2,1,0:T(8,128)(2,1)S(1)}, bf16[1,1,1,128,2048]{4,3,2,1,0:T(8,128)(2,1)S(1)}, u32[]{:S(2)}, u32[]{:S(2)}) collective-permute-start(bf16[1,1,1,128,2048]{4,3,2,1,0:T(8,128)(2,1)S(1)} %constant_dynamic-slice_fusion.4), channel_id=1, source_target_pairs={{0,16},{4,20},{8,24},{12,28},{16,0},{20,4},{24,8},{28,12},{1,17},{... | collective-permute-start | bytes 1572872 | tf_op jit(solution)/shard_map/ppermute | solution.py:69
  468.1 33.0 %collective-permute-start.29 = (bf16[2,2,1,128,768]{4,3,2,1,0:T(8,128)(2,1)S(1)}, bf16[2,2,1,128,768]{4,3,2,1,0:T(8,128)(2,1)S(1)}, u32[]{:S(2)}, u32[]{:S(2)}) collective-permute-start(bf16[2,2,1,128,768]{4,3,2,1,0:T(8,128)(2,1)S(1)} %fusion.2), channel_id=1, source_target_pairs={{0,4},{4,0},{8,12},{12,8},{16,20},{20,16},{24,28},{28,24},{1,5},{5... | collective-permute-start | bytes 2359304 | tf_op jit(solution)/shard_map/ppermute | solution.py:69
  501.2 20.9 %collective-permute-start.41 = (bf16[512,256]{1,0:T(8,128)(2,1)S(1)}, bf16[512,256]{1,0:T(8,128)(2,1)S(1)}, u32[]{:S(2)}, u32[]{:S(2)}) collective-permute-start(bf16[512,256]{1,0:T(8,128)(2,1)S(1)} %bitcast.156), channel_id=1, source_target_pairs={{0,1},{1,0},{2,3},{3,2},{4,5},{5,4},{6,7},{7,6},{8,9},{9,8},{10,11... | collective-permute-start | bytes 786440 | tf_op jit(solution)/shard_map/ppermute | solution.py:67
  501.3 20.9 %collective-permute-start.42 = (bf16[512,256]{1,0:T(8,128)(2,1)S(1)}, bf16[512,256]{1,0:T(8,128)(2,1)S(1)}, u32[]{:S(2)}, u32[]{:S(2)}) collective-permute-start(bf16[512,256]{1,0:T(8,128)(2,1)S(1)} %bitcast.157), channel_id=1, source_target_pairs={{0,2},{1,3},{2,0},{3,1},{4,6},{5,7},{6,4},{7,5},{8,10},{9,11},{10,... | collective-permute-start | bytes 786440 | tf_op jit(solution)/shard_map/ppermute | solution.py:67
  501.9 20.3 %collective-permute-start.43 = (bf16[512,256]{1,0:T(8,128)(2,1)S(1)}, bf16[512,256]{1,0:T(8,128)(2,1)}, u32[]{:S(2)}, u32[]{:S(2)}) collective-permute-start(bf16[512,256]{1,0:T(8,128)(2,1)S(1)} %bitcast.158), channel_id=1, source_target_pairs={{0,3},{1,2},{2,1},{3,0},{4,7},{5,6},{6,5},{7,4},{8,11},{9,10},{10,... | collective-permute-start | bytes 786440 | tf_op jit(solution)/shard_map/ppermute | solution.py:67
  503.6 23.3 %collective-permute-start.34 = (bf16[1,1,1,128,2048]{4,3,2,1,0:T(8,128)(2,1)S(1)}, bf16[1,1,1,128,2048]{4,3,2,1,0:T(8,128)(2,1)S(1)}, u32[]{:S(2)}, u32[]{:S(2)}) collective-permute-start(bf16[1,1,1,128,2048]{4,3,2,1,0:T(8,128)(2,1)S(1)} %add_convert_fusion.10), channel_id=1, source_target_pairs={{0,2},{1,3},{2,0},{3,1},{4,6},{5,7},{6,4},{7,5},{8,10},{9,11},{10,... | collective-permute-start | bytes 1572872 | tf_op jit(solution)/shard_map/ppermute | solution.py:67
  506.2 18.8 %collective-permute-start.33 = (bf16[2,1,1,128,768]{4,3,2,1,0:T(8,128)(2,1)S(1)}, bf16[2,1,1,128,768]{4,3,2,1,0:T(8,128)(2,1)S(1)}, u32[]{:S(2)}, u32[]{:S(2)}) collective-permute-start(bf16[2,1,1,128,768]{4,3,2,1,0:T(8,128)(2,1)S(1)} %constant_dynamic-slice_fusion.2), channel_id=1, source_target_pairs={{0,8},{4,12},{8,0},{12,4},{16,24},{20,28},{24,16},{28,20},{1,9},{5... | collective-permute-start | bytes 1179656 | tf_op jit(solution)/shard_map/ppermute | solution.py:69
  522.2 5.6 %collective-permute-start.39 = (bf16[128,1024]{1,0:T(8,128)(2,1)S(1)}, bf16[128,1024]{1,0:T(8,128)(2,1)S(1)}, u32[]{:S(2)}, u32[]{:S(2)}) collective-permute-start(bf16[128,1024]{1,0:T(8,128)(2,1)S(1)} %bitcast.154), channel_id=1, source_target_pairs={{0,1},{1,0},{2,3},{3,2},{4,5},{5,4},{6,7},{7,6},{8,9},{9,8},{10,11... | collective-permute-start | bytes 786440 | tf_op jit(solution)/shard_map/ppermute | solution.py:67
  527.1 27.8 %collective-permute-start.40 = (bf16[128,2048]{1,0:T(8,128)(2,1)S(1)}, bf16[128,2048]{1,0:T(8,128)(2,1)S(1)}, u32[]{:S(2)}, u32[]{:S(2)}) collective-permute-start(bf16[128,2048]{1,0:T(8,128)(2,1)S(1)} %get-tuple-element.286), channel_id=1, source_target_pairs={{0,1},{1,0},{2,3},{3,2},{4,5},{5,4},{6,7},{7,6},{8,9},{9,8},{10,11... | collective-permute-start | bytes 1572872 | tf_op jit(solution)/shard_map/ppermute | solution.py:67
  529.3 12.4 %collective-permute-start.35 = (bf16[1,1,1,128,768]{4,3,2,1,0:T(8,128)(2,1)S(1)}, bf16[1,1,1,128,768]{4,3,2,1,0:T(8,128)(2,1)S(1)}, u32[]{:S(2)}, u32[]{:S(2)}) collective-permute-start(bf16[1,1,1,128,768]{4,3,2,1,0:T(8,128)(2,1)S(1)} %constant_dynamic-slice_fusion.1), channel_id=1, source_target_pairs={{0,16},{4,20},{8,24},{12,28},{16,0},{20,4},{24,8},{28,12},{1,17},{... | collective-permute-start | bytes 589832 | tf_op jit(solution)/shard_map/ppermute | solution.py:69
  541.8 2.6 collective-permute-start.36
  541.9 7.7 %collective-permute-start.37 = (bf16[128,768]{1,0:T(8,128)(2,1)S(1)}, bf16[128,768]{1,0:T(8,128)(2,1)S(1)}, u32[]{:S(2)}, u32[]{:S(2)}) collective-permute-start(bf16[128,768]{1,0:T(8,128)(2,1)S(1)} %get-tuple-element.293), channel_id=1, source_target_pairs={{0,2},{1,3},{2,0},{3,1},{4,6},{5,7},{6,4},{7,5},{8,10},{9,11},{10,... | collective-permute-start | bytes 589832 | tf_op jit(solution)/shard_map/ppermute | solution.py:67
  542.5 10.4 %collective-permute-start.38 = (bf16[128,768]{1,0:T(8,128)(2,1)S(1)}, bf16[128,768]{1,0:T(8,128)(2,1)S(1)}, u32[]{:S(2)}, u32[]{:S(2)}) collective-permute-start(bf16[128,768]{1,0:T(8,128)(2,1)S(1)} %get-tuple-element.293), channel_id=1, source_target_pairs={{0,3},{1,2},{2,1},{3,0},{4,7},{5,6},{6,5},{7,4},{8,11},{9,10},{10,... | collective-permute-start | bytes 589832 | tf_op jit(solution)/shard_map/ppermute | solution.py:67
  (25 other events, 75.3 us)

commit v6 on v5

--- a/solution.py
+++ b/solution.py
@@ -323,11 +323,11 @@
     return lax.fori_loop(lo + 2 * pairs, hi, lambda kb, c: step(kb, 1, c), carry)
 
 
-def attend_kernel(count, heads, lo_ref, hi_ref, *refs):
+def attend_kernel(count, heads, start, held, lo_ref, hi_ref, *refs):
     q_ref, k_ref, vt_ref, imgq_ref, imgk_ref = refs[:5]
-    outs, (ot_ref, lse_ref) = refs[5 : 5 + count], refs[5 + count : 7 + count]
-    s_ref, qs_ref, acc_ref = refs[7 + count :]
-    block = pl.program_id(0)
+    refs = refs[5 + held :]
+    outs, (ot_ref, lse_ref), (s_ref, qs_ref, acc_ref) = refs[:count], refs[count : count + 2], refs[count + 2 :]
+    block = pl.program_id(0) + start
     lo, hi = lo_ref[block], hi_ref[block]
     per_head(qs_ref, q_ref[...], heads)
     imgq = imgq_ref[...]
@@ -377,29 +377,32 @@
         outs[d][...] = out[d * (BLK // count) : (d + 1) * (BLK // count)]
 
 
-def attend_call(q, k, vt, imgq, imgk, lo, hi, count):
+def attend_call(q, k, vt, imgq, imgk, lo, hi, count, part, held=()):
     blocks, features = vt.shape[0], q.shape[1]
     heads = features // HEAD
     piece_rows = BLK // count
+    steps = blocks // 2
+    start = part * steps
     whole = lambda a: pl.BlockSpec(
         a.shape, lambda b, *_: (0,) * a.ndim, pipeline_mode=pl.Buffered(1)
     )
     return pl.pallas_call(
-        functools.partial(attend_kernel, count, heads),
+        functools.partial(attend_kernel, count, heads, start, len(held)),
         grid_spec=pltpu.PrefetchScalarGridSpec(
             num_scalar_prefetch=2,
-            grid=(blocks,),
+            grid=(steps,),
             in_specs=[
-                pl.BlockSpec((BLK, features), lambda b, *_: (b, 0)),
+                pl.BlockSpec((BLK, features), lambda b, *_: (b + start, 0)),
                 whole(k),
                 whole(vt),
-                pl.BlockSpec((1, BLK), lambda b, *_: (0, b)),
+                pl.BlockSpec((1, BLK), lambda b, *_: (0, b + start)),
                 whole(imgk),
-            ],
+            ]
+            + [ANYWHERE] * len(held),
             out_specs=[pl.BlockSpec((piece_rows, features), lambda b, *_: (b, 0))] * count
             + [
-                pl.BlockSpec((1, features, BLK), lambda b, *_: (b, 0, 0)),
-                pl.BlockSpec((8, BLK), lambda b, *_: (0, b)),
+                pl.BlockSpec((1, features, BLK), lambda b, *_: (b + start, 0, 0)),
+                pl.BlockSpec((8, BLK), lambda b, *_: (0, b + start)),
             ],
             scratch_shapes=[
                 pltpu.VMEM((blocks, BLK, heads * BLK), f32),
@@ -407,18 +410,19 @@
                 pltpu.VMEM((features, BLK), f32),
             ],
         ),
-        out_shape=[jax.ShapeDtypeStruct((blocks * piece_rows, features), bf16)] * count
+        out_shape=[jax.ShapeDtypeStruct((steps * piece_rows, features), bf16)] * count
         + [
             jax.ShapeDtypeStruct((blocks, features, BLK), f32),
             jax.ShapeDtypeStruct((8, blocks * BLK), f32),
         ],
+        input_output_aliases={7 + i: count + i for i in range(len(held))},
         compiler_params=params(),
         cost_estimate=pl.CostEstimate(
-            flops=10 * (blocks * BLK) ** 2 * features,
-            bytes_accessed=2 * blocks * BLK * features * 8,
+            flops=5 * (blocks * BLK) ** 2 * features,
+            bytes_accessed=2 * blocks * BLK * features * 6,
             transcendentals=0,
         ),
-    )(lo, hi, q, k, vt, imgq, imgk)
+    )(lo, hi, q, k, vt, imgq, imgk, *held)
 
 
 def attend_back_kernel(count, heads, first, waits, lo_ref, hi_ref, *refs):
@@ -575,8 +579,8 @@
         out_bias_ref,
         pooled_grad_ref,
     ) = refs[:11]
-    attended = refs[11 : 11 + count]
-    at = 11 + count
+    upper, lower = refs[11 : 11 + count], refs[11 + count : 11 + 2 * count]
+    at = 11 + 2 * count
     (
         n2_ref,
         gated_ref,
@@ -609,7 +613,10 @@
 
     position = lax.broadcasted_iota(jnp.int32, (rows, 1), 0) + step * rows
     tok = jnp.where(position < local_rows, tok_ref[...].astype(f32), 0.0)
-    low = jnp.concatenate([ref[...] for ref in attended], axis=1)
+    early = step < pl.num_programs(0) // 2
+    low = jnp.concatenate(
+        [jnp.where(early, a[...], b[...]) for a, b in zip(upper, lower)], axis=1
+    )
     hidden = tok + matmul(low, w_out_ref[...]) + vec(0)
     hid_ref[...] = hidden
     unit, _ = norm_parts(hidden)
@@ -685,12 +692,14 @@
 
 
 def rows_call(tok, img, attended, w_out, w_up, w_down, learn_in, learn_out, vecs, up_bias, out_bias, pooled_grad, splits):
-    count, (rows, features) = len(attended), attended[0].shape
+    count, (rows, features) = len(attended) // 2, attended[0].shape
+    rows *= 2
     local_rows, width = tok.shape
     hidden_units = w_up.shape[1]
     inner = learn_in.shape[1]
     spread = learn_out.shape[1]
-    block = min(ROW_BLOCK, rows)
+    block = min(ROW_BLOCK, rows // 2)
+    half = rows // block // 2
     chunk = UP_BLOCK
     wide = features // splits
     once = lambda a: pl.BlockSpec(a.shape, lambda i: (0,) * a.ndim, pipeline_mode=pl.Buffered(1))
@@ -710,7 +719,8 @@
         grid=(rows // block,),
         in_specs=[by_rows(width), by_rows(1)]
         + [once(a) for a in resident]
-        + [by_rows(features)] * count,
+        + [pl.BlockSpec((block, features), lambda i: (jnp.minimum(i, half - 1), 0))] * count
+        + [pl.BlockSpec((block, features), lambda i: (jnp.maximum(i - half, 0), 0))] * count,
         out_specs=[by_rows(n) for n in lows]
         + [by_rows(width)]
         + [by_rows(wide)] * (count * splits)
@@ -818,15 +828,18 @@
 
 def small_grad_kernel(count, me_ref, *refs):
     n3_ref, glearn_ref, ghid_ref, inner_ref, glogit_ref = refs[:5]
-    attended = refs[5 : 5 + count]
-    keep_ref, send_ref, lout_ref, learn_ref, wout_ref = refs[5 + count :]
+    attended = refs[5 : 5 + 2 * count]
+    keep_ref, send_ref, lout_ref, learn_ref, wout_ref = refs[5 + 2 * count :]
+    half = attended[0].shape[0]
     learn_ref[...] = tn(n3_ref[...], glearn_ref[...]).astype(bf16)
     lout_ref[...] = tn(inner_ref[...], glogit_ref[...])
     features = attended[0].shape[1]
     for d in range(count):
         owner = jnp.bitwise_xor(me_ref[0], d)
         to = pl.ds(pl.multiple_of(owner * features, features), features)
-        wout_ref[to, :] = tn(attended[d][...], ghid_ref[...]).astype(bf16)
+        part = tn(attended[d][...], ghid_ref[:half])
+        part = part + tn(attended[count + d][...], ghid_ref[half:])
+        wout_ref[to, :] = part.astype(bf16)
     first = me_ref[0] % 2 == 0
 
     @pl.when(first)
@@ -847,7 +860,7 @@
     lout = jax.ShapeDtypeStruct((inner.shape[1], glogit.shape[1]), f32)
     once = lambda a: pl.BlockSpec(a.shape, lambda j, m: (0, 0), pipeline_mode=pl.Buffered(1))
     return pl.pallas_call(
-        functools.partial(small_grad_kernel, len(attended)),
+        functools.partial(small_grad_kernel, len(attended) // 2),
         grid_spec=pltpu.PrefetchScalarGridSpec(
             num_scalar_prefetch=1,
             grid=(1,),
@@ -1118,8 +1131,11 @@
     q, k, v = (a.reshape(-1, features) for a in (q, k, v))
     slot_grads = behind(cotangent[0].reshape(slots_here, LT * width).astype(bf16), [lo, unit])
     grads_in = gather_pieces(slot_grads, row_count)
-    *attended, ot, lse = attend_call(q, k, vt, imgq, imgk, lo, hi, row_count)
-    attended = send_pieces(attended)
+    *upper, ot, lse = attend_call(q, k, vt, imgq, imgk, lo, hi, row_count, 0)
+    upper = send_pieces(upper)
+    *lower, ot, lse = attend_call(q, k, vt, imgq, imgk, lo, hi, row_count, 1, (ot, lse))
+    upper[1:], ot, lse, lower = lax.optimization_barrier((upper[1:], ot, lse, lower))
+    attended = upper + send_pieces(lower)
 
     slot_rel = ((owner[0] // slots_here) ^ device) * slots_here + owner[0] % slots_here
     select = (slot_rel[:, None] == jnp.arange(IMGS, dtype=jnp.int32)[None, :]).astype(f32)

time: 565 us -> 554 us (0.981)
  waiting for transfers between devices: 89.1 us -> 73.3 us
    ppermute x32 -> x35, waiting for transfers between devices: 68.9 us -> 51.9 us  [jump(): return lax.ppermute(value, 'row', [(i, i ^ row_mask) for i in range(rows)])]
    pallas_call x2 -> x3, Pallas kernels: 55.6 us -> 59.4 us  [the longest x2 47.8 us: attend_call(): pl.pallas_call(functools.partial(attend_kernel, count, heads, start, len(...]
    ppermute x32 -> x35, starting transfers between devices: 20.5 us -> 23.6 us  [jump(): return lax.ppermute(value, 'row', [(i, i ^ row_mask) for i in range(rows)])]
  transfers between devices with their start and end apart: 44 -> 47, of which waited for: 12 -> 12; matrix products, arithmetic and copies ran while one was open for 13% -> 13% of each run, Pallas kernels for 31% -> 40%
where the time goes in v6:
time: 554 us; the launch traced here: 543 us
  Pallas kernels  347 us (63%)
  waiting for transfers between devices  73.3 us (13%)
  starting transfers between devices  39.9 us (7%)
  local copies, waits for them, and re-layouts  39.6 us (7%)
  other arithmetic  39.5 us (7%)
    pallas_call x1, Pallas kernels, rows_call(): pl.pallas_call(functools.partial(rows_kernel, count, splits, local_rows),...  89.5 us
    pallas_call x2, Pallas kernels, attend_back_call(): pl.pallas_call(functools.partial(attend_back_kernel, count, heads, split...  79.4 us
    ppermute x35, waiting for transfers between devices, jump(): return lax.ppermute(value, 'row', [(i, i ^ row_mask) for i in range(rows)])  51.9 us
    pallas_call x2, Pallas kernels, attend_call(): pl.pallas_call(functools.partial(attend_kernel, count, heads, start, len(...  47.8 us
    pallas_call x1, Pallas kernels, vectors_call(): pl.pallas_call(functools.partial(vectors_kernel, count, row_bits, img_bit...  29.6 us
    pallas_call x2, Pallas kernels, qkv_call(): pl.pallas_call(functools.partial(qkv_kernel, count, splits, local_rows, f...  24.9 us
    convert_element_type x16, other arithmetic, finish(): return tree([v.astype(f32) for v in values]).astype(bf16)  23.8 us
    ppermute x35, starting transfers between devices, jump(): return lax.ppermute(value, 'row', [(i, i ^ row_mask) for i in range(rows)])  23.6 us
  transfers between devices with their start and end apart: 47, of which 12 were waited for; matrix products, arithmetic and copies ran while one was open for 13% of the time, Pallas kernels for 40%

profile of v6, /device:TPU:0, one launch (start us, length us, event | category | flops | bytes accessed | tf_op | source)
XLA Modules:
  0.0 542.7 jit_solution(16262872714797062475)
XLA Ops:
  1.2 2.6 collective-permute-start
  6.7 1.7 constant_dynamic-slice_fusion.16
  8.4 1.5 pad_maximum_fusion.1.refs_2_
  9.9 1.3 constant_dynamic-slice_fusion.17.refs_8_
  12.7 12.5 %shard_map.297 = (bf16[4,1024,1024]{2,1,0:T(8,128)(2,1)}, bf16[16,2,128,256]{3,2,1,0:T(8,128)(2,1)}, bf16[16,2,128,256]{3,2,1,0:T(8,128)(2,1)}, bf16[16,2,128,25...) custom-call(s32[1]{0:T(128)} %bitcast.1.me_ref, bf16[1016,1024]{1,0:T(8,128)(2,1)} %bitcast.195, ...), custom_call_target="tpu_custom_call" | custom-call | flops 19327352832 | bytes 13631488 | tf_op jit(solution)/shard_map/pallas_call | solution.py:282
  25.2 24.6 %collective-permute-done.refs_0_ = bf16[1016,1024]{1,0:T(8,128)(2,1)S(1)} collective-permute-done((bf16[1016,1024]{1,0:T(8,128)(2,1)}, bf16[1016,1024]{1,0:T(8,128)(2,1)S(1)}, u32[]{:S(2)}, u32[]{:S(2)}) %collective-permute-start) | collective-permute-done | bytes 2080800 | tf_op jit(solution)/shard_map/ppermute | solution.py:67
  49.9 2.0 copy.77.refs_4_.refs_14_.refs_12_
  51.9 2.2 collective-permute-done.2.refs_1_
  54.1 12.5 %shard_map.298 = (bf16[4,1024,1024]{2,1,0:T(8,128)(2,1)}, bf16[16,2,128,256]{3,2,1,0:T(8,128)(2,1)}, bf16[16,2,128,256]{3,2,1,0:T(8,128)(2,1)}, bf16[16,2,128,25...) custom-call(s32[1]{0:T(128)} %bitcast.1.me_ref, ...), custom_call_target="tpu_custom_call", output_to_operand_aliasing={{0}: (12, {}), {1}: (13, {}), {2}: (14, {}), {3}: (15, {}),... | custom-call | flops 19327352832 | bytes 13631488 | tf_op jit(solution)/shard_map/pallas_call | solution.py:282
  66.6 1.8 collective-permute-start.4
  68.4 22.3 %shard_map.299 = (bf16[512,256]{1,0:T(8,128)(2,1)}, bf16[512,256]{1,0:T(8,128)(2,1)}, bf16[512,256]{1,0:T(8,128)(2,1)}, bf16[512,256]{1,0:T(8,128)(2,1)}, f32[16,256,256]{2,1,0:T(8,128)}, /*index=5*/f32[8,4096]{1,0:T(8,128)}) custom-call(s32[16]{0:T(128)} %get-tuple-element.139.lo_ref, s32[16]{0:T(128)} %get-tuple-element.140.hi_ref, ...), custom_call_target="tpu_custom_call" | custom-call | flops 21474836480 | bytes 12582912 | tf_op jit(solution)/shard_map/pallas_call | solution.py:389
  91.6 1.2 collective-permute-start.8
  92.8 25.5 %shard_map.300 = (bf16[512,256]{1,0:T(8,128)(2,1)}, bf16[512,256]{1,0:T(8,128)(2,1)}, bf16[512,256]{1,0:T(8,128)(2,1)}, bf16[512,256]{1,0:T(8,128)(2,1)}, f32[16,256,256]{2,1,0:T(8,128)}, /*index=5*/f32[8,4096]{1,0:T(8,128)}) custom-call(s32[16]{0:T(128)} %get-tuple-element.139.lo_ref, ...), custom_call_target="tpu_custom_call", output_to_operand_aliasing={{4}: (7, {}), {5}: (8, {})} | custom-call | flops 21474836480 | bytes 12582912 | tf_op jit(solution)/shard_map/pallas_call | solution.py:389
  119.4 1.1 collective-permute-start.11
  125.5 3.1 collective-permute-done.10.refs_17_.refs_11_
  128.5 3.8 collective-permute-done.11.refs_18_.refs_12_
  133.1 89.5 %shard_map.301 = (bf16[1024,1024]{1,0:T(8,128)(2,1)}, bf16[1024,4096]{1,0:T(8,128)(2,1)}, bf16[1024,4096]{1,0:T(8,128)(2,1)}, bf16[1024,1024]{1,0:T(8,128)(2,1)}...) custom-call(bf16[1016,1024]{1,0:T(8,128)(2,1)} %bitcast.196, ...), custom_call_target="tpu_custom_call" | custom-call | flops 42949672960 | bytes 58720256 | tf_op jit(solution)/shard_map/pallas_call | solution.py:717
  222.6 11.5 %shard_map.302 = (bf16[1024,1024]{1,0:T(8,128)(2,1)}, bf16[1024,1024]{1,0:T(8,128)(2,1)}, f32[1024,64]{1,0:T(8,128)}) custom-call(s32[1]{0:T(128)} %bitcast.1.me_ref, bf16[1024,1024]{1,0:T(8,128)(2,1)} %get-tuple-element.180.refs_0_, bf16[1024,1024]{1,0:T(8,128)(2,1)} %get-tuple-element.181.refs_1_, bf16[1024,1024]{1,0:T(8,128)(2,1)} %get-tuple-element.182.refs_2_, ...), custom_call_target="tpu_custom_call" | custom-call | flops 6442450944 | bytes 20971520 | tf_op jit(solution)/shard_map/pallas_call | solution.py:862
  234.2 13.9 %shard_map.303 = (bf16[4096,512]{1,0:T(8,128)(2,1)}, bf16[4096,512]{1,0:T(8,128)(2,1)}) custom-call(s32[1]{0:T(128)} %bitcast.1.me_ref, bf16[1024,4096]{1,0:T(8,128)(2,1)} %get-tuple-element.187.left_ref, bf16[1024,1024]{1,0:T(8,128)(2,1)} %get-tuple-element.188.right_ref, bf16[1024,1024]{1,0:T(8,128)(2,1)} %get-tuple-element.186.refs_0_), custom_call_target="tpu_custom_call" | custom-call | flops 12884901888 | bytes 16777216 | tf_op jit(solution)/shard_map/pallas_call | solution.py:764
  249.6 1.1 copy.83.shift_ref
  252.3 1.1 collective-permute-start.14
  256.5 14.7 %shard_map.304 = (bf16[1024,2048]{1,0:T(8,128)(2,1)}, bf16[1024,2048]{1,0:T(8,128)(2,1)}) custom-call(s32[1]{0:T(128)} %bitcast.1.me_ref, bf16[1024,1024]{1,0:T(8,128)(2,1)} %get-tuple-element.190.left_ref, bf16[1024,4096]{1,0:T(8,128)(2,1)} %get-tuple-element.191.right_ref, bf16[4096,512]{1,0:T(8,128)(2,1)} %get-tuple-element.189.refs_0_), custom_call_target="tpu_custom_call" | custom-call | flops 12884901888 | bytes 16777216 | tf_op jit(solution)/shard_map/pallas_call | solution.py:806
  271.9 4.8 add_convert_fusion.1
  278.7 1.5 constant_dynamic-slice_fusion.11
  280.5 5.3 collective-permute-start.18
  286.0 39.8 %shard_map.305 = (bf16[2,1024,384]{2,1,0:T(8,128)(2,1)}, bf16[2,1024,384]{2,1,0:T(8,128)(2,1)}, f32[8,128]{1,0:T(8,128)}) custom-call(s32[16]{0:T(128)} %get-tuple-element.139.lo_ref, s32[16]{0:T(128)} %get-tuple-element.140.hi_ref, bf16[1024,128]{1,0:T(8,128)(2,1)} %get-tuple-element.176.refs_0_, bf16[1024,128]{1,0:T(8,128)(2,1)} %collective-permute-done.12.refs_1_, ...), custom_call_target="tpu_custom_call" | custom-call | flops 34359738368 | bytes 12582912 | tf_op jit(solution)/shard_map/pallas_call | solution.py:519
  326.5 2.1 slice.193
  330.2 1.9 collective-permute-done.18
  332.1 1.6 add_convert_fusion.7
  334.6 1.7 collective-permute-start.22
  336.3 2.2 add_convert_fusion.3.refs_6_
  338.5 6.8 %add_convert_fusion = bf16[1024,2048]{1,0:T(8,128)(2,1)} fusion(bf16[1024,2048]{1,0:T(8,128)(2,1)} %collective-permute-done.19, bf16[1024,2048]{1,0:T(8,128)(2,1)S(1)} %copy-done.10), kind=kLoop, calls=%fused_computation.3 | loop fusion | flops 8388608 | bytes 12582912 | tf_op jit(solution)/shard_map/convert_element_type | solution.py:136
  346.4 10.0 %shard_map.306 = (bf16[1024,384]{1,0:T(8,128)(2,1)}, f32[1024,2]{1,0:T(8,128)}) custom-call(s32[1]{0:T(128)} %bitcast.1.me_ref, bf16[4,1024,1024]{2,1,0:T(8,128)(2,1)} %get-tuple-element.150.n_ref, f32[1024,1]{1,0:T(8,128)} %copy.82.gain_ref, f32[1024,1]{1,0:T(8,128)} %copy.83.shift_ref, bf16[2,1024,384]{2,1,0:T(8,128)(2,1)} %get-tuple-element.200.refs_0_, ...), custom_call_target="tpu_custom_call" | custom-call | flops 17179869184 | bytes 1024 | tf_op jit(solution)/shard_map/pallas_call | solution.py:910
  356.4 3.2 constant_dynamic-slice_fusion.10
  360.2 39.7 %shard_map.307 = (bf16[2,1024,384]{2,1,0:T(8,128)(2,1)}, bf16[2,1024,384]{2,1,0:T(8,128)(2,1)}, f32[8,128]{1,0:T(8,128)}) custom-call(s32[16]{0:T(128)} %get-tuple-element.139.lo_ref, s32[16]{0:T(128)} %get-tuple-element.140.hi_ref, bf16[1024,128]{1,0:T(8,128)(2,1)} %get-tuple-element.207.refs_0_, bf16[1024,128]{1,0:T(8,128)(2,1)} %collective-permute-done.24.refs_1_, ...), custom_call_target="tpu_custom_call" | custom-call | flops 34359738368 | bytes 12582912 | tf_op jit(solution)/shard_map/pallas_call | solution.py:519
  399.9 1.2 collective-permute-start.28
  401.8 2.1 slice.195
  404.0 3.6 collective-permute-done.21
  407.6 2.4 add_convert_fusion.2.refs_5_
  410.2 1.8 collective-permute-start.30
  412.3 1.5 add_convert_fusion.6.refs_6_
  416.0 10.1 %shard_map.308 = (bf16[1024,384]{1,0:T(8,128)(2,1)}, f32[1024,2]{1,0:T(8,128)}) custom-call(s32[1]{0:T(128)} %bitcast.1.me_ref, bf16[4,1024,1024]{2,1,0:T(8,128)(2,1)} %get-tuple-element.150.n_ref, f32[1024,1]{1,0:T(8,128)} %copy.82.gain_ref, f32[1024,1]{1,0:T(8,128)} %copy.83.shift_ref, bf16[2,1024,384]{2,1,0:T(8,128)(2,1)} %get-tuple-element.214.refs_0_.refs_2_, ...), custom_call_target="tpu_custom_call" | custom-call | flops 17179869184 | bytes 1024 | tf_op jit(solution)/shard_map/pallas_call | solution.py:910
  426.1 1.2 slice.194
  427.3 8.6 %collective-permute-done.28.refs_3_ = bf16[2,1024,384]{2,1,0:T(8,128)(2,1)} collective-permute-done((bf16[2,1024,384]{2,1,0:T(8,128)(2,1)}, bf16[2,1024,384]{2,1,0:T(8,128)(2,1)}, u32[]{:S(2)}, u32[]{:S(2)}) %collective-permute-start.28) | collective-permute-done | bytes 1572896 | tf_op jit(solution)/shard_map/ppermute | solution.py:67
  435.9 10.3 %collective-permute-done.27 = bf16[2,1,1,128,2048]{4,3,2,1,0:T(8,128)(2,1)} collective-permute-done((bf16[2,1,1,128,2048]{4,3,2,1,0:T(8,128)(2,1)S(1)}, bf16[2,1,1,128,2048]{4,3,2,1,0:T(8,128)(2,1)}, u32[]{:S(2)}, u32[]{:S(2)}) %collective-permute-start.27) | collective-permute-done | bytes 1048608 | tf_op jit(solution)/shard_map/ppermute | solution.py:69
  446.2 1.2 add_bitcast_fusion
  448.7 1.1 collective-permute-start.35
  449.7 1.2 slice.196
  452.5 1.1 collective-permute-start.34
  453.6 1.6 add_convert_fusion.5
  456.3 29.6 %shard_map.309 = (f32[200,128]{1,0:T(8,128)S(1)}, f32[128,128]{1,0:T(8,128)S(1)}) custom-call(f32[200,128]{1,0:T(8,128)S(1)} %pad_bitcast_fusion.vec_ref, bf16[4,128,128]{2,1,0:T(8,128)(2,1)S(1)} %reshape.494.slot_ref), custom_call_target="tpu_custom_call" | custom-call | flops 17179869184 | bytes 1024 | tf_op jit(solution)/shard_map/pallas_call | solution.py:1044
  486.1 1.1 collective-permute-start.45
  489.5 2.0 fusion.29
  492.4 15.4 %shard_map.310 = f32[1,1016,1024]{2,1,0:T(8,128)} custom-call(s32[1]{0:T(128)} %bitcast.1.me_ref, bf16[1016,1024]{1,0:T(8,128)(2,1)} %bitcast.197, f32[1024,1024]{1,0:T(8,128)} %get-tuple-element.242.ghid_ref, bf16[1024,3072]{1,0:T(8,128)(2,1)} %w_ref.1, f32[1,1024]{1,0:T(1,128)} %get-tuple-element.350.refs_9_.gain_ref, ...), custom_call_target="tpu_custom_call" | custom-call | flops 17179869184 | bytes 1024 | tf_op jit(solution)/shard_map/pallas_call | solution.py:961
  507.9 1.1 pad_maximum_fusion.2
  509.1 1.6 maximum_convert_fusion.1
  512.9 1.1 fusion.30
  514.1 3.7 collective-permute-start.38
  521.8 5.5 %collective-permute-done.38 = bf16[1,1,1,128,768]{4,3,2,1,0:T(8,128)(2,1)S(1)} collective-permute-done((bf16[1,1,1,128,768]{4,3,2,1,0:T(8,128)(2,1)S(1)}, bf16[1,1,1,128,768]{4,3,2,1,0:T(8,128)(2,1)S(1)}, u32[]{:S(2)}, u32[]{:S(2)}) %collective-permute-start.38) | collective-permute-done | bytes 196640 | tf_op jit(solution)/shard_map/ppermute | solution.py:69
  527.5 1.1 collective-permute-start.40
  530.0 5.3 collective-permute-done.40
  535.2 3.3 collective-permute-done.41
  539.2 1.3 convert_element_type.281
  540.9 1.5 maximum_convert_fusion
  (291 shorter events, 46.4 us)
Async XLA Ops:
  0.6 49.3 %copy-start = (bf16[1024,8]{0,1:T(8,128)(2,1)S(1)}, bf16[1024,8]{0,1:T(8,128)(2,1)}, u32[]{:S(2)}) copy-start(bf16[1024,8]{0,1:T(8,128)(2,1)} %param.33) | copy-start | bytes 49156
  0.7 12.0 %collective-permute-start.1 = (bf16[1016,1024]{1,0:T(8,128)(2,1)}, bf16[1016,1024]{1,0:T(8,128)(2,1)}, u32[]{:S(2)}, u32[]{:S(2)}) collective-permute-start(bf16[1016,1024]{1,0:T(8,128)(2,1)} %bitcast.193), channel_id=1, source_target_pairs={{0,1},{1,0},{2,3},{3,2},{4,5},{5,4},{6,7},{7,6},{8,9},{9,8},{10,11... | collective-permute-start | bytes 6242312 | tf_op jit(solution)/shard_map/ppermute | solution.py:67
  1.2 48.6 %collective-permute-start = (bf16[1016,1024]{1,0:T(8,128)(2,1)}, bf16[1016,1024]{1,0:T(8,128)(2,1)S(1)}, u32[]{:S(2)}, u32[]{:S(2)}) collective-permute-start(bf16[1016,1024]{1,0:T(8,128)(2,1)} %bitcast.194), channel_id=1, source_target_pairs={{0,2},{1,3},{2,0},{3,1},{4,6},{5,7},{6,4},{7,5},{8,10},{9,11},{10,... | collective-permute-start | bytes 6242312 | tf_op jit(solution)/shard_map/ppermute | solution.py:67
  12.7 37.1 %copy-start.25 = (f32[1,2,8,1024]{3,2,1,0:T(8,128)S(1)}, f32[1,2,8,1024]{3,2,1,0:T(8,128)}, u32[]{:S(2)}) copy-start(f32[1,2,8,1024]{3,2,1,0:T(8,128)} %param.35) | copy-start | bytes 196612
  12.7 37.2 %copy-start.38 = (s32[1,8]{1,0:T(1,128)S(1)}, s32[1,8]{1,0:T(1,128)}, u32[]{:S(2)}) copy-start(s32[1,8]{1,0:T(1,128)} %param.19) | copy-start | bytes 100
  49.8 4.3 collective-permute-start.2
  66.6 51.7 %collective-permute-start.4 = (bf16[2,8192]{1,0:T(2,128)(2,1)S(1)}, bf16[2,8192]{1,0:T(2,128)(2,1)S(1)}, u32[]{:S(2)}, u32[]{:S(2)}) collective-permute-start(bf16[2,8192]{1,0:T(2,128)(2,1)S(1)} %bitcast.170), channel_id=1, source_target_pairs={{0,2},{1,3},{2,0},{3,1},{4,6},{5,7},{6,4},{7,5},{8,10},{9,11},{10,... | collective-permute-start | bytes 98312 | tf_op jit(solution)/shard_map/ppermute | solution.py:67
  68.4 56.1 %collective-permute-start.3 = (bf16[2,8192]{1,0:T(2,128)(2,1)S(1)}, bf16[2,8192]{1,0:T(2,128)(2,1)S(1)}, u32[]{:S(2)}, u32[]{:S(2)}) collective-permute-start(bf16[2,8192]{1,0:T(2,128)(2,1)S(1)} %bitcast.171), channel_id=1, source_target_pairs={{0,1},{1,0},{2,3},{3,2},{4,5},{5,4},{6,7},{7,6},{8,9},{9,8},{10,11... | collective-permute-start | bytes 98312 | tf_op jit(solution)/shard_map/ppermute | solution.py:67
  90.7 28.3 %collective-permute-start.6 = (bf16[512,256]{1,0:T(8,128)(2,1)}, bf16[512,256]{1,0:T(8,128)(2,1)S(1)}, u32[]{:S(2)}, u32[]{:S(2)}) collective-permute-start(bf16[512,256]{1,0:T(8,128)(2,1)} %get-tuple-element.158), channel_id=1, source_target_pairs={{0,1},{1,0},{2,3},{3,2},{4,5},{5,4},{6,7},{7,6},{8,9},{9,8},{10,11... | collective-permute-start | bytes 786440 | tf_op jit(solution)/shard_map/ppermute | solution.py:67
  91.3 27.7 %collective-permute-start.7 = (bf16[512,256]{1,0:T(8,128)(2,1)}, bf16[512,256]{1,0:T(8,128)(2,1)S(1)}, u32[]{:S(2)}, u32[]{:S(2)}) collective-permute-start(bf16[512,256]{1,0:T(8,128)(2,1)} %get-tuple-element.159), channel_id=1, source_target_pairs={{0,2},{1,3},{2,0},{3,1},{4,6},{5,7},{6,4},{7,5},{8,10},{9,11},{10,... | collective-permute-start | bytes 786440 | tf_op jit(solution)/shard_map/ppermute | solution.py:67
  91.6 27.5 %collective-permute-start.8 = (bf16[512,256]{1,0:T(8,128)(2,1)}, bf16[512,256]{1,0:T(8,128)(2,1)S(1)}, u32[]{:S(2)}, u32[]{:S(2)}) collective-permute-start(bf16[512,256]{1,0:T(8,128)(2,1)} %get-tuple-element.160), channel_id=1, source_target_pairs={{0,3},{1,2},{2,1},{3,0},{4,7},{5,6},{6,5},{7,4},{8,11},{9,10},{10,... | collective-permute-start | bytes 786440 | tf_op jit(solution)/shard_map/ppermute | solution.py:67
  92.7 28.5 %copy-start.46 = (s32[1,8]{1,0:T(1,128)S(1)}, s32[1,8]{1,0:T(1,128)}, u32[]{:S(2)}) copy-start(s32[1,8]{1,0:T(1,128)} %param.20) | copy-start | bytes 100
  92.7 29.4 %copy-start.36 = (f32[8]{0:T(128)S(1)}, f32[8]{0:T(128)}, u32[]{:S(2)}) copy-start(f32[8]{0:T(128)} %param.34) | copy-start | bytes 100
  92.7 30.0 %copy-start.32 = (f32[1024]{0:T(1024)S(1)}, f32[1024]{0:T(1024)}, u32[]{:S(2)}) copy-start(f32[1024]{0:T(1024)} %param.24) | copy-start | bytes 12292
  92.7 30.0 %copy-start.33 = (f32[1024]{0:T(1024)S(1)}, f32[1024]{0:T(1024)}, u32[]{:S(2)}) copy-start(f32[1024]{0:T(1024)} %param.28) | copy-start | bytes 12292
  92.8 30.0 %copy-start.34 = (f32[1024]{0:T(1024)S(1)}, f32[1024]{0:T(1024)}, u32[]{:S(2)}) copy-start(f32[1024]{0:T(1024)} %param.32) | copy-start | bytes 12292
  118.3 6.2 %collective-permute-start.5 = (bf16[2,8192]{1,0:T(2,128)(2,1)S(1)}, bf16[2,8192]{1,0:T(2,128)(2,1)S(1)}, u32[]{:S(2)}, u32[]{:S(2)}) collective-permute-start(bf16[2,8192]{1,0:T(2,128)(2,1)S(1)} %collective-permute-done.4), channel_id=1, source_target_pairs={{0,1},{1,0},{2,3},{3,2},{4,5},{5,4},{6,7},{7,6},{8,9},{9,8},{10,11... | collective-permute-start | bytes 98312 | tf_op jit(solution)/shard_map/ppermute | solution.py:67
  119.0 13.3 %copy-start.40 = (bf16[512,256]{1,0:T(8,128)(2,1)}, bf16[512,256]{1,0:T(8,128)(2,1)S(1)}, u32[]{:S(2)}) copy-start(bf16[512,256]{1,0:T(8,128)(2,1)S(1)} %collective-permute-done.6.refs_12_.refs_6_) | copy-start | bytes 786436
  119.0 13.3 %copy-start.41 = (bf16[512,256]{1,0:T(8,128)(2,1)}, bf16[512,256]{1,0:T(8,128)(2,1)S(1)}, u32[]{:S(2)}) copy-start(bf16[512,256]{1,0:T(8,128)(2,1)S(1)} %collective-permute-done.7.refs_13_.refs_7_) | copy-start | bytes 786436
  119.1 13.2 %copy-start.42 = (bf16[512,256]{1,0:T(8,128)(2,1)}, bf16[512,256]{1,0:T(8,128)(2,1)S(1)}, u32[]{:S(2)}) copy-start(bf16[512,256]{1,0:T(8,128)(2,1)S(1)} %collective-permute-done.8.refs_14_.refs_8_) | copy-start | bytes 786436
  119.1 9.4 %collective-permute-start.10 = (bf16[512,256]{1,0:T(8,128)(2,1)}, bf16[512,256]{1,0:T(8,128)(2,1)S(1)}, u32[]{:S(2)}, u32[]{:S(2)}) collective-permute-start(bf16[512,256]{1,0:T(8,128)(2,1)} %get-tuple-element.174), channel_id=1, source_target_pairs={{0,2},{1,3},{2,0},{3,1},{4,6},{5,7},{6,4},{7,5},{8,10},{9,11},{10,... | collective-permute-start | bytes 786440 | tf_op jit(solution)/shard_map/ppermute | solution.py:67
  119.4 12.9 %collective-permute-start.11 = (bf16[512,256]{1,0:T(8,128)(2,1)}, bf16[512,256]{1,0:T(8,128)(2,1)S(1)}, u32[]{:S(2)}, u32[]{:S(2)}) collective-permute-start(bf16[512,256]{1,0:T(8,128)(2,1)} %get-tuple-element.175), channel_id=1, source_target_pairs={{0,3},{1,2},{2,1},{3,0},{4,7},{5,6},{6,5},{7,4},{8,11},{9,10},{10,... | collective-permute-start | bytes 786440 | tf_op jit(solution)/shard_map/ppermute | solution.py:67
  120.5 11.8 %collective-permute-start.9 = (bf16[512,256]{1,0:T(8,128)(2,1)}, bf16[512,256]{1,0:T(8,128)(2,1)S(1)}, u32[]{:S(2)}, u32[]{:S(2)}) collective-permute-start(bf16[512,256]{1,0:T(8,128)(2,1)} %get-tuple-element.173), channel_id=1, source_target_pairs={{0,1},{1,0},{2,3},{3,2},{4,5},{5,4},{6,7},{7,6},{8,9},{9,8},{10,11... | collective-permute-start | bytes 786440 | tf_op jit(solution)/shard_map/ppermute | solution.py:67
  234.2 14.4 %copy-start.28 = (f32[1024,1]{0,1:T(1,128)S(1)}, f32[1024,1]{0,1:T(1,128)}, u32[]{:S(2)}) copy-start(f32[1024,1]{0,1:T(1,128)} %get-tuple-element.351) | copy-start | bytes 12292
  234.2 15.5 %copy-start.27 = (f32[1024,1]{0,1:T(1,128)S(1)}, f32[1024,1]{0,1:T(1,128)}, u32[]{:S(2)}) copy-start(f32[1024,1]{0,1:T(1,128)} %get-tuple-element.335) | copy-start | bytes 12292
  234.2 19.3 %copy-start.19 = (f32[1024,64]{1,0:T(8,128)S(1)}, f32[1024,64]{1,0:T(8,128)}, u32[]{:S(2)}) copy-start(f32[1024,64]{1,0:T(8,128)} %get-tuple-element.228) | copy-start | bytes 786436
  248.1 23.8 %collective-permute-start.16 = (bf16[4096,512]{1,0:T(8,128)(2,1)}, bf16[4096,512]{1,0:T(8,128)(2,1)}, u32[]{:S(2)}, u32[]{:S(2)}) collective-permute-start(bf16[4096,512]{1,0:T(8,128)(2,1)} %get-tuple-element.189.refs_0_), channel_id=1, source_target_pairs={{0,1},{1,0},{2,3},{3,2},{4,5},{5,4},{6,7},{7,6},{8,9},{9,8},{10,11... | collective-permute-start | bytes 12582920 | tf_op jit(solution)/shard_map/ppermute | solution.py:67
  250.7 20.5 %collective-permute-start.15 = (bf16[1024,1024]{1,0:T(8,128)(2,1)}, bf16[1024,1024]{1,0:T(8,128)(2,1)S(1)}, u32[]{:S(2)}, u32[]{:S(2)}) collective-permute-start(bf16[1024,1024]{1,0:T(8,128)(2,1)} %get-tuple-element.186.refs_0_), channel_id=1, source_target_pairs={{0,1},{1,0},{2,3},{3,2},{4,5},{5,4},{6,7},{7,6},{8,9},{9,8},{10,11... | collective-permute-start | bytes 6291464 | tf_op jit(solution)/shard_map/ppermute | solution.py:67
  251.6 28.6 %collective-permute-start.12 = (bf16[1024,128]{1,0:T(8,128)(2,1)}, bf16[1024,128]{1,0:T(8,128)(2,1)}, u32[]{:S(2)}, u32[]{:S(2)}) collective-permute-start(bf16[1024,128]{1,0:T(8,128)(2,1)} %get-tuple-element.177), channel_id=1, source_target_pairs={{0,1},{1,0},{2,3},{3,2},{4,5},{5,4},{6,7},{7,6},{8,9},{9,8},{10,11... | collective-permute-start | bytes 786440 | tf_op jit(solution)/shard_map/ppermute | solution.py:67
  251.9 28.6 %collective-permute-start.13 = (bf16[1024,128]{1,0:T(8,128)(2,1)}, bf16[1024,128]{1,0:T(8,128)(2,1)}, u32[]{:S(2)}, u32[]{:S(2)}) collective-permute-start(bf16[1024,128]{1,0:T(8,128)(2,1)} %get-tuple-element.178), channel_id=1, source_target_pairs={{0,2},{1,3},{2,0},{3,1},{4,6},{5,7},{6,4},{7,5},{8,10},{9,11},{10,... | collective-permute-start | bytes 786440 | tf_op jit(solution)/shard_map/ppermute | solution.py:67
  252.3 33.5 %collective-permute-start.14 = (bf16[1024,128]{1,0:T(8,128)(2,1)}, bf16[1024,128]{1,0:T(8,128)(2,1)}, u32[]{:S(2)}, u32[]{:S(2)}) collective-permute-start(bf16[1024,128]{1,0:T(8,128)(2,1)} %get-tuple-element.179), channel_id=1, source_target_pairs={{0,3},{1,2},{2,1},{3,0},{4,7},{5,6},{6,5},{7,4},{8,11},{9,10},{10,... | collective-permute-start | bytes 786440 | tf_op jit(solution)/shard_map/ppermute | solution.py:67
  271.2 57.4 %collective-permute-start.19 = (bf16[1024,2048]{1,0:T(8,128)(2,1)}, bf16[1024,2048]{1,0:T(8,128)(2,1)}, u32[]{:S(2)}, u32[]{:S(2)}) collective-permute-start(bf16[1024,2048]{1,0:T(8,128)(2,1)} %get-tuple-element.192.refs_6_), channel_id=1, source_target_pairs={{0,1},{1,0},{2,3},{3,2},{4,5},{5,4},{6,7},{7,6},{8,9},{9,8},{10,11... | collective-permute-start | bytes 12582920 | tf_op jit(solution)/shard_map/ppermute | solution.py:67
  271.8 87.7 %collective-permute-start.24 = (bf16[1024,128]{1,0:T(8,128)(2,1)}, bf16[1024,128]{1,0:T(8,128)(2,1)}, u32[]{:S(2)}, u32[]{:S(2)}) collective-permute-start(bf16[1024,128]{1,0:T(8,128)(2,1)} %get-tuple-element.208), channel_id=1, source_target_pairs={{0,1},{1,0},{2,3},{3,2},{4,5},{5,4},{6,7},{7,6},{8,9},{9,8},{10,11... | collective-permute-start | bytes 786440 | tf_op jit(solution)/shard_map/ppermute | solution.py:67
  280.2 79.4 %collective-permute-start.25 = (bf16[1024,128]{1,0:T(8,128)(2,1)}, bf16[1024,128]{1,0:T(8,128)(2,1)}, u32[]{:S(2)}, u32[]{:S(2)}) collective-permute-start(bf16[1024,128]{1,0:T(8,128)(2,1)} %get-tuple-element.209), channel_id=1, source_target_pairs={{0,2},{1,3},{2,0},{3,1},{4,6},{5,7},{6,4},{7,5},{8,10},{9,11},{10,... | collective-permute-start | bytes 786440 | tf_op jit(solution)/shard_map/ppermute | solution.py:67
  280.5 51.6 %collective-permute-start.18 = (bf16[2,1,2,512,512]{4,3,2,1,0:T(8,128)(2,1)}, bf16[2,1,2,512,512]{4,3,2,1,0:T(8,128)(2,1)}, u32[]{:S(2)}, u32[]{:S(2)}) collective-permute-start(bf16[2,1,2,512,512]{4,3,2,1,0:T(8,128)(2,1)} %constant_dynamic-slice_fusion.11), channel_id=1, source_target_pairs={{0,8},{4,12},{8,0},{12,4},{16,24},{20,28},{24,16},{28,20},{1,9},{5... | collective-permute-start | bytes 6291464 | tf_op jit(solution)/shard_map/ppermute | solution.py:69
  285.8 43.6 %collective-permute-start.17 = (bf16[2,2,1,128,1024]{4,3,2,1,0:T(8,128)(2,1)S(1)}, bf16[2,2,1,128,1024]{4,3,2,1,0:T(8,128)(2,1)}, u32[]{:S(2)}, u32[]{:S(2)}) collective-permute-start(bf16[2,2,1,128,1024]{4,3,2,1,0:T(8,128)(2,1)S(1)} %constant_dynamic-slice_fusion.12), channel_id=1, source_target_pairs={{0,4},{4,0},{8,12},{12,8},{16,20},{20,16},{24,28},{28,24},{1,5},{5... | collective-permute-start | bytes 3145736 | tf_op jit(solution)/shard_map/ppermute | solution.py:69
  286.0 46.1 %copy-start.9 = (bf16[1024,1024]{1,0:T(8,128)(2,1)S(1)}, bf16[1024,1024]{1,0:T(8,128)(2,1)}, u32[]{:S(2)}) copy-start(bf16[1024,1024]{1,0:T(8,128)(2,1)} %copy-done.8) | copy-start | bytes 6291460
  328.6 31.6 %collective-permute-start.26 = (bf16[1024,128]{1,0:T(8,128)(2,1)}, bf16[1024,128]{1,0:T(8,128)(2,1)}, u32[]{:S(2)}, u32[]{:S(2)}) collective-permute-start(bf16[1024,128]{1,0:T(8,128)(2,1)} %get-tuple-element.210), channel_id=1, source_target_pairs={{0,3},{1,2},{2,1},{3,0},{4,7},{5,6},{6,5},{7,4},{8,11},{9,10},{10,... | collective-permute-start | bytes 786440 | tf_op jit(solution)/shard_map/ppermute | solution.py:67
  329.5 74.5 %collective-permute-start.23 = (bf16[2,1024,384]{2,1,0:T(8,128)(2,1)}, bf16[2,1024,384]{2,1,0:T(8,128)(2,1)}, u32[]{:S(2)}, u32[]{:S(2)}) collective-permute-start(bf16[2,1024,384]{2,1,0:T(8,128)(2,1)} %get-tuple-element.206.refs_1_), channel_id=1, source_target_pairs={{0,2},{1,3},{2,0},{3,1},{4,6},{5,7},{6,4},{7,5},{8,10},{9,11},{10,... | collective-permute-start | bytes 4718600 | tf_op jit(solution)/shard_map/ppermute | solution.py:67
  334.6 69.4 %collective-permute-start.22 = (bf16[2,1,1,128,1024]{4,3,2,1,0:T(8,128)(2,1)}, bf16[2,1,1,128,1024]{4,3,2,1,0:T(8,128)(2,1)S(1)}, u32[]{:S(2)}, u32[]{:S(2)}) collective-permute-start(bf16[2,1,1,128,1024]{4,3,2,1,0:T(8,128)(2,1)} %constant_dynamic-slice_fusion.8), channel_id=1, source_target_pairs={{0,8},{4,12},{8,0},{12,4},{16,24},{20,28},{24,16},{28,20},{1,9},{5... | collective-permute-start | bytes 1572872 | tf_op jit(solution)/shard_map/ppermute | solution.py:69
  359.6 48.0 %collective-permute-start.21 = (bf16[1,1,2,512,512]{4,3,2,1,0:T(8,128)(2,1)}, bf16[1,1,2,512,512]{4,3,2,1,0:T(8,128)(2,1)}, u32[]{:S(2)}, u32[]{:S(2)}) collective-permute-start(bf16[1,1,2,512,512]{4,3,2,1,0:T(8,128)(2,1)} %constant_dynamic-slice_fusion.9), channel_id=1, source_target_pairs={{0,16},{4,20},{8,24},{12,28},{16,0},{20,4},{24,8},{28,12},{1,17},{... | collective-permute-start | bytes 3145736 | tf_op jit(solution)/shard_map/ppermute | solution.py:69
  359.6 48.0 %collective-permute-start.20 = (bf16[2,2,1,128,2048]{4,3,2,1,0:T(8,128)(2,1)}, bf16[2,2,1,128,2048]{4,3,2,1,0:T(8,128)(2,1)S(1)}, u32[]{:S(2)}, u32[]{:S(2)}) collective-permute-start(bf16[2,2,1,128,2048]{4,3,2,1,0:T(8,128)(2,1)} %constant_dynamic-slice_fusion.10), channel_id=1, source_target_pairs={{0,4},{4,0},{8,12},{12,8},{16,20},{20,16},{24,28},{28,24},{1,5},{5... | collective-permute-start | bytes 6291464 | tf_op jit(solution)/shard_map/ppermute | solution.py:69
  399.9 36.0 %collective-permute-start.28 = (bf16[2,1024,384]{2,1,0:T(8,128)(2,1)}, bf16[2,1024,384]{2,1,0:T(8,128)(2,1)}, u32[]{:S(2)}, u32[]{:S(2)}) collective-permute-start(bf16[2,1024,384]{2,1,0:T(8,128)(2,1)} %get-tuple-element.216.refs_1_), channel_id=1, source_target_pairs={{0,2},{1,3},{2,0},{3,1},{4,6},{5,7},{6,4},{7,5},{8,10},{9,11},{10,... | collective-permute-start | bytes 4718600 | tf_op jit(solution)/shard_map/ppermute | solution.py:67
  410.2 25.7 %collective-permute-start.30 = (bf16[1,1,1,128,1024]{4,3,2,1,0:T(8,128)(2,1)S(1)}, bf16[1,1,1,128,1024]{4,3,2,1,0:T(8,128)(2,1)}, u32[]{:S(2)}, u32[]{:S(2)}) collective-permute-start(bf16[1,1,1,128,1024]{4,3,2,1,0:T(8,128)(2,1)S(1)} %constant_dynamic-slice_fusion.5), channel_id=1, source_target_pairs={{0,16},{4,20},{8,24},{12,28},{16,0},{20,4},{24,8},{28,12},{1,17},{... | collective-permute-start | bytes 786440 | tf_op jit(solution)/shard_map/ppermute | solution.py:69
  414.7 21.2 %collective-permute-start.29 = (bf16[1,1,1,512,512]{4,3,2,1,0:T(8,128)(2,1)}, bf16[1,1,1,512,512]{4,3,2,1,0:T(8,128)(2,1)S(1)}, u32[]{:S(2)}, u32[]{:S(2)}) collective-permute-start(bf16[1,1,1,512,512]{4,3,2,1,0:T(8,128)(2,1)} %constant_dynamic-slice_fusion.6), channel_id=1, source_target_pairs={{0,4},{4,0},{8,12},{12,8},{16,20},{20,16},{24,28},{28,24},{1,5},{5... | collective-permute-start | bytes 1572872 | tf_op jit(solution)/shard_map/ppermute | solution.py:69
  415.7 30.5 %copy-start.18 = (f32[1024,2]{1,0:T(8,128)S(1)}, f32[1024,2]{1,0:T(8,128)}, u32[]{:S(2)}) copy-start(f32[1024,2]{1,0:T(8,128)} %get-tuple-element.229) | copy-start | bytes 24580
  415.7 30.5 %collective-permute-start.27 = (bf16[2,1,1,128,2048]{4,3,2,1,0:T(8,128)(2,1)S(1)}, bf16[2,1,1,128,2048]{4,3,2,1,0:T(8,128)(2,1)}, u32[]{:S(2)}, u32[]{:S(2)}) collective-permute-start(bf16[2,1,1,128,2048]{4,3,2,1,0:T(8,128)(2,1)S(1)} %constant_dynamic-slice_fusion.7), channel_id=1, source_target_pairs={{0,8},{4,12},{8,0},{12,4},{16,24},{20,28},{24,16},{28,20},{1,9},{5... | collective-permute-start | bytes 3145736 | tf_op jit(solution)/shard_map/ppermute | solution.py:69
  435.9 10.3 %copy-start.20 = (bf16[1,1,1,512,512]{4,3,2,1,0:T(8,128)(2,1)}, bf16[1,1,1,512,512]{4,3,2,1,0:T(8,128)(2,1)S(1)}, u32[]{:S(2)}) copy-start(bf16[1,1,1,512,512]{4,3,2,1,0:T(8,128)(2,1)S(1)} %collective-permute-done.29) | copy-start | bytes 1572868
  448.7 37.2 %collective-permute-start.35 = (bf16[1,1,1,128,1024]{4,3,2,1,0:T(8,128)(2,1)S(1)}, bf16[1,1,1,128,1024]{4,3,2,1,0:T(8,128)(2,1)S(1)}, u32[]{:S(2)}, u32[]{:S(2)}) collective-permute-start(bf16[1,1,1,128,1024]{4,3,2,1,0:T(8,128)(2,1)S(1)} %add_convert_fusion.16), channel_id=1, source_target_pairs={{0,2},{1,3},{2,0},{3,1},{4,6},{5,7},{6,4},{7,5},{8,10},{9,11},{10,... | collective-permute-start | bytes 786440 | tf_op jit(solution)/shard_map/ppermute | solution.py:67
  451.5 34.4 %collective-permute-start.31 = (bf16[4,1024,384]{2,1,0:T(8,128)(2,1)S(1)}, bf16[4,1024,384]{2,1,0:T(8,128)(2,1)S(1)}, u32[]{:S(2)}, u32[]{:S(2)}) collective-permute-start(bf16[4,1024,384]{2,1,0:T(8,128)(2,1)S(1)} %pad_maximum_fusion), channel_id=1, source_target_pairs={{0,1},{1,0},{2,3},{3,2},{4,5},{5,4},{6,7},{7,6},{8,9},{9,8},{10,11... | collective-permute-start | bytes 9437192 | tf_op jit(solution)/shard_map/ppermute | solution.py:67
  452.5 33.4 %collective-permute-start.34 = (bf16[1,1,1,512,256]{4,3,2,1,0:T(8,128)(2,1)S(1)}, bf16[1,1,1,512,256]{4,3,2,1,0:T(8,128)(2,1)S(1)}, u32[]{:S(2)}, u32[]{:S(2)}) collective-permute-start(bf16[1,1,1,512,256]{4,3,2,1,0:T(8,128)(2,1)S(1)} %constant_dynamic-slice_fusion.3), channel_id=1, source_target_pairs={{0,2},{1,3},{2,0},{3,1},{4,6},{5,7},{6,4},{7,5},{8,10},{9,11},{10,... | collective-permute-start | bytes 786440 | tf_op jit(solution)/shard_map/ppermute | solution.py:67
  455.3 30.6 %collective-permute-start.33 = (bf16[1,1,1,128,2048]{4,3,2,1,0:T(8,128)(2,1)S(1)}, bf16[1,1,1,128,2048]{4,3,2,1,0:T(8,128)(2,1)S(1)}, u32[]{:S(2)}, u32[]{:S(2)}) collective-permute-start(bf16[1,1,1,128,2048]{4,3,2,1,0:T(8,128)(2,1)S(1)} %constant_dynamic-slice_fusion.4), channel_id=1, source_target_pairs={{0,16},{4,20},{8,24},{12,28},{16,0},{20,4},{24,8},{28,12},{1,17},{... | collective-permute-start | bytes 1572872 | tf_op jit(solution)/shard_map/ppermute | solution.py:69
  455.5 30.4 %collective-permute-start.32 = (bf16[2,2,1,128,768]{4,3,2,1,0:T(8,128)(2,1)S(1)}, bf16[2,2,1,128,768]{4,3,2,1,0:T(8,128)(2,1)S(1)}, u32[]{:S(2)}, u32[]{:S(2)}) collective-permute-start(bf16[2,2,1,128,768]{4,3,2,1,0:T(8,128)(2,1)S(1)} %fusion.2), channel_id=1, source_target_pairs={{0,4},{4,0},{8,12},{12,8},{16,20},{20,16},{24,28},{28,24},{1,5},{5... | collective-permute-start | bytes 2359304 | tf_op jit(solution)/shard_map/ppermute | solution.py:69
  486.0 21.8 %collective-permute-start.44 = (bf16[512,256]{1,0:T(8,128)(2,1)S(1)}, bf16[512,256]{1,0:T(8,128)(2,1)S(1)}, u32[]{:S(2)}, u32[]{:S(2)}) collective-permute-start(bf16[512,256]{1,0:T(8,128)(2,1)S(1)} %bitcast.156), channel_id=1, source_target_pairs={{0,1},{1,0},{2,3},{3,2},{4,5},{5,4},{6,7},{7,6},{8,9},{9,8},{10,11... | collective-permute-start | bytes 786440 | tf_op jit(solution)/shard_map/ppermute | solution.py:67
  486.1 21.8 %collective-permute-start.45 = (bf16[512,256]{1,0:T(8,128)(2,1)S(1)}, bf16[512,256]{1,0:T(8,128)(2,1)S(1)}, u32[]{:S(2)}, u32[]{:S(2)}) collective-permute-start(bf16[512,256]{1,0:T(8,128)(2,1)S(1)} %bitcast.157), channel_id=1, source_target_pairs={{0,2},{1,3},{2,0},{3,1},{4,6},{5,7},{6,4},{7,5},{8,10},{9,11},{10,... | collective-permute-start | bytes 786440 | tf_op jit(solution)/shard_map/ppermute | solution.py:67
  487.1 20.8 %collective-permute-start.46 = (bf16[512,256]{1,0:T(8,128)(2,1)S(1)}, bf16[512,256]{1,0:T(8,128)(2,1)}, u32[]{:S(2)}, u32[]{:S(2)}) collective-permute-start(bf16[512,256]{1,0:T(8,128)(2,1)S(1)} %bitcast.158), channel_id=1, source_target_pairs={{0,3},{1,2},{2,1},{3,0},{4,7},{5,6},{6,5},{7,4},{8,11},{9,10},{10,... | collective-permute-start | bytes 786440 | tf_op jit(solution)/shard_map/ppermute | solution.py:67
  488.4 23.3 %collective-permute-start.37 = (bf16[1,1,1,128,2048]{4,3,2,1,0:T(8,128)(2,1)S(1)}, bf16[1,1,1,128,2048]{4,3,2,1,0:T(8,128)(2,1)S(1)}, u32[]{:S(2)}, u32[]{:S(2)}) collective-permute-start(bf16[1,1,1,128,2048]{4,3,2,1,0:T(8,128)(2,1)S(1)} %add_convert_fusion.10), channel_id=1, source_target_pairs={{0,2},{1,3},{2,0},{3,1},{4,6},{5,7},{6,4},{7,5},{8,10},{9,11},{10,... | collective-permute-start | bytes 1572872 | tf_op jit(solution)/shard_map/ppermute | solution.py:67
  491.4 19.2 %collective-permute-start.36 = (bf16[2,1,1,128,768]{4,3,2,1,0:T(8,128)(2,1)S(1)}, bf16[2,1,1,128,768]{4,3,2,1,0:T(8,128)(2,1)S(1)}, u32[]{:S(2)}, u32[]{:S(2)}) collective-permute-start(bf16[2,1,1,128,768]{4,3,2,1,0:T(8,128)(2,1)S(1)} %constant_dynamic-slice_fusion.2), channel_id=1, source_target_pairs={{0,8},{4,12},{8,0},{12,4},{16,24},{20,28},{24,16},{28,20},{1,9},{5... | collective-permute-start | bytes 1179656 | tf_op jit(solution)/shard_map/ppermute | solution.py:69
  507.8 4.7 collective-permute-start.42
  511.9 28.6 %collective-permute-start.43 = (bf16[128,2048]{1,0:T(8,128)(2,1)S(1)}, bf16[128,2048]{1,0:T(8,128)(2,1)S(1)}, u32[]{:S(2)}, u32[]{:S(2)}) collective-permute-start(bf16[128,2048]{1,0:T(8,128)(2,1)S(1)} %get-tuple-element.316), channel_id=1, source_target_pairs={{0,1},{1,0},{2,3},{3,2},{4,5},{5,4},{6,7},{7,6},{8,9},{9,8},{10,11... | collective-permute-start | bytes 1572872 | tf_op jit(solution)/shard_map/ppermute | solution.py:67
  514.1 13.3 %collective-permute-start.38 = (bf16[1,1,1,128,768]{4,3,2,1,0:T(8,128)(2,1)S(1)}, bf16[1,1,1,128,768]{4,3,2,1,0:T(8,128)(2,1)S(1)}, u32[]{:S(2)}, u32[]{:S(2)}) collective-permute-start(bf16[1,1,1,128,768]{4,3,2,1,0:T(8,128)(2,1)S(1)} %constant_dynamic-slice_fusion.1), channel_id=1, source_target_pairs={{0,16},{4,20},{8,24},{12,28},{16,0},{20,4},{24,8},{28,12},{1,17},{... | collective-permute-start | bytes 589832 | tf_op jit(solution)/shard_map/ppermute | solution.py:69
  527.4 2.6 collective-permute-start.39
  527.5 7.8 %collective-permute-start.40 = (bf16[128,768]{1,0:T(8,128)(2,1)S(1)}, bf16[128,768]{1,0:T(8,128)(2,1)S(1)}, u32[]{:S(2)}, u32[]{:S(2)}) collective-permute-start(bf16[128,768]{1,0:T(8,128)(2,1)S(1)} %get-tuple-element.323), channel_id=1, source_target_pairs={{0,2},{1,3},{2,0},{3,1},{4,6},{5,7},{6,4},{7,5},{8,10},{9,11},{10,... | collective-permute-start | bytes 589832 | tf_op jit(solution)/shard_map/ppermute | solution.py:67
  528.5 10.0 %collective-permute-start.41 = (bf16[128,768]{1,0:T(8,128)(2,1)S(1)}, bf16[128,768]{1,0:T(8,128)(2,1)S(1)}, u32[]{:S(2)}, u32[]{:S(2)}) collective-permute-start(bf16[128,768]{1,0:T(8,128)(2,1)S(1)} %get-tuple-element.323), channel_id=1, source_target_pairs={{0,3},{1,2},{2,1},{3,0},{4,7},{5,6},{6,5},{7,4},{8,11},{9,10},{10,... | collective-permute-start | bytes 589832 | tf_op jit(solution)/shard_map/ppermute | solution.py:67
  (31 other events, 117.8 us)

commit v7 on v6

--- a/solution.py
+++ b/solution.py
@@ -570,9 +570,9 @@
         tok_ref,
         img_ref,
         w_out_ref,
-        w_up_ref,
-        w_down_ref,
-        learn_in_ref,
+        w_up_far,
+        w_down_far,
+        learn_in_far,
         learn_out_ref,
         vec_ref,
         up_bias_ref,
@@ -596,17 +596,30 @@
     gatt = refs[at + 10 : at + 10 + count * splits]
     at += 10 + count * splits
     pooled_ref, vsum_ref, usum_ref, lsum_ref = refs[at : at + 4]
-    hid_ref, res_ref, dgate_ref, up0_ref, up1_ref = refs[at + 4 :]
+    hid_ref, res_ref, dgate_ref, up0_ref, up1_ref = refs[at + 4 : at + 9]
+    w_up_ref, w_down_ref, learn_in_ref, sems = refs[at + 9 :]
     step = pl.program_id(0)
     rows, width = tok_ref.shape
     hidden_units = w_up_ref.shape[1]
     chunk = up0_ref.shape[1]
     chunks = hidden_units // chunk
+    copies = [
+        pltpu.make_async_copy(w_up_far, w_up_ref, sems.at[0]),
+        pltpu.make_async_copy(w_down_far, w_down_ref, sems.at[1]),
+        pltpu.make_async_copy(learn_in_far, learn_in_ref, sems.at[2]),
+    ]
 
     @pl.when(step == 0)
     def _():
+        for copy in copies:
+            copy.start()
         for ref in (pooled_ref, vsum_ref, usum_ref, lsum_ref):
             ref[...] = jnp.zeros_like(ref)
+
+    def need(i):
+        @pl.when(step == 0)
+        def _():
+            copies[i].wait()
 
     def vec(i):
         return vec_ref[i : i + 1, :]
@@ -633,6 +646,7 @@
         gated_ref[:, columns(j)] = value.astype(bf16)
         dgate_ref[:, columns(j)] = slope
 
+    need(0)
     up(up0_ref, 0)
 
     def pair(i, _):
@@ -643,6 +657,8 @@
         return 0
 
     lax.fori_loop(0, chunks // 2, pair, 0)
+    need(1)
+    need(2)
     result = hid_ref[...] + matmul(gated_ref[...], w_down_ref[...]) + vec(1)
     res_ref[...] = result
     unit, rstd = norm_parts(result)
@@ -718,7 +734,7 @@
         functools.partial(rows_kernel, count, splits, local_rows),
         grid=(rows // block,),
         in_specs=[by_rows(width), by_rows(1)]
-        + [once(a) for a in resident]
+        + [ANYWHERE if a.size >= width * inner and i else once(a) for i, a in enumerate(resident)]
         + [pl.BlockSpec((block, features), lambda i: (jnp.minimum(i, half - 1), 0))] * count
         + [pl.BlockSpec((block, features), lambda i: (jnp.maximum(i - half, 0), 0))] * count,
         out_specs=[by_rows(n) for n in lows]
@@ -735,6 +751,10 @@
             pltpu.VMEM((block, hidden_units), f32),
             pltpu.VMEM((block, chunk), f32),
             pltpu.VMEM((block, chunk), f32),
+            pltpu.VMEM(w_up.shape, bf16),
+            pltpu.VMEM(w_down.shape, bf16),
+            pltpu.VMEM(learn_in.shape, bf16),
+            pltpu.SemaphoreType.DMA((3,)),
         ],
         compiler_params=params(),
         cost_estimate=pl.CostEstimate(

time: 554 us -> 550 us (level)
  transfers between devices with their start and end apart: 47 -> 47, of which waited for: 12 -> 13; matrix products, arithmetic and copies ran while one was open for 13% -> 14% of each run, Pallas kernels for 40% -> 40%
where the time goes in v7:
time: 550 us; the launch traced here: 541 us
  Pallas kernels  343 us (62%)
  waiting for transfers between devices  72.6 us (13%)
  local copies, waits for them, and re-layouts  41.5 us (8%)
  starting transfers between devices  40.4 us (7%)
  other arithmetic  39.5 us (7%)
    pallas_call x1, Pallas kernels, rows_call(): pl.pallas_call(functools.partial(rows_kernel, count, splits, local_rows),...  87 us
    pallas_call x2, Pallas kernels, attend_back_call(): pl.pallas_call(functools.partial(attend_back_kernel, count, heads, split...  78.2 us
    ppermute x35, waiting for transfers between devices, jump(): return lax.ppermute(value, 'row', [(i, i ^ row_mask) for i in range(rows)])  51.8 us
    pallas_call x2, Pallas kernels, attend_call(): pl.pallas_call(functools.partial(attend_kernel, count, heads, start, len(...  47.2 us
    pallas_call x1, Pallas kernels, vectors_call(): pl.pallas_call(functools.partial(vectors_kernel, count, row_bits, img_bit...  30.2 us
    pallas_call x2, Pallas kernels, qkv_call(): pl.pallas_call(functools.partial(qkv_kernel, count, splits, local_rows, f...  24.9 us
    ppermute x35, starting transfers between devices, jump(): return lax.ppermute(value, 'row', [(i, i ^ row_mask) for i in range(rows)])  24.7 us
    convert_element_type x16, other arithmetic, finish(): return tree([v.astype(f32) for v in values]).astype(bf16)  23.8 us
  transfers between devices with their start and end apart: 47, of which 13 were waited for; matrix products, arithmetic and copies ran while one was open for 14% of the time, Pallas kernels for 40%

profile of v7, /device:TPU:0, one launch (start us, length us, event | category | flops | bytes accessed | tf_op | source)
XLA Modules:
  0.0 540.6 jit_solution(6150926708331927636)
XLA Ops:
  1.2 2.6 collective-permute-start
  6.7 1.7 constant_dynamic-slice_fusion.16
  8.4 1.5 pad_maximum_fusion.1.refs_2_
  9.9 1.3 constant_dynamic-slice_fusion.17.refs_8_
  12.7 12.5 %shard_map.297 = (bf16[4,1024,1024]{2,1,0:T(8,128)(2,1)}, bf16[16,2,128,256]{3,2,1,0:T(8,128)(2,1)}, bf16[16,2,128,256]{3,2,1,0:T(8,128)(2,1)}, bf16[16,2,128,25...) custom-call(s32[1]{0:T(128)} %bitcast.1.me_ref, bf16[1016,1024]{1,0:T(8,128)(2,1)} %bitcast.195, ...), custom_call_target="tpu_custom_call" | custom-call | flops 19327352832 | bytes 13631488 | tf_op jit(solution)/shard_map/pallas_call | solution.py:282
  25.2 24.6 %collective-permute-done.refs_0_ = bf16[1016,1024]{1,0:T(8,128)(2,1)S(1)} collective-permute-done((bf16[1016,1024]{1,0:T(8,128)(2,1)}, bf16[1016,1024]{1,0:T(8,128)(2,1)S(1)}, u32[]{:S(2)}, u32[]{:S(2)}) %collective-permute-start) | collective-permute-done | bytes 2080800 | tf_op jit(solution)/shard_map/ppermute | solution.py:67
  49.9 2.0 copy.77.refs_4_.refs_14_.refs_12_
  51.9 2.2 collective-permute-done.2.refs_1_
  54.1 12.5 %shard_map.298 = (bf16[4,1024,1024]{2,1,0:T(8,128)(2,1)}, bf16[16,2,128,256]{3,2,1,0:T(8,128)(2,1)}, bf16[16,2,128,256]{3,2,1,0:T(8,128)(2,1)}, bf16[16,2,128,25...) custom-call(s32[1]{0:T(128)} %bitcast.1.me_ref, ...), custom_call_target="tpu_custom_call", output_to_operand_aliasing={{0}: (12, {}), {1}: (13, {}), {2}: (14, {}), {3}: (15, {}),... | custom-call | flops 19327352832 | bytes 13631488 | tf_op jit(solution)/shard_map/pallas_call | solution.py:282
  66.6 1.8 collective-permute-start.4
  68.4 23.3 %shard_map.299 = (bf16[512,256]{1,0:T(8,128)(2,1)}, bf16[512,256]{1,0:T(8,128)(2,1)}, bf16[512,256]{1,0:T(8,128)(2,1)}, bf16[512,256]{1,0:T(8,128)(2,1)}, f32[16,256,256]{2,1,0:T(8,128)}, /*index=5*/f32[8,4096]{1,0:T(8,128)}) custom-call(s32[16]{0:T(128)} %get-tuple-element.139.lo_ref, s32[16]{0:T(128)} %get-tuple-element.140.hi_ref, ...), custom_call_target="tpu_custom_call" | custom-call | flops 21474836480 | bytes 12582912 | tf_op jit(solution)/shard_map/pallas_call | solution.py:389
  92.5 1.2 collective-permute-start.8
  93.7 23.9 %shard_map.300 = (bf16[512,256]{1,0:T(8,128)(2,1)}, bf16[512,256]{1,0:T(8,128)(2,1)}, bf16[512,256]{1,0:T(8,128)(2,1)}, bf16[512,256]{1,0:T(8,128)(2,1)}, f32[16,256,256]{2,1,0:T(8,128)}, /*index=5*/f32[8,4096]{1,0:T(8,128)}) custom-call(s32[16]{0:T(128)} %get-tuple-element.139.lo_ref, ...), custom_call_target="tpu_custom_call", output_to_operand_aliasing={{4}: (7, {}), {5}: (8, {})} | custom-call | flops 21474836480 | bytes 12582912 | tf_op jit(solution)/shard_map/pallas_call | solution.py:389
  118.7 1.1 collective-permute-start.11
  124.8 3.1 collective-permute-done.10.refs_17_.refs_11_
  127.9 3.8 collective-permute-done.11.refs_18_.refs_12_
  132.5 87.0 %shard_map.301 = (bf16[1024,1024]{1,0:T(8,128)(2,1)}, bf16[1024,4096]{1,0:T(8,128)(2,1)}, bf16[1024,4096]{1,0:T(8,128)(2,1)}, bf16[1024,1024]{1,0:T(8,128)(2,1)}...) custom-call(bf16[1016,1024]{1,0:T(8,128)(2,1)} %bitcast.196, ...), custom_call_target="tpu_custom_call" | custom-call | flops 42949672960 | bytes 58720256 | tf_op jit(solution)/shard_map/pallas_call | solution.py:733
  219.5 11.5 %shard_map.302 = (bf16[1024,1024]{1,0:T(8,128)(2,1)}, bf16[1024,1024]{1,0:T(8,128)(2,1)}, f32[1024,64]{1,0:T(8,128)}) custom-call(s32[1]{0:T(128)} %bitcast.1.me_ref, bf16[1024,1024]{1,0:T(8,128)(2,1)} %get-tuple-element.180.refs_0_, bf16[1024,1024]{1,0:T(8,128)(2,1)} %get-tuple-element.181.refs_1_, bf16[1024,1024]{1,0:T(8,128)(2,1)} %get-tuple-element.182.refs_2_, ...), custom_call_target="tpu_custom_call" | custom-call | flops 6442450944 | bytes 20971520 | tf_op jit(solution)/shard_map/pallas_call | solution.py:882
  231.0 13.9 %shard_map.303 = (bf16[4096,512]{1,0:T(8,128)(2,1)}, bf16[4096,512]{1,0:T(8,128)(2,1)}) custom-call(s32[1]{0:T(128)} %bitcast.1.me_ref, bf16[1024,4096]{1,0:T(8,128)(2,1)} %get-tuple-element.187.left_ref, bf16[1024,1024]{1,0:T(8,128)(2,1)} %get-tuple-element.188.right_ref, bf16[1024,1024]{1,0:T(8,128)(2,1)} %get-tuple-element.186.refs_0_), custom_call_target="tpu_custom_call" | custom-call | flops 12884901888 | bytes 16777216 | tf_op jit(solution)/shard_map/pallas_call | solution.py:784
  249.1 1.1 collective-permute-start.14
  253.3 14.7 %shard_map.304 = (bf16[1024,2048]{1,0:T(8,128)(2,1)}, bf16[1024,2048]{1,0:T(8,128)(2,1)}) custom-call(s32[1]{0:T(128)} %bitcast.1.me_ref, bf16[1024,1024]{1,0:T(8,128)(2,1)} %get-tuple-element.190.left_ref, bf16[1024,4096]{1,0:T(8,128)(2,1)} %get-tuple-element.191.right_ref, bf16[4096,512]{1,0:T(8,128)(2,1)} %get-tuple-element.189.refs_0_), custom_call_target="tpu_custom_call" | custom-call | flops 12884901888 | bytes 16777216 | tf_op jit(solution)/shard_map/pallas_call | solution.py:826
  268.7 4.8 add_convert_fusion.1
  275.5 1.5 constant_dynamic-slice_fusion.11
  277.3 5.0 collective-permute-start.18
  282.3 39.2 %shard_map.305 = (bf16[2,1024,384]{2,1,0:T(8,128)(2,1)}, bf16[2,1024,384]{2,1,0:T(8,128)(2,1)}, f32[8,128]{1,0:T(8,128)}) custom-call(s32[16]{0:T(128)} %get-tuple-element.139.lo_ref, s32[16]{0:T(128)} %get-tuple-element.140.hi_ref, bf16[1024,128]{1,0:T(8,128)(2,1)} %get-tuple-element.176.refs_0_, bf16[1024,128]{1,0:T(8,128)(2,1)} %collective-permute-done.12.refs_1_, ...), custom_call_target="tpu_custom_call" | custom-call | flops 34359738368 | bytes 12582912 | tf_op jit(solution)/shard_map/pallas_call | solution.py:519
  322.2 2.1 slice.193
  325.9 2.6 collective-permute-done.18
  328.6 1.6 add_convert_fusion.7
  331.0 1.7 collective-permute-start.22
  332.8 2.2 add_convert_fusion.3.refs_6_
  335.0 6.8 %add_convert_fusion = bf16[1024,2048]{1,0:T(8,128)(2,1)} fusion(bf16[1024,2048]{1,0:T(8,128)(2,1)} %collective-permute-done.19, bf16[1024,2048]{1,0:T(8,128)(2,1)S(1)} %copy-done.10), kind=kLoop, calls=%fused_computation.3 | loop fusion | flops 8388608 | bytes 12582912 | tf_op jit(solution)/shard_map/convert_element_type | solution.py:136
  342.8 10.0 %shard_map.306 = (bf16[1024,384]{1,0:T(8,128)(2,1)}, f32[1024,2]{1,0:T(8,128)}) custom-call(s32[1]{0:T(128)} %bitcast.1.me_ref, bf16[4,1024,1024]{2,1,0:T(8,128)(2,1)} %get-tuple-element.150.n_ref, f32[1024,1]{1,0:T(8,128)} %copy.82.gain_ref, f32[1024,1]{1,0:T(8,128)} %copy.83.shift_ref, bf16[2,1024,384]{2,1,0:T(8,128)(2,1)} %get-tuple-element.200.refs_0_, ...), custom_call_target="tpu_custom_call" | custom-call | flops 17179869184 | bytes 1024 | tf_op jit(solution)/shard_map/pallas_call | solution.py:930
  352.9 3.2 constant_dynamic-slice_fusion.10
  356.0 3.6 collective-permute-start.21
  360.2 39.1 %shard_map.307 = (bf16[2,1024,384]{2,1,0:T(8,128)(2,1)}, bf16[2,1024,384]{2,1,0:T(8,128)(2,1)}, f32[8,128]{1,0:T(8,128)}) custom-call(s32[16]{0:T(128)} %get-tuple-element.139.lo_ref, s32[16]{0:T(128)} %get-tuple-element.140.hi_ref, bf16[1024,128]{1,0:T(8,128)(2,1)} %get-tuple-element.207.refs_0_, bf16[1024,128]{1,0:T(8,128)(2,1)} %collective-permute-done.24.refs_1_, ...), custom_call_target="tpu_custom_call" | custom-call | flops 34359738368 | bytes 12582912 | tf_op jit(solution)/shard_map/pallas_call | solution.py:519
  399.3 1.6 collective-permute-start.28
  401.5 2.1 slice.195
  403.7 1.3 collective-permute-done.21
  405.1 1.5 collective-permute-done.20
  406.6 2.4 add_convert_fusion.2.refs_5_
  409.6 1.7 copy-done.5
  411.3 1.5 add_convert_fusion.6.refs_6_
  415.0 10.0 %shard_map.308 = (bf16[1024,384]{1,0:T(8,128)(2,1)}, f32[1024,2]{1,0:T(8,128)}) custom-call(s32[1]{0:T(128)} %bitcast.1.me_ref, bf16[4,1024,1024]{2,1,0:T(8,128)(2,1)} %get-tuple-element.150.n_ref, f32[1024,1]{1,0:T(8,128)} %copy.82.gain_ref, f32[1024,1]{1,0:T(8,128)} %copy.83.shift_ref, bf16[2,1024,384]{2,1,0:T(8,128)(2,1)} %get-tuple-element.214.refs_0_.refs_2_, ...), custom_call_target="tpu_custom_call" | custom-call | flops 17179869184 | bytes 1024 | tf_op jit(solution)/shard_map/pallas_call | solution.py:930
  425.0 1.2 slice.194
  426.2 8.6 %collective-permute-done.28.refs_3_ = bf16[2,1024,384]{2,1,0:T(8,128)(2,1)} collective-permute-done((bf16[2,1024,384]{2,1,0:T(8,128)(2,1)}, bf16[2,1024,384]{2,1,0:T(8,128)(2,1)}, u32[]{:S(2)}, u32[]{:S(2)}) %collective-permute-start.28) | collective-permute-done | bytes 1572896 | tf_op jit(solution)/shard_map/ppermute | solution.py:67
  434.8 8.2 %collective-permute-done.27 = bf16[2,1,1,128,2048]{4,3,2,1,0:T(8,128)(2,1)} collective-permute-done((bf16[2,1,1,128,2048]{4,3,2,1,0:T(8,128)(2,1)S(1)}, bf16[2,1,1,128,2048]{4,3,2,1,0:T(8,128)(2,1)}, u32[]{:S(2)}, u32[]{:S(2)}) %collective-permute-start.27) | collective-permute-done | bytes 1048608 | tf_op jit(solution)/shard_map/ppermute | solution.py:69
  443.0 1.2 add_bitcast_fusion
  445.5 1.9 collective-permute-start.35
  447.4 1.2 slice.196
  450.9 1.6 add_convert_fusion.5
  452.8 1.6 collective-permute-start.32
  454.3 30.2 %shard_map.309 = (f32[200,128]{1,0:T(8,128)S(1)}, f32[128,128]{1,0:T(8,128)S(1)}) custom-call(f32[200,128]{1,0:T(8,128)S(1)} %pad_bitcast_fusion.vec_ref, bf16[4,128,128]{2,1,0:T(8,128)(2,1)S(1)} %reshape.494.slot_ref), custom_call_target="tpu_custom_call" | custom-call | flops 17179869184 | bytes 1024 | tf_op jit(solution)/shard_map/pallas_call | solution.py:1064
  484.8 1.7 collective-permute-start.45
  487.1 1.7 collective-permute-start.37
  488.8 2.0 fusion.29
  491.2 15.4 %shard_map.310 = f32[1,1016,1024]{2,1,0:T(8,128)} custom-call(s32[1]{0:T(128)} %bitcast.1.me_ref, bf16[1016,1024]{1,0:T(8,128)(2,1)} %bitcast.197, f32[1024,1024]{1,0:T(8,128)} %get-tuple-element.242.ghid_ref, bf16[1024,3072]{1,0:T(8,128)(2,1)} %w_ref.1, f32[1,1024]{1,0:T(1,128)} %get-tuple-element.350.refs_9_.gain_ref, ...), custom_call_target="tpu_custom_call" | custom-call | flops 17179869184 | bytes 1024 | tf_op jit(solution)/shard_map/pallas_call | solution.py:981
  507.9 1.6 maximum_convert_fusion.1
  512.8 1.3 collective-permute-start.38
  518.2 7.1 %collective-permute-done.38 = bf16[1,1,1,128,768]{4,3,2,1,0:T(8,128)(2,1)S(1)} collective-permute-done((bf16[1,1,1,128,768]{4,3,2,1,0:T(8,128)(2,1)S(1)}, bf16[1,1,1,128,768]{4,3,2,1,0:T(8,128)(2,1)S(1)}, u32[]{:S(2)}, u32[]{:S(2)}) %collective-permute-start.38) | collective-permute-done | bytes 196640 | tf_op jit(solution)/shard_map/ppermute | solution.py:69
  525.4 1.5 collective-permute-start.40
  527.9 5.3 collective-permute-done.40
  533.2 3.3 collective-permute-done.41
  537.1 1.3 convert_element_type.281
  538.8 1.5 maximum_convert_fusion
  (291 shorter events, 46.5 us)
Async XLA Ops:
  0.6 49.3 %copy-start = (bf16[1024,8]{0,1:T(8,128)(2,1)S(1)}, bf16[1024,8]{0,1:T(8,128)(2,1)}, u32[]{:S(2)}) copy-start(bf16[1024,8]{0,1:T(8,128)(2,1)} %param.33) | copy-start | bytes 49156
  0.7 12.0 %collective-permute-start.1 = (bf16[1016,1024]{1,0:T(8,128)(2,1)}, bf16[1016,1024]{1,0:T(8,128)(2,1)}, u32[]{:S(2)}, u32[]{:S(2)}) collective-permute-start(bf16[1016,1024]{1,0:T(8,128)(2,1)} %bitcast.193), channel_id=1, source_target_pairs={{0,1},{1,0},{2,3},{3,2},{4,5},{5,4},{6,7},{7,6},{8,9},{9,8},{10,11... | collective-permute-start | bytes 6242312 | tf_op jit(solution)/shard_map/ppermute | solution.py:67
  1.2 48.6 %collective-permute-start = (bf16[1016,1024]{1,0:T(8,128)(2,1)}, bf16[1016,1024]{1,0:T(8,128)(2,1)S(1)}, u32[]{:S(2)}, u32[]{:S(2)}) collective-permute-start(bf16[1016,1024]{1,0:T(8,128)(2,1)} %bitcast.194), channel_id=1, source_target_pairs={{0,2},{1,3},{2,0},{3,1},{4,6},{5,7},{6,4},{7,5},{8,10},{9,11},{10,... | collective-permute-start | bytes 6242312 | tf_op jit(solution)/shard_map/ppermute | solution.py:67
  12.7 37.1 %copy-start.25 = (f32[1,2,8,1024]{3,2,1,0:T(8,128)S(1)}, f32[1,2,8,1024]{3,2,1,0:T(8,128)}, u32[]{:S(2)}) copy-start(f32[1,2,8,1024]{3,2,1,0:T(8,128)} %param.35) | copy-start | bytes 196612
  12.7 37.2 %copy-start.38 = (s32[1,8]{1,0:T(1,128)S(1)}, s32[1,8]{1,0:T(1,128)}, u32[]{:S(2)}) copy-start(s32[1,8]{1,0:T(1,128)} %param.19) | copy-start | bytes 100
  49.8 4.3 collective-permute-start.2
  66.6 51.0 %collective-permute-start.4 = (bf16[2,8192]{1,0:T(2,128)(2,1)S(1)}, bf16[2,8192]{1,0:T(2,128)(2,1)S(1)}, u32[]{:S(2)}, u32[]{:S(2)}) collective-permute-start(bf16[2,8192]{1,0:T(2,128)(2,1)S(1)} %bitcast.170), channel_id=1, source_target_pairs={{0,2},{1,3},{2,0},{3,1},{4,6},{5,7},{6,4},{7,5},{8,10},{9,11},{10,... | collective-permute-start | bytes 98312 | tf_op jit(solution)/shard_map/ppermute | solution.py:67
  68.4 55.4 %collective-permute-start.3 = (bf16[2,8192]{1,0:T(2,128)(2,1)S(1)}, bf16[2,8192]{1,0:T(2,128)(2,1)S(1)}, u32[]{:S(2)}, u32[]{:S(2)}) collective-permute-start(bf16[2,8192]{1,0:T(2,128)(2,1)S(1)} %bitcast.171), channel_id=1, source_target_pairs={{0,1},{1,0},{2,3},{3,2},{4,5},{5,4},{6,7},{7,6},{8,9},{9,8},{10,11... | collective-permute-start | bytes 98312 | tf_op jit(solution)/shard_map/ppermute | solution.py:67
  91.7 26.7 %collective-permute-start.6 = (bf16[512,256]{1,0:T(8,128)(2,1)}, bf16[512,256]{1,0:T(8,128)(2,1)S(1)}, u32[]{:S(2)}, u32[]{:S(2)}) collective-permute-start(bf16[512,256]{1,0:T(8,128)(2,1)} %get-tuple-element.158), channel_id=1, source_target_pairs={{0,1},{1,0},{2,3},{3,2},{4,5},{5,4},{6,7},{7,6},{8,9},{9,8},{10,11... | collective-permute-start | bytes 786440 | tf_op jit(solution)/shard_map/ppermute | solution.py:67
  92.3 26.1 %collective-permute-start.7 = (bf16[512,256]{1,0:T(8,128)(2,1)}, bf16[512,256]{1,0:T(8,128)(2,1)S(1)}, u32[]{:S(2)}, u32[]{:S(2)}) collective-permute-start(bf16[512,256]{1,0:T(8,128)(2,1)} %get-tuple-element.159), channel_id=1, source_target_pairs={{0,2},{1,3},{2,0},{3,1},{4,6},{5,7},{6,4},{7,5},{8,10},{9,11},{10,... | collective-permute-start | bytes 786440 | tf_op jit(solution)/shard_map/ppermute | solution.py:67
  92.5 25.9 %collective-permute-start.8 = (bf16[512,256]{1,0:T(8,128)(2,1)}, bf16[512,256]{1,0:T(8,128)(2,1)S(1)}, u32[]{:S(2)}, u32[]{:S(2)}) collective-permute-start(bf16[512,256]{1,0:T(8,128)(2,1)} %get-tuple-element.160), channel_id=1, source_target_pairs={{0,3},{1,2},{2,1},{3,0},{4,7},{5,6},{6,5},{7,4},{8,11},{9,10},{10,... | collective-permute-start | bytes 786440 | tf_op jit(solution)/shard_map/ppermute | solution.py:67
  93.7 26.9 %copy-start.46 = (s32[1,8]{1,0:T(1,128)S(1)}, s32[1,8]{1,0:T(1,128)}, u32[]{:S(2)}) copy-start(s32[1,8]{1,0:T(1,128)} %param.20) | copy-start | bytes 100
  93.7 27.8 %copy-start.36 = (f32[8]{0:T(128)S(1)}, f32[8]{0:T(128)}, u32[]{:S(2)}) copy-start(f32[8]{0:T(128)} %param.34) | copy-start | bytes 100
  93.7 28.4 %copy-start.32 = (f32[1024]{0:T(1024)S(1)}, f32[1024]{0:T(1024)}, u32[]{:S(2)}) copy-start(f32[1024]{0:T(1024)} %param.24) | copy-start | bytes 12292
  93.7 28.4 %copy-start.33 = (f32[1024]{0:T(1024)S(1)}, f32[1024]{0:T(1024)}, u32[]{:S(2)}) copy-start(f32[1024]{0:T(1024)} %param.28) | copy-start | bytes 12292
  93.7 28.4 %copy-start.34 = (f32[1024]{0:T(1024)S(1)}, f32[1024]{0:T(1024)}, u32[]{:S(2)}) copy-start(f32[1024]{0:T(1024)} %param.32) | copy-start | bytes 12292
  117.6 6.2 %collective-permute-start.5 = (bf16[2,8192]{1,0:T(2,128)(2,1)S(1)}, bf16[2,8192]{1,0:T(2,128)(2,1)S(1)}, u32[]{:S(2)}, u32[]{:S(2)}) collective-permute-start(bf16[2,8192]{1,0:T(2,128)(2,1)S(1)} %collective-permute-done.4), channel_id=1, source_target_pairs={{0,1},{1,0},{2,3},{3,2},{4,5},{5,4},{6,7},{7,6},{8,9},{9,8},{10,11... | collective-permute-start | bytes 98312 | tf_op jit(solution)/shard_map/ppermute | solution.py:67
  118.4 13.3 %copy-start.40 = (bf16[512,256]{1,0:T(8,128)(2,1)}, bf16[512,256]{1,0:T(8,128)(2,1)S(1)}, u32[]{:S(2)}) copy-start(bf16[512,256]{1,0:T(8,128)(2,1)S(1)} %collective-permute-done.6.refs_12_.refs_6_) | copy-start | bytes 786436
  118.4 13.3 %copy-start.41 = (bf16[512,256]{1,0:T(8,128)(2,1)}, bf16[512,256]{1,0:T(8,128)(2,1)S(1)}, u32[]{:S(2)}) copy-start(bf16[512,256]{1,0:T(8,128)(2,1)S(1)} %collective-permute-done.7.refs_13_.refs_7_) | copy-start | bytes 786436
  118.4 13.2 %copy-start.42 = (bf16[512,256]{1,0:T(8,128)(2,1)}, bf16[512,256]{1,0:T(8,128)(2,1)S(1)}, u32[]{:S(2)}) copy-start(bf16[512,256]{1,0:T(8,128)(2,1)S(1)} %collective-permute-done.8.refs_14_.refs_8_) | copy-start | bytes 786436
  118.4 9.4 %collective-permute-start.10 = (bf16[512,256]{1,0:T(8,128)(2,1)}, bf16[512,256]{1,0:T(8,128)(2,1)S(1)}, u32[]{:S(2)}, u32[]{:S(2)}) collective-permute-start(bf16[512,256]{1,0:T(8,128)(2,1)} %get-tuple-element.174), channel_id=1, source_target_pairs={{0,2},{1,3},{2,0},{3,1},{4,6},{5,7},{6,4},{7,5},{8,10},{9,11},{10,... | collective-permute-start | bytes 786440 | tf_op jit(solution)/shard_map/ppermute | solution.py:67
  118.7 12.9 %collective-permute-start.11 = (bf16[512,256]{1,0:T(8,128)(2,1)}, bf16[512,256]{1,0:T(8,128)(2,1)S(1)}, u32[]{:S(2)}, u32[]{:S(2)}) collective-permute-start(bf16[512,256]{1,0:T(8,128)(2,1)} %get-tuple-element.175), channel_id=1, source_target_pairs={{0,3},{1,2},{2,1},{3,0},{4,7},{5,6},{6,5},{7,4},{8,11},{9,10},{10,... | collective-permute-start | bytes 786440 | tf_op jit(solution)/shard_map/ppermute | solution.py:67
  119.9 11.8 %collective-permute-start.9 = (bf16[512,256]{1,0:T(8,128)(2,1)}, bf16[512,256]{1,0:T(8,128)(2,1)S(1)}, u32[]{:S(2)}, u32[]{:S(2)}) collective-permute-start(bf16[512,256]{1,0:T(8,128)(2,1)} %get-tuple-element.173), channel_id=1, source_target_pairs={{0,1},{1,0},{2,3},{3,2},{4,5},{5,4},{6,7},{7,6},{8,9},{9,8},{10,11... | collective-permute-start | bytes 786440 | tf_op jit(solution)/shard_map/ppermute | solution.py:67
  231.0 14.4 %copy-start.28 = (f32[1024,1]{0,1:T(1,128)S(1)}, f32[1024,1]{0,1:T(1,128)}, u32[]{:S(2)}) copy-start(f32[1024,1]{0,1:T(1,128)} %get-tuple-element.351) | copy-start | bytes 12292
  231.0 15.4 %copy-start.27 = (f32[1024,1]{0,1:T(1,128)S(1)}, f32[1024,1]{0,1:T(1,128)}, u32[]{:S(2)}) copy-start(f32[1024,1]{0,1:T(1,128)} %get-tuple-element.335) | copy-start | bytes 12292
  231.0 19.2 %copy-start.19 = (f32[1024,64]{1,0:T(8,128)S(1)}, f32[1024,64]{1,0:T(8,128)}, u32[]{:S(2)}) copy-start(f32[1024,64]{1,0:T(8,128)} %get-tuple-element.228) | copy-start | bytes 786436
  244.9 23.8 %collective-permute-start.16 = (bf16[4096,512]{1,0:T(8,128)(2,1)}, bf16[4096,512]{1,0:T(8,128)(2,1)}, u32[]{:S(2)}, u32[]{:S(2)}) collective-permute-start(bf16[4096,512]{1,0:T(8,128)(2,1)} %get-tuple-element.189.refs_0_), channel_id=1, source_target_pairs={{0,1},{1,0},{2,3},{3,2},{4,5},{5,4},{6,7},{7,6},{8,9},{9,8},{10,11... | collective-permute-start | bytes 12582920 | tf_op jit(solution)/shard_map/ppermute | solution.py:67
  247.5 20.5 %collective-permute-start.15 = (bf16[1024,1024]{1,0:T(8,128)(2,1)}, bf16[1024,1024]{1,0:T(8,128)(2,1)S(1)}, u32[]{:S(2)}, u32[]{:S(2)}) collective-permute-start(bf16[1024,1024]{1,0:T(8,128)(2,1)} %get-tuple-element.186.refs_0_), channel_id=1, source_target_pairs={{0,1},{1,0},{2,3},{3,2},{4,5},{5,4},{6,7},{7,6},{8,9},{9,8},{10,11... | collective-permute-start | bytes 6291464 | tf_op jit(solution)/shard_map/ppermute | solution.py:67
  248.4 28.6 %collective-permute-start.12 = (bf16[1024,128]{1,0:T(8,128)(2,1)}, bf16[1024,128]{1,0:T(8,128)(2,1)}, u32[]{:S(2)}, u32[]{:S(2)}) collective-permute-start(bf16[1024,128]{1,0:T(8,128)(2,1)} %get-tuple-element.177), channel_id=1, source_target_pairs={{0,1},{1,0},{2,3},{3,2},{4,5},{5,4},{6,7},{7,6},{8,9},{9,8},{10,11... | collective-permute-start | bytes 786440 | tf_op jit(solution)/shard_map/ppermute | solution.py:67
  248.7 28.6 %collective-permute-start.13 = (bf16[1024,128]{1,0:T(8,128)(2,1)}, bf16[1024,128]{1,0:T(8,128)(2,1)}, u32[]{:S(2)}, u32[]{:S(2)}) collective-permute-start(bf16[1024,128]{1,0:T(8,128)(2,1)} %get-tuple-element.178), channel_id=1, source_target_pairs={{0,2},{1,3},{2,0},{3,1},{4,6},{5,7},{6,4},{7,5},{8,10},{9,11},{10,... | collective-permute-start | bytes 786440 | tf_op jit(solution)/shard_map/ppermute | solution.py:67
  249.1 33.2 %collective-permute-start.14 = (bf16[1024,128]{1,0:T(8,128)(2,1)}, bf16[1024,128]{1,0:T(8,128)(2,1)}, u32[]{:S(2)}, u32[]{:S(2)}) collective-permute-start(bf16[1024,128]{1,0:T(8,128)(2,1)} %get-tuple-element.179), channel_id=1, source_target_pairs={{0,3},{1,2},{2,1},{3,0},{4,7},{5,6},{6,5},{7,4},{8,11},{9,10},{10,... | collective-permute-start | bytes 786440 | tf_op jit(solution)/shard_map/ppermute | solution.py:67
  268.0 56.3 %collective-permute-start.19 = (bf16[1024,2048]{1,0:T(8,128)(2,1)}, bf16[1024,2048]{1,0:T(8,128)(2,1)}, u32[]{:S(2)}, u32[]{:S(2)}) collective-permute-start(bf16[1024,2048]{1,0:T(8,128)(2,1)} %get-tuple-element.192.refs_6_), channel_id=1, source_target_pairs={{0,1},{1,0},{2,3},{3,2},{4,5},{5,4},{6,7},{7,6},{8,9},{9,8},{10,11... | collective-permute-start | bytes 12582920 | tf_op jit(solution)/shard_map/ppermute | solution.py:67
  268.6 87.4 %collective-permute-start.24 = (bf16[1024,128]{1,0:T(8,128)(2,1)}, bf16[1024,128]{1,0:T(8,128)(2,1)}, u32[]{:S(2)}, u32[]{:S(2)}) collective-permute-start(bf16[1024,128]{1,0:T(8,128)(2,1)} %get-tuple-element.208), channel_id=1, source_target_pairs={{0,1},{1,0},{2,3},{3,2},{4,5},{5,4},{6,7},{7,6},{8,9},{9,8},{10,11... | collective-permute-start | bytes 786440 | tf_op jit(solution)/shard_map/ppermute | solution.py:67
  276.9 82.7 %collective-permute-start.25 = (bf16[1024,128]{1,0:T(8,128)(2,1)}, bf16[1024,128]{1,0:T(8,128)(2,1)}, u32[]{:S(2)}, u32[]{:S(2)}) collective-permute-start(bf16[1024,128]{1,0:T(8,128)(2,1)} %get-tuple-element.209), channel_id=1, source_target_pairs={{0,2},{1,3},{2,0},{3,1},{4,6},{5,7},{6,4},{7,5},{8,10},{9,11},{10,... | collective-permute-start | bytes 786440 | tf_op jit(solution)/shard_map/ppermute | solution.py:67
  277.3 51.2 %collective-permute-start.18 = (bf16[2,1,2,512,512]{4,3,2,1,0:T(8,128)(2,1)}, bf16[2,1,2,512,512]{4,3,2,1,0:T(8,128)(2,1)}, u32[]{:S(2)}, u32[]{:S(2)}) collective-permute-start(bf16[2,1,2,512,512]{4,3,2,1,0:T(8,128)(2,1)} %constant_dynamic-slice_fusion.11), channel_id=1, source_target_pairs={{0,8},{4,12},{8,0},{12,4},{16,24},{20,28},{24,16},{28,20},{1,9},{5... | collective-permute-start | bytes 6291464 | tf_op jit(solution)/shard_map/ppermute | solution.py:69
  282.3 43.0 %collective-permute-start.17 = (bf16[2,2,1,128,1024]{4,3,2,1,0:T(8,128)(2,1)S(1)}, bf16[2,2,1,128,1024]{4,3,2,1,0:T(8,128)(2,1)}, u32[]{:S(2)}, u32[]{:S(2)}) collective-permute-start(bf16[2,2,1,128,1024]{4,3,2,1,0:T(8,128)(2,1)S(1)} %constant_dynamic-slice_fusion.12), channel_id=1, source_target_pairs={{0,4},{4,0},{8,12},{12,8},{16,20},{20,16},{24,28},{28,24},{1,5},{5... | collective-permute-start | bytes 3145736 | tf_op jit(solution)/shard_map/ppermute | solution.py:69
  282.3 46.3 %copy-start.9 = (bf16[1024,1024]{1,0:T(8,128)(2,1)S(1)}, bf16[1024,1024]{1,0:T(8,128)(2,1)}, u32[]{:S(2)}) copy-start(bf16[1024,1024]{1,0:T(8,128)(2,1)} %copy-done.8) | copy-start | bytes 6291460
  324.3 35.9 %collective-permute-start.26 = (bf16[1024,128]{1,0:T(8,128)(2,1)}, bf16[1024,128]{1,0:T(8,128)(2,1)}, u32[]{:S(2)}, u32[]{:S(2)}) collective-permute-start(bf16[1024,128]{1,0:T(8,128)(2,1)} %get-tuple-element.210), channel_id=1, source_target_pairs={{0,3},{1,2},{2,1},{3,0},{4,7},{5,6},{6,5},{7,4},{8,11},{9,10},{10,... | collective-permute-start | bytes 786440 | tf_op jit(solution)/shard_map/ppermute | solution.py:67
  325.3 78.4 %collective-permute-start.23 = (bf16[2,1024,384]{2,1,0:T(8,128)(2,1)}, bf16[2,1024,384]{2,1,0:T(8,128)(2,1)}, u32[]{:S(2)}, u32[]{:S(2)}) collective-permute-start(bf16[2,1024,384]{2,1,0:T(8,128)(2,1)} %get-tuple-element.206.refs_1_), channel_id=1, source_target_pairs={{0,2},{1,3},{2,0},{3,1},{4,6},{5,7},{6,4},{7,5},{8,10},{9,11},{10,... | collective-permute-start | bytes 4718600 | tf_op jit(solution)/shard_map/ppermute | solution.py:67
  331.0 72.7 %collective-permute-start.22 = (bf16[2,1,1,128,1024]{4,3,2,1,0:T(8,128)(2,1)}, bf16[2,1,1,128,1024]{4,3,2,1,0:T(8,128)(2,1)S(1)}, u32[]{:S(2)}, u32[]{:S(2)}) collective-permute-start(bf16[2,1,1,128,1024]{4,3,2,1,0:T(8,128)(2,1)} %constant_dynamic-slice_fusion.8), channel_id=1, source_target_pairs={{0,8},{4,12},{8,0},{12,4},{16,24},{20,28},{24,16},{28,20},{1,9},{5... | collective-permute-start | bytes 1572872 | tf_op jit(solution)/shard_map/ppermute | solution.py:69
  356.0 49.0 %collective-permute-start.21 = (bf16[1,1,2,512,512]{4,3,2,1,0:T(8,128)(2,1)}, bf16[1,1,2,512,512]{4,3,2,1,0:T(8,128)(2,1)}, u32[]{:S(2)}, u32[]{:S(2)}) collective-permute-start(bf16[1,1,2,512,512]{4,3,2,1,0:T(8,128)(2,1)} %constant_dynamic-slice_fusion.9), channel_id=1, source_target_pairs={{0,16},{4,20},{8,24},{12,28},{16,0},{20,4},{24,8},{28,12},{1,17},{... | collective-permute-start | bytes 3145736 | tf_op jit(solution)/shard_map/ppermute | solution.py:69
  359.6 47.0 %collective-permute-start.20 = (bf16[2,2,1,128,2048]{4,3,2,1,0:T(8,128)(2,1)}, bf16[2,2,1,128,2048]{4,3,2,1,0:T(8,128)(2,1)S(1)}, u32[]{:S(2)}, u32[]{:S(2)}) collective-permute-start(bf16[2,2,1,128,2048]{4,3,2,1,0:T(8,128)(2,1)} %constant_dynamic-slice_fusion.10), channel_id=1, source_target_pairs={{0,4},{4,0},{8,12},{12,8},{16,20},{20,16},{24,28},{28,24},{1,5},{5... | collective-permute-start | bytes 6291464 | tf_op jit(solution)/shard_map/ppermute | solution.py:69
  399.3 35.5 %collective-permute-start.28 = (bf16[2,1024,384]{2,1,0:T(8,128)(2,1)}, bf16[2,1024,384]{2,1,0:T(8,128)(2,1)}, u32[]{:S(2)}, u32[]{:S(2)}) collective-permute-start(bf16[2,1024,384]{2,1,0:T(8,128)(2,1)} %get-tuple-element.216.refs_1_), channel_id=1, source_target_pairs={{0,2},{1,3},{2,0},{3,1},{4,6},{5,7},{6,4},{7,5},{8,10},{9,11},{10,... | collective-permute-start | bytes 4718600 | tf_op jit(solution)/shard_map/ppermute | solution.py:67
  409.2 25.6 %collective-permute-start.30 = (bf16[1,1,1,128,1024]{4,3,2,1,0:T(8,128)(2,1)S(1)}, bf16[1,1,1,128,1024]{4,3,2,1,0:T(8,128)(2,1)}, u32[]{:S(2)}, u32[]{:S(2)}) collective-permute-start(bf16[1,1,1,128,1024]{4,3,2,1,0:T(8,128)(2,1)S(1)} %constant_dynamic-slice_fusion.5), channel_id=1, source_target_pairs={{0,16},{4,20},{8,24},{12,28},{16,0},{20,4},{24,8},{28,12},{1,17},{... | collective-permute-start | bytes 786440 | tf_op jit(solution)/shard_map/ppermute | solution.py:69
  413.7 21.1 %collective-permute-start.29 = (bf16[1,1,1,512,512]{4,3,2,1,0:T(8,128)(2,1)}, bf16[1,1,1,512,512]{4,3,2,1,0:T(8,128)(2,1)S(1)}, u32[]{:S(2)}, u32[]{:S(2)}) collective-permute-start(bf16[1,1,1,512,512]{4,3,2,1,0:T(8,128)(2,1)} %constant_dynamic-slice_fusion.6), channel_id=1, source_target_pairs={{0,4},{4,0},{8,12},{12,8},{16,20},{20,16},{24,28},{28,24},{1,5},{5... | collective-permute-start | bytes 1572872 | tf_op jit(solution)/shard_map/ppermute | solution.py:69
  414.4 28.6 %copy-start.18 = (f32[1024,2]{1,0:T(8,128)S(1)}, f32[1024,2]{1,0:T(8,128)}, u32[]{:S(2)}) copy-start(f32[1024,2]{1,0:T(8,128)} %get-tuple-element.229) | copy-start | bytes 24580
  414.4 28.6 %collective-permute-start.27 = (bf16[2,1,1,128,2048]{4,3,2,1,0:T(8,128)(2,1)S(1)}, bf16[2,1,1,128,2048]{4,3,2,1,0:T(8,128)(2,1)}, u32[]{:S(2)}, u32[]{:S(2)}) collective-permute-start(bf16[2,1,1,128,2048]{4,3,2,1,0:T(8,128)(2,1)S(1)} %constant_dynamic-slice_fusion.7), channel_id=1, source_target_pairs={{0,8},{4,12},{8,0},{12,4},{16,24},{20,28},{24,16},{28,20},{1,9},{5... | collective-permute-start | bytes 3145736 | tf_op jit(solution)/shard_map/ppermute | solution.py:69
  434.8 8.2 %copy-start.20 = (bf16[1,1,1,512,512]{4,3,2,1,0:T(8,128)(2,1)}, bf16[1,1,1,512,512]{4,3,2,1,0:T(8,128)(2,1)S(1)}, u32[]{:S(2)}) copy-start(bf16[1,1,1,512,512]{4,3,2,1,0:T(8,128)(2,1)S(1)} %collective-permute-done.29) | copy-start | bytes 1572868
  445.5 39.1 %collective-permute-start.35 = (bf16[1,1,1,128,1024]{4,3,2,1,0:T(8,128)(2,1)S(1)}, bf16[1,1,1,128,1024]{4,3,2,1,0:T(8,128)(2,1)S(1)}, u32[]{:S(2)}, u32[]{:S(2)}) collective-permute-start(bf16[1,1,1,128,1024]{4,3,2,1,0:T(8,128)(2,1)S(1)} %add_convert_fusion.16), channel_id=1, source_target_pairs={{0,2},{1,3},{2,0},{3,1},{4,6},{5,7},{6,4},{7,5},{8,10},{9,11},{10,... | collective-permute-start | bytes 786440 | tf_op jit(solution)/shard_map/ppermute | solution.py:67
  449.2 35.4 %collective-permute-start.31 = (bf16[4,1024,384]{2,1,0:T(8,128)(2,1)S(1)}, bf16[4,1024,384]{2,1,0:T(8,128)(2,1)S(1)}, u32[]{:S(2)}, u32[]{:S(2)}) collective-permute-start(bf16[4,1024,384]{2,1,0:T(8,128)(2,1)S(1)} %pad_maximum_fusion), channel_id=1, source_target_pairs={{0,1},{1,0},{2,3},{3,2},{4,5},{5,4},{6,7},{7,6},{8,9},{9,8},{10,11... | collective-permute-start | bytes 9437192 | tf_op jit(solution)/shard_map/ppermute | solution.py:67
  450.2 34.4 %collective-permute-start.34 = (bf16[1,1,1,512,256]{4,3,2,1,0:T(8,128)(2,1)S(1)}, bf16[1,1,1,512,256]{4,3,2,1,0:T(8,128)(2,1)S(1)}, u32[]{:S(2)}, u32[]{:S(2)}) collective-permute-start(bf16[1,1,1,512,256]{4,3,2,1,0:T(8,128)(2,1)S(1)} %constant_dynamic-slice_fusion.3), channel_id=1, source_target_pairs={{0,2},{1,3},{2,0},{3,1},{4,6},{5,7},{6,4},{7,5},{8,10},{9,11},{10,... | collective-permute-start | bytes 786440 | tf_op jit(solution)/shard_map/ppermute | solution.py:67
  452.6 32.0 %collective-permute-start.33 = (bf16[1,1,1,128,2048]{4,3,2,1,0:T(8,128)(2,1)S(1)}, bf16[1,1,1,128,2048]{4,3,2,1,0:T(8,128)(2,1)S(1)}, u32[]{:S(2)}, u32[]{:S(2)}) collective-permute-start(bf16[1,1,1,128,2048]{4,3,2,1,0:T(8,128)(2,1)S(1)} %constant_dynamic-slice_fusion.4), channel_id=1, source_target_pairs={{0,16},{4,20},{8,24},{12,28},{16,0},{20,4},{24,8},{28,12},{1,17},{... | collective-permute-start | bytes 1572872 | tf_op jit(solution)/shard_map/ppermute | solution.py:69
  452.8 31.9 %collective-permute-start.32 = (bf16[2,2,1,128,768]{4,3,2,1,0:T(8,128)(2,1)S(1)}, bf16[2,2,1,128,768]{4,3,2,1,0:T(8,128)(2,1)S(1)}, u32[]{:S(2)}, u32[]{:S(2)}) collective-permute-start(bf16[2,2,1,128,768]{4,3,2,1,0:T(8,128)(2,1)S(1)} %fusion.2), channel_id=1, source_target_pairs={{0,4},{4,0},{8,12},{12,8},{16,20},{20,16},{24,28},{28,24},{1,5},{5... | collective-permute-start | bytes 2359304 | tf_op jit(solution)/shard_map/ppermute | solution.py:69
  484.7 21.9 %collective-permute-start.44 = (bf16[512,256]{1,0:T(8,128)(2,1)S(1)}, bf16[512,256]{1,0:T(8,128)(2,1)S(1)}, u32[]{:S(2)}, u32[]{:S(2)}) collective-permute-start(bf16[512,256]{1,0:T(8,128)(2,1)S(1)} %bitcast.156), channel_id=1, source_target_pairs={{0,1},{1,0},{2,3},{3,2},{4,5},{5,4},{6,7},{7,6},{8,9},{9,8},{10,11... | collective-permute-start | bytes 786440 | tf_op jit(solution)/shard_map/ppermute | solution.py:67
  484.8 21.9 %collective-permute-start.45 = (bf16[512,256]{1,0:T(8,128)(2,1)S(1)}, bf16[512,256]{1,0:T(8,128)(2,1)S(1)}, u32[]{:S(2)}, u32[]{:S(2)}) collective-permute-start(bf16[512,256]{1,0:T(8,128)(2,1)S(1)} %bitcast.157), channel_id=1, source_target_pairs={{0,2},{1,3},{2,0},{3,1},{4,6},{5,7},{6,4},{7,5},{8,10},{9,11},{10,... | collective-permute-start | bytes 786440 | tf_op jit(solution)/shard_map/ppermute | solution.py:67
  486.5 20.2 %collective-permute-start.46 = (bf16[512,256]{1,0:T(8,128)(2,1)S(1)}, bf16[512,256]{1,0:T(8,128)(2,1)}, u32[]{:S(2)}, u32[]{:S(2)}) collective-permute-start(bf16[512,256]{1,0:T(8,128)(2,1)S(1)} %bitcast.158), channel_id=1, source_target_pairs={{0,3},{1,2},{2,1},{3,0},{4,7},{5,6},{6,5},{7,4},{8,11},{9,10},{10,... | collective-permute-start | bytes 786440 | tf_op jit(solution)/shard_map/ppermute | solution.py:67
  487.1 23.3 %collective-permute-start.37 = (bf16[1,1,1,128,2048]{4,3,2,1,0:T(8,128)(2,1)S(1)}, bf16[1,1,1,128,2048]{4,3,2,1,0:T(8,128)(2,1)S(1)}, u32[]{:S(2)}, u32[]{:S(2)}) collective-permute-start(bf16[1,1,1,128,2048]{4,3,2,1,0:T(8,128)(2,1)S(1)} %add_convert_fusion.10), channel_id=1, source_target_pairs={{0,2},{1,3},{2,0},{3,1},{4,6},{5,7},{6,4},{7,5},{8,10},{9,11},{10,... | collective-permute-start | bytes 1572872 | tf_op jit(solution)/shard_map/ppermute | solution.py:67
  490.8 18.7 %collective-permute-start.36 = (bf16[2,1,1,128,768]{4,3,2,1,0:T(8,128)(2,1)S(1)}, bf16[2,1,1,128,768]{4,3,2,1,0:T(8,128)(2,1)S(1)}, u32[]{:S(2)}, u32[]{:S(2)}) collective-permute-start(bf16[2,1,1,128,768]{4,3,2,1,0:T(8,128)(2,1)S(1)} %constant_dynamic-slice_fusion.2), channel_id=1, source_target_pairs={{0,8},{4,12},{8,0},{12,4},{16,24},{20,28},{24,16},{28,20},{1,9},{5... | collective-permute-start | bytes 1179656 | tf_op jit(solution)/shard_map/ppermute | solution.py:69
  506.6 4.7 collective-permute-start.42
  510.6 27.8 %collective-permute-start.43 = (bf16[128,2048]{1,0:T(8,128)(2,1)S(1)}, bf16[128,2048]{1,0:T(8,128)(2,1)S(1)}, u32[]{:S(2)}, u32[]{:S(2)}) collective-permute-start(bf16[128,2048]{1,0:T(8,128)(2,1)S(1)} %get-tuple-element.316), channel_id=1, source_target_pairs={{0,1},{1,0},{2,3},{3,2},{4,5},{5,4},{6,7},{7,6},{8,9},{9,8},{10,11... | collective-permute-start | bytes 1572872 | tf_op jit(solution)/shard_map/ppermute | solution.py:67
  512.8 12.5 %collective-permute-start.38 = (bf16[1,1,1,128,768]{4,3,2,1,0:T(8,128)(2,1)S(1)}, bf16[1,1,1,128,768]{4,3,2,1,0:T(8,128)(2,1)S(1)}, u32[]{:S(2)}, u32[]{:S(2)}) collective-permute-start(bf16[1,1,1,128,768]{4,3,2,1,0:T(8,128)(2,1)S(1)} %constant_dynamic-slice_fusion.1), channel_id=1, source_target_pairs={{0,16},{4,20},{8,24},{12,28},{16,0},{20,4},{24,8},{28,12},{1,17},{... | collective-permute-start | bytes 589832 | tf_op jit(solution)/shard_map/ppermute | solution.py:69
  525.3 2.6 collective-permute-start.39
  525.4 7.8 %collective-permute-start.40 = (bf16[128,768]{1,0:T(8,128)(2,1)S(1)}, bf16[128,768]{1,0:T(8,128)(2,1)S(1)}, u32[]{:S(2)}, u32[]{:S(2)}) collective-permute-start(bf16[128,768]{1,0:T(8,128)(2,1)S(1)} %get-tuple-element.323), channel_id=1, source_target_pairs={{0,2},{1,3},{2,0},{3,1},{4,6},{5,7},{6,4},{7,5},{8,10},{9,11},{10,... | collective-permute-start | bytes 589832 | tf_op jit(solution)/shard_map/ppermute | solution.py:67
  526.9 9.6 %collective-permute-start.41 = (bf16[128,768]{1,0:T(8,128)(2,1)S(1)}, bf16[128,768]{1,0:T(8,128)(2,1)S(1)}, u32[]{:S(2)}, u32[]{:S(2)}) collective-permute-start(bf16[128,768]{1,0:T(8,128)(2,1)S(1)} %get-tuple-element.323), channel_id=1, source_target_pairs={{0,3},{1,2},{2,1},{3,0},{4,7},{5,6},{6,5},{7,4},{8,11},{9,10},{10,... | collective-permute-start | bytes 589832 | tf_op jit(solution)/shard_map/ppermute | solution.py:67
  (31 other events, 117.0 us)
